TPU v7x, 32 devices: a whole 2x2x4 slice. The times are simulated.
32 devices in a mesh: dp: 4 (over y, x), ctx: 8 (over z, core).
Axes of the slice: x: 2, y: 2, z: 4, core: 2. Of those that a mesh axis runs over, the one named last changes fastest.
Arguments:
- tokens: bfloat16 [8192, 2048], P(('dp', 'ctx')), may hold values from -6 to 6
- in_weight: bfloat16 [3, 2048, 2048], P(None, ('dp', 'ctx')), may hold values from -0.125 to 0.125
- short_taps: float32 [7, 3, 2048], replicated, may hold values from -2.4 to 2.4
- long_taps: bfloat16 [128, 128], replicated, may hold values from -0.5 to 0.5
- out_weight: bfloat16 [2048, 2048], P(('dp', 'ctx')), may hold values from -0.125 to 0.125
Outputs:
- block_out: bfloat16 [8192, 2048], P(('dp', 'ctx'))
All inputs are finite; a program needn't handle non-finite values.
Results may differ from a plain program's by a relative error of at most 0.0076.
Values may be sent and summed in bfloat16 or wider, within the bound.
No kernel may reach another device: no remote copies, remote signals or barrier semaphores. Data moves between devices by JAX's collectives and lax.ppermute only.
A program may use at most 128 MiB of HBM per device.

v0:
```python
import jax
import jax.numpy as jnp
from jax import lax
from jax.sharding import PartitionSpec as P

GSIZE = 16
SHORT = 7
TAPS = 128


def shifted(block, axis, distance):
    devices = range(lax.axis_size(axis))
    route = [(i - distance, i) for i in devices if i - distance in devices]
    return lax.ppermute(block, axis, route)


def featurize(extended, taps):
    length = extended.shape[1] - (SHORT - 1)
    total = jnp.zeros(extended.shape[:1] + (length,) + extended.shape[2:], jnp.float32)
    for j in range(SHORT):
        total = total + taps[j] * extended[:, SHORT - 1 - j : SHORT - 1 - j + length].astype(
            jnp.float32
        )
    return total


def toeplitz_tiles(filters, block_rows):
    group_count = filters.shape[0]
    reverse = filters[:, ::-1]
    span = block_rows + TAPS - 1
    vector = jnp.concatenate([reverse, jnp.zeros((group_count, block_rows), filters.dtype)], axis=1)
    tiled = jnp.tile(vector, (1, block_rows))
    return tiled[:, : block_rows * span].reshape(group_count, block_rows, span)


def mix_streams(streams, taps, long_taps):
    seq_count, rows, _, width = streams.shape
    edge = shifted(streams[:, rows - (SHORT - 1) :], "ctx", 1)
    feat = featurize(jnp.concatenate([edge, streams], axis=1), taps)
    gated = (feat[:, :, 1] * feat[:, :, 2]).astype(jnp.bfloat16)
    edge_gated = shifted(gated[:, rows - (TAPS - 1) :], "ctx", 1)
    gated_ext = jnp.concatenate([edge_gated, gated], axis=1)
    query = feat[:, :, 0]
    local_groups = width // GSIZE
    block_rows = 128
    span = block_rows + TAPS - 1
    tiles = jnp.swapaxes(toeplitz_tiles(long_taps, block_rows), 1, 2)
    time_last = jnp.transpose(gated_ext, (0, 2, 1)).reshape(
        seq_count, local_groups, GSIZE, rows + TAPS - 1
    )
    pieces = []
    for blk in range(rows // block_rows):
        window = time_last[:, :, :, blk * block_rows : blk * block_rows + span]
        pieces.append(
            jnp.einsum("ngcs,gsi->ngci", window, tiles, preferred_element_type=jnp.float32)
        )
    longconv = jnp.concatenate(pieces, axis=3).reshape(seq_count, width, rows)
    longconv = jnp.transpose(longconv, (0, 2, 1))
    return (query * longconv).astype(jnp.bfloat16)


def shards(tokens, in_weight, short_taps, long_taps, out_weight):
    streams = jnp.einsum(
        "rd,kcd->rkc",
        tokens,
        lax.all_gather(in_weight, ("dp", "ctx"), axis=1, tiled=True),
        preferred_element_type=jnp.float32,
    ).astype(jnp.bfloat16)
    mixed = mix_streams(streams[None], short_taps, long_taps)[0]
    result = jnp.dot(
        mixed,
        lax.all_gather(out_weight, ("dp", "ctx"), axis=0, tiled=True),
        preferred_element_type=jnp.float32,
    )
    return result.astype(jnp.bfloat16)


def solution(mesh):
    in_specs = (
        P(("dp", "ctx"), None),
        P(None, ("dp", "ctx"), None),
        P(),
        P(),
        P(("dp", "ctx"), None),
    )
    out_specs = P(("dp", "ctx"), None)
    return jax.shard_map(shards, mesh=mesh, in_specs=in_specs, out_specs=out_specs, check_vma=False)
```

profile of v0, /device:TPU:0, one launch (start us, length us, event | category | flops | bytes accessed | tf_op | source)
XLA Modules:
  0.0 288.5 jit_solution(6398887480003782112)
XLA Ops:
  6.5 0.0 copy-start
  6.5 0.0 all-gather.3.cloned.1.call-start
  6.5 0.7 all-gather.3.cloned.1.call-update
  7.3 0.0 all-gather.5.cloned.1.call-start
  7.3 0.7 all-gather.5.cloned.1.call-update
  8.0 1.8 fusion.17
  9.9 157.7 %all-gather.3.cloned.1.call-done = bf16[3,2048,2048]{2,1,0:T(8,128)(2,1)} async-done(((bf16[3,64,2048]{2,1,0:T(8,128)(2,1)}), bf16[3,2048,2048]{2,1,0:T(8,128)(2,1)}) %all-gather.3.cloned.1.call-update) | async-done | bytes 25165840 | tf_op jit(solution)/shard_map/all_gather | solution.py:66
  167.6 0.0 copy-done
  167.6 12.8 %convolution_convert_fusion = bf16[256,3,2048]{2,0,1:T(8,128)(2,1)} fusion(bf16[3,2048,2048]{2,1,0:T(8,128)(2,1)} %all-gather.3.cloned.1.call-done, bf16[256,2048]{1,0:T(8,128)(2,1)S(1)} %copy-done), kind=kOutput, calls=%fused_computation.11 | convolution fusion | flops 6444023808 | bytes 29360128 | tf_op jit(solution)/shard_map/rd,kcd->rkc/dot_general | solution.py:63
  180.5 0.9 slice.84
  181.4 2.2 collective-permute-start
  183.6 0.9 collective-permute-done
  184.5 12.5 %fusion.4 = f32[1,256,3,2048]{3,1,2,0:T(8,128)S(1)} fusion(bf16[256,3,2048]{2,0,1:T(8,128)(2,1)} %convolution_convert_fusion, bf16[1,6,3,2048]{3,1,2,0:T(8,128)(2,1)S(1)} %collective-permute-done, bf16[1,256,3,2048]{3,1,2,0:T(8,128)(2,1)} %bitcast.77, f32[3,2048]{1,0:T(4,128)S(1)} %get-tuple-element.12, f32[3,2048]{1,0:T(4,128)S(1)} %get-tuple-element.13, ...), kind=kLoop, calls=%fused_computation.10 | loop fusion | flops 59768832 | bytes 12828672 | tf_op jit(solution)/shard_map/add | solution.py:21
  197.0 0.0 copy-start.2
  197.0 2.6 copy-done.2
  199.7 0.0 copy-start.3
  199.7 0.3 fusion.15
  199.9 0.1 slice.99
  200.1 3.3 %collective-permute-start.1 = (bf16[1,127,2048]{2,1,0:T(8,128)(2,1)S(1)}, bf16[1,127,2048]{2,1,0:T(8,128)(2,1)S(1)}, u32[]{:S(2)}, u32[]{:S(2)}) collective-permute-start(bf16[1,127,2048]{2,1,0:T(8,128)(2,1)S(1)} %slice.99), channel_id=1, source_target_pairs={{0,1},{1,2},{2,3},{3,4},{4,5},{5,6},{6,7},{8,9},{9,10},{10,11},{11... | collective-permute-start | bytes 1560584 | tf_op jit(solution)/shard_map/ppermute | solution.py:14
  203.4 0.0 copy-done.3
  203.4 0.1 rev.3
  203.5 3.8 %tile.4 = bf16[128,128,256]{2,1,0:T(8,128)(2,1)} broadcast(bf16[128,256]{1,0:T(8,128)(2,1)S(1)} %concatenate.13), dimensions={0,2} | broadcast | bytes 8454144 | tf_op jit(solution)/shard_map/tile | solution.py:32
  207.3 12.9 %copy.18 = bf16[16,8,128,256]{3,1,2,0:T(8,128)(2,1)} copy(bf16[16,8,128,256]{3,2,1,0:T(8,128)(2,1)} %bitcast.74) | data formatting | bytes 16777216
  220.2 7.2 %slice.96 = bf16[128,32640]{1,0:T(8,128)(2,1)} slice(bf16[128,32768]{1,0:T(8,128)(2,1)} %bitcast.75), slice={[0:128], [0:32640]} | slice | bytes 16711680 | tf_op jit(solution)/shard_map/slice | solution.py:33
  227.4 29.5 %reshape.70 = bf16[128,128,255]{2,1,0:T(8,128)(2,1)} reshape(bf16[128,32640]{1,0:T(8,128)(2,1)} %slice.96) | data formatting | bytes 16711680 | tf_op jit(solution)/shard_map/reshape | solution.py:33
  256.9 0.0 collective-permute-done.1
  256.9 1.4 maximum_bitcast_fusion
  258.3 1.9 copy.9
  260.2 5.6 %convolution_bitcast_fusion.1 = f32[1,128,16,128]{3,2,1,0:T(8,128)S(1)} fusion(bf16[128,128,255]{2,1,0:T(8,128)(2,1)} %reshape.70, bf16[1,128,16,383]{3,2,1,0:T(8,128)(2,1)S(1)} %bitcast.78), kind=kOutput, calls=%fused_computation.30 | convolution fusion | flops 133693440 | bytes 10452992 | tf_op jit(solution)/shard_map/ngcs,gsi->ngci/dot_general | solution.py:55
  265.9 5.7 %convolution_bitcast_fusion = f32[1,128,16,128]{3,2,1,0:T(8,128)S(1)} fusion(bf16[128,128,255]{2,1,0:T(8,128)(2,1)} %reshape.70, bf16[1,128,16,383]{3,2,1,0:T(8,128)(2,1)S(1)} %bitcast.79), kind=kOutput, calls=%fused_computation.29 | convolution fusion | flops 133693440 | bytes 10452992 | tf_op jit(solution)/shard_map/ngcs,gsi->ngci/dot_general | solution.py:55
  271.5 0.2 pad_maximum_fusion.1
  271.8 1.9 copy.10
  273.6 0.0 all-gather.5.cloned.1.call-done
  273.6 0.0 copy-start.1
  273.6 8.0 %convolution_convert_fusion.1 = bf16[256,2048]{1,0:T(8,128)(2,1)} fusion(bf16[2048,2048]{1,0:T(8,128)(2,1)} %all-gather.5.cloned.1.call-done, f32[1,2048,256]{1,2,0:T(8,128)} %copy.10, f32[1,256,3,2048]{3,1,2,0:T(8,128)} %copy-done.2), kind=kOutput, calls=%fused_computation.21 | convolution fusion | flops 2149056512 | bytes 13631488 | tf_op jit(solution)/shard_map/dot_general | solution.py:70
  281.7 0.0 copy-done.1
  (5 shorter events, 0.1 us)
Async XLA Ops:
  6.5 161.1 %copy-start = (bf16[256,2048]{1,0:T(8,128)(2,1)S(1)}, bf16[256,2048]{1,0:T(8,128)(2,1)}, u32[]{:S(2)}) copy-start(bf16[256,2048]{1,0:T(8,128)(2,1)} %param.5) | copy-start | bytes 3145732
  6.5 161.1 %all-gather.3.cloned.1.call-start = ((), (), s32[]{:S(2)}) async-start(), calls=%async_computation | async-start | bytes 25952256 | tf_op jit(solution)/shard_map/all_gather | solution.py:66
  7.3 266.4 %all-gather.5.cloned.1.call-start = ((), (), s32[]{:S(2)}) async-start(), calls=%async_computation.1 | async-start | bytes 8650752 | tf_op jit(solution)/shard_map/all_gather | solution.py:72
  181.4 3.1 %collective-permute-start = (bf16[1,6,3,2048]{3,1,2,0:T(8,128)(2,1)S(1)}, bf16[1,6,3,2048]{3,1,2,0:T(8,128)(2,1)S(1)}, u32[]{:S(2)}, u32[]{:S(2)}) collective-permute-start(bf16[1,6,3,2048]{3,1,2,0:T(8,128)(2,1)S(1)} %slice.84), channel_id=1, source_target_pairs={{0,1},{1,2},{2,3},{3,4},{4,5},{5,6},{6,7},{8,9},{9,10},{10,11},{11... | collective-permute-start | bytes 221192 | tf_op jit(solution)/shard_map/ppermute | solution.py:14
  197.0 2.7 copy-start.2
  199.7 3.8 %copy-start.3 = (bf16[128,128]{1,0:T(8,128)(2,1)S(1)}, bf16[128,128]{1,0:T(8,128)(2,1)}, u32[]{:S(2)}) copy-start(bf16[128,128]{1,0:T(8,128)(2,1)} %param.8) | copy-start | bytes 98308
  200.1 56.9 %collective-permute-start.1 = (bf16[1,127,2048]{2,1,0:T(8,128)(2,1)S(1)}, bf16[1,127,2048]{2,1,0:T(8,128)(2,1)S(1)}, u32[]{:S(2)}, u32[]{:S(2)}) collective-permute-start(bf16[1,127,2048]{2,1,0:T(8,128)(2,1)S(1)} %slice.99), channel_id=1, source_target_pairs={{0,1},{1,2},{2,3},{3,4},{4,5},{5,6},{6,7},{8,9},{9,10},{10,11},{11... | collective-permute-start | bytes 1560584 | tf_op jit(solution)/shard_map/ppermute | solution.py:14
  273.6 8.0 %copy-start.1 = (bf16[256,2048]{1,0:T(8,128)(2,1)S(1)}, bf16[256,2048]{1,0:T(8,128)(2,1)}, u32[]{:S(2)}) copy-start(bf16[256,2048]{1,0:T(8,128)(2,1)} %param.5) | copy-start | bytes 3145732
Sparse Core Ops, SparseCore 0:
  10.4 157.1 all-gather.2
  170.6 76.2 all-gather.4
where the time goes:
time: 290 us; the launch traced here: 288 us
  waiting for transfers between devices  160 us (55%)
  local copies, waits for them, and re-layouts  62.8 us (22%)
  matrix products  32.2 us (11%)
  other arithmetic  14.4 us (5%)
  between operations  13.5 us (5%)
  starting transfers between devices  5.55 us (2%)
    all_gather x1, waiting for transfers between devices, shards(): lax.all_gather(in_weight, ('dp', 'ctx'), axis=1, tiled=True)  158 us
    reshape x1, local copies, waits for them, and re-layouts, toeplitz_tiles(): return tiled[:, :block_rows * span].reshape(group_count, block_rows, span)  29.5 us
    unnamed x13, local copies, waits for them, and re-layouts  15.6 us
    dot_general x1, matrix products, shards(): jnp.einsum('rd,kcd->rkc', tokens, lax.all_gather(in_weight, ('dp', 'ctx')...  12.8 us
    add x1, other arithmetic, featurize(): total + taps[j] * extended[:, SHORT - 1 - j:SHORT - 1 - j + length].astyp...  12.5 us
    dot_general x2, matrix products, mix_streams(): jnp.einsum('ngcs,gsi->ngci', window, tiles, preferred_element_type=jnp.fl...  11.3 us
    dot_general x1, matrix products, shards(): jnp.dot(mixed, lax.all_gather(out_weight, ('dp', 'ctx'), axis=0, tiled=Tr...  8.03 us
    slice x1, local copies, waits for them, and re-layouts, toeplitz_tiles(): return tiled[:, :block_rows * span].reshape(group_count, block_rows, span)  7.16 us
  transfers between devices with their start and end apart: 4, of which 2 were waited for; matrix products, arithmetic and copies ran while one was open for 34% of the time, Pallas kernels for 0%

commit v1 on v0

v1 whole, which is shorter than its diff:
```python
import functools

import jax
import jax.numpy as jnp
from jax import lax
from jax.experimental import pallas as pl
from jax.experimental.pallas import tpu as pltpu
from jax.sharding import Mesh
from jax.sharding import PartitionSpec as P

GSIZE = 16
SHORT = 7
TAPS = 128
LANES = 128
WIDE = 64
HALO = 160
ANY = pl.BlockSpec(memory_space=pl.ANY)
SMEM = pl.BlockSpec(memory_space=pltpu.SMEM)
VMEM = pl.BlockSpec(memory_space=pltpu.VMEM)
LIMIT = pltpu.CompilerParams(vmem_limit_bytes=48 * 1024 * 1024)


def ring_of(count):
    order = [i for i in range(count) if i == 0 or i % 2 == 1]
    order += [i for i in reversed(range(1, count)) if i % 2 == 0]
    return [(order[i], order[(i + 1) % count]) for i in range(count)]


def origins_of(count):
    previous = dict((target, source) for source, target in ring_of(count))
    table = [list(range(count))]
    for _ in range(count - 1):
        table.append([previous[i] for i in table[-1]])
    return table


def swap(block):
    return lax.ppermute(block, "core", [(0, 1), (1, 0)])


def across(block, r):
    count = lax.axis_size("dp")
    return lax.ppermute(block, "dp", [(i, i ^ r) for i in range(count)])


def tie(*groups):
    return lax.optimization_barrier(groups)


def dot(a, b):
    return jnp.dot(a, b, preferred_element_type=jnp.float32)


def nt(a, b):
    return lax.dot_general(a, b, (((1,), (1,)), ((), ())), preferred_element_type=jnp.float32)


def mix_kernel(step, slots, parts, place_ref, taps_ref, long_ref, wa_ref, wb_ref, *rest):
    pieces, rest = rest[: len(parts)], rest[len(parts) :]
    outs, rest = rest[:slots], rest[slots:]
    tokens, w, first, second, packed, turned, tiles, sems, w_sems = rest
    span = tokens.shape[1] - HALO
    rows = span // 2
    core = place_ref[0]
    origin = place_ref[2 + step]
    count = WIDE // GSIZE

    cut = wa_ref.shape[0]
    w_copies = [
        pltpu.make_async_copy(wa_ref, w.at[pl.ds(0, cut)], w_sems.at[0]),
        pltpu.make_async_copy(
            wb_ref.at[pl.ds(0, 2 * WIDE - cut)], w.at[pl.ds(cut, 2 * WIDE - cut)], w_sems.at[1]
        ),
        pltpu.make_async_copy(
            wb_ref.at[pl.ds(2 * WIDE - cut, WIDE)], w.at[pl.ds(3 * WIDE, WIDE)], w_sems.at[2]
        ),
    ]
    for copy in w_copies:
        copy.start()
    copies = [[] for _ in range(slots)]
    number = 0
    for ref, (slot, side, start) in zip(pieces, parts):
        owner = core if side == 0 else 1 - core
        end = start + ref.shape[0]
        bounds = []
        if start < rows:
            bounds.append((start, min(end, rows), HALO + owner * rows + start))
        if end > rows:
            low = max(start, rows)
            bounds.append((low, end, owner * (HALO // 2) + low - rows))
        for low, high, at in bounds:
            copies[slot].append(
                pltpu.make_async_copy(
                    ref.at[pl.ds(low - start, high - low)],
                    tokens.at[slot, pl.ds(pl.multiple_of(at, 16), high - low)],
                    sems.at[number],
                )
            )
            number += 1
    for group in copies:
        for copy in group:
            copy.start()

    w[2 * WIDE : 3 * WIDE, :] = jnp.zeros((WIDE, w.shape[1]), w.dtype)
    filters = long_ref[origin]
    for g in range(count):
        line = jnp.concatenate([jnp.zeros((1, TAPS), jnp.float32), filters[g : g + 1, :]], axis=1)
        square = pltpu.roll(
            jnp.broadcast_to(line, (2 * TAPS, 2 * TAPS)), 0, 1, stride=1, stride_axis=0
        )
        tiles[g] = square[:, :TAPS].astype(jnp.bfloat16)
    taps = taps_ref[origin]
    band = 64
    blocks = span // TAPS
    lower = lax.broadcasted_iota(jnp.int32, (band, LANES), 1) < WIDE

    def project_slot(slot):
        result = nt(tokens[slot], w[...]).astype(jnp.bfloat16).astype(jnp.float32)
        first[slot % 2] = result[:, :LANES]
        second[slot % 2] = result[:, LANES:]

    def feat(ref, slot, at, lanes):
        total = None
        for j in range(SHORT):
            term = taps[j : j + 1, lanes] * ref[slot % 2, at - j : at - j + band, :]
            total = term if total is None else total + term
        return total

    for copy in w_copies + copies[0]:
        copy.wait()
    project_slot(0)
    for slot in range(slots):
        if slot + 1 < slots:
            for copy in copies[slot + 1]:
                copy.wait()
            project_slot(slot + 1)
        for n in range((TAPS + span) // band):
            at = HALO - TAPS + n * band
            a = feat(first, slot, at, slice(0, LANES))
            b = feat(second, slot, at, slice(LANES, 2 * LANES))
            packed[slot % 2, n * band : (n + 1) * band, :] = jnp.where(lower, a, a * b).astype(
                jnp.bfloat16
            )
        turned[slot] = packed[slot % 2].T

    for g in range(count):
        channels = slice(WIDE + g * GSIZE, WIDE + (g + 1) * GSIZE)
        window = jnp.concatenate(
            [
                turned[slot, channels, b * TAPS : (b + 2) * TAPS]
                for slot in range(slots)
                for b in range(blocks)
            ],
            axis=0,
        )
        conv = dot(window, tiles[g])
        for slot in range(slots):
            row = jnp.concatenate(
                [
                    conv[(slot * blocks + b) * GSIZE : (slot * blocks + b + 1) * GSIZE]
                    for b in range(blocks)
                ],
                axis=1,
            )
            query = turned[slot, g * GSIZE : (g + 1) * GSIZE, TAPS:].astype(jnp.float32)
            outs[slot][g * GSIZE : (g + 1) * GSIZE, :] = (query * row).astype(jnp.bfloat16)


def mix_chunk(step, rows, slots, place, taps, filters, wa, wb, parts, pieces):
    features = wa.shape[1]
    count = WIDE // GSIZE
    return pl.pallas_call(
        functools.partial(mix_kernel, step, slots, parts),
        out_shape=[jax.ShapeDtypeStruct((WIDE, 2 * rows), jnp.bfloat16)] * slots,
        in_specs=[SMEM, VMEM, VMEM] + [ANY] * (2 + len(pieces)),
        out_specs=[VMEM] * slots,
        scratch_shapes=[
            pltpu.VMEM((slots, HALO + 2 * rows, features), jnp.bfloat16),
            pltpu.VMEM((4 * WIDE, features), jnp.bfloat16),
            pltpu.VMEM((2, HALO + 2 * rows, LANES), jnp.float32),
            pltpu.VMEM((2, HALO + 2 * rows, LANES), jnp.float32),
            pltpu.VMEM((2, TAPS + 2 * rows, LANES), jnp.bfloat16),
            pltpu.VMEM((slots, LANES, TAPS + 2 * rows), jnp.bfloat16),
            pltpu.VMEM((count, 2 * TAPS, TAPS), jnp.bfloat16),
            pltpu.SemaphoreType.DMA((2 * len(pieces),)),
            pltpu.SemaphoreType.DMA((3,)),
        ],
        compiler_params=LIMIT,
        cost_estimate=pl.CostEstimate(
            flops=4 * slots * 2 * rows * 4 * WIDE * features,
            bytes_accessed=2 * slots * 2 * rows * features,
            transcendentals=0,
        ),
    )(place, taps, filters, wa, wb, *pieces)


def out_kernel(mirror, slots, chips, width, place_ref, v_ref, *refs):
    parts = refs[: len(refs) - 5]
    out_ref, left, right, total, sems = refs[len(refs) - 5 :]
    rows = out_ref.shape[0]
    core, dp = place_ref[0], place_ref[1]
    if mirror:
        core = 1 - core
    depth = slots * width
    groups = []
    if width == WIDE:
        for s in range(chips):
            group = []
            for r in range(slots):
                source = lax.bitwise_xor(dp, r) * chips + place_ref[2 + s]
                here = pl.ds((s * slots + r) * width, width)
                n = s * slots + r
                group.append(pltpu.make_async_copy(parts[n], left.at[here], sems.at[0, n]))
                group.append(pltpu.make_async_copy(v_ref.at[source], right.at[here], sems.at[1, n]))
            groups.append((group, s * depth, depth))
    else:
        group = [
            pltpu.make_async_copy(parts[0], left, sems.at[0, 0]),
            pltpu.make_async_copy(v_ref, right, sems.at[1, 0]),
        ]
        groups.append((group, 0, depth * chips))
    for group, _, _ in groups:
        for copy in group:
            copy.start()
    at = pl.multiple_of(core * rows, LANES)
    tile = 512
    for n, (group, start, size) in enumerate(groups):
        for copy in group:
            copy.wait()
        a = left[start : start + size, pl.ds(at, rows)].T
        for t in range(0, out_ref.shape[1], tile):
            here = slice(t, t + tile)
            value = dot(a, right[start : start + size, here])
            if n:
                value = value + total[:, here]
            if n + 1 < len(groups):
                total[:, here] = value
            else:
                out_ref[:, here] = value.astype(out_ref.dtype)


def project(mirror, slots, chips, width, place, v, parts, dtype):
    span, features = parts[0].shape[1], v.shape[-1]
    rows, depth = span // 2, slots * chips * width
    return pl.pallas_call(
        functools.partial(out_kernel, mirror, slots, chips, width),
        out_shape=jax.ShapeDtypeStruct((rows, features), dtype),
        in_specs=[SMEM, ANY] + [ANY] * len(parts),
        out_specs=VMEM,
        scratch_shapes=[
            pltpu.VMEM((depth, span), jnp.bfloat16),
            pltpu.VMEM((depth, features), jnp.bfloat16),
            pltpu.VMEM((rows, features), jnp.float32),
            pltpu.SemaphoreType.DMA((2, len(parts))),
        ],
        compiler_params=LIMIT,
        cost_estimate=pl.CostEstimate(
            flops=4 * rows * features * depth,
            bytes_accessed=2 * depth * (features + span),
            transcendentals=0,
        ),
    )(place, v, *parts)


def local_filters(chips, width, dp, core, short_taps, long_taps):
    part = short_taps.reshape(SHORT, 3, -1, 2, width)
    part = lax.dynamic_slice(
        part, (0, 0, dp * chips, core, 0), (SHORT, 3, chips, 1, width)
    ).reshape(SHORT, 3, chips, width)
    part = jnp.pad(part, ((0, 1), (0, 0), (0, 0), (0, WIDE - width)))
    part = jnp.transpose(part, (2, 0, 1, 3))
    taps = jnp.concatenate(
        [part[:, :, 0], part[:, :, 1], jnp.zeros_like(part[:, :, 0]), part[:, :, 2]], axis=2
    )
    groups = max(1, width // GSIZE)
    each = [
        lax.dynamic_slice_in_dim(
            long_taps, (2 * (dp * chips + i) + core) * width // GSIZE, groups, 0
        )
        for i in range(chips)
    ]
    filters = jnp.stack(each).astype(jnp.float32)
    return taps, jnp.pad(filters, ((0, 0), (0, WIDE // GSIZE - groups), (0, 0)))


def shards(chips, tokens, in_weight, short_taps, long_taps, out_weight):
    _, width, features = in_weight.shape
    rows = tokens.shape[0]
    slots = lax.axis_size("dp")
    dp = lax.axis_index("dp")
    z = lax.axis_index("z")
    core = lax.axis_index("core")
    ring = ring_of(chips)
    forward = lambda block: lax.ppermute(block, "z", ring)

    table = jnp.array(origins_of(chips), jnp.int32)
    origins = lax.dynamic_index_in_dim(table, z, 1, False)
    place = jnp.concatenate([jnp.stack([core, dp]).astype(jnp.int32), origins])
    taps, filters = local_filters(chips, width, dp, core, short_taps, long_taps)

    pairs = lambda c: [(2 * i + 1, 2 * (i + 1) + c) for i in range(chips - 1)]
    half = HALO // 2
    edge = lax.ppermute(tokens[rows - HALO : rows - half], ("z", "core"), pairs(0)) + lax.ppermute(
        tokens[rows - half :], ("z", "core"), pairs(1)
    )
    block = jnp.concatenate([tokens, edge])

    if slots == 4 and chips == 4 and width == WIDE:
        flat = in_weight.reshape(3 * width, features)
        cut = 3 * width // 2
        wa, wb = [flat[:cut]], [flat[cut:]]
        x, y, twin = across(block, 1), across(block, 2), swap(block)
        wa.append(forward(wa[0]))
        wb.append(forward(wb[0]))
        wa.append(forward(wa[1]))
        x, y, twin, wa[1], wa[2], wb[1], v_own = tie(x, y, twin, wa[1], wa[2], wb[1], out_weight)

        v = lax.all_gather(v_own, ("dp", "z"))
        mid = HALO
        x_far, y_far = across(y[:mid], 1), across(x[mid:], 2)
        x_twin, y_twin = swap(x), swap(y)
        wb.append(forward(wb[1]))
        wa.append(forward(wa[2]))
        x_far, y_far, x_twin, y_twin, wb[2], wa[3] = tie(x_far, y_far, x_twin, y_twin, wb[2], wa[3])

        wb.append(forward(wb[2]))
        parts = [(0, 0, 0), (0, 1, 0), (1, 0, 0), (1, 1, 0), (2, 0, 0), (2, 1, 0)]
        parts += [(3, 0, 0), (3, 0, mid), (3, 1, 0), (3, 1, mid)]
        pieces = [block, twin, x, x_twin, y, y_twin, x_far, y_far, swap(x_far), swap(y_far)]
    else:
        v = lax.all_gather(out_weight, ("dp", "z"))
        w, wa, wb = in_weight, [], []
        for s in range(chips):
            padded = jnp.pad(w, ((0, 0), (0, WIDE - width), (0, 0))).reshape(3 * WIDE, features)
            wa.append(padded[: 3 * WIDE // 2])
            wb.append(padded[3 * WIDE // 2 :])
            if s + 1 < chips:
                w = forward(w)
        pieces = [block] + [across(block, r) for r in range(1, slots)]
        pieces += [swap(piece) for piece in pieces]
        parts = [(r, side, 0) for side in range(2) for r in range(slots)]

    moved = []
    for s in range(chips):
        last = s + 1 == chips
        if last and s > 1:
            wb[s], moved[: s - 1] = tie(wb[s], moved[: s - 1])
        mixed = mix_chunk(s, rows, slots, place, taps, filters, wa[s], wb[s], parts, pieces)
        mixed = [m[:width] for m in mixed]
        moved.append([mixed[0]] + [across(mixed[r], r) for r in range(1, slots)])
    if width == WIDE:
        v = v.reshape(slots * chips, width, -1)
        together = [part for one in moved for part in one]
    else:
        order = lax.bitwise_xor(dp, jnp.arange(slots))
        v = v.reshape(slots, chips, width, -1)[order][:, origins].reshape(slots * chips * width, -1)
        together = [jnp.concatenate([one[r] for r in range(slots) for one in moved])]
    run = lambda mirror, dtype: project(mirror, slots, chips, width, place, v, together, dtype)
    theirs = swap(run(True, jnp.bfloat16))
    mine = run(False, jnp.float32)
    return (mine + theirs.astype(jnp.float32)).astype(jnp.bfloat16)


def solution(mesh):
    count = mesh.shape["dp"]
    chips = mesh.shape["ctx"] // 2
    fine = Mesh(mesh.devices.reshape(count, chips, 2), ("dp", "z", "core"))
    every = ("dp", "z", "core")
    in_specs = (P(every, None), P(None, every, None), P(), P(), P(every, None))
    return jax.shard_map(
        functools.partial(shards, chips),
        mesh=fine,
        in_specs=in_specs,
        out_specs=P(every, None),
        check_vma=False,
    )
```

time: 290 us -> 170 us (0.59)
  waiting for transfers between devices: 160 us -> 42.1 us
  Pallas kernels: 0 us -> 48.9 us
  local copies, waits for them, and re-layouts: 62.8 us -> 21.2 us
  starting transfers between devices: 5.55 us -> 41.9 us
  matrix products: 32.2 us -> 0 us
  other arithmetic: 14.4 us -> 1.64 us
    all_gather x2 -> x1, waiting for transfers between devices: 158 us -> 0.01 us  [shards(): v = lax.all_gather(v_own, ('dp', 'z'))]
    pallas_call x0 -> x6, Pallas kernels: none -> 48.9 us  [the longest x4 40.9 us: mix_chunk(): pl.pallas_call(functools.partial(mix_kernel, step, slots, parts), out_sha...]
    ppermute x2 -> x30, waiting for transfers between devices: 0.87 us -> 42.1 us  [the longest x6 38.6 us: shards(): forward = lambda block: lax.ppermute(block, 'z', ring)]
    ppermute x2 -> x30, starting transfers between devices: 5.51 us -> 41.9 us  [the longest x16 20.1 us: across(): return lax.ppermute(block, 'dp', [(i, i ^ r) for i in range(count)])]
    dot_general x4 -> x0, matrix products: 32.2 us -> none  [the longest x1 12.8 us: shards(): jnp.einsum('rd,kcd->rkc', tokens, lax.all_gather(in_weight, ('dp', 'ctx')...]
    reshape x2 -> x1, local copies, waits for them, and re-layouts: 31.4 us -> 1.94 us  [local_filters(): part = short_taps.reshape(SHORT, 3, -1, 2, width)]
    add x1, other arithmetic: 12.5 us -> 0.08 us  [shards(): lax.ppermute(tokens[rows - HALO:rows - half], ('z', 'core'), pairs(0))]
    slice x4, local copies, waits for them, and re-layouts: 10 us -> 5.3 us  [the longest x2 4.03 us: shards(): x_far, y_far = (across(y[:mid], 1), across(x[mid:], 2))]
  transfers between devices with their start and end apart: 4 -> 31, of which waited for: 2 -> 8; matrix products, arithmetic and copies ran while one was open for 34% -> 5% of each run, Pallas kernels for 0% -> 26%
where the time goes in v1:
time: 170 us; the launch traced here: 169 us
  Pallas kernels  48.9 us (29%)
  waiting for transfers between devices  42.1 us (25%)
  starting transfers between devices  41.9 us (25%)
  local copies, waits for them, and re-layouts  21.2 us (12%)
  between operations  13.7 us (8%)
    pallas_call x4, Pallas kernels, mix_chunk(): pl.pallas_call(functools.partial(mix_kernel, step, slots, parts), out_sha...  40.9 us
    ppermute x6, waiting for transfers between devices, shards(): forward = lambda block: lax.ppermute(block, 'z', ring)  38.6 us
    ppermute x16, starting transfers between devices, across(): return lax.ppermute(block, 'dp', [(i, i ^ r) for i in range(count)])  20.1 us
    unnamed x41, local copies, waits for them, and re-layouts  11.5 us
    ppermute x6, starting transfers between devices, swap(): return lax.ppermute(block, 'core', [(0, 1), (1, 0)])  10.4 us
    ppermute x6, starting transfers between devices, shards(): forward = lambda block: lax.ppermute(block, 'z', ring)  10 us
    pallas_call x2, Pallas kernels, project(): pl.pallas_call(functools.partial(out_kernel, mirror, slots, chips, width)...  8.04 us
    slice x2, local copies, waits for them, and re-layouts, shards(): x_far, y_far = (across(y[:mid], 1), across(x[mid:], 2))  4.03 us
  transfers between devices with their start and end apart: 31, of which 8 were waited for; matrix products, arithmetic and copies ran while one was open for 5% of the time, Pallas kernels for 26%

profile of v1, /device:TPU:0, one launch (start us, length us, event | category | flops | bytes accessed | tf_op | source)
XLA Modules:
  0.0 169.5 jit_solution(1040392859643909614)
XLA Ops:
  6.5 1.2 fusion.5
  9.4 3.0 %collective-permute-start.2 = (bf16[336,2048]{1,0:T(8,128)(2,1)S(1)}, bf16[336,2048]{1,0:T(8,128)(2,1)S(1)}, u32[]{:S(2)}, u32[]{:S(2)}) collective-permute-start(bf16[336,2048]{1,0:T(8,128)(2,1)S(1)} %pad_maximum_fusion.rest_0_), channel_id=1, source_target_pairs={{0,8},{8,0},{16,24},{24,16},{1,9},{9,1},{17,25},{25,17},{2,10},{10... | collective-permute-start | bytes 4128776 | tf_op jit(solution)/shard_map/ppermute | solution.py:43
  12.4 1.5 collective-permute-start.3
  13.9 9.2 %collective-permute-start.4 = (bf16[336,2048]{1,0:T(8,128)(2,1)S(1)}, bf16[336,2048]{1,0:T(8,128)(2,1)}, u32[]{:S(2)}, u32[]{:S(2)}) collective-permute-start(bf16[336,2048]{1,0:T(8,128)(2,1)S(1)} %pad_maximum_fusion.rest_0_), channel_id=1, source_target_pairs={{0,1},{1,0},{2,3},{3,2},{4,5},{5,4},{6,7},{7,6},{8,9},{9,8},{10,11... | collective-permute-start | bytes 4128776 | tf_op jit(solution)/shard_map/ppermute | solution.py:38
  23.2 2.2 %collective-permute-start.5 = (bf16[96,2048]{1,0:T(8,128)(2,1)S(1)}, bf16[96,2048]{1,0:T(8,128)(2,1)S(1)}, u32[]{:S(2)}, u32[]{:S(2)}) collective-permute-start(bf16[96,2048]{1,0:T(8,128)(2,1)S(1)} %get-tuple-element.84.wa_ref), channel_id=1, source_target_pairs={{0,2},{2,6},{6,4},{4,0},{1,3},{3,7},{7,5},{5,1},{8,10},{10,14},{14... | collective-permute-start | bytes 1179656 | tf_op jit(solution)/shard_map/ppermute | solution.py:294
  25.4 2.6 %collective-permute-start.7 = (bf16[96,2048]{1,0:T(8,128)(2,1)S(1)}, bf16[96,2048]{1,0:T(8,128)(2,1)}, u32[]{:S(2)}, u32[]{:S(2)}) collective-permute-start(bf16[96,2048]{1,0:T(8,128)(2,1)S(1)} %get-tuple-element.83.wb_ref), channel_id=1, source_target_pairs={{0,2},{2,6},{6,4},{4,0},{1,3},{3,7},{7,5},{5,1},{8,10},{10,14},{14... | collective-permute-start | bytes 1179656 | tf_op jit(solution)/shard_map/ppermute | solution.py:294
  28.0 8.3 %collective-permute-done.5.wa_ref = bf16[96,2048]{1,0:T(8,128)(2,1)S(1)} collective-permute-done((bf16[96,2048]{1,0:T(8,128)(2,1)S(1)}, bf16[96,2048]{1,0:T(8,128)(2,1)S(1)}, u32[]{:S(2)}, u32[]{:S(2)}) %collective-permute-start.5) | collective-permute-done | bytes 393248 | tf_op jit(solution)/shard_map/ppermute | solution.py:294
  36.3 1.2 collective-permute-start.6
  37.5 0.8 copy-done
  38.2 6.6 %collective-permute-done.7.wb_ref = bf16[96,2048]{1,0:T(8,128)(2,1)} collective-permute-done((bf16[96,2048]{1,0:T(8,128)(2,1)S(1)}, bf16[96,2048]{1,0:T(8,128)(2,1)}, u32[]{:S(2)}, u32[]{:S(2)}) %collective-permute-start.7) | collective-permute-done | bytes 393248 | tf_op jit(solution)/shard_map/ppermute | solution.py:294
  44.9 7.8 %collective-permute-done.6.wa_ref = bf16[96,2048]{1,0:T(8,128)(2,1)} collective-permute-done((bf16[96,2048]{1,0:T(8,128)(2,1)S(1)}, bf16[96,2048]{1,0:T(8,128)(2,1)}, u32[]{:S(2)}, u32[]{:S(2)}) %collective-permute-start.6) | collective-permute-done | bytes 393248 | tf_op jit(solution)/shard_map/ppermute | solution.py:294
  52.7 1.1 copy-done.18
  53.7 1.2 copy-done.19
  55.5 0.7 collective-permute-start.12
  56.2 2.0 %slice.32 = bf16[176,2048]{1,0:T(8,128)(2,1)} slice(bf16[336,2048]{1,0:T(8,128)(2,1)} %copy-done.18), slice={[160:336], [0:2048]} | slice | bytes 1441792 | tf_op jit(solution)/shard_map/slice | solution.py:320
  58.8 2.0 %slice.31 = bf16[160,2048]{1,0:T(8,128)(2,1)} slice(bf16[336,2048]{1,0:T(8,128)(2,1)} %copy-done.19), slice={[0:160], [0:2048]} | slice | bytes 1310720 | tf_op jit(solution)/shard_map/slice | solution.py:320
  60.8 1.1 collective-permute-start.8
  61.8 7.1 %collective-permute-done.12.wb_ref = bf16[96,2048]{1,0:T(8,128)(2,1)} collective-permute-done((bf16[96,2048]{1,0:T(8,128)(2,1)}, bf16[96,2048]{1,0:T(8,128)(2,1)}, u32[]{:S(2)}, u32[]{:S(2)}) %collective-permute-start.12) | collective-permute-done | bytes 393248 | tf_op jit(solution)/shard_map/ppermute | solution.py:294
  68.9 1.7 collective-permute-start.13
  70.6 1.9 %reshape.10 = f32[7,3,16,2,64]{4,3,2,0,1:T(2,128)} reshape(f32[7,3,2048]{2,0,1:T(8,128)} %param.8) | data formatting | bytes 344064 | tf_op jit(solution)/shard_map/reshape | solution.py:266
  72.6 0.8 fusion
  73.3 0.9 constant_dynamic-slice_fusion.4
  74.3 8.7 %collective-permute-done.13.wa_ref = bf16[96,2048]{1,0:T(8,128)(2,1)} collective-permute-done((bf16[96,2048]{1,0:T(8,128)(2,1)}, bf16[96,2048]{1,0:T(8,128)(2,1)}, u32[]{:S(2)}, u32[]{:S(2)}) %collective-permute-start.13) | collective-permute-done | bytes 393248 | tf_op jit(solution)/shard_map/ppermute | solution.py:294
  84.6 1.7 collective-permute-start.14
  86.2 1.0 copy-done.1
  87.2 10.2 %shard_map.65 = (bf16[64,512]{1,0:T(8,128)(2,1)S(1)}, bf16[64,512]{1,0:T(8,128)(2,1)S(1)}, bf16[64,512]{1,0:T(8,128)(2,1)S(1)}, bf16[64,512]{1,0:T(8,128)(2,1)S(1)}) custom-call(s32[6]{0:T(128)S(1)} %pad_add_fusion.place_ref, f32[4,8,256]{2,1,0:T(8,128)S(1)} %pad_maximum_fusion.1.taps_ref, f32[4,4,128]{2,1,0:T(4,128)S(1)} %maximum_convert_fusion.long_ref, ...), custom_call_target="tpu_custom_call" | custom-call | flops 4294967296 | bytes 8388608 | tf_op jit(solution)/shard_map/pallas_call | solution.py:172
  98.7 1.2 collective-permute-start.21
  99.9 1.7 collective-permute-start.22
  101.6 10.4 %shard_map.64 = (bf16[64,512]{1,0:T(8,128)(2,1)S(1)}, bf16[64,512]{1,0:T(8,128)(2,1)S(1)}, bf16[64,512]{1,0:T(8,128)(2,1)S(1)}, bf16[64,512]{1,0:T(8,128)(2,1)S(1)}) custom-call(s32[6]{0:T(128)S(1)} %pad_add_fusion.place_ref, f32[4,8,256]{2,1,0:T(8,128)S(1)} %pad_maximum_fusion.1.taps_ref, f32[4,4,128]{2,1,0:T(4,128)S(1)} %maximum_convert_fusion.long_ref, ...), custom_call_target="tpu_custom_call" | custom-call | flops 4294967296 | bytes 8388608 | tf_op jit(solution)/shard_map/pallas_call | solution.py:172
  113.2 1.2 collective-permute-start.18
  114.4 1.7 collective-permute-start.19
  116.1 10.1 %shard_map.66 = (bf16[64,512]{1,0:T(8,128)(2,1)S(1)}, bf16[64,512]{1,0:T(8,128)(2,1)S(1)}, bf16[64,512]{1,0:T(8,128)(2,1)S(1)}, bf16[64,512]{1,0:T(8,128)(2,1)S(1)}) custom-call(s32[6]{0:T(128)S(1)} %pad_add_fusion.place_ref, f32[4,8,256]{2,1,0:T(8,128)S(1)} %pad_maximum_fusion.1.taps_ref, f32[4,4,128]{2,1,0:T(4,128)S(1)} %maximum_convert_fusion.long_ref, ...), custom_call_target="tpu_custom_call" | custom-call | flops 4294967296 | bytes 8388608 | tf_op jit(solution)/shard_map/pallas_call | solution.py:172
  127.4 1.2 collective-permute-start.24
  128.6 1.7 %collective-permute-start.25 = (bf16[64,512]{1,0:T(8,128)(2,1)S(1)}, bf16[64,512]{1,0:T(8,128)(2,1)S(1)}, u32[]{:S(2)}, u32[]{:S(2)}) collective-permute-start(bf16[64,512]{1,0:T(8,128)(2,1)S(1)} %get-tuple-element.74), channel_id=1, source_target_pairs={{0,24},{8,16},{16,8},{24,0},{1,25},{9,17},{17,9},{25,1},{2,26},{10... | collective-permute-start | bytes 196616 | tf_op jit(solution)/shard_map/ppermute | solution.py:43
  130.3 10.2 %shard_map.67 = (bf16[64,512]{1,0:T(8,128)(2,1)S(1)}, bf16[64,512]{1,0:T(8,128)(2,1)S(1)}, bf16[64,512]{1,0:T(8,128)(2,1)S(1)}, bf16[64,512]{1,0:T(8,128)(2,1)S(1)}) custom-call(s32[6]{0:T(128)S(1)} %pad_add_fusion.place_ref, f32[4,8,256]{2,1,0:T(8,128)S(1)} %pad_maximum_fusion.1.taps_ref, f32[4,4,128]{2,1,0:T(4,128)S(1)} %maximum_convert_fusion.long_ref, ...), custom_call_target="tpu_custom_call" | custom-call | flops 4294967296 | bytes 8388608 | tf_op jit(solution)/shard_map/pallas_call | solution.py:172
  141.8 1.2 collective-permute-start.27
  143.0 1.7 %collective-permute-start.28 = (bf16[64,512]{1,0:T(8,128)(2,1)S(1)}, bf16[64,512]{1,0:T(8,128)(2,1)S(1)}, u32[]{:S(2)}, u32[]{:S(2)}) collective-permute-start(bf16[64,512]{1,0:T(8,128)(2,1)S(1)} %get-tuple-element.80), channel_id=1, source_target_pairs={{0,24},{8,16},{16,8},{24,0},{1,25},{9,17},{17,9},{25,1},{2,26},{10... | collective-permute-start | bytes 196616 | tf_op jit(solution)/shard_map/ppermute | solution.py:43
  144.7 0.8 collective-permute-done.26.refs_13_
  146.1 2.1 %collective-permute-done.28.refs_15_ = bf16[64,512]{1,0:T(8,128)(2,1)S(1)} collective-permute-done((bf16[64,512]{1,0:T(8,128)(2,1)S(1)}, bf16[64,512]{1,0:T(8,128)(2,1)S(1)}, u32[]{:S(2)}, u32[]{:S(2)}) %collective-permute-start.28) | collective-permute-done | bytes 65568 | tf_op jit(solution)/shard_map/ppermute | solution.py:43
  148.2 0.8 copy-done.5
  149.0 0.8 copy-done.7
  149.9 0.8 copy-done.9
  150.7 0.8 copy-done.11
  151.5 0.8 copy-done.13
  152.4 0.8 copy-done.15
  153.2 4.0 %shard_map.69 = bf16[256,2048]{1,0:T(8,128)(2,1)S(1)} custom-call(s32[6]{0:T(128)S(1)} %pad_add_fusion.place_ref, bf16[16,64,2048]{2,1,0:T(8,128)(2,1)} %bitcast.29, bf16[64,512]{1,0:T(8,128)(2,1)S(1)} %copy-done.11, bf16[64,512]{1,0:T(8,128)(2,1)S(1)} %collective-permute-done.17.refs_1_, bf16[64,512]{1,0:T(8,128)(2,1)S(1)} %collective-permute-done.18.refs_2_, ...), custom_call_target="tpu_custom_call" | custom-call | flops 2147483648 | bytes 5242880 | tf_op jit(solution)/shard_map/pallas_call | solution.py:245
  157.3 4.0 %shard_map.68 = f32[256,2048]{1,0:T(8,128)S(1)} custom-call(s32[6]{0:T(128)S(1)} %pad_add_fusion.place_ref, bf16[16,64,2048]{2,1,0:T(8,128)(2,1)} %bitcast.30, bf16[64,512]{1,0:T(8,128)(2,1)S(1)} %copy-done.11, bf16[64,512]{1,0:T(8,128)(2,1)S(1)} %collective-permute-done.17.refs_1_, bf16[64,512]{1,0:T(8,128)(2,1)S(1)} %collective-permute-done.18.refs_2_, ...), custom_call_target="tpu_custom_call" | custom-call | flops 2147483648 | bytes 5242880 | tf_op jit(solution)/shard_map/pallas_call | solution.py:245
  161.4 1.3 add_convert_fusion
  (80 shorter events, 9.9 us)
Async XLA Ops:
  6.5 2.7 %copy-start.16 = (bf16[256,2048]{1,0:T(8,128)(2,1)S(1)}, bf16[256,2048]{1,0:T(8,128)(2,1)}, u32[]{:S(2)}) copy-start(bf16[256,2048]{1,0:T(8,128)(2,1)} %param.6) | copy-start | bytes 3145732
  6.5 141.6 %all-gather.3.cloned.1.call-start = ((), (), s32[]{:S(2)}) async-start(), calls=%async_computation | async-start | bytes 4456448 | tf_op jit(solution)/shard_map/all_gather | solution.py:318
  7.8 1.4 collective-permute-start
  8.4 0.7 collective-permute-start.1
  9.3 13.8 %copy-start.17 = (bf16[3,64,2048]{2,1,0:T(8,128)(2,1)S(1)}, bf16[3,64,2048]{2,1,0:T(8,128)(2,1)}, u32[]{:S(2)}) copy-start(bf16[3,64,2048]{2,1,0:T(8,128)(2,1)} %param.7) | copy-start | bytes 2359300
  9.4 43.2 %collective-permute-start.2 = (bf16[336,2048]{1,0:T(8,128)(2,1)S(1)}, bf16[336,2048]{1,0:T(8,128)(2,1)S(1)}, u32[]{:S(2)}, u32[]{:S(2)}) collective-permute-start(bf16[336,2048]{1,0:T(8,128)(2,1)S(1)} %pad_maximum_fusion.rest_0_), channel_id=1, source_target_pairs={{0,8},{8,0},{16,24},{24,16},{1,9},{9,1},{17,25},{25,17},{2,10},{10... | collective-permute-start | bytes 4128776 | tf_op jit(solution)/shard_map/ppermute | solution.py:43
  12.4 40.2 %collective-permute-start.3 = (bf16[336,2048]{1,0:T(8,128)(2,1)S(1)}, bf16[336,2048]{1,0:T(8,128)(2,1)S(1)}, u32[]{:S(2)}, u32[]{:S(2)}) collective-permute-start(bf16[336,2048]{1,0:T(8,128)(2,1)S(1)} %pad_maximum_fusion.rest_0_), channel_id=1, source_target_pairs={{0,16},{8,24},{16,0},{24,8},{1,17},{9,25},{17,1},{25,9},{2,18},{10... | collective-permute-start | bytes 4128776 | tf_op jit(solution)/shard_map/ppermute | solution.py:43
  13.9 40.9 %collective-permute-start.4 = (bf16[336,2048]{1,0:T(8,128)(2,1)S(1)}, bf16[336,2048]{1,0:T(8,128)(2,1)}, u32[]{:S(2)}, u32[]{:S(2)}) collective-permute-start(bf16[336,2048]{1,0:T(8,128)(2,1)S(1)} %pad_maximum_fusion.rest_0_), channel_id=1, source_target_pairs={{0,1},{1,0},{2,3},{3,2},{4,5},{5,4},{6,7},{7,6},{8,9},{9,8},{10,11... | collective-permute-start | bytes 4128776 | tf_op jit(solution)/shard_map/ppermute | solution.py:38
  23.2 13.2 %collective-permute-start.5 = (bf16[96,2048]{1,0:T(8,128)(2,1)S(1)}, bf16[96,2048]{1,0:T(8,128)(2,1)S(1)}, u32[]{:S(2)}, u32[]{:S(2)}) collective-permute-start(bf16[96,2048]{1,0:T(8,128)(2,1)S(1)} %get-tuple-element.84.wa_ref), channel_id=1, source_target_pairs={{0,2},{2,6},{6,4},{4,0},{1,3},{3,7},{7,5},{5,1},{8,10},{10,14},{14... | collective-permute-start | bytes 1179656 | tf_op jit(solution)/shard_map/ppermute | solution.py:294
  25.4 19.5 %collective-permute-start.7 = (bf16[96,2048]{1,0:T(8,128)(2,1)S(1)}, bf16[96,2048]{1,0:T(8,128)(2,1)}, u32[]{:S(2)}, u32[]{:S(2)}) collective-permute-start(bf16[96,2048]{1,0:T(8,128)(2,1)S(1)} %get-tuple-element.83.wb_ref), channel_id=1, source_target_pairs={{0,2},{2,6},{6,4},{4,0},{1,3},{3,7},{7,5},{5,1},{8,10},{10,14},{14... | collective-permute-start | bytes 1179656 | tf_op jit(solution)/shard_map/ppermute | solution.py:294
  36.3 16.3 %collective-permute-start.6 = (bf16[96,2048]{1,0:T(8,128)(2,1)S(1)}, bf16[96,2048]{1,0:T(8,128)(2,1)}, u32[]{:S(2)}, u32[]{:S(2)}) collective-permute-start(bf16[96,2048]{1,0:T(8,128)(2,1)S(1)} %collective-permute-done.5.wa_ref), channel_id=1, source_target_pairs={{0,2},{2,6},{6,4},{4,0},{1,3},{3,7},{7,5},{5,1},{8,10},{10,14},{14... | collective-permute-start | bytes 1179656 | tf_op jit(solution)/shard_map/ppermute | solution.py:294
  37.5 0.8 copy-start
  52.6 1.1 copy-start.18
  53.7 1.2 copy-start.19
  54.9 28.1 %collective-permute-start.10 = (bf16[336,2048]{1,0:T(8,128)(2,1)}, bf16[336,2048]{1,0:T(8,128)(2,1)}, u32[]{:S(2)}, u32[]{:S(2)}) collective-permute-start(bf16[336,2048]{1,0:T(8,128)(2,1)} %copy-done.18), channel_id=1, source_target_pairs={{0,1},{1,0},{2,3},{3,2},{4,5},{5,4},{6,7},{7,6},{8,9},{9,8},{10,11... | collective-permute-start | bytes 4128776 | tf_op jit(solution)/shard_map/ppermute | solution.py:38
  55.0 28.0 %collective-permute-start.11 = (bf16[336,2048]{1,0:T(8,128)(2,1)}, bf16[336,2048]{1,0:T(8,128)(2,1)}, u32[]{:S(2)}, u32[]{:S(2)}) collective-permute-start(bf16[336,2048]{1,0:T(8,128)(2,1)} %copy-done.19), channel_id=1, source_target_pairs={{0,1},{1,0},{2,3},{3,2},{4,5},{5,4},{6,7},{7,6},{8,9},{9,8},{10,11... | collective-permute-start | bytes 4128776 | tf_op jit(solution)/shard_map/ppermute | solution.py:38
  55.5 13.5 %collective-permute-start.12 = (bf16[96,2048]{1,0:T(8,128)(2,1)}, bf16[96,2048]{1,0:T(8,128)(2,1)}, u32[]{:S(2)}, u32[]{:S(2)}) collective-permute-start(bf16[96,2048]{1,0:T(8,128)(2,1)} %collective-permute-done.7.wb_ref), channel_id=1, source_target_pairs={{0,2},{2,6},{6,4},{4,0},{1,3},{3,7},{7,5},{5,1},{8,10},{10,14},{14... | collective-permute-start | bytes 1179656 | tf_op jit(solution)/shard_map/ppermute | solution.py:294
  58.3 24.8 %collective-permute-start.9 = (bf16[176,2048]{1,0:T(8,128)(2,1)}, bf16[176,2048]{1,0:T(8,128)(2,1)S(1)}, u32[]{:S(2)}, u32[]{:S(2)}) collective-permute-start(bf16[176,2048]{1,0:T(8,128)(2,1)} %slice.32), channel_id=1, source_target_pairs={{0,16},{8,24},{16,0},{24,8},{1,17},{9,25},{17,1},{25,9},{2,18},{10... | collective-permute-start | bytes 2162696 | tf_op jit(solution)/shard_map/ppermute | solution.py:43
  60.8 22.2 %collective-permute-start.8 = (bf16[160,2048]{1,0:T(8,128)(2,1)}, bf16[160,2048]{1,0:T(8,128)(2,1)S(1)}, u32[]{:S(2)}, u32[]{:S(2)}) collective-permute-start(bf16[160,2048]{1,0:T(8,128)(2,1)} %slice.31), channel_id=1, source_target_pairs={{0,8},{8,0},{16,24},{24,16},{1,9},{9,1},{17,25},{25,17},{2,10},{10... | collective-permute-start | bytes 1966088 | tf_op jit(solution)/shard_map/ppermute | solution.py:43
  68.9 14.1 %collective-permute-start.13 = (bf16[96,2048]{1,0:T(8,128)(2,1)}, bf16[96,2048]{1,0:T(8,128)(2,1)}, u32[]{:S(2)}, u32[]{:S(2)}) collective-permute-start(bf16[96,2048]{1,0:T(8,128)(2,1)} %collective-permute-done.6.wa_ref), channel_id=1, source_target_pairs={{0,2},{2,6},{6,4},{4,0},{1,3},{3,7},{7,5},{5,1},{8,10},{10,14},{14... | collective-permute-start | bytes 1179656 | tf_op jit(solution)/shard_map/ppermute | solution.py:294
  83.0 3.2 %collective-permute-start.16 = (bf16[176,2048]{1,0:T(8,128)(2,1)S(1)}, bf16[176,2048]{1,0:T(8,128)(2,1)S(1)}, u32[]{:S(2)}, u32[]{:S(2)}) collective-permute-start(bf16[176,2048]{1,0:T(8,128)(2,1)S(1)} %collective-permute-done.9.rest_7_), channel_id=1, source_target_pairs={{0,1},{1,0},{2,3},{3,2},{4,5},{5,4},{6,7},{7,6},{8,9},{9,8},{10,11... | collective-permute-start | bytes 2162696 | tf_op jit(solution)/shard_map/ppermute | solution.py:38
  83.8 2.4 %collective-permute-start.15 = (bf16[160,2048]{1,0:T(8,128)(2,1)S(1)}, bf16[160,2048]{1,0:T(8,128)(2,1)S(1)}, u32[]{:S(2)}, u32[]{:S(2)}) collective-permute-start(bf16[160,2048]{1,0:T(8,128)(2,1)S(1)} %collective-permute-done.8.rest_6_), channel_id=1, source_target_pairs={{0,1},{1,0},{2,3},{3,2},{4,5},{5,4},{6,7},{7,6},{8,9},{9,8},{10,11... | collective-permute-start | bytes 1966088 | tf_op jit(solution)/shard_map/ppermute | solution.py:38
  84.6 28.6 %collective-permute-start.14 = (bf16[96,2048]{1,0:T(8,128)(2,1)}, bf16[96,2048]{1,0:T(8,128)(2,1)S(1)}, u32[]{:S(2)}, u32[]{:S(2)}) collective-permute-start(bf16[96,2048]{1,0:T(8,128)(2,1)} %collective-permute-done.12.wb_ref), channel_id=1, source_target_pairs={{0,2},{2,6},{6,4},{4,0},{1,3},{3,7},{7,5},{5,1},{8,10},{10,14},{14... | collective-permute-start | bytes 1179656 | tf_op jit(solution)/shard_map/ppermute | solution.py:294
  86.2 1.0 copy-start.1
  97.5 0.6 copy-start.8
  98.1 16.3 %collective-permute-start.20 = (bf16[64,512]{1,0:T(8,128)(2,1)S(1)}, bf16[64,512]{1,0:T(8,128)(2,1)S(1)}, u32[]{:S(2)}, u32[]{:S(2)}) collective-permute-start(bf16[64,512]{1,0:T(8,128)(2,1)S(1)} %get-tuple-element.60), channel_id=1, source_target_pairs={{0,8},{8,0},{16,24},{24,16},{1,9},{9,1},{17,25},{25,17},{2,10},{10... | collective-permute-start | bytes 196616 | tf_op jit(solution)/shard_map/ppermute | solution.py:43
  98.7 28.1 %collective-permute-start.21 = (bf16[64,512]{1,0:T(8,128)(2,1)S(1)}, bf16[64,512]{1,0:T(8,128)(2,1)S(1)}, u32[]{:S(2)}, u32[]{:S(2)}) collective-permute-start(bf16[64,512]{1,0:T(8,128)(2,1)S(1)} %get-tuple-element.61), channel_id=1, source_target_pairs={{0,16},{8,24},{16,0},{24,8},{1,17},{9,25},{17,1},{25,9},{2,18},{10... | collective-permute-start | bytes 196616 | tf_op jit(solution)/shard_map/ppermute | solution.py:43
  99.9 27.5 %collective-permute-start.22 = (bf16[64,512]{1,0:T(8,128)(2,1)S(1)}, bf16[64,512]{1,0:T(8,128)(2,1)S(1)}, u32[]{:S(2)}, u32[]{:S(2)}) collective-permute-start(bf16[64,512]{1,0:T(8,128)(2,1)S(1)} %get-tuple-element.62), channel_id=1, source_target_pairs={{0,24},{8,16},{16,8},{24,0},{1,25},{9,17},{17,9},{25,1},{2,26},{10... | collective-permute-start | bytes 196616 | tf_op jit(solution)/shard_map/ppermute | solution.py:43
  112.6 16.1 %collective-permute-start.17 = (bf16[64,512]{1,0:T(8,128)(2,1)S(1)}, bf16[64,512]{1,0:T(8,128)(2,1)S(1)}, u32[]{:S(2)}, u32[]{:S(2)}) collective-permute-start(bf16[64,512]{1,0:T(8,128)(2,1)S(1)} %get-tuple-element.55), channel_id=1, source_target_pairs={{0,8},{8,0},{16,24},{24,16},{1,9},{9,1},{17,25},{25,17},{2,10},{10... | collective-permute-start | bytes 196616 | tf_op jit(solution)/shard_map/ppermute | solution.py:43
  113.2 17.2 %collective-permute-start.18 = (bf16[64,512]{1,0:T(8,128)(2,1)S(1)}, bf16[64,512]{1,0:T(8,128)(2,1)S(1)}, u32[]{:S(2)}, u32[]{:S(2)}) collective-permute-start(bf16[64,512]{1,0:T(8,128)(2,1)S(1)} %get-tuple-element.56), channel_id=1, source_target_pairs={{0,16},{8,24},{16,0},{24,8},{1,17},{9,25},{17,1},{25,9},{2,18},{10... | collective-permute-start | bytes 196616 | tf_op jit(solution)/shard_map/ppermute | solution.py:43
  114.4 11.8 %copy-start.2 = (bf16[64,512]{1,0:T(8,128)(2,1)}, bf16[64,512]{1,0:T(8,128)(2,1)S(1)}, u32[]{:S(2)}) copy-start(bf16[64,512]{1,0:T(8,128)(2,1)S(1)} %collective-permute-done.20.refs_5_) | copy-start | bytes 196612
  114.4 16.0 %collective-permute-start.19 = (bf16[64,512]{1,0:T(8,128)(2,1)S(1)}, bf16[64,512]{1,0:T(8,128)(2,1)S(1)}, u32[]{:S(2)}, u32[]{:S(2)}) collective-permute-start(bf16[64,512]{1,0:T(8,128)(2,1)S(1)} %get-tuple-element.57), channel_id=1, source_target_pairs={{0,24},{8,16},{16,8},{24,0},{1,25},{9,17},{17,9},{25,1},{2,26},{10... | collective-permute-start | bytes 196616 | tf_op jit(solution)/shard_map/ppermute | solution.py:43
  126.8 13.7 %copy-start.4 = (bf16[64,512]{1,0:T(8,128)(2,1)}, bf16[64,512]{1,0:T(8,128)(2,1)S(1)}, u32[]{:S(2)}) copy-start(bf16[64,512]{1,0:T(8,128)(2,1)S(1)} %collective-permute-done.21.refs_6_) | copy-start | bytes 196612
  126.8 16.2 %collective-permute-start.23 = (bf16[64,512]{1,0:T(8,128)(2,1)S(1)}, bf16[64,512]{1,0:T(8,128)(2,1)S(1)}, u32[]{:S(2)}, u32[]{:S(2)}) collective-permute-start(bf16[64,512]{1,0:T(8,128)(2,1)S(1)} %get-tuple-element.72), channel_id=1, source_target_pairs={{0,8},{8,0},{16,24},{24,16},{1,9},{9,1},{17,25},{25,17},{2,10},{10... | collective-permute-start | bytes 196616 | tf_op jit(solution)/shard_map/ppermute | solution.py:43
  127.4 13.1 %copy-start.6 = (bf16[64,512]{1,0:T(8,128)(2,1)}, bf16[64,512]{1,0:T(8,128)(2,1)S(1)}, u32[]{:S(2)}) copy-start(bf16[64,512]{1,0:T(8,128)(2,1)S(1)} %collective-permute-done.22.refs_7_) | copy-start | bytes 196612
  127.4 17.3 %collective-permute-start.24 = (bf16[64,512]{1,0:T(8,128)(2,1)S(1)}, bf16[64,512]{1,0:T(8,128)(2,1)S(1)}, u32[]{:S(2)}, u32[]{:S(2)}) collective-permute-start(bf16[64,512]{1,0:T(8,128)(2,1)S(1)} %get-tuple-element.73), channel_id=1, source_target_pairs={{0,16},{8,24},{16,0},{24,8},{1,17},{9,25},{17,1},{25,9},{2,18},{10... | collective-permute-start | bytes 196616 | tf_op jit(solution)/shard_map/ppermute | solution.py:43
  128.6 16.1 %collective-permute-start.25 = (bf16[64,512]{1,0:T(8,128)(2,1)S(1)}, bf16[64,512]{1,0:T(8,128)(2,1)S(1)}, u32[]{:S(2)}, u32[]{:S(2)}) collective-permute-start(bf16[64,512]{1,0:T(8,128)(2,1)S(1)} %get-tuple-element.74), channel_id=1, source_target_pairs={{0,24},{8,16},{16,8},{24,0},{1,25},{9,17},{17,9},{25,1},{2,26},{10... | collective-permute-start | bytes 196616 | tf_op jit(solution)/shard_map/ppermute | solution.py:43
  130.3 17.8 %copy-start.3 = (bf16[64,512]{1,0:T(8,128)(2,1)S(1)}, bf16[64,512]{1,0:T(8,128)(2,1)}, u32[]{:S(2)}) copy-start(bf16[64,512]{1,0:T(8,128)(2,1)} %copy-done.2) | copy-start | bytes 196612
  141.2 4.3 %collective-permute-start.26 = (bf16[64,512]{1,0:T(8,128)(2,1)S(1)}, bf16[64,512]{1,0:T(8,128)(2,1)S(1)}, u32[]{:S(2)}, u32[]{:S(2)}) collective-permute-start(bf16[64,512]{1,0:T(8,128)(2,1)S(1)} %get-tuple-element.78), channel_id=1, source_target_pairs={{0,8},{8,0},{16,24},{24,16},{1,9},{9,1},{17,25},{25,17},{2,10},{10... | collective-permute-start | bytes 196616 | tf_op jit(solution)/shard_map/ppermute | solution.py:43
  141.8 4.3 %collective-permute-start.27 = (bf16[64,512]{1,0:T(8,128)(2,1)S(1)}, bf16[64,512]{1,0:T(8,128)(2,1)S(1)}, u32[]{:S(2)}, u32[]{:S(2)}) collective-permute-start(bf16[64,512]{1,0:T(8,128)(2,1)S(1)} %get-tuple-element.79), channel_id=1, source_target_pairs={{0,16},{8,24},{16,0},{24,8},{1,17},{9,25},{17,1},{25,9},{2,18},{10... | collective-permute-start | bytes 196616 | tf_op jit(solution)/shard_map/ppermute | solution.py:43
  143.0 5.2 %collective-permute-start.28 = (bf16[64,512]{1,0:T(8,128)(2,1)S(1)}, bf16[64,512]{1,0:T(8,128)(2,1)S(1)}, u32[]{:S(2)}, u32[]{:S(2)}) collective-permute-start(bf16[64,512]{1,0:T(8,128)(2,1)S(1)} %get-tuple-element.80), channel_id=1, source_target_pairs={{0,24},{8,16},{16,8},{24,0},{1,25},{9,17},{17,9},{25,1},{2,26},{10... | collective-permute-start | bytes 196616 | tf_op jit(solution)/shard_map/ppermute | solution.py:43
  148.2 0.8 copy-start.5
  149.0 0.8 copy-start.7
  149.8 0.8 copy-start.9
  150.7 0.8 copy-start.11
  151.5 0.8 copy-start.13
  152.4 0.8 copy-start.15
  157.2 4.1 %collective-permute-start.29 = (bf16[256,2048]{1,0:T(8,128)(2,1)S(1)}, bf16[256,2048]{1,0:T(8,128)(2,1)S(1)}, u32[]{:S(2)}, u32[]{:S(2)}) collective-permute-start(bf16[256,2048]{1,0:T(8,128)(2,1)S(1)} %shard_map.69), channel_id=1, source_target_pairs={{0,1},{1,0},{2,3},{3,2},{4,5},{5,4},{6,7},{7,6},{8,9},{9,8},{10,11... | collective-permute-start | bytes 3145736 | tf_op jit(solution)/shard_map/ppermute | solution.py:38
  (3 other events, 1.9 us)
Sparse Core Ops, SparseCore 0:
  55.0 90.1 all-gather.2

commit v2 on v1

v2 whole, which is shorter than its diff:
```python
import functools

import jax
import jax.numpy as jnp
from jax import lax
from jax.experimental import pallas as pl
from jax.experimental.pallas import tpu as pltpu
from jax.sharding import Mesh
from jax.sharding import PartitionSpec as P

GSIZE = 16
SHORT = 7
TAPS = 128
LANES = 128
WIDE = 64
HALO = 160
SMEM = pl.BlockSpec(memory_space=pltpu.SMEM)
VMEM = pl.BlockSpec(memory_space=pltpu.VMEM)
LIMIT = pltpu.CompilerParams(vmem_limit_bytes=32 * 1024 * 1024)


def ring_of(count):
    order = [i for i in range(count) if i == 0 or i % 2 == 1]
    order += [i for i in reversed(range(1, count)) if i % 2 == 0]
    return [(order[i], order[(i + 1) % count]) for i in range(count)]


def origins_of(count):
    previous = dict((target, source) for source, target in ring_of(count))
    table = [list(range(count))]
    for _ in range(count - 1):
        table.append([previous[i] for i in table[-1]])
    return table


def swap(block):
    return lax.ppermute(block, "core", [(0, 1), (1, 0)])


def across(block, r):
    count = lax.axis_size("dp")
    return lax.ppermute(block, "dp", [(i, i ^ r) for i in range(count)])


def tie(*groups):
    return lax.optimization_barrier(groups)


def dot(a, b):
    return jnp.dot(a, b, preferred_element_type=jnp.float32)


def nt(a, b):
    return lax.dot_general(a, b, (((1,), (1,)), ((), ())), preferred_element_type=jnp.float32)


def mix_kernel(steps, slots, parts, place_ref, taps_ref, long_ref, *rest):
    weights, rest = rest[: 2 * len(steps)], rest[2 * len(steps) :]
    pieces, rest = rest[: len(parts)], rest[len(parts) :]
    outs, rest = rest[: len(slots)], rest[len(slots) :]
    w, first, second, packed, turned, tiles = rest
    span = first.shape[1] - HALO
    rows = span // 2
    core = place_ref[0]
    count = WIDE // GSIZE
    band = 64
    blocks = span // TAPS
    lower = lax.broadcasted_iota(jnp.int32, (band, LANES), 1) < WIDE
    taps = [taps_ref[place_ref[2 + step]] for step in steps]

    for c, step in enumerate(steps):
        wa, wb = weights[2 * c], weights[2 * c + 1]
        cut = wa.shape[0]
        w[c, :cut] = wa[...]
        w[c, cut : 2 * WIDE] = wb[: 2 * WIDE - cut]
        w[c, 2 * WIDE : 3 * WIDE] = jnp.zeros((WIDE, w.shape[2]), w.dtype)
        w[c, 3 * WIDE :] = wb[2 * WIDE - cut :]
        filters = long_ref[place_ref[2 + step]]
        for g in range(count):
            line = jnp.concatenate(
                [jnp.zeros((1, TAPS), jnp.float32), filters[g : g + 1, :]], axis=1
            )
            square = pltpu.roll(
                jnp.broadcast_to(line, (2 * TAPS, 2 * TAPS)), 0, 1, stride=1, stride_axis=0
            )
            tiles[c * count + g] = square[:, :TAPS].astype(jnp.bfloat16)

    def put(half, value, at):
        here = pl.ds(pl.multiple_of(at, 16), value.shape[0])
        first[half, here] = value[:, :LANES]
        second[half, here] = value[:, LANES:]

    def project_unit(n, c, i):
        for ref, (slot, side, start) in zip(pieces, parts):
            if slot != slots[i]:
                continue
            owner = core if side == 0 else 1 - core
            value = nt(ref[...], w[c]).astype(jnp.bfloat16).astype(jnp.float32)
            end = start + ref.shape[0]
            if start < rows:
                put(n % 2, value[: min(end, rows) - start], HALO + owner * rows + start)
            if end > rows:
                low = max(start, rows)
                put(n % 2, value[low - start :], owner * (HALO // 2) + low - rows)

    def feat(ref, n, at, c, lanes):
        total = None
        for j in range(SHORT):
            term = taps[c][j : j + 1, lanes] * ref[n % 2, at - j : at - j + band, :]
            total = term if total is None else total + term
        return total

    units = [(c, i) for c in range(len(steps)) for i in range(len(slots))]
    project_unit(0, *units[0])
    for n, (c, i) in enumerate(units):
        if n + 1 < len(units):
            project_unit(n + 1, *units[n + 1])
        for m in range((TAPS + span) // band):
            at = HALO - TAPS + m * band
            x = feat(first, n, at, c, slice(0, LANES))
            y = feat(second, n, at, c, slice(LANES, 2 * LANES))
            packed[n % 2, m * band : (m + 1) * band, :] = jnp.where(lower, x, x * y).astype(
                jnp.bfloat16
            )
        turned[n] = packed[n % 2].T

    for c in range(len(steps)):
        mine = [n for n in range(len(units)) if units[n][0] == c]
        for g in range(count):
            channels = slice(WIDE + g * GSIZE, WIDE + (g + 1) * GSIZE)
            window = jnp.concatenate(
                [
                    turned[n, channels, b * TAPS : (b + 2) * TAPS]
                    for n in mine
                    for b in range(blocks)
                ],
                axis=0,
            )
            conv = dot(window, tiles[c * count + g])
            for k, n in enumerate(mine):
                row = jnp.concatenate(
                    [
                        conv[(k * blocks + b) * GSIZE : (k * blocks + b + 1) * GSIZE]
                        for b in range(blocks)
                    ],
                    axis=1,
                )
                query = turned[n, g * GSIZE : (g + 1) * GSIZE, TAPS:].astype(jnp.float32)
                at = c * WIDE + g * GSIZE
                outs[units[n][1]][at : at + GSIZE, :] = (query * row).astype(jnp.bfloat16)


def mix_chunks(steps, slots, rows, place, taps, filters, wa, wb, parts, pieces):
    features = wa[0].shape[1]
    chosen = [n for n, part in enumerate(parts) if part[0] in slots]
    parts, pieces = [parts[n] for n in chosen], [pieces[n] for n in chosen]
    weights = [half[s] for s in steps for half in (wa, wb)]
    units = len(steps) * len(slots)
    return pl.pallas_call(
        functools.partial(mix_kernel, steps, slots, parts),
        out_shape=[jax.ShapeDtypeStruct((len(steps) * WIDE, 2 * rows), jnp.bfloat16)] * len(slots),
        in_specs=[SMEM] + [VMEM] * (2 + len(weights) + len(pieces)),
        out_specs=[VMEM] * len(slots),
        scratch_shapes=[
            pltpu.VMEM((len(steps), 4 * WIDE, features), jnp.bfloat16),
            pltpu.VMEM((2, HALO + 2 * rows, LANES), jnp.float32),
            pltpu.VMEM((2, HALO + 2 * rows, LANES), jnp.float32),
            pltpu.VMEM((2, TAPS + 2 * rows, LANES), jnp.bfloat16),
            pltpu.VMEM((units, LANES, TAPS + 2 * rows), jnp.bfloat16),
            pltpu.VMEM((len(steps) * WIDE // GSIZE, 2 * TAPS, TAPS), jnp.bfloat16),
        ],
        compiler_params=LIMIT,
        cost_estimate=pl.CostEstimate(
            flops=4 * units * 2 * rows * 4 * WIDE * features,
            bytes_accessed=2 * units * 2 * rows * features,
            transcendentals=0,
        ),
    )(place, taps, filters, *weights, *pieces)


def out_kernel(mirror, order, chips, width, place_ref, v_ref, *refs):
    parts = refs[: len(refs) - 4]
    out_ref, left, right, total = refs[len(refs) - 4 :]
    rows = out_ref.shape[0]
    core, dp = place_ref[0], place_ref[1]
    if mirror:
        core = 1 - core
    depth = left.shape[0]
    if order is None:
        left[...] = parts[0][...]
        right[...] = v_ref[...]
        size = depth
    else:
        for n, (r, s, k, row) in enumerate(order):
            here = slice(n * width, (n + 1) * width)
            left[here] = parts[k][row : row + width]
            right[here] = v_ref[lax.bitwise_xor(dp, r) * chips + place_ref[2 + s]]
        size = depth // 2
    at = pl.multiple_of(core * rows, LANES)
    tile = 512
    for start in range(0, depth, size):
        a = left[start : start + size, pl.ds(at, rows)].T
        for t in range(0, out_ref.shape[1], tile):
            here = slice(t, t + tile)
            value = dot(a, right[start : start + size, here])
            if start:
                value = value + total[:, here]
            if start + size < depth:
                total[:, here] = value
            else:
                out_ref[:, here] = value.astype(out_ref.dtype)


def project(mirror, order, chips, width, depth, place, v, parts, dtype):
    span, features = parts[0].shape[1], v.shape[-1]
    rows = span // 2
    return pl.pallas_call(
        functools.partial(out_kernel, mirror, order, chips, width),
        out_shape=jax.ShapeDtypeStruct((rows, features), dtype),
        in_specs=[SMEM, VMEM] + [VMEM] * len(parts),
        out_specs=VMEM,
        scratch_shapes=[
            pltpu.VMEM((depth, span), jnp.bfloat16),
            pltpu.VMEM((depth, features), jnp.bfloat16),
            pltpu.VMEM((rows, features), jnp.float32),
        ],
        compiler_params=LIMIT,
        cost_estimate=pl.CostEstimate(
            flops=4 * rows * features * depth,
            bytes_accessed=2 * depth * (features + span),
            transcendentals=0,
        ),
    )(place, v, *parts)


def local_filters(chips, width, dp, core, short_taps, long_taps):
    part = short_taps.reshape(SHORT, 3, -1, 2, width)
    part = lax.dynamic_slice(
        part, (0, 0, dp * chips, core, 0), (SHORT, 3, chips, 1, width)
    ).reshape(SHORT, 3, chips, width)
    part = jnp.pad(part, ((0, 1), (0, 0), (0, 0), (0, WIDE - width)))
    part = jnp.transpose(part, (2, 0, 1, 3))
    taps = jnp.concatenate(
        [part[:, :, 0], part[:, :, 1], jnp.zeros_like(part[:, :, 0]), part[:, :, 2]], axis=2
    )
    groups = max(1, width // GSIZE)
    each = [
        lax.dynamic_slice_in_dim(
            long_taps, (2 * (dp * chips + i) + core) * width // GSIZE, groups, 0
        )
        for i in range(chips)
    ]
    filters = jnp.stack(each).astype(jnp.float32)
    return taps, jnp.pad(filters, ((0, 0), (0, WIDE // GSIZE - groups), (0, 0)))


def shards(chips, tokens, in_weight, short_taps, long_taps, out_weight):
    _, width, features = in_weight.shape
    rows = tokens.shape[0]
    slots = lax.axis_size("dp")
    dp = lax.axis_index("dp")
    z = lax.axis_index("z")
    core = lax.axis_index("core")
    ring = ring_of(chips)
    forward = lambda block: lax.ppermute(block, "z", ring)

    table = jnp.array(origins_of(chips), jnp.int32)
    origins = lax.dynamic_index_in_dim(table, z, 1, False)
    place = jnp.concatenate([jnp.stack([core, dp]).astype(jnp.int32), origins])
    taps, filters = local_filters(chips, width, dp, core, short_taps, long_taps)

    pairs = lambda c: [(2 * i + 1, 2 * (i + 1) + c) for i in range(chips - 1)]
    half = HALO // 2
    edge = lax.ppermute(tokens[rows - HALO : rows - half], ("z", "core"), pairs(0)) + lax.ppermute(
        tokens[rows - half :], ("z", "core"), pairs(1)
    )
    v = lax.all_gather(out_weight, ("dp", "z"))
    run_mix = lambda steps, which: mix_chunks(
        steps, which, rows, place, taps, filters, wa, wb, parts, pieces
    )

    if slots == 4 and chips == 4 and width == WIDE:
        flat = in_weight.reshape(3 * width, features)
        cut = 3 * width // 2
        wa, wb = [flat[:cut]], [flat[cut:]]
        wa.append(forward(wa[0]))
        edge, wa[1] = tie(edge, wa[1])

        block = jnp.concatenate([tokens, edge])
        x, y, twin = across(block, 1), across(block, 2), swap(block)
        wb.append(forward(wb[0]))
        wa.append(forward(wa[1]))
        wb.append(forward(wb[1]))
        x, y, twin, wa, wb, taps, filters, place = tie(x, y, twin, wa, wb, taps, filters, place)
        wa, wb = list(wa), list(wb)

        mid = HALO
        x_twin, y_twin = swap(x), swap(y)
        wa.append(forward(wa[2]))
        wb.append(forward(wb[2]))
        x_far, y_far = across(y[:mid], 1), across(x[mid:], 2)
        parts = [(0, 0, 0), (0, 1, 0), (1, 0, 0), (1, 1, 0), (2, 0, 0), (2, 1, 0)]
        pieces = [block, twin, x, x_twin, y, y_twin]
        early = run_mix((0, 1, 2), (0, 1, 2))
        early, x_far, y_far, wa, wb = tie(early, x_far, y_far, wa, wb)

        parts += [(3, 0, 0), (3, 0, mid), (3, 1, 0), (3, 1, mid)]
        pieces += [x_far, y_far, swap(x_far), swap(y_far)]
        late = run_mix((3,), (0, 1, 2))
        (far,) = run_mix((0, 1, 2, 3), (3,))
        together = [early[0], late[0]]
        for r in (1, 2):
            together += [across(early[r], r), across(late[r], r)]
        together.append(across(far, 3))
        v = v.reshape(slots * chips, width, -1)
        order = [(r, s, 2 * r, s * width) for s in range(3) for r in range(3)]
        order += [(r, 3, 2 * r + 1, 0) for r in range(3)]
        order += [(3, s, 6, s * width) for s in range(chips)]
    else:
        block = jnp.concatenate([tokens, edge])
        w, wa, wb = in_weight, [], []
        for s in range(chips):
            padded = jnp.pad(w, ((0, 0), (0, WIDE - width), (0, 0))).reshape(3 * WIDE, features)
            wa.append(padded[: 3 * WIDE // 2])
            wb.append(padded[3 * WIDE // 2 :])
            if s + 1 < chips:
                w = forward(w)
        pieces = [block] + [across(block, r) for r in range(1, slots)]
        pieces += [swap(piece) for piece in pieces]
        parts = [(r, side, 0) for side in range(2) for r in range(slots)]
        moved = []
        for s in range(chips):
            mixed = []
            for r in range(0, slots, 4):
                mixed += run_mix((s,), tuple(range(r, min(r + 4, slots))))
            mixed = [m[:width] for m in mixed]
            moved.append([mixed[0]] + [across(mixed[r], r) for r in range(1, slots)])
        turn = lax.bitwise_xor(dp, jnp.arange(slots))
        v = v.reshape(slots, chips, width, -1)[turn][:, origins].reshape(slots * chips * width, -1)
        together = [jnp.concatenate([one[r] for r in range(slots) for one in moved])]
        order = None
    depth = slots * chips * width
    run = lambda mirror, dtype: project(
        mirror, order, chips, width, depth, place, v, together, dtype
    )
    theirs = swap(run(True, jnp.bfloat16))
    mine = run(False, jnp.float32)
    return (mine + theirs.astype(jnp.float32)).astype(jnp.bfloat16)


def solution(mesh):
    count = mesh.shape["dp"]
    chips = mesh.shape["ctx"] // 2
    fine = Mesh(mesh.devices.reshape(count, chips, 2), ("dp", "z", "core"))
    every = ("dp", "z", "core")
    in_specs = (P(every, None), P(None, every, None), P(), P(), P(every, None))
    return jax.shard_map(
        functools.partial(shards, chips),
        mesh=fine,
        in_specs=in_specs,
        out_specs=P(every, None),
        check_vma=False,
    )
```

time: 170 us -> 172 us (1.012)
  waiting for transfers between devices: 42.1 us -> 61 us
  Pallas kernels: 48.9 us -> 31 us
    pallas_call x6 -> x5, Pallas kernels: 48.9 us -> 31 us  [the longest x3 27.2 us: mix_chunks(): pl.pallas_call(functools.partial(mix_kernel, steps, slots, parts), out_sh...]
    ppermute x6, waiting for transfers between devices: 38.6 us -> 56.4 us  [shards(): forward = lambda block: lax.ppermute(block, 'z', ring)]
    ppermute x16 -> x9, starting transfers between devices: 20.1 us -> 16.4 us  [across(): return lax.ppermute(block, 'dp', [(i, i ^ r) for i in range(count)])]
    slice x2, local copies, waits for them, and re-layouts: 4.03 us -> 1.18 us  [shards(): x_far, y_far = (across(y[:mid], 1), across(x[mid:], 2))]
    ppermute x6, starting transfers between devices: 10 us -> 12.9 us  [shards(): forward = lambda block: lax.ppermute(block, 'z', ring)]
    unnamed x41 -> x50, local copies, waits for them, and re-layouts: 11.5 us -> 13.9 us
    ppermute x16 -> x9, waiting for transfers between devices: 3.49 us -> 2.85 us  [across(): return lax.ppermute(block, 'dp', [(i, i ^ r) for i in range(count)])]
  transfers between devices with their start and end apart: 31 -> 24, of which waited for: 8 -> 8; matrix products, arithmetic and copies ran while one was open for 5% -> 4% of each run, Pallas kernels for 26% -> 17%
where the time goes in v2:
time: 172 us; the launch traced here: 170 us
  waiting for transfers between devices  61 us (35%)
  starting transfers between devices  42.2 us (25%)
  Pallas kernels  31 us (18%)
  local copies, waits for them, and re-layouts  20.8 us (12%)
  between operations  13.7 us (8%)
    ppermute x6, waiting for transfers between devices, shards(): forward = lambda block: lax.ppermute(block, 'z', ring)  56.4 us
    pallas_call x3, Pallas kernels, mix_chunks(): pl.pallas_call(functools.partial(mix_kernel, steps, slots, parts), out_sh...  27.2 us
    ppermute x9, starting transfers between devices, across(): return lax.ppermute(block, 'dp', [(i, i ^ r) for i in range(count)])  16.4 us
    unnamed x50, local copies, waits for them, and re-layouts  13.9 us
    ppermute x6, starting transfers between devices, shards(): forward = lambda block: lax.ppermute(block, 'z', ring)  12.9 us
    ppermute x6, starting transfers between devices, swap(): return lax.ppermute(block, 'core', [(0, 1), (1, 0)])  11.5 us
    pallas_call x2, Pallas kernels, project(): pl.pallas_call(functools.partial(out_kernel, mirror, order, chips, width)...  3.77 us
  transfers between devices with their start and end apart: 24, of which 8 were waited for; matrix products, arithmetic and copies ran while one was open for 4% of the time, Pallas kernels for 17%

profile of v2, /device:TPU:0, one launch (start us, length us, event | category | flops | bytes accessed | tf_op | source)
XLA Modules:
  0.0 170.2 jit_solution(14240578544077729410)
XLA Ops:
  6.5 0.7 all-gather.3.cloned.1.call-update
  7.3 1.3 fusion.6
  8.5 3.1 %collective-permute-start.2 = (bf16[96,2048]{1,0:T(8,128)(2,1)S(1)}, bf16[96,2048]{1,0:T(8,128)(2,1)S(1)}, u32[]{:S(2)}, u32[]{:S(2)}) collective-permute-start(bf16[96,2048]{1,0:T(8,128)(2,1)S(1)} %get-tuple-element.63.rest_0_), channel_id=1, source_target_pairs={{0,2},{2,6},{6,4},{4,0},{1,3},{3,7},{7,5},{5,1},{8,10},{10,14},{14... | collective-permute-start | bytes 1179656 | tf_op jit(solution)/shard_map/ppermute | solution.py:265
  11.7 0.7 collective-permute-start
  12.4 0.7 collective-permute-start.1
  13.3 8.5 %collective-permute-done.2.rest_2_ = bf16[96,2048]{1,0:T(8,128)(2,1)S(1)} collective-permute-done((bf16[96,2048]{1,0:T(8,128)(2,1)S(1)}, bf16[96,2048]{1,0:T(8,128)(2,1)S(1)}, u32[]{:S(2)}, u32[]{:S(2)}) %collective-permute-start.2) | collective-permute-done | bytes 393248 | tf_op jit(solution)/shard_map/ppermute | solution.py:265
  21.8 0.7 copy-done.1
  22.5 1.6 collective-permute-start.3
  24.1 1.5 collective-permute-start.4
  25.6 10.5 %collective-permute-start.5 = (bf16[336,2048]{1,0:T(8,128)(2,1)S(1)}, bf16[336,2048]{1,0:T(8,128)(2,1)}, u32[]{:S(2)}, u32[]{:S(2)}) collective-permute-start(bf16[336,2048]{1,0:T(8,128)(2,1)S(1)} %constant_dynamic-update-slice_fusion.rest_6_.rest_2_), channel_id=1, source_target_pairs={{0,1},{1,0},{2,3},{3,2},{4,5},{5,4},{6,7},{7,6},{8,9},{9,8},{10,11... | collective-permute-start | bytes 4128776 | tf_op jit(solution)/shard_map/ppermute | solution.py:37
  36.1 2.6 %collective-permute-start.7 = (bf16[96,2048]{1,0:T(8,128)(2,1)S(1)}, bf16[96,2048]{1,0:T(8,128)(2,1)}, u32[]{:S(2)}, u32[]{:S(2)}) collective-permute-start(bf16[96,2048]{1,0:T(8,128)(2,1)S(1)} %get-tuple-element.64.rest_1_), channel_id=1, source_target_pairs={{0,2},{2,6},{6,4},{4,0},{1,3},{3,7},{7,5},{5,1},{8,10},{10,14},{14... | collective-permute-start | bytes 1179656 | tf_op jit(solution)/shard_map/ppermute | solution.py:265
  38.7 2.0 %reshape.10 = f32[7,3,16,2,64]{4,3,2,0,1:T(2,128)} reshape(f32[7,3,2048]{2,0,1:T(8,128)} %param.8) | data formatting | bytes 344064 | tf_op jit(solution)/shard_map/reshape | solution.py:237
  40.7 0.8 fusion
  41.5 0.9 constant_dynamic-slice_fusion.5
  42.4 0.7 fusion.4
  43.1 3.5 %collective-permute-start.6 = (bf16[96,2048]{1,0:T(8,128)(2,1)}, bf16[96,2048]{1,0:T(8,128)(2,1)S(1)}, u32[]{:S(2)}, u32[]{:S(2)}) collective-permute-start(bf16[96,2048]{1,0:T(8,128)(2,1)} %copy-done.1), channel_id=1, source_target_pairs={{0,2},{2,6},{6,4},{4,0},{1,3},{3,7},{7,5},{5,1},{8,10},{10,14},{14... | collective-permute-start | bytes 1179656 | tf_op jit(solution)/shard_map/ppermute | solution.py:265
  46.6 10.8 %collective-permute-done.7.rest_3_ = bf16[96,2048]{1,0:T(8,128)(2,1)} collective-permute-done((bf16[96,2048]{1,0:T(8,128)(2,1)S(1)}, bf16[96,2048]{1,0:T(8,128)(2,1)}, u32[]{:S(2)}, u32[]{:S(2)}) %collective-permute-start.7) | collective-permute-done | bytes 393248 | tf_op jit(solution)/shard_map/ppermute | solution.py:265
  57.5 0.7 collective-permute-start.8
  58.3 12.0 %collective-permute-done.6.rest_4_ = bf16[96,2048]{1,0:T(8,128)(2,1)S(1)} collective-permute-done((bf16[96,2048]{1,0:T(8,128)(2,1)}, bf16[96,2048]{1,0:T(8,128)(2,1)S(1)}, u32[]{:S(2)}, u32[]{:S(2)}) %collective-permute-start.6) | collective-permute-done | bytes 393248 | tf_op jit(solution)/shard_map/ppermute | solution.py:265
  70.3 7.8 %collective-permute-done.8.rest_5_ = bf16[96,2048]{1,0:T(8,128)(2,1)S(1)} collective-permute-done((bf16[96,2048]{1,0:T(8,128)(2,1)}, bf16[96,2048]{1,0:T(8,128)(2,1)S(1)}, u32[]{:S(2)}, u32[]{:S(2)}) %collective-permute-start.8) | collective-permute-done | bytes 393248 | tf_op jit(solution)/shard_map/ppermute | solution.py:265
  78.8 1.1 slice.34
  80.9 0.7 collective-permute-start.13
  81.7 1.1 collective-permute-done.10.rest_11_.rest_7_
  82.7 2.3 %collective-permute-start.14 = (bf16[96,2048]{1,0:T(8,128)(2,1)S(1)}, bf16[96,2048]{1,0:T(8,128)(2,1)S(1)}, u32[]{:S(2)}, u32[]{:S(2)}) collective-permute-start(bf16[96,2048]{1,0:T(8,128)(2,1)S(1)} %collective-permute-done.8.rest_5_), channel_id=1, source_target_pairs={{0,2},{2,6},{6,4},{4,0},{1,3},{3,7},{7,5},{5,1},{8,10},{10,14},{14... | collective-permute-start | bytes 1179656 | tf_op jit(solution)/shard_map/ppermute | solution.py:265
  85.0 12.9 %shard_map.64 = (bf16[192,512]{1,0:T(8,128)(2,1)S(1)}, bf16[192,512]{1,0:T(8,128)(2,1)S(1)}, bf16[192,512]{1,0:T(8,128)(2,1)S(1)}) custom-call(s32[6]{0:T(128)S(1)} %pad_add_fusion.place_ref, f32[4,8,256]{2,1,0:T(8,128)S(1)} %pad_maximum_fusion.taps_ref, f32[4,4,128]{2,1,0:T(4,128)S(1)} %maximum_convert_fusion.long_ref, ...), custom_call_target="tpu_custom_call" | custom-call | flops 9663676416 | bytes 18874368 | tf_op jit(solution)/shard_map/pallas_call | solution.py:159
  98.0 0.7 copy-done.16
  98.7 5.2 %collective-permute-done.13.rest_0_.rest_6_ = bf16[96,2048]{1,0:T(8,128)(2,1)S(1)} collective-permute-done((bf16[96,2048]{1,0:T(8,128)(2,1)S(1)}, bf16[96,2048]{1,0:T(8,128)(2,1)S(1)}, u32[]{:S(2)}, u32[]{:S(2)}) %collective-permute-start.13) | collective-permute-done | bytes 393248 | tf_op jit(solution)/shard_map/ppermute | solution.py:265
  103.9 12.1 %collective-permute-done.14.rest_1_.rest_7_ = bf16[96,2048]{1,0:T(8,128)(2,1)S(1)} collective-permute-done((bf16[96,2048]{1,0:T(8,128)(2,1)S(1)}, bf16[96,2048]{1,0:T(8,128)(2,1)S(1)}, u32[]{:S(2)}, u32[]{:S(2)}) %collective-permute-start.14) | collective-permute-done | bytes 393248 | tf_op jit(solution)/shard_map/ppermute | solution.py:265
  116.5 3.9 %collective-permute-start.15 = (bf16[192,512]{1,0:T(8,128)(2,1)S(1)}, bf16[192,512]{1,0:T(8,128)(2,1)S(1)}, u32[]{:S(2)}, u32[]{:S(2)}) collective-permute-start(bf16[192,512]{1,0:T(8,128)(2,1)S(1)} %get-tuple-element.59), channel_id=1, source_target_pairs={{0,8},{8,0},{16,24},{24,16},{1,9},{9,1},{17,25},{25,17},{2,10},{10... | collective-permute-start | bytes 589832 | tf_op jit(solution)/shard_map/ppermute | solution.py:42
  120.4 4.8 %collective-permute-start.17 = (bf16[192,512]{1,0:T(8,128)(2,1)S(1)}, bf16[192,512]{1,0:T(8,128)(2,1)S(1)}, u32[]{:S(2)}, u32[]{:S(2)}) collective-permute-start(bf16[192,512]{1,0:T(8,128)(2,1)S(1)} %get-tuple-element.61), channel_id=1, source_target_pairs={{0,16},{8,24},{16,0},{24,8},{1,17},{9,25},{17,1},{25,9},{2,18},{10... | collective-permute-start | bytes 589832 | tf_op jit(solution)/shard_map/ppermute | solution.py:42
  125.2 8.4 %shard_map.66 = bf16[256,512]{1,0:T(8,128)(2,1)S(1)} custom-call(s32[6]{0:T(128)S(1)} %pad_add_fusion.place_ref, f32[4,8,256]{2,1,0:T(8,128)S(1)} %pad_maximum_fusion.taps_ref, f32[4,4,128]{2,1,0:T(4,128)S(1)} %maximum_convert_fusion.long_ref, bf16[96,2048]{1,0:T(8,128)(2,1)S(1)} %get-tuple-element.63.rest_0_, ...), custom_call_target="tpu_custom_call" | custom-call | flops 4294967296 | bytes 8388608 | tf_op jit(solution)/shard_map/pallas_call | solution.py:159
  133.6 2.1 %collective-permute-start.21 = (bf16[256,512]{1,0:T(8,128)(2,1)S(1)}, bf16[256,512]{1,0:T(8,128)(2,1)S(1)}, u32[]{:S(2)}, u32[]{:S(2)}) collective-permute-start(bf16[256,512]{1,0:T(8,128)(2,1)S(1)} %shard_map.66), channel_id=1, source_target_pairs={{0,24},{8,16},{16,8},{24,0},{1,25},{9,17},{17,9},{25,1},{2,26},{10... | collective-permute-start | bytes 786440 | tf_op jit(solution)/shard_map/ppermute | solution.py:42
  135.7 5.8 %shard_map.65 = (bf16[64,512]{1,0:T(8,128)(2,1)S(1)}, bf16[64,512]{1,0:T(8,128)(2,1)S(1)}, bf16[64,512]{1,0:T(8,128)(2,1)S(1)}) custom-call(s32[6]{0:T(128)S(1)} %pad_add_fusion.place_ref, f32[4,8,256]{2,1,0:T(8,128)S(1)} %pad_maximum_fusion.taps_ref, f32[4,4,128]{2,1,0:T(4,128)S(1)} %maximum_convert_fusion.long_ref, ...), custom_call_target="tpu_custom_call" | custom-call | flops 3221225472 | bytes 6291456 | tf_op jit(solution)/shard_map/pallas_call | solution.py:159
  142.2 1.4 collective-permute-start.18
  143.6 2.8 %collective-permute-done.16.refs_3_ = bf16[64,512]{1,0:T(8,128)(2,1)S(1)} collective-permute-done((bf16[64,512]{1,0:T(8,128)(2,1)S(1)}, bf16[64,512]{1,0:T(8,128)(2,1)S(1)}, u32[]{:S(2)}, u32[]{:S(2)}) %collective-permute-start.16) | collective-permute-done | bytes 65568 | tf_op jit(solution)/shard_map/ppermute | solution.py:42
  146.5 0.7 copy-done.6
  147.8 0.7 copy-done.3
  148.5 2.2 %copy-done = bf16[1024,2048]{1,0:T(8,128)(2,1)S(1)} copy-done((bf16[1024,2048]{1,0:T(8,128)(2,1)S(1)}, bf16[1024,2048]{1,0:T(8,128)(2,1)}, u32[]{:S(2)}) %copy-start) | copy-done | bytes 4194328
  150.7 0.9 copy-done.4
  151.7 0.9 copy-done.7
  152.6 0.9 copy-done.10
  153.5 0.9 copy-done.17
  154.4 0.8 copy-done.20
  155.3 1.9 %shard_map.68 = bf16[256,2048]{1,0:T(8,128)(2,1)S(1)} custom-call(s32[6]{0:T(128)S(1)} %pad_add_fusion.place_ref, bf16[16,64,2048]{2,1,0:T(8,128)(2,1)S(1)} %bitcast.27, bf16[192,512]{1,0:T(8,128)(2,1)S(1)} %copy-done.17, bf16[64,512]{1,0:T(8,128)(2,1)S(1)} %copy-done.20, bf16[192,512]{1,0:T(8,128)(2,1)S(1)} %copy-done.7, ...), custom_call_target="tpu_custom_call" | custom-call | flops 2147483648 | bytes 5242880 | tf_op jit(solution)/shard_map/pallas_call | solution.py:217
  158.5 0.8 copy-done.13
  159.3 0.8 copy-done.15
  160.2 1.9 %shard_map.67 = f32[256,2048]{1,0:T(8,128)S(1)} custom-call(s32[6]{0:T(128)S(1)} %pad_add_fusion.place_ref, bf16[16,64,2048]{2,1,0:T(8,128)(2,1)S(1)} %bitcast.28, bf16[192,512]{1,0:T(8,128)(2,1)S(1)} %copy-done.18, bf16[64,512]{1,0:T(8,128)(2,1)S(1)} %copy-done.21, bf16[192,512]{1,0:T(8,128)(2,1)S(1)} %copy-done.8, bf16[64,512]{1,0:T(8,128)(2,1)S(1)} %copy-done.13, ...), custom_call_target="tpu_custom_call" | custom-call | flops 2147483648 | bytes 5242880 | tf_op jit(solution)/shard_map/pallas_call | solution.py:217
  162.1 1.3 add_convert_fusion
  (74 shorter events, 5.2 us)
Async XLA Ops:
  6.5 5.1 %copy-start.22 = (bf16[256,2048]{1,0:T(8,128)(2,1)S(1)}, bf16[256,2048]{1,0:T(8,128)(2,1)}, u32[]{:S(2)}) copy-start(bf16[256,2048]{1,0:T(8,128)(2,1)} %param.6) | copy-start | bytes 3145732
  6.5 142.0 %all-gather.3.cloned.1.call-start = ((), (), s32[]{:S(2)}) async-start(), calls=%async_computation | async-start | bytes 4456448 | tf_op jit(solution)/shard_map/all_gather | solution.py:277
  7.3 5.8 %copy-start.23 = (bf16[256,2048]{1,0:T(8,128)(2,1)S(1)}, bf16[256,2048]{1,0:T(8,128)(2,1)}, u32[]{:S(2)}) copy-start(bf16[256,2048]{1,0:T(8,128)(2,1)} %param.6) | copy-start | bytes 3145732
  8.5 13.2 %collective-permute-start.2 = (bf16[96,2048]{1,0:T(8,128)(2,1)S(1)}, bf16[96,2048]{1,0:T(8,128)(2,1)S(1)}, u32[]{:S(2)}, u32[]{:S(2)}) collective-permute-start(bf16[96,2048]{1,0:T(8,128)(2,1)S(1)} %get-tuple-element.63.rest_0_), channel_id=1, source_target_pairs={{0,2},{2,6},{6,4},{4,0},{1,3},{3,7},{7,5},{5,1},{8,10},{10,14},{14... | collective-permute-start | bytes 1179656 | tf_op jit(solution)/shard_map/ppermute | solution.py:265
  11.7 1.5 collective-permute-start
  12.4 0.8 collective-permute-start.1
  21.7 0.7 copy-start.1
  22.5 55.6 %collective-permute-start.3 = (bf16[336,2048]{1,0:T(8,128)(2,1)S(1)}, bf16[336,2048]{1,0:T(8,128)(2,1)S(1)}, u32[]{:S(2)}, u32[]{:S(2)}) collective-permute-start(bf16[336,2048]{1,0:T(8,128)(2,1)S(1)} %constant_dynamic-update-slice_fusion.rest_6_.rest_2_), channel_id=1, source_target_pairs={{0,8},{8,0},{16,24},{24,16},{1,9},{9,1},{17,25},{25,17},{2,10},{10... | collective-permute-start | bytes 4128776 | tf_op jit(solution)/shard_map/ppermute | solution.py:42
  24.1 54.0 %collective-permute-start.4 = (bf16[336,2048]{1,0:T(8,128)(2,1)S(1)}, bf16[336,2048]{1,0:T(8,128)(2,1)}, u32[]{:S(2)}, u32[]{:S(2)}) collective-permute-start(bf16[336,2048]{1,0:T(8,128)(2,1)S(1)} %constant_dynamic-update-slice_fusion.rest_6_.rest_2_), channel_id=1, source_target_pairs={{0,16},{8,24},{16,0},{24,8},{1,17},{9,25},{17,1},{25,9},{2,18},{10... | collective-permute-start | bytes 4128776 | tf_op jit(solution)/shard_map/ppermute | solution.py:42
  25.6 52.5 %collective-permute-start.5 = (bf16[336,2048]{1,0:T(8,128)(2,1)S(1)}, bf16[336,2048]{1,0:T(8,128)(2,1)}, u32[]{:S(2)}, u32[]{:S(2)}) collective-permute-start(bf16[336,2048]{1,0:T(8,128)(2,1)S(1)} %constant_dynamic-update-slice_fusion.rest_6_.rest_2_), channel_id=1, source_target_pairs={{0,1},{1,0},{2,3},{3,2},{4,5},{5,4},{6,7},{7,6},{8,9},{9,8},{10,11... | collective-permute-start | bytes 4128776 | tf_op jit(solution)/shard_map/ppermute | solution.py:37
  36.1 21.4 %collective-permute-start.7 = (bf16[96,2048]{1,0:T(8,128)(2,1)S(1)}, bf16[96,2048]{1,0:T(8,128)(2,1)}, u32[]{:S(2)}, u32[]{:S(2)}) collective-permute-start(bf16[96,2048]{1,0:T(8,128)(2,1)S(1)} %get-tuple-element.64.rest_1_), channel_id=1, source_target_pairs={{0,2},{2,6},{6,4},{4,0},{1,3},{3,7},{7,5},{5,1},{8,10},{10,14},{14... | collective-permute-start | bytes 1179656 | tf_op jit(solution)/shard_map/ppermute | solution.py:265
  43.1 27.2 %collective-permute-start.6 = (bf16[96,2048]{1,0:T(8,128)(2,1)}, bf16[96,2048]{1,0:T(8,128)(2,1)S(1)}, u32[]{:S(2)}, u32[]{:S(2)}) collective-permute-start(bf16[96,2048]{1,0:T(8,128)(2,1)} %copy-done.1), channel_id=1, source_target_pairs={{0,2},{2,6},{6,4},{4,0},{1,3},{3,7},{7,5},{5,1},{8,10},{10,14},{14... | collective-permute-start | bytes 1179656 | tf_op jit(solution)/shard_map/ppermute | solution.py:265
  57.5 20.7 %collective-permute-start.8 = (bf16[96,2048]{1,0:T(8,128)(2,1)}, bf16[96,2048]{1,0:T(8,128)(2,1)S(1)}, u32[]{:S(2)}, u32[]{:S(2)}) collective-permute-start(bf16[96,2048]{1,0:T(8,128)(2,1)} %collective-permute-done.7.rest_3_), channel_id=1, source_target_pairs={{0,2},{2,6},{6,4},{4,0},{1,3},{3,7},{7,5},{5,1},{8,10},{10,14},{14... | collective-permute-start | bytes 1179656 | tf_op jit(solution)/shard_map/ppermute | solution.py:265
  58.3 26.7 %copy-start.2 = (bf16[96,2048]{1,0:T(8,128)(2,1)S(1)}, bf16[96,2048]{1,0:T(8,128)(2,1)}, u32[]{:S(2)}) copy-start(bf16[96,2048]{1,0:T(8,128)(2,1)} %copy-done.1) | copy-start | bytes 1179652
  78.1 4.6 %collective-permute-start.10 = (bf16[336,2048]{1,0:T(8,128)(2,1)}, bf16[336,2048]{1,0:T(8,128)(2,1)S(1)}, u32[]{:S(2)}, u32[]{:S(2)}) collective-permute-start(bf16[336,2048]{1,0:T(8,128)(2,1)} %collective-permute-done.4.rest_10_.rest_6_), channel_id=1, source_target_pairs={{0,1},{1,0},{2,3},{3,2},{4,5},{5,4},{6,7},{7,6},{8,9},{9,8},{10,11... | collective-permute-start | bytes 4128776 | tf_op jit(solution)/shard_map/ppermute | solution.py:37
  78.2 6.8 %collective-permute-start.9 = (bf16[336,2048]{1,0:T(8,128)(2,1)S(1)}, bf16[336,2048]{1,0:T(8,128)(2,1)S(1)}, u32[]{:S(2)}, u32[]{:S(2)}) collective-permute-start(bf16[336,2048]{1,0:T(8,128)(2,1)S(1)} %collective-permute-done.3.rest_8_.rest_4_), channel_id=1, source_target_pairs={{0,1},{1,0},{2,3},{3,2},{4,5},{5,4},{6,7},{7,6},{8,9},{9,8},{10,11... | collective-permute-start | bytes 4128776 | tf_op jit(solution)/shard_map/ppermute | solution.py:37
  79.9 36.1 %collective-permute-start.12 = (bf16[176,2048]{1,0:T(8,128)(2,1)S(1)}, bf16[176,2048]{1,0:T(8,128)(2,1)S(1)}, u32[]{:S(2)}, u32[]{:S(2)}) collective-permute-start(bf16[176,2048]{1,0:T(8,128)(2,1)S(1)} %slice.35), channel_id=1, source_target_pairs={{0,16},{8,24},{16,0},{24,8},{1,17},{9,25},{17,1},{25,9},{2,18},{10... | collective-permute-start | bytes 2162696 | tf_op jit(solution)/shard_map/ppermute | solution.py:42
  80.5 35.5 %collective-permute-start.11 = (bf16[160,2048]{1,0:T(8,128)(2,1)S(1)}, bf16[160,2048]{1,0:T(8,128)(2,1)S(1)}, u32[]{:S(2)}, u32[]{:S(2)}) collective-permute-start(bf16[160,2048]{1,0:T(8,128)(2,1)S(1)} %slice.34), channel_id=1, source_target_pairs={{0,8},{8,0},{16,24},{24,16},{1,9},{9,1},{17,25},{25,17},{2,10},{10... | collective-permute-start | bytes 1966088 | tf_op jit(solution)/shard_map/ppermute | solution.py:42
  80.9 23.0 %collective-permute-start.13 = (bf16[96,2048]{1,0:T(8,128)(2,1)S(1)}, bf16[96,2048]{1,0:T(8,128)(2,1)S(1)}, u32[]{:S(2)}, u32[]{:S(2)}) collective-permute-start(bf16[96,2048]{1,0:T(8,128)(2,1)S(1)} %collective-permute-done.6.rest_4_), channel_id=1, source_target_pairs={{0,2},{2,6},{6,4},{4,0},{1,3},{3,7},{7,5},{5,1},{8,10},{10,14},{14... | collective-permute-start | bytes 1179656 | tf_op jit(solution)/shard_map/ppermute | solution.py:265
  82.7 33.2 %collective-permute-start.14 = (bf16[96,2048]{1,0:T(8,128)(2,1)S(1)}, bf16[96,2048]{1,0:T(8,128)(2,1)S(1)}, u32[]{:S(2)}, u32[]{:S(2)}) collective-permute-start(bf16[96,2048]{1,0:T(8,128)(2,1)S(1)} %collective-permute-done.8.rest_5_), channel_id=1, source_target_pairs={{0,2},{2,6},{6,4},{4,0},{1,3},{3,7},{7,5},{5,1},{8,10},{10,14},{14... | collective-permute-start | bytes 1179656 | tf_op jit(solution)/shard_map/ppermute | solution.py:265
  98.0 0.7 copy-start.16
  116.0 9.2 %collective-permute-start.20 = (bf16[176,2048]{1,0:T(8,128)(2,1)S(1)}, bf16[176,2048]{1,0:T(8,128)(2,1)S(1)}, u32[]{:S(2)}, u32[]{:S(2)}) collective-permute-start(bf16[176,2048]{1,0:T(8,128)(2,1)S(1)} %collective-permute-done.12.rest_9_), channel_id=1, source_target_pairs={{0,1},{1,0},{2,3},{3,2},{4,5},{5,4},{6,7},{7,6},{8,9},{9,8},{10,11... | collective-permute-start | bytes 2162696 | tf_op jit(solution)/shard_map/ppermute | solution.py:37
  116.0 9.2 %collective-permute-start.19 = (bf16[160,2048]{1,0:T(8,128)(2,1)S(1)}, bf16[160,2048]{1,0:T(8,128)(2,1)S(1)}, u32[]{:S(2)}, u32[]{:S(2)}) collective-permute-start(bf16[160,2048]{1,0:T(8,128)(2,1)S(1)} %collective-permute-done.11.rest_8_), channel_id=1, source_target_pairs={{0,1},{1,0},{2,3},{3,2},{4,5},{5,4},{6,7},{7,6},{8,9},{9,8},{10,11... | collective-permute-start | bytes 1966088 | tf_op jit(solution)/shard_map/ppermute | solution.py:37
  116.5 30.0 %collective-permute-start.15 = (bf16[192,512]{1,0:T(8,128)(2,1)S(1)}, bf16[192,512]{1,0:T(8,128)(2,1)S(1)}, u32[]{:S(2)}, u32[]{:S(2)}) collective-permute-start(bf16[192,512]{1,0:T(8,128)(2,1)S(1)} %get-tuple-element.59), channel_id=1, source_target_pairs={{0,8},{8,0},{16,24},{24,16},{1,9},{9,1},{17,25},{25,17},{2,10},{10... | collective-permute-start | bytes 589832 | tf_op jit(solution)/shard_map/ppermute | solution.py:42
  120.4 26.7 %collective-permute-start.17 = (bf16[192,512]{1,0:T(8,128)(2,1)S(1)}, bf16[192,512]{1,0:T(8,128)(2,1)S(1)}, u32[]{:S(2)}, u32[]{:S(2)}) collective-permute-start(bf16[192,512]{1,0:T(8,128)(2,1)S(1)} %get-tuple-element.61), channel_id=1, source_target_pairs={{0,16},{8,24},{16,0},{24,8},{1,17},{9,25},{17,1},{25,9},{2,18},{10... | collective-permute-start | bytes 589832 | tf_op jit(solution)/shard_map/ppermute | solution.py:42
  133.6 14.2 %collective-permute-start.21 = (bf16[256,512]{1,0:T(8,128)(2,1)S(1)}, bf16[256,512]{1,0:T(8,128)(2,1)S(1)}, u32[]{:S(2)}, u32[]{:S(2)}) collective-permute-start(bf16[256,512]{1,0:T(8,128)(2,1)S(1)} %shard_map.66), channel_id=1, source_target_pairs={{0,24},{8,16},{16,8},{24,0},{1,25},{9,17},{17,9},{25,1},{2,26},{10... | collective-permute-start | bytes 786440 | tf_op jit(solution)/shard_map/ppermute | solution.py:42
  141.5 0.6 copy-start.19
  142.2 4.3 %collective-permute-start.16 = (bf16[64,512]{1,0:T(8,128)(2,1)S(1)}, bf16[64,512]{1,0:T(8,128)(2,1)S(1)}, u32[]{:S(2)}, u32[]{:S(2)}) collective-permute-start(bf16[64,512]{1,0:T(8,128)(2,1)S(1)} %get-tuple-element.60), channel_id=1, source_target_pairs={{0,8},{8,0},{16,24},{24,16},{1,9},{9,1},{17,25},{25,17},{2,10},{10... | collective-permute-start | bytes 196616 | tf_op jit(solution)/shard_map/ppermute | solution.py:42
  142.2 4.3 %collective-permute-start.18 = (bf16[64,512]{1,0:T(8,128)(2,1)S(1)}, bf16[64,512]{1,0:T(8,128)(2,1)S(1)}, u32[]{:S(2)}, u32[]{:S(2)}) collective-permute-start(bf16[64,512]{1,0:T(8,128)(2,1)S(1)} %get-tuple-element.62), channel_id=1, source_target_pairs={{0,16},{8,24},{16,0},{24,8},{1,17},{9,25},{17,1},{25,9},{2,18},{10... | collective-permute-start | bytes 196616 | tf_op jit(solution)/shard_map/ppermute | solution.py:42
  146.4 0.7 copy-start.6
  147.1 0.7 copy-start.9
  147.8 0.7 copy-start.3
  148.5 2.2 %copy-start = (bf16[1024,2048]{1,0:T(8,128)(2,1)S(1)}, bf16[1024,2048]{1,0:T(8,128)(2,1)}, u32[]{:S(2)}) copy-start(bf16[1024,2048]{1,0:T(8,128)(2,1)} %all-gather.3.cloned.1.call-done) | copy-start | bytes 12582916
  150.7 0.9 copy-start.4
  151.7 0.9 copy-start.7
  152.6 0.9 copy-start.10
  153.5 0.9 copy-start.17
  154.4 0.8 copy-start.20
  155.3 3.2 %copy-start.5 = (bf16[256,512]{1,0:T(8,128)(2,1)S(1)}, bf16[256,512]{1,0:T(8,128)(2,1)}, u32[]{:S(2)}) copy-start(bf16[256,512]{1,0:T(8,128)(2,1)} %copy-done.3) | copy-start | bytes 786436
  155.3 3.2 %copy-start.8 = (bf16[192,512]{1,0:T(8,128)(2,1)S(1)}, bf16[192,512]{1,0:T(8,128)(2,1)}, u32[]{:S(2)}) copy-start(bf16[192,512]{1,0:T(8,128)(2,1)} %copy-done.6) | copy-start | bytes 589828
  155.3 3.2 %copy-start.11 = (bf16[192,512]{1,0:T(8,128)(2,1)S(1)}, bf16[192,512]{1,0:T(8,128)(2,1)}, u32[]{:S(2)}) copy-start(bf16[192,512]{1,0:T(8,128)(2,1)} %copy-done.9) | copy-start | bytes 589828
  155.3 3.2 %copy-start.18 = (bf16[192,512]{1,0:T(8,128)(2,1)S(1)}, bf16[192,512]{1,0:T(8,128)(2,1)}, u32[]{:S(2)}) copy-start(bf16[192,512]{1,0:T(8,128)(2,1)} %copy-done.16) | copy-start | bytes 589828
  155.3 3.2 %copy-start.21 = (bf16[64,512]{1,0:T(8,128)(2,1)S(1)}, bf16[64,512]{1,0:T(8,128)(2,1)}, u32[]{:S(2)}) copy-start(bf16[64,512]{1,0:T(8,128)(2,1)} %copy-done.19) | copy-start | bytes 196612
  157.2 0.6 copy-start.12
  157.8 0.6 copy-start.14
  158.4 3.6 %collective-permute-start.22 = (bf16[256,2048]{1,0:T(8,128)(2,1)S(1)}, bf16[256,2048]{1,0:T(8,128)(2,1)S(1)}, u32[]{:S(2)}, u32[]{:S(2)}) collective-permute-start(bf16[256,2048]{1,0:T(8,128)(2,1)S(1)} %shard_map.68), channel_id=1, source_target_pairs={{0,1},{1,0},{2,3},{3,2},{4,5},{5,4},{6,7},{7,6},{8,9},{9,8},{10,11... | collective-permute-start | bytes 3145736 | tf_op jit(solution)/shard_map/ppermute | solution.py:37
  158.5 0.8 copy-start.13
  159.3 0.8 copy-start.15
Sparse Core Ops, SparseCore 0:
  10.1 113.9 all-gather.2

commit v3 on v2

--- a/solution.py
+++ b/solution.py
@@ -16,7 +16,7 @@
 HALO = 160
 SMEM = pl.BlockSpec(memory_space=pltpu.SMEM)
 VMEM = pl.BlockSpec(memory_space=pltpu.VMEM)
-LIMIT = pltpu.CompilerParams(vmem_limit_bytes=32 * 1024 * 1024)
+LIMIT = pltpu.CompilerParams(vmem_limit_bytes=24 * 1024 * 1024)
 
 
 def ring_of(count):
@@ -274,7 +274,6 @@
     edge = lax.ppermute(tokens[rows - HALO : rows - half], ("z", "core"), pairs(0)) + lax.ppermute(
         tokens[rows - half :], ("z", "core"), pairs(1)
     )
-    v = lax.all_gather(out_weight, ("dp", "z"))
     run_mix = lambda steps, which: mix_chunks(
         steps, which, rows, place, taps, filters, wa, wb, parts, pieces
     )
@@ -282,41 +281,52 @@
     if slots == 4 and chips == 4 and width == WIDE:
         flat = in_weight.reshape(3 * width, features)
         cut = 3 * width // 2
+        mid = HALO
         wa, wb = [flat[:cut]], [flat[cut:]]
+        v = lax.all_gather(out_weight, "z")
+
+        low = tokens[:mid]
+        low_x, low_y, low_twin = across(low, 1), across(low, 2), swap(low)
         wa.append(forward(wa[0]))
-        edge, wa[1] = tie(edge, wa[1])
-
-        block = jnp.concatenate([tokens, edge])
-        x, y, twin = across(block, 1), across(block, 2), swap(block)
+        edge, wa[1], low_x, low_y, low_twin = tie(edge, wa[1], low_x, low_y, low_twin)
+
+        high = jnp.concatenate([tokens[mid:], edge])
+        high_x, high_y, high_twin = across(high, 1), across(high, 2), swap(high)
+        low_x_twin, low_y_twin = swap(low_x), swap(low_y)
         wb.append(forward(wb[0]))
         wa.append(forward(wa[1]))
+        (high_x, high_y, high_twin, low_x_twin, low_y_twin, wa, wb, taps, filters, place, v) = tie(
+            high_x, high_y, high_twin, low_x_twin, low_y_twin, wa, wb, taps, filters, place, v
+        )
+        wa, wb = list(wa), list(wb)
+
+        v = lax.all_gather(v, "dp")
         wb.append(forward(wb[1]))
-        x, y, twin, wa, wb, taps, filters, place = tie(x, y, twin, wa, wb, taps, filters, place)
+        wa.append(forward(wa[2]))
+        far_x, far_y = across(low_y, 1), across(high_x, 2)
+        parts = [(r, side, at) for r in range(3) for side in range(2) for at in (0, mid)]
+        pieces = [low, high, low_twin, high_twin]
+        pieces += [low_x, high_x, low_x_twin, swap(high_x)]
+        pieces += [low_y, high_y, low_y_twin, swap(high_y)]
+        early = run_mix((0, 1), (0, 1, 2))
+        early, far_x, far_y, wa, wb = tie(early, far_x, far_y, wa, wb)
         wa, wb = list(wa), list(wb)
 
-        mid = HALO
-        x_twin, y_twin = swap(x), swap(y)
-        wa.append(forward(wa[2]))
         wb.append(forward(wb[2]))
-        x_far, y_far = across(y[:mid], 1), across(x[mid:], 2)
-        parts = [(0, 0, 0), (0, 1, 0), (1, 0, 0), (1, 1, 0), (2, 0, 0), (2, 1, 0)]
-        pieces = [block, twin, x, x_twin, y, y_twin]
-        early = run_mix((0, 1, 2), (0, 1, 2))
-        early, x_far, y_far, wa, wb = tie(early, x_far, y_far, wa, wb)
-
         parts += [(3, 0, 0), (3, 0, mid), (3, 1, 0), (3, 1, mid)]
-        pieces += [x_far, y_far, swap(x_far), swap(y_far)]
-        late = run_mix((3,), (0, 1, 2))
-        (far,) = run_mix((0, 1, 2, 3), (3,))
+        pieces += [far_x, far_y, swap(far_x), swap(far_y)]
+        (far,) = run_mix((0, 1, 2), (3,))
+        late = run_mix((2, 3), (0, 1, 2))
+        (last,) = run_mix((3,), (3,))
         together = [early[0], late[0]]
         for r in (1, 2):
             together += [across(early[r], r), across(late[r], r)]
-        together.append(across(far, 3))
+        together += [across(far, 3), across(last, 3)]
         v = v.reshape(slots * chips, width, -1)
-        order = [(r, s, 2 * r, s * width) for s in range(3) for r in range(3)]
-        order += [(r, 3, 2 * r + 1, 0) for r in range(3)]
-        order += [(3, s, 6, s * width) for s in range(chips)]
+        order = [(r, s, 2 * r + s // 2, s % 2 * width) for s in range(chips) for r in range(3)]
+        order += [(3, s, 6 + s // 3, s % 3 * width) for s in range(chips)]
     else:
+        v = lax.all_gather(out_weight, ("dp", "z"))
         block = jnp.concatenate([tokens, edge])
         w, wa, wb = in_weight, [], []
         for s in range(chips):

time: 172 us -> 159 us (0.924)
  waiting for transfers between devices: 61 us -> 13.8 us
  starting transfers between devices: 42.2 us -> 69.7 us
  Pallas kernels: 31 us -> 39.2 us
    ppermute x6, waiting for transfers between devices: 56.4 us -> 0.02 us  [shards(): forward = lambda block: lax.ppermute(block, 'z', ring)]
    ppermute x6 -> x9, starting transfers between devices: 11.5 us -> 31.9 us  [swap(): return lax.ppermute(block, 'core', [(0, 1), (1, 0)])]
    pallas_call x3 -> x4, Pallas kernels: 27.2 us -> 35.4 us  [mix_chunks(): pl.pallas_call(functools.partial(mix_kernel, steps, slots, parts), out_sh...]
    ppermute x9 -> x12, waiting for transfers between devices: 2.85 us -> 10.3 us  [across(): return lax.ppermute(block, 'dp', [(i, i ^ r) for i in range(count)])]
    ppermute x6, starting transfers between devices: 12.9 us -> 18.2 us  [shards(): forward = lambda block: lax.ppermute(block, 'z', ring)]
    slice x1, local copies, waits for them, and re-layouts: 0.05 us -> 1.98 us  [shards(): tokens[rows - half:]]
    all_gather x1 -> x2, waiting for transfers between devices: 0.01 us -> 1.76 us  [the longest x1 1.76 us: shards(): v = lax.all_gather(v, 'dp')]
    unnamed x50 -> x47, local copies, waits for them, and re-layouts: 13.9 us -> 14.5 us
  transfers between devices with their start and end apart: 24 -> 31, of which waited for: 8 -> 8; matrix products, arithmetic and copies ran while one was open for 4% -> 3% of each run, Pallas kernels for 17% -> 23%
where the time goes in v3:
time: 159 us
  starting transfers between devices  69.7 us (44%)
  Pallas kernels  39.2 us (25%)
  local copies, waits for them, and re-layouts  19.6 us (12%)
  waiting for transfers between devices  13.8 us (9%)
  between operations  13.7 us (9%)
  other arithmetic  2.7 us (2%)
    pallas_call x4, Pallas kernels, mix_chunks(): pl.pallas_call(functools.partial(mix_kernel, steps, slots, parts), out_sh...  35.4 us
    ppermute x9, starting transfers between devices, swap(): return lax.ppermute(block, 'core', [(0, 1), (1, 0)])  31.9 us
    ppermute x6, starting transfers between devices, shards(): forward = lambda block: lax.ppermute(block, 'z', ring)  18.2 us
    ppermute x12, starting transfers between devices, across(): return lax.ppermute(block, 'dp', [(i, i ^ r) for i in range(count)])  16.8 us
    unnamed x47, local copies, waits for them, and re-layouts  14.5 us
    ppermute x12, waiting for transfers between devices, across(): return lax.ppermute(block, 'dp', [(i, i ^ r) for i in range(count)])  10.3 us
    pallas_call x2, Pallas kernels, project(): pl.pallas_call(functools.partial(out_kernel, mirror, order, chips, width)...  3.77 us
  transfers between devices with their start and end apart: 31, of which 8 were waited for; matrix products, arithmetic and copies ran while one was open for 3% of the time, Pallas kernels for 23%

profile of v3, /device:TPU:0, one launch (start us, length us, event | category | flops | bytes accessed | tf_op | source)
XLA Modules:
  0.0 158.8 jit_solution(13262890878427612236)
XLA Ops:
  6.5 1.2 slice.31.rest_4_
  7.8 3.0 %collective-permute-start.3 = (bf16[160,2048]{1,0:T(8,128)(2,1)S(1)}, bf16[160,2048]{1,0:T(8,128)(2,1)}, u32[]{:S(2)}, u32[]{:S(2)}) collective-permute-start(bf16[160,2048]{1,0:T(8,128)(2,1)S(1)} %slice.31.rest_4_), channel_id=1, source_target_pairs={{0,8},{8,0},{16,24},{24,16},{1,9},{9,1},{17,25},{25,17},{2,10},{10... | collective-permute-start | bytes 1966088 | tf_op jit(solution)/shard_map/ppermute | solution.py:42
  10.8 1.5 collective-permute-start.4
  12.3 2.0 %fusion.5 = (bf16[80,2048]{1,0:T(8,128)(2,1)}, bf16[80,2048]{1,0:T(8,128)(2,1)}) fusion(bf16[256,2048]{1,0:T(8,128)(2,1)} %param.6), kind=kLoop, calls=%fused_computation.21 | loop fusion | bytes 1310720 | tf_op jit(solution)/shard_map/slice | solution.py:275
  14.3 1.4 collective-permute-start
  15.9 1.5 collective-permute-start.2
  17.4 1.4 collective-permute-start.1
  19.9 11.3 %collective-permute-start.12 = (bf16[96,2048]{1,0:T(8,128)(2,1)S(1)}, bf16[96,2048]{1,0:T(8,128)(2,1)}, u32[]{:S(2)}, u32[]{:S(2)}) collective-permute-start(bf16[96,2048]{1,0:T(8,128)(2,1)S(1)} %get-tuple-element.74.rest_1_), channel_id=1, source_target_pairs={{0,2},{2,6},{6,4},{4,0},{1,3},{3,7},{7,5},{5,1},{8,10},{10,14},{14... | collective-permute-start | bytes 1179656 | tf_op jit(solution)/shard_map/ppermute | solution.py:265
  31.2 1.1 add.55
  32.4 0.9 copy-done.7
  33.3 1.6 %collective-permute-start.11 = (bf16[96,2048]{1,0:T(8,128)(2,1)S(1)}, bf16[96,2048]{1,0:T(8,128)(2,1)}, u32[]{:S(2)}, u32[]{:S(2)}) collective-permute-start(bf16[96,2048]{1,0:T(8,128)(2,1)S(1)} %collective-permute-done.2.rest_2_), channel_id=1, source_target_pairs={{0,2},{2,6},{6,4},{4,0},{1,3},{3,7},{7,5},{5,1},{8,10},{10,14},{14... | collective-permute-start | bytes 1179656 | tf_op jit(solution)/shard_map/ppermute | solution.py:265
  35.0 1.6 %collective-permute-start.6 = (bf16[176,2048]{1,0:T(8,128)(2,1)S(1)}, bf16[176,2048]{1,0:T(8,128)(2,1)S(1)}, u32[]{:S(2)}, u32[]{:S(2)}) collective-permute-start(bf16[176,2048]{1,0:T(8,128)(2,1)S(1)} %pad_maximum_fusion.rest_5_), channel_id=1, source_target_pairs={{0,8},{8,0},{16,24},{24,16},{1,9},{9,1},{17,25},{25,17},{2,10},{10... | collective-permute-start | bytes 2162696 | tf_op jit(solution)/shard_map/ppermute | solution.py:42
  36.6 1.4 collective-permute-start.7
  38.0 24.6 %collective-permute-start.8 = (bf16[176,2048]{1,0:T(8,128)(2,1)S(1)}, bf16[176,2048]{1,0:T(8,128)(2,1)S(1)}, u32[]{:S(2)}, u32[]{:S(2)}) collective-permute-start(bf16[176,2048]{1,0:T(8,128)(2,1)S(1)} %pad_maximum_fusion.rest_5_), channel_id=1, source_target_pairs={{0,1},{1,0},{2,3},{3,2},{4,5},{5,4},{6,7},{7,6},{8,9},{9,8},{10,11... | collective-permute-start | bytes 2162696 | tf_op jit(solution)/shard_map/ppermute | solution.py:37
  63.4 1.8 %collective-permute-start.10 = (bf16[160,2048]{1,0:T(8,128)(2,1)}, bf16[160,2048]{1,0:T(8,128)(2,1)S(1)}, u32[]{:S(2)}, u32[]{:S(2)}) collective-permute-start(bf16[160,2048]{1,0:T(8,128)(2,1)} %collective-permute-done.4.rest_12_), channel_id=1, source_target_pairs={{0,1},{1,0},{2,3},{3,2},{4,5},{5,4},{6,7},{7,6},{8,9},{9,8},{10,11... | collective-permute-start | bytes 1966088 | tf_op jit(solution)/shard_map/ppermute | solution.py:37
  65.2 4.2 %collective-permute-start.9 = (bf16[160,2048]{1,0:T(8,128)(2,1)}, bf16[160,2048]{1,0:T(8,128)(2,1)S(1)}, u32[]{:S(2)}, u32[]{:S(2)}) collective-permute-start(bf16[160,2048]{1,0:T(8,128)(2,1)} %collective-permute-done.3.rest_8_), channel_id=1, source_target_pairs={{0,1},{1,0},{2,3},{3,2},{4,5},{5,4},{6,7},{7,6},{8,9},{9,8},{10,11... | collective-permute-start | bytes 1966088 | tf_op jit(solution)/shard_map/ppermute | solution.py:37
  69.6 0.8 copy-done.10
  70.4 0.9 collective-permute-done.9.rest_10_
  71.3 0.9 copy-done.13
  72.2 0.9 copy-done.1
  73.1 0.9 copy-done.4
  75.0 1.6 collective-permute-start.15
  76.5 1.5 collective-permute-start.17
  78.8 1.2 copy-done.2
  80.0 1.2 copy-done.5
  81.2 1.2 copy-done.8
  82.4 1.1 copy-done.11
  83.5 1.1 copy-done.14
  84.6 12.7 %shard_map.64 = (bf16[128,512]{1,0:T(8,128)(2,1)S(1)}, bf16[128,512]{1,0:T(8,128)(2,1)S(1)}, bf16[128,512]{1,0:T(8,128)(2,1)S(1)}) custom-call(s32[6]{0:T(128)S(1)} %pad_add_fusion.place_ref, f32[4,8,256]{2,1,0:T(8,128)S(1)} %pad_maximum_fusion.1.taps_ref, f32[4,4,128]{2,1,0:T(4,128)S(1)} %maximum_convert_fusion.long_ref, ...), custom_call_target="tpu_custom_call" | custom-call | flops 6442450944 | bytes 12582912 | tf_op jit(solution)/shard_map/pallas_call | solution.py:159
  98.0 4.0 %collective-permute-done.15.rest_6_.rest_2_ = bf16[160,2048]{1,0:T(8,128)(2,1)S(1)} collective-permute-done((bf16[160,2048]{1,0:T(8,128)(2,1)}, bf16[160,2048]{1,0:T(8,128)(2,1)S(1)}, u32[]{:S(2)}, u32[]{:S(2)}) %collective-permute-start.15) | collective-permute-done | bytes 655392 | tf_op jit(solution)/shard_map/ppermute | solution.py:42
  102.0 0.9 collective-permute-done.16.rest_7_.rest_3_
  103.4 1.5 collective-permute-start.19
  104.9 1.8 %collective-permute-start.20 = (bf16[128,512]{1,0:T(8,128)(2,1)S(1)}, bf16[128,512]{1,0:T(8,128)(2,1)S(1)}, u32[]{:S(2)}, u32[]{:S(2)}) collective-permute-start(bf16[128,512]{1,0:T(8,128)(2,1)S(1)} %get-tuple-element.69), channel_id=1, source_target_pairs={{0,8},{8,0},{16,24},{24,16},{1,9},{9,1},{17,25},{25,17},{2,10},{10... | collective-permute-start | bytes 393224 | tf_op jit(solution)/shard_map/ppermute | solution.py:42
  106.7 1.5 collective-permute-start.22
  108.2 7.1 %shard_map.66 = bf16[192,512]{1,0:T(8,128)(2,1)S(1)} custom-call(s32[6]{0:T(128)S(1)} %pad_add_fusion.place_ref, f32[4,8,256]{2,1,0:T(8,128)S(1)} %pad_maximum_fusion.1.taps_ref, f32[4,4,128]{2,1,0:T(4,128)S(1)} %maximum_convert_fusion.long_ref, bf16[96,2048]{1,0:T(8,128)(2,1)S(1)} %get-tuple-element.73.rest_0_, ...), custom_call_target="tpu_custom_call" | custom-call | flops 3221225472 | bytes 6291456 | tf_op jit(solution)/shard_map/pallas_call | solution.py:159
  115.8 12.7 %shard_map.65 = (bf16[128,512]{1,0:T(8,128)(2,1)S(1)}, bf16[128,512]{1,0:T(8,128)(2,1)S(1)}, bf16[128,512]{1,0:T(8,128)(2,1)S(1)}) custom-call(s32[6]{0:T(128)S(1)} %pad_add_fusion.place_ref, f32[4,8,256]{2,1,0:T(8,128)S(1)} %pad_maximum_fusion.1.taps_ref, f32[4,4,128]{2,1,0:T(4,128)S(1)} %maximum_convert_fusion.long_ref, ...), custom_call_target="tpu_custom_call" | custom-call | flops 6442450944 | bytes 12582912 | tf_op jit(solution)/shard_map/pallas_call | solution.py:159
  128.5 1.6 collective-permute-start.21
  130.1 1.6 collective-permute-start.23
  131.7 2.8 %shard_map.67 = bf16[64,512]{1,0:T(8,128)(2,1)S(1)} custom-call(s32[6]{0:T(128)S(1)} %pad_add_fusion.place_ref, f32[4,8,256]{2,1,0:T(8,128)S(1)} %pad_maximum_fusion.1.taps_ref, f32[4,4,128]{2,1,0:T(4,128)S(1)} %maximum_convert_fusion.long_ref, bf16[96,2048]{1,0:T(8,128)(2,1)S(1)} %collective-permute-done.17.rest_2_.rest_0_, ...), custom_call_target="tpu_custom_call" | custom-call | flops 1073741824 | bytes 2097152 | tf_op jit(solution)/shard_map/pallas_call | solution.py:159
  135.7 2.1 %collective-permute-done.21.refs_3_ = bf16[128,512]{1,0:T(8,128)(2,1)S(1)} collective-permute-done((bf16[128,512]{1,0:T(8,128)(2,1)S(1)}, bf16[128,512]{1,0:T(8,128)(2,1)S(1)}, u32[]{:S(2)}, u32[]{:S(2)}) %collective-permute-start.21) | collective-permute-done | bytes 131104 | tf_op jit(solution)/shard_map/ppermute | solution.py:42
  137.7 1.7 %collective-permute-done.23.refs_5_ = bf16[128,512]{1,0:T(8,128)(2,1)S(1)} collective-permute-done((bf16[128,512]{1,0:T(8,128)(2,1)S(1)}, bf16[128,512]{1,0:T(8,128)(2,1)S(1)}, u32[]{:S(2)}, u32[]{:S(2)}) %collective-permute-start.23) | collective-permute-done | bytes 131104 | tf_op jit(solution)/shard_map/ppermute | solution.py:42
  139.4 1.7 %collective-permute-done.27.refs_7_ = bf16[64,512]{1,0:T(8,128)(2,1)S(1)} collective-permute-done((bf16[64,512]{1,0:T(8,128)(2,1)S(1)}, bf16[64,512]{1,0:T(8,128)(2,1)S(1)}, u32[]{:S(2)}, u32[]{:S(2)}) %collective-permute-start.27) | collective-permute-done | bytes 65568 | tf_op jit(solution)/shard_map/ppermute | solution.py:42
  141.1 1.8 %all-gather.7.cloned.1.call-done.v_ref = bf16[16,64,2048]{2,1,0:T(8,128)(2,1)} async-done(((bf16[4,64,2048]{2,1,0:T(8,128)(2,1)}), bf16[16,64,2048]{2,1,0:T(8,128)(2,1)}) %all-gather.7.cloned.1.call-update) | async-done | bytes 4194320 | tf_op jit(solution)/shard_map/all_gather | solution.py:303
  142.9 2.2 %copy-done = bf16[16,64,2048]{2,1,0:T(8,128)(2,1)S(1)} copy-done((bf16[16,64,2048]{2,1,0:T(8,128)(2,1)S(1)}, bf16[16,64,2048]{2,1,0:T(8,128)(2,1)}, u32[]{:S(2)}) %copy-start) | copy-done | bytes 4194328
  145.1 0.9 copy-done.17
  146.0 1.9 %shard_map.69 = bf16[256,2048]{1,0:T(8,128)(2,1)S(1)} custom-call(s32[6]{0:T(128)S(1)} %pad_add_fusion.place_ref, bf16[16,64,2048]{2,1,0:T(8,128)(2,1)S(1)} %copy-done, bf16[128,512]{1,0:T(8,128)(2,1)S(1)} %copy-done.20, bf16[128,512]{1,0:T(8,128)(2,1)S(1)} %get-tuple-element.68.refs_1_, bf16[128,512]{1,0:T(8,128)(2,1)S(1)} %collective-permute-done.20.refs_2_, ...), custom_call_target="tpu_custom_call" | custom-call | flops 2147483648 | bytes 5242880 | tf_op jit(solution)/shard_map/pallas_call | solution.py:217
  148.0 1.9 %shard_map.68 = f32[256,2048]{1,0:T(8,128)S(1)} custom-call(s32[6]{0:T(128)S(1)} %pad_add_fusion.place_ref, bf16[16,64,2048]{2,1,0:T(8,128)(2,1)S(1)} %copy-done, bf16[128,512]{1,0:T(8,128)(2,1)S(1)} %copy-done.20, bf16[128,512]{1,0:T(8,128)(2,1)S(1)} %get-tuple-element.68.refs_1_, bf16[128,512]{1,0:T(8,128)(2,1)S(1)} %collective-permute-done.20.refs_2_, ...), custom_call_target="tpu_custom_call" | custom-call | flops 2147483648 | bytes 5242880 | tf_op jit(solution)/shard_map/pallas_call | solution.py:217
  150.6 1.3 add_convert_fusion
  (88 shorter events, 7.7 us)
Async XLA Ops:
  6.5 9.2 %copy-start.21 = (bf16[3,64,2048]{2,1,0:T(8,128)(2,1)S(1)}, bf16[3,64,2048]{2,1,0:T(8,128)(2,1)}, u32[]{:S(2)}) copy-start(bf16[3,64,2048]{2,1,0:T(8,128)(2,1)} %param.7) | copy-start | bytes 2359300
  6.5 12.2 %copy-start.22 = (f32[7,3,2048]{2,0,1:T(8,128)S(1)}, f32[7,3,2048]{2,0,1:T(8,128)}, u32[]{:S(2)}) copy-start(f32[7,3,2048]{2,0,1:T(8,128)} %param.8) | copy-start | bytes 516100
  6.5 67.4 %all-gather.5.cloned.1.call-start = ((), (), s32[]{:S(2)}) async-start(), calls=%async_computation | async-start | bytes 1310720 | tf_op jit(solution)/shard_map/all_gather | solution.py:286
  7.8 24.6 %collective-permute-start.3 = (bf16[160,2048]{1,0:T(8,128)(2,1)S(1)}, bf16[160,2048]{1,0:T(8,128)(2,1)}, u32[]{:S(2)}, u32[]{:S(2)}) collective-permute-start(bf16[160,2048]{1,0:T(8,128)(2,1)S(1)} %slice.31.rest_4_), channel_id=1, source_target_pairs={{0,8},{8,0},{16,24},{24,16},{1,9},{9,1},{17,25},{25,17},{2,10},{10... | collective-permute-start | bytes 1966088 | tf_op jit(solution)/shard_map/ppermute | solution.py:42
  10.8 21.6 %collective-permute-start.4 = (bf16[160,2048]{1,0:T(8,128)(2,1)S(1)}, bf16[160,2048]{1,0:T(8,128)(2,1)}, u32[]{:S(2)}, u32[]{:S(2)}) collective-permute-start(bf16[160,2048]{1,0:T(8,128)(2,1)S(1)} %slice.31.rest_4_), channel_id=1, source_target_pairs={{0,16},{8,24},{16,0},{24,8},{1,17},{9,25},{17,1},{25,9},{2,18},{10... | collective-permute-start | bytes 1966088 | tf_op jit(solution)/shard_map/ppermute | solution.py:42
  12.3 20.1 %collective-permute-start.5 = (bf16[160,2048]{1,0:T(8,128)(2,1)S(1)}, bf16[160,2048]{1,0:T(8,128)(2,1)S(1)}, u32[]{:S(2)}, u32[]{:S(2)}) collective-permute-start(bf16[160,2048]{1,0:T(8,128)(2,1)S(1)} %slice.31.rest_4_), channel_id=1, source_target_pairs={{0,1},{1,0},{2,3},{3,2},{4,5},{5,4},{6,7},{7,6},{8,9},{9,8},{10,11... | collective-permute-start | bytes 1966088 | tf_op jit(solution)/shard_map/ppermute | solution.py:37
  14.3 3.1 %collective-permute-start = (bf16[80,2048]{1,0:T(8,128)(2,1)}, bf16[80,2048]{1,0:T(8,128)(2,1)}, u32[]{:S(2)}, u32[]{:S(2)}) collective-permute-start(bf16[80,2048]{1,0:T(8,128)(2,1)} %get-tuple-element.80), channel_id=1, source_target_pairs={{1,2},{3,4},{5,6},{9,10},{11,12},{13,14},{17,18},{19,20},{21,22},{... | collective-permute-start | bytes 983048 | tf_op jit(solution)/shard_map/ppermute | solution.py:274
  15.7 127.2 %all-gather.7.cloned.1.call-start = ((), (), s32[]{:S(2)}) async-start(), calls=%async_computation.1 | async-start | bytes 5242880 | tf_op jit(solution)/shard_map/all_gather | solution.py:303
  15.8 19.1 %slice-start = ((bf16[256,2048]{1,0:T(8,128)(2,1)}), bf16[96,2048]{1,0:T(8,128)(2,1)S(1)}, s32[]{:S(2)}) async-start(bf16[256,2048]{1,0:T(8,128)(2,1)} %param.6), calls=%async_computation.2 | async-start | bytes 786432 | tf_op jit(solution)/shard_map/slice | solution.py:293
  15.9 16.5 %collective-permute-start.2 = (bf16[96,2048]{1,0:T(8,128)(2,1)S(1)}, bf16[96,2048]{1,0:T(8,128)(2,1)S(1)}, u32[]{:S(2)}, u32[]{:S(2)}) collective-permute-start(bf16[96,2048]{1,0:T(8,128)(2,1)S(1)} %get-tuple-element.73.rest_0_), channel_id=1, source_target_pairs={{0,2},{2,6},{6,4},{4,0},{1,3},{3,7},{7,5},{5,1},{8,10},{10,14},{14... | collective-permute-start | bytes 1179656 | tf_op jit(solution)/shard_map/ppermute | solution.py:265
  17.4 2.5 %collective-permute-start.1 = (bf16[80,2048]{1,0:T(8,128)(2,1)}, bf16[80,2048]{1,0:T(8,128)(2,1)}, u32[]{:S(2)}, u32[]{:S(2)}) collective-permute-start(bf16[80,2048]{1,0:T(8,128)(2,1)} %get-tuple-element.79), channel_id=1, source_target_pairs={{1,3},{3,5},{5,7},{9,11},{11,13},{13,15},{17,19},{19,21},{21,23},{... | collective-permute-start | bytes 983048 | tf_op jit(solution)/shard_map/ppermute | solution.py:274
  19.9 43.4 %collective-permute-start.12 = (bf16[96,2048]{1,0:T(8,128)(2,1)S(1)}, bf16[96,2048]{1,0:T(8,128)(2,1)}, u32[]{:S(2)}, u32[]{:S(2)}) collective-permute-start(bf16[96,2048]{1,0:T(8,128)(2,1)S(1)} %get-tuple-element.74.rest_1_), channel_id=1, source_target_pairs={{0,2},{2,6},{6,4},{4,0},{1,3},{3,7},{7,5},{5,1},{8,10},{10,14},{14... | collective-permute-start | bytes 1179656 | tf_op jit(solution)/shard_map/ppermute | solution.py:265
  33.3 31.9 %collective-permute-start.11 = (bf16[96,2048]{1,0:T(8,128)(2,1)S(1)}, bf16[96,2048]{1,0:T(8,128)(2,1)}, u32[]{:S(2)}, u32[]{:S(2)}) collective-permute-start(bf16[96,2048]{1,0:T(8,128)(2,1)S(1)} %collective-permute-done.2.rest_2_), channel_id=1, source_target_pairs={{0,2},{2,6},{6,4},{4,0},{1,3},{3,7},{7,5},{5,1},{8,10},{10,14},{14... | collective-permute-start | bytes 1179656 | tf_op jit(solution)/shard_map/ppermute | solution.py:265
  35.0 37.2 %collective-permute-start.6 = (bf16[176,2048]{1,0:T(8,128)(2,1)S(1)}, bf16[176,2048]{1,0:T(8,128)(2,1)S(1)}, u32[]{:S(2)}, u32[]{:S(2)}) collective-permute-start(bf16[176,2048]{1,0:T(8,128)(2,1)S(1)} %pad_maximum_fusion.rest_5_), channel_id=1, source_target_pairs={{0,8},{8,0},{16,24},{24,16},{1,9},{9,1},{17,25},{25,17},{2,10},{10... | collective-permute-start | bytes 2162696 | tf_op jit(solution)/shard_map/ppermute | solution.py:42
  36.6 35.7 %collective-permute-start.7 = (bf16[176,2048]{1,0:T(8,128)(2,1)S(1)}, bf16[176,2048]{1,0:T(8,128)(2,1)S(1)}, u32[]{:S(2)}, u32[]{:S(2)}) collective-permute-start(bf16[176,2048]{1,0:T(8,128)(2,1)S(1)} %pad_maximum_fusion.rest_5_), channel_id=1, source_target_pairs={{0,16},{8,24},{16,0},{24,8},{1,17},{9,25},{17,1},{25,9},{2,18},{10... | collective-permute-start | bytes 2162696 | tf_op jit(solution)/shard_map/ppermute | solution.py:42
  38.0 35.1 %collective-permute-start.8 = (bf16[176,2048]{1,0:T(8,128)(2,1)S(1)}, bf16[176,2048]{1,0:T(8,128)(2,1)S(1)}, u32[]{:S(2)}, u32[]{:S(2)}) collective-permute-start(bf16[176,2048]{1,0:T(8,128)(2,1)S(1)} %pad_maximum_fusion.rest_5_), channel_id=1, source_target_pairs={{0,1},{1,0},{2,3},{3,2},{4,5},{5,4},{6,7},{7,6},{8,9},{9,8},{10,11... | collective-permute-start | bytes 2162696 | tf_op jit(solution)/shard_map/ppermute | solution.py:37
  63.4 6.2 %collective-permute-start.10 = (bf16[160,2048]{1,0:T(8,128)(2,1)}, bf16[160,2048]{1,0:T(8,128)(2,1)S(1)}, u32[]{:S(2)}, u32[]{:S(2)}) collective-permute-start(bf16[160,2048]{1,0:T(8,128)(2,1)} %collective-permute-done.4.rest_12_), channel_id=1, source_target_pairs={{0,1},{1,0},{2,3},{3,2},{4,5},{5,4},{6,7},{7,6},{8,9},{9,8},{10,11... | collective-permute-start | bytes 1966088 | tf_op jit(solution)/shard_map/ppermute | solution.py:37
  65.2 6.1 %collective-permute-start.9 = (bf16[160,2048]{1,0:T(8,128)(2,1)}, bf16[160,2048]{1,0:T(8,128)(2,1)S(1)}, u32[]{:S(2)}, u32[]{:S(2)}) collective-permute-start(bf16[160,2048]{1,0:T(8,128)(2,1)} %collective-permute-done.3.rest_8_), channel_id=1, source_target_pairs={{0,1},{1,0},{2,3},{3,2},{4,5},{5,4},{6,7},{7,6},{8,9},{9,8},{10,11... | collective-permute-start | bytes 1966088 | tf_op jit(solution)/shard_map/ppermute | solution.py:37
  74.0 4.1 %collective-permute-start.13 = (bf16[176,2048]{1,0:T(8,128)(2,1)S(1)}, bf16[176,2048]{1,0:T(8,128)(2,1)S(1)}, u32[]{:S(2)}, u32[]{:S(2)}) collective-permute-start(bf16[176,2048]{1,0:T(8,128)(2,1)S(1)} %collective-permute-done.6.rest_9_), channel_id=1, source_target_pairs={{0,1},{1,0},{2,3},{3,2},{4,5},{5,4},{6,7},{7,6},{8,9},{9,8},{10,11... | collective-permute-start | bytes 2162696 | tf_op jit(solution)/shard_map/ppermute | solution.py:37
  74.5 4.3 %collective-permute-start.14 = (bf16[176,2048]{1,0:T(8,128)(2,1)}, bf16[176,2048]{1,0:T(8,128)(2,1)S(1)}, u32[]{:S(2)}, u32[]{:S(2)}) collective-permute-start(bf16[176,2048]{1,0:T(8,128)(2,1)} %copy-done.1), channel_id=1, source_target_pairs={{0,1},{1,0},{2,3},{3,2},{4,5},{5,4},{6,7},{7,6},{8,9},{9,8},{10,11... | collective-permute-start | bytes 2162696 | tf_op jit(solution)/shard_map/ppermute | solution.py:37
  74.6 28.3 %collective-permute-start.16 = (bf16[176,2048]{1,0:T(8,128)(2,1)S(1)}, bf16[176,2048]{1,0:T(8,128)(2,1)S(1)}, u32[]{:S(2)}, u32[]{:S(2)}) collective-permute-start(bf16[176,2048]{1,0:T(8,128)(2,1)S(1)} %collective-permute-done.6.rest_9_), channel_id=1, source_target_pairs={{0,16},{8,24},{16,0},{24,8},{1,17},{9,25},{17,1},{25,9},{2,18},{10... | collective-permute-start | bytes 2162696 | tf_op jit(solution)/shard_map/ppermute | solution.py:42
  75.0 27.0 %collective-permute-start.15 = (bf16[160,2048]{1,0:T(8,128)(2,1)}, bf16[160,2048]{1,0:T(8,128)(2,1)S(1)}, u32[]{:S(2)}, u32[]{:S(2)}) collective-permute-start(bf16[160,2048]{1,0:T(8,128)(2,1)} %collective-permute-done.4.rest_12_), channel_id=1, source_target_pairs={{0,8},{8,0},{16,24},{24,16},{1,9},{9,1},{17,25},{25,17},{2,10},{10... | collective-permute-start | bytes 1966088 | tf_op jit(solution)/shard_map/ppermute | solution.py:42
  76.5 25.4 %collective-permute-start.17 = (bf16[96,2048]{1,0:T(8,128)(2,1)}, bf16[96,2048]{1,0:T(8,128)(2,1)S(1)}, u32[]{:S(2)}, u32[]{:S(2)}) collective-permute-start(bf16[96,2048]{1,0:T(8,128)(2,1)} %collective-permute-done.11.rest_0_.rest_4_), channel_id=1, source_target_pairs={{0,2},{2,6},{6,4},{4,0},{1,3},{3,7},{7,5},{5,1},{8,10},{10,14},{14... | collective-permute-start | bytes 1179656 | tf_op jit(solution)/shard_map/ppermute | solution.py:265
  78.1 23.9 %collective-permute-start.18 = (bf16[96,2048]{1,0:T(8,128)(2,1)}, bf16[96,2048]{1,0:T(8,128)(2,1)S(1)}, u32[]{:S(2)}, u32[]{:S(2)}) collective-permute-start(bf16[96,2048]{1,0:T(8,128)(2,1)} %collective-permute-done.12.rest_3_), channel_id=1, source_target_pairs={{0,2},{2,6},{6,4},{4,0},{1,3},{3,7},{7,5},{5,1},{8,10},{10,14},{14... | collective-permute-start | bytes 1179656 | tf_op jit(solution)/shard_map/ppermute | solution.py:265
  78.8 1.2 copy-start.2
  80.0 1.2 copy-start.5
  81.2 1.2 copy-start.8
  82.4 1.1 copy-start.11
  83.5 1.1 copy-start.14
  102.8 13.0 %copy-start.3 = (bf16[176,2048]{1,0:T(8,128)(2,1)S(1)}, bf16[176,2048]{1,0:T(8,128)(2,1)}, u32[]{:S(2)}) copy-start(bf16[176,2048]{1,0:T(8,128)(2,1)} %copy-done.1) | copy-start | bytes 2162692
  102.8 13.0 %copy-start.6 = (bf16[176,2048]{1,0:T(8,128)(2,1)S(1)}, bf16[176,2048]{1,0:T(8,128)(2,1)}, u32[]{:S(2)}) copy-start(bf16[176,2048]{1,0:T(8,128)(2,1)} %copy-done.4) | copy-start | bytes 2162692
  102.8 13.0 %copy-start.9 = (bf16[160,2048]{1,0:T(8,128)(2,1)S(1)}, bf16[160,2048]{1,0:T(8,128)(2,1)}, u32[]{:S(2)}) copy-start(bf16[160,2048]{1,0:T(8,128)(2,1)} %copy-done.7) | copy-start | bytes 1966084
  102.8 13.0 %copy-start.12 = (bf16[160,2048]{1,0:T(8,128)(2,1)S(1)}, bf16[160,2048]{1,0:T(8,128)(2,1)}, u32[]{:S(2)}) copy-start(bf16[160,2048]{1,0:T(8,128)(2,1)} %copy-done.10) | copy-start | bytes 1966084
  102.8 13.0 %copy-start.15 = (bf16[160,2048]{1,0:T(8,128)(2,1)S(1)}, bf16[160,2048]{1,0:T(8,128)(2,1)}, u32[]{:S(2)}) copy-start(bf16[160,2048]{1,0:T(8,128)(2,1)} %copy-done.13) | copy-start | bytes 1966084
  102.9 5.3 %collective-permute-start.25 = (bf16[176,2048]{1,0:T(8,128)(2,1)S(1)}, bf16[176,2048]{1,0:T(8,128)(2,1)S(1)}, u32[]{:S(2)}, u32[]{:S(2)}) collective-permute-start(bf16[176,2048]{1,0:T(8,128)(2,1)S(1)} %collective-permute-done.16.rest_7_.rest_3_), channel_id=1, source_target_pairs={{0,1},{1,0},{2,3},{3,2},{4,5},{5,4},{6,7},{7,6},{8,9},{9,8},{10,11... | collective-permute-start | bytes 2162696 | tf_op jit(solution)/shard_map/ppermute | solution.py:37
  102.9 5.2 %collective-permute-start.24 = (bf16[160,2048]{1,0:T(8,128)(2,1)S(1)}, bf16[160,2048]{1,0:T(8,128)(2,1)S(1)}, u32[]{:S(2)}, u32[]{:S(2)}) collective-permute-start(bf16[160,2048]{1,0:T(8,128)(2,1)S(1)} %collective-permute-done.15.rest_6_.rest_2_), channel_id=1, source_target_pairs={{0,1},{1,0},{2,3},{3,2},{4,5},{5,4},{6,7},{7,6},{8,9},{9,8},{10,11... | collective-permute-start | bytes 1966088 | tf_op jit(solution)/shard_map/ppermute | solution.py:37
  103.4 12.4 %collective-permute-start.19 = (bf16[96,2048]{1,0:T(8,128)(2,1)S(1)}, bf16[96,2048]{1,0:T(8,128)(2,1)S(1)}, u32[]{:S(2)}, u32[]{:S(2)}) collective-permute-start(bf16[96,2048]{1,0:T(8,128)(2,1)S(1)} %collective-permute-done.18.rest_1_.rest_5_), channel_id=1, source_target_pairs={{0,2},{2,6},{6,4},{4,0},{1,3},{3,7},{7,5},{5,1},{8,10},{10,14},{14... | collective-permute-start | bytes 1179656 | tf_op jit(solution)/shard_map/ppermute | solution.py:265
  104.9 29.6 %collective-permute-start.20 = (bf16[128,512]{1,0:T(8,128)(2,1)S(1)}, bf16[128,512]{1,0:T(8,128)(2,1)S(1)}, u32[]{:S(2)}, u32[]{:S(2)}) collective-permute-start(bf16[128,512]{1,0:T(8,128)(2,1)S(1)} %get-tuple-element.69), channel_id=1, source_target_pairs={{0,8},{8,0},{16,24},{24,16},{1,9},{9,1},{17,25},{25,17},{2,10},{10... | collective-permute-start | bytes 393224 | tf_op jit(solution)/shard_map/ppermute | solution.py:42
  106.7 28.3 %collective-permute-start.22 = (bf16[128,512]{1,0:T(8,128)(2,1)S(1)}, bf16[128,512]{1,0:T(8,128)(2,1)S(1)}, u32[]{:S(2)}, u32[]{:S(2)}) collective-permute-start(bf16[128,512]{1,0:T(8,128)(2,1)S(1)} %get-tuple-element.71), channel_id=1, source_target_pairs={{0,16},{8,24},{16,0},{24,8},{1,17},{9,25},{17,1},{25,9},{2,18},{10... | collective-permute-start | bytes 393224 | tf_op jit(solution)/shard_map/ppermute | solution.py:42
  115.3 25.8 %collective-permute-start.26 = (bf16[192,512]{1,0:T(8,128)(2,1)S(1)}, bf16[192,512]{1,0:T(8,128)(2,1)S(1)}, u32[]{:S(2)}, u32[]{:S(2)}) collective-permute-start(bf16[192,512]{1,0:T(8,128)(2,1)S(1)} %shard_map.66), channel_id=1, source_target_pairs={{0,24},{8,16},{16,8},{24,0},{1,25},{9,17},{17,9},{25,1},{2,26},{10... | collective-permute-start | bytes 589832 | tf_op jit(solution)/shard_map/ppermute | solution.py:42
  128.5 14.4 %copy-start.20 = (bf16[128,512]{1,0:T(8,128)(2,1)S(1)}, bf16[128,512]{1,0:T(8,128)(2,1)}, u32[]{:S(2)}) copy-start(bf16[128,512]{1,0:T(8,128)(2,1)} %copy-done.19) | copy-start | bytes 393220
  128.5 9.2 %collective-permute-start.21 = (bf16[128,512]{1,0:T(8,128)(2,1)S(1)}, bf16[128,512]{1,0:T(8,128)(2,1)S(1)}, u32[]{:S(2)}, u32[]{:S(2)}) collective-permute-start(bf16[128,512]{1,0:T(8,128)(2,1)S(1)} %get-tuple-element.70), channel_id=1, source_target_pairs={{0,8},{8,0},{16,24},{24,16},{1,9},{9,1},{17,25},{25,17},{2,10},{10... | collective-permute-start | bytes 393224 | tf_op jit(solution)/shard_map/ppermute | solution.py:42
  130.1 9.3 %collective-permute-start.23 = (bf16[128,512]{1,0:T(8,128)(2,1)S(1)}, bf16[128,512]{1,0:T(8,128)(2,1)S(1)}, u32[]{:S(2)}, u32[]{:S(2)}) collective-permute-start(bf16[128,512]{1,0:T(8,128)(2,1)S(1)} %get-tuple-element.72), channel_id=1, source_target_pairs={{0,16},{8,24},{16,0},{24,8},{1,17},{9,25},{17,1},{25,9},{2,18},{10... | collective-permute-start | bytes 393224 | tf_op jit(solution)/shard_map/ppermute | solution.py:42
  134.5 6.6 %collective-permute-start.27 = (bf16[64,512]{1,0:T(8,128)(2,1)S(1)}, bf16[64,512]{1,0:T(8,128)(2,1)S(1)}, u32[]{:S(2)}, u32[]{:S(2)}) collective-permute-start(bf16[64,512]{1,0:T(8,128)(2,1)S(1)} %shard_map.67), channel_id=1, source_target_pairs={{0,24},{8,16},{16,8},{24,0},{1,25},{9,17},{17,9},{25,1},{2,26},{10... | collective-permute-start | bytes 196616 | tf_op jit(solution)/shard_map/ppermute | solution.py:42
  142.9 2.2 %copy-start = (bf16[16,64,2048]{2,1,0:T(8,128)(2,1)S(1)}, bf16[16,64,2048]{2,1,0:T(8,128)(2,1)}, u32[]{:S(2)}) copy-start(bf16[16,64,2048]{2,1,0:T(8,128)(2,1)} %all-gather.7.cloned.1.call-done.v_ref) | copy-start | bytes 12582916
  145.1 0.9 copy-start.17
  146.0 2.0 %copy-start.18 = (bf16[128,512]{1,0:T(8,128)(2,1)S(1)}, bf16[128,512]{1,0:T(8,128)(2,1)}, u32[]{:S(2)}) copy-start(bf16[128,512]{1,0:T(8,128)(2,1)} %copy-done.16) | copy-start | bytes 393220
  147.9 2.7 %collective-permute-start.28 = (bf16[256,2048]{1,0:T(8,128)(2,1)S(1)}, bf16[256,2048]{1,0:T(8,128)(2,1)S(1)}, u32[]{:S(2)}, u32[]{:S(2)}) collective-permute-start(bf16[256,2048]{1,0:T(8,128)(2,1)S(1)} %shard_map.69), channel_id=1, source_target_pairs={{0,1},{1,0},{2,3},{3,2},{4,5},{5,4},{6,7},{7,6},{8,9},{9,8},{10,11... | collective-permute-start | bytes 3145736 | tf_op jit(solution)/shard_map/ppermute | solution.py:37
  (7 other events, 5.7 us)
Sparse Core Ops, SparseCore 0:
  15.8 41.3 all-gather.4
  74.1 68.7 all-gather.6

commit v4 on v3

--- a/solution.py
+++ b/solution.py
@@ -55,7 +55,7 @@
 
 
 def mix_kernel(steps, slots, parts, place_ref, taps_ref, long_ref, *rest):
-    weights, rest = rest[: 2 * len(steps)], rest[2 * len(steps) :]
+    weights, rest = rest[: len(steps)], rest[len(steps) :]
     pieces, rest = rest[: len(parts)], rest[len(parts) :]
     outs, rest = rest[: len(slots)], rest[len(slots) :]
     w, first, second, packed, turned, tiles = rest
@@ -69,12 +69,9 @@
     taps = [taps_ref[place_ref[2 + step]] for step in steps]
 
     for c, step in enumerate(steps):
-        wa, wb = weights[2 * c], weights[2 * c + 1]
-        cut = wa.shape[0]
-        w[c, :cut] = wa[...]
-        w[c, cut : 2 * WIDE] = wb[: 2 * WIDE - cut]
+        w[c, : 2 * WIDE] = weights[c][: 2 * WIDE]
         w[c, 2 * WIDE : 3 * WIDE] = jnp.zeros((WIDE, w.shape[2]), w.dtype)
-        w[c, 3 * WIDE :] = wb[2 * WIDE - cut :]
+        w[c, 3 * WIDE :] = weights[c][2 * WIDE :]
         filters = long_ref[place_ref[2 + step]]
         for g in range(count):
             line = jnp.concatenate(
@@ -150,11 +147,11 @@
                 outs[units[n][1]][at : at + GSIZE, :] = (query * row).astype(jnp.bfloat16)
 
 
-def mix_chunks(steps, slots, rows, place, taps, filters, wa, wb, parts, pieces):
-    features = wa[0].shape[1]
+def mix_chunks(steps, slots, rows, place, taps, filters, ws, parts, pieces):
+    features = ws[0].shape[1]
     chosen = [n for n, part in enumerate(parts) if part[0] in slots]
     parts, pieces = [parts[n] for n in chosen], [pieces[n] for n in chosen]
-    weights = [half[s] for s in steps for half in (wa, wb)]
+    weights = [ws[s] for s in steps]
     units = len(steps) * len(slots)
     return pl.pallas_call(
         functools.partial(mix_kernel, steps, slots, parts),
@@ -178,24 +175,26 @@
     )(place, taps, filters, *weights, *pieces)
 
 
-def out_kernel(mirror, order, chips, width, place_ref, v_ref, *refs):
-    parts = refs[: len(refs) - 4]
-    out_ref, left, right, total = refs[len(refs) - 4 :]
+def out_kernel(mirror, order, chips, width, counts, place_ref, *refs):
+    weights, refs = refs[: counts[0]], refs[counts[0] :]
+    parts, refs = refs[: counts[1]], refs[counts[1] :]
+    out_ref, left, right, total = refs
     rows = out_ref.shape[0]
-    core, dp = place_ref[0], place_ref[1]
+    core = place_ref[0]
     if mirror:
         core = 1 - core
     depth = left.shape[0]
     if order is None:
         left[...] = parts[0][...]
-        right[...] = v_ref[...]
-        size = depth
     else:
-        for n, (r, s, k, row) in enumerate(order):
-            here = slice(n * width, (n + 1) * width)
-            left[here] = parts[k][row : row + width]
-            right[here] = v_ref[lax.bitwise_xor(dp, r) * chips + place_ref[2 + s]]
-        size = depth // 2
+        for n, (k, row) in enumerate(order):
+            at = pl.multiple_of((n // chips * chips + place_ref[2 + n % chips]) * width, width)
+            left[pl.ds(at, width)] = parts[k][row : row + width]
+    at = 0
+    for ref in weights:
+        right[at : at + ref.shape[0]] = ref[...]
+        at += ref.shape[0]
+    size = depth // 2
     at = pl.multiple_of(core * rows, LANES)
     tile = 512
     for start in range(0, depth, size):
@@ -212,12 +211,13 @@
 
 
 def project(mirror, order, chips, width, depth, place, v, parts, dtype):
-    span, features = parts[0].shape[1], v.shape[-1]
+    span, features = parts[0].shape[1], v[0].shape[-1]
     rows = span // 2
+    counts = (len(v), len(parts))
     return pl.pallas_call(
-        functools.partial(out_kernel, mirror, order, chips, width),
+        functools.partial(out_kernel, mirror, order, chips, width, counts),
         out_shape=jax.ShapeDtypeStruct((rows, features), dtype),
-        in_specs=[SMEM, VMEM] + [VMEM] * len(parts),
+        in_specs=[SMEM] + [VMEM] * sum(counts),
         out_specs=VMEM,
         scratch_shapes=[
             pltpu.VMEM((depth, span), jnp.bfloat16),
@@ -230,7 +230,7 @@
             bytes_accessed=2 * depth * (features + span),
             transcendentals=0,
         ),
-    )(place, v, *parts)
+    )(place, *v, *parts)
 
 
 def local_filters(chips, width, dp, core, short_taps, long_taps):
@@ -275,64 +275,62 @@
         tokens[rows - half :], ("z", "core"), pairs(1)
     )
     run_mix = lambda steps, which: mix_chunks(
-        steps, which, rows, place, taps, filters, wa, wb, parts, pieces
+        steps, which, rows, place, taps, filters, ws, parts, pieces
     )
 
     if slots == 4 and chips == 4 and width == WIDE:
-        flat = in_weight.reshape(3 * width, features)
-        cut = 3 * width // 2
         mid = HALO
-        wa, wb = [flat[:cut]], [flat[cut:]]
-        v = lax.all_gather(out_weight, "z")
-
+        ws = [in_weight.reshape(3 * width, features)]
         low = tokens[:mid]
-        low_x, low_y, low_twin = across(low, 1), across(low, 2), swap(low)
-        wa.append(forward(wa[0]))
-        edge, wa[1], low_x, low_y, low_twin = tie(edge, wa[1], low_x, low_y, low_twin)
-
+        low_x, low_y = across(low, 1), across(low, 2)
+        edge, low, low_x, low_y, v, ws[0] = tie(edge, low, low_x, low_y, out_weight, ws[0])
+
+        v = lax.all_gather(v, "z")
         high = jnp.concatenate([tokens[mid:], edge])
         high_x, high_y, high_twin = across(high, 1), across(high, 2), swap(high)
-        low_x_twin, low_y_twin = swap(low_x), swap(low_y)
-        wb.append(forward(wb[0]))
-        wa.append(forward(wa[1]))
-        (high_x, high_y, high_twin, low_x_twin, low_y_twin, wa, wb, taps, filters, place, v) = tie(
-            high_x, high_y, high_twin, low_x_twin, low_y_twin, wa, wb, taps, filters, place, v
+        low_twin, low_x_twin, low_y_twin = swap(low), swap(low_x), swap(low_y)
+        ws.append(forward(ws[0]))
+        (high_x, high_y, high_twin, low_twin, low_x_twin, low_y_twin, ws, taps, filters, place, v) = tie(
+            high_x, high_y, high_twin, low_twin, low_x_twin, low_y_twin, ws, taps, filters, place, v
         )
-        wa, wb = list(wa), list(wb)
-
-        v = lax.all_gather(v, "dp")
-        wb.append(forward(wb[1]))
-        wa.append(forward(wa[2]))
+
+        ws = list(ws) + [forward(ws[1])]
         far_x, far_y = across(low_y, 1), across(high_x, 2)
         parts = [(r, side, at) for r in range(3) for side in range(2) for at in (0, mid)]
         pieces = [low, high, low_twin, high_twin]
         pieces += [low_x, high_x, low_x_twin, swap(high_x)]
         pieces += [low_y, high_y, low_y_twin, swap(high_y)]
         early = run_mix((0, 1), (0, 1, 2))
-        early, far_x, far_y, wa, wb = tie(early, far_x, far_y, wa, wb)
-        wa, wb = list(wa), list(wb)
-
-        wb.append(forward(wb[2]))
+        v = v.reshape(chips * width, -1)
+        v_x, v_y = across(v, 1), across(v, 2)
+        early, far_x, far_y, ws = tie(early, far_x, far_y, ws)
+
+        ws = list(ws) + [forward(ws[2])]
         parts += [(3, 0, 0), (3, 0, mid), (3, 1, 0), (3, 1, mid)]
         pieces += [far_x, far_y, swap(far_x), swap(far_y)]
         (far,) = run_mix((0, 1, 2), (3,))
-        late = run_mix((2, 3), (0, 1, 2))
-        (last,) = run_mix((3,), (3,))
-        together = [early[0], late[0]]
+        late = run_mix((2,), (0, 1, 2))
+        late, far, v_x, v_y = tie(late, far, v_x, v_y)
+        cut = v.shape[0] // 2
+        v = [v, v_x, v_y, across(v_y[:cut], 1), across(v_x[cut:], 2)]
+        last = run_mix((3,), (0, 1, 2, 3))
+        together = [early[0], late[0], last[0]]
         for r in (1, 2):
-            together += [across(early[r], r), across(late[r], r)]
-        together += [across(far, 3), across(last, 3)]
-        v = v.reshape(slots * chips, width, -1)
-        order = [(r, s, 2 * r + s // 2, s % 2 * width) for s in range(chips) for r in range(3)]
-        order += [(3, s, 6 + s // 3, s % 3 * width) for s in range(chips)]
+            together += [across(early[r], r), across(late[r], r), across(last[r], r)]
+        together += [across(far, 3), across(last[3], 3)]
+        order = [
+            (3 * r + max(0, s - 1), s * width if s < 2 else 0)
+            for r in range(3)
+            for s in range(chips)
+        ]
+        order += [(9 + s // 3, s % 3 * width) for s in range(chips)]
     else:
         v = lax.all_gather(out_weight, ("dp", "z"))
         block = jnp.concatenate([tokens, edge])
-        w, wa, wb = in_weight, [], []
+        w, ws = in_weight, []
         for s in range(chips):
-            padded = jnp.pad(w, ((0, 0), (0, WIDE - width), (0, 0))).reshape(3 * WIDE, features)
-            wa.append(padded[: 3 * WIDE // 2])
-            wb.append(padded[3 * WIDE // 2 :])
+            padded = jnp.pad(w, ((0, 0), (0, WIDE - width), (0, 0)))
+            ws.append(padded.reshape(3 * WIDE, features))
             if s + 1 < chips:
                 w = forward(w)
         pieces = [block] + [across(block, r) for r in range(1, slots)]
@@ -346,7 +344,7 @@
             mixed = [m[:width] for m in mixed]
             moved.append([mixed[0]] + [across(mixed[r], r) for r in range(1, slots)])
         turn = lax.bitwise_xor(dp, jnp.arange(slots))
-        v = v.reshape(slots, chips, width, -1)[turn][:, origins].reshape(slots * chips * width, -1)
+        v = [v.reshape(slots, chips, width, -1)[turn][:, origins].reshape(slots * chips * width, -1)]
         together = [jnp.concatenate([one[r] for r in range(slots) for one in moved])]
         order = None
     depth = slots * chips * width

time: 159 us -> 155 us (0.975)
  waiting for transfers between devices: 13.8 us -> 54.9 us
  starting transfers between devices: 69.7 us -> 30.1 us
  local copies, waits for them, and re-layouts: 19.6 us -> 16.2 us
    ppermute x9, starting transfers between devices: 31.9 us -> 1.86 us  [swap(): return lax.ppermute(block, 'core', [(0, 1), (1, 0)])]
    ppermute x12 -> x18, waiting for transfers between devices: 10.3 us -> 31.3 us  [across(): return lax.ppermute(block, 'dp', [(i, i ^ r) for i in range(count)])]
    ppermute x6 -> x3, waiting for transfers between devices: 0.02 us -> 19.6 us  [shards(): forward = lambda block: lax.ppermute(block, 'z', ring)]
    ppermute x6 -> x3, starting transfers between devices: 18.2 us -> 5.86 us  [shards(): forward = lambda block: lax.ppermute(block, 'z', ring)]
    ppermute x12 -> x18, starting transfers between devices: 16.8 us -> 20.9 us  [across(): return lax.ppermute(block, 'dp', [(i, i ^ r) for i in range(count)])]
    unnamed x47, local copies, waits for them, and re-layouts: 14.5 us -> 12.1 us
  transfers between devices with their start and end apart: 31 -> 33, of which waited for: 8 -> 11; matrix products, arithmetic and copies ran while one was open for 3% -> 2% of each run, Pallas kernels for 23% -> 23%
where the time goes in v4:
time: 155 us
  waiting for transfers between devices  54.9 us (35%)
  Pallas kernels  38.2 us (25%)
  starting transfers between devices  30.1 us (19%)
  local copies, waits for them, and re-layouts  16.2 us (10%)
  between operations  13.9 us (9%)
  other arithmetic  1.57 us (1%)
    pallas_call x4, Pallas kernels, mix_chunks(): pl.pallas_call(functools.partial(mix_kernel, steps, slots, parts), out_sh...  34.4 us
    ppermute x18, waiting for transfers between devices, across(): return lax.ppermute(block, 'dp', [(i, i ^ r) for i in range(count)])  31.3 us
    ppermute x18, starting transfers between devices, across(): return lax.ppermute(block, 'dp', [(i, i ^ r) for i in range(count)])  20.9 us
    ppermute x3, waiting for transfers between devices, shards(): forward = lambda block: lax.ppermute(block, 'z', ring)  19.6 us
    unnamed x47, local copies, waits for them, and re-layouts  12.1 us
    ppermute x3, starting transfers between devices, shards(): forward = lambda block: lax.ppermute(block, 'z', ring)  5.86 us
    pallas_call x2, Pallas kernels, project(): pl.pallas_call(functools.partial(out_kernel, mirror, order, chips, width,...  3.8 us
  transfers between devices with their start and end apart: 33, of which 11 were waited for; matrix products, arithmetic and copies ran while one was open for 2% of the time, Pallas kernels for 23%

profile of v4, /device:TPU:0, one launch (start us, length us, event | category | flops | bytes accessed | tf_op | source)
XLA Modules:
  0.0 154.8 jit_solution(16775185602144745931)
XLA Ops:
  6.5 1.1 slice.30.rest_2_.rest_1_
  7.7 3.0 %collective-permute-start.3 = (bf16[160,2048]{1,0:T(8,128)(2,1)S(1)}, bf16[160,2048]{1,0:T(8,128)(2,1)S(1)}, u32[]{:S(2)}, u32[]{:S(2)}) collective-permute-start(bf16[160,2048]{1,0:T(8,128)(2,1)S(1)} %slice.30.rest_2_.rest_1_), channel_id=1, source_target_pairs={{0,16},{8,24},{16,0},{24,8},{1,17},{9,25},{17,1},{25,9},{2,18},{10... | collective-permute-start | bytes 1966088 | tf_op jit(solution)/shard_map/ppermute | solution.py:42
  10.7 1.5 collective-permute-start.2
  12.2 1.1 fusion.5
  14.1 0.8 collective-permute-start
  15.0 10.5 %collective-permute-done.3.rest_10_.rest_9_ = bf16[160,2048]{1,0:T(8,128)(2,1)S(1)} collective-permute-done((bf16[160,2048]{1,0:T(8,128)(2,1)S(1)}, bf16[160,2048]{1,0:T(8,128)(2,1)S(1)}, u32[]{:S(2)}, u32[]{:S(2)}) %collective-permute-start.3) | collective-permute-done | bytes 655392 | tf_op jit(solution)/shard_map/ppermute | solution.py:42
  25.5 1.6 %collective-permute-done.2.rest_6_.rest_5_ = bf16[160,2048]{1,0:T(8,128)(2,1)} collective-permute-done((bf16[160,2048]{1,0:T(8,128)(2,1)S(1)}, bf16[160,2048]{1,0:T(8,128)(2,1)}, u32[]{:S(2)}, u32[]{:S(2)}) %collective-permute-start.2) | collective-permute-done | bytes 655392 | tf_op jit(solution)/shard_map/ppermute | solution.py:42
  28.0 0.8 fusion
  29.1 1.1 collective-permute-start.5
  30.1 1.5 collective-permute-start.4
  31.6 0.8 copy-done.13
  32.5 1.6 %collective-permute-start.10 = (bf16[192,2048]{1,0:T(8,128)(2,1)S(1)}, bf16[192,2048]{1,0:T(8,128)(2,1)S(1)}, u32[]{:S(2)}, u32[]{:S(2)}) collective-permute-start(bf16[192,2048]{1,0:T(8,128)(2,1)S(1)} %bitcast.28), channel_id=1, source_target_pairs={{0,2},{2,6},{6,4},{4,0},{1,3},{3,7},{7,5},{5,1},{8,10},{10,14},{14... | collective-permute-start | bytes 2359304 | tf_op jit(solution)/shard_map/ppermute | solution.py:265
  34.8 0.8 copy-done.16
  35.8 2.1 %collective-permute-done.9.rest_12_.rest_11_ = bf16[160,2048]{1,0:T(8,128)(2,1)S(1)} collective-permute-done((bf16[160,2048]{1,0:T(8,128)(2,1)}, bf16[160,2048]{1,0:T(8,128)(2,1)S(1)}, u32[]{:S(2)}, u32[]{:S(2)}) %collective-permute-start.9) | collective-permute-done | bytes 655392 | tf_op jit(solution)/shard_map/ppermute | solution.py:37
  37.9 0.8 copy-done.19
  38.8 0.9 copy-done.2
  39.6 7.9 %collective-permute-done.5.rest_11_.rest_10_ = bf16[176,2048]{1,0:T(8,128)(2,1)S(1)} collective-permute-done((bf16[176,2048]{1,0:T(8,128)(2,1)S(1)}, bf16[176,2048]{1,0:T(8,128)(2,1)S(1)}, u32[]{:S(2)}, u32[]{:S(2)}) %collective-permute-start.5) | collective-permute-done | bytes 720928 | tf_op jit(solution)/shard_map/ppermute | solution.py:42
  48.4 0.9 copy-done.8
  49.3 19.6 %collective-permute-done.10.rest_1_ = bf16[192,2048]{1,0:T(8,128)(2,1)S(1)} collective-permute-done((bf16[192,2048]{1,0:T(8,128)(2,1)S(1)}, bf16[192,2048]{1,0:T(8,128)(2,1)S(1)}, u32[]{:S(2)}, u32[]{:S(2)}) %collective-permute-start.10) | collective-permute-done | bytes 786464 | tf_op jit(solution)/shard_map/ppermute | solution.py:265
  68.9 1.0 all-gather.3.cloned.1.call-done
  70.5 1.0 collective-permute-start.15
  71.4 1.0 collective-permute-start.14
  73.0 1.0 collective-permute-start.19
  74.0 1.5 collective-permute-start.18
  75.5 1.1 copy-done.3
  76.6 1.1 copy-done.6
  77.7 1.1 copy-done.9
  78.8 1.1 copy-done.12
  79.9 1.1 copy-done.14
  81.0 1.1 copy-done.17
  82.1 1.1 copy-done.20
  83.2 12.6 %shard_map.64 = (bf16[128,512]{1,0:T(8,128)(2,1)S(1)}, bf16[128,512]{1,0:T(8,128)(2,1)S(1)}, bf16[128,512]{1,0:T(8,128)(2,1)S(1)}) custom-call(s32[6]{0:T(128)S(1)} %pad_add_fusion.place_ref, f32[4,8,256]{2,1,0:T(8,128)S(1)} %pad_maximum_fusion.1.taps_ref, f32[4,4,128]{2,1,0:T(4,128)S(1)} %maximum_convert_fusion.long_ref, bf16[192,2048]{1,0:T(8,128)(2,1)S(1)} %bitcast.29, ...), custom_call_target="tpu_custom_call" | custom-call | flops 6442450944 | bytes 12582912 | tf_op jit(solution)/shard_map/pallas_call | solution.py:156
  96.4 3.3 %collective-permute-start.22 = (bf16[192,2048]{1,0:T(8,128)(2,1)S(1)}, bf16[192,2048]{1,0:T(8,128)(2,1)S(1)}, u32[]{:S(2)}, u32[]{:S(2)}) collective-permute-start(bf16[192,2048]{1,0:T(8,128)(2,1)S(1)} %collective-permute-done.15.rest_0_.rest_2_), channel_id=1, source_target_pairs={{0,2},{2,6},{6,4},{4,0},{1,3},{3,7},{7,5},{5,1},{8,10},{10,14},{14... | collective-permute-start | bytes 2359304 | tf_op jit(solution)/shard_map/ppermute | solution.py:265
  99.7 7.0 %shard_map.65 = (bf16[64,512]{1,0:T(8,128)(2,1)S(1)}, bf16[64,512]{1,0:T(8,128)(2,1)S(1)}, bf16[64,512]{1,0:T(8,128)(2,1)S(1)}) custom-call(s32[6]{0:T(128)S(1)} %pad_add_fusion.place_ref, f32[4,8,256]{2,1,0:T(8,128)S(1)} %pad_maximum_fusion.1.taps_ref, f32[4,4,128]{2,1,0:T(4,128)S(1)} %maximum_convert_fusion.long_ref, ...), custom_call_target="tpu_custom_call" | custom-call | flops 3221225472 | bytes 6291456 | tf_op jit(solution)/shard_map/pallas_call | solution.py:156
  106.9 1.0 collective-permute-start.26
  107.8 6.3 %shard_map.66 = bf16[192,512]{1,0:T(8,128)(2,1)S(1)} custom-call(s32[6]{0:T(128)S(1)} %pad_add_fusion.place_ref, f32[4,8,256]{2,1,0:T(8,128)S(1)} %pad_maximum_fusion.1.taps_ref, f32[4,4,128]{2,1,0:T(4,128)S(1)} %maximum_convert_fusion.long_ref, bf16[192,2048]{1,0:T(8,128)(2,1)S(1)} %bitcast.30, bf16[192,2048]{1,0:T(8,128)(2,1)S(1)} %collective-permute-done.10.rest_1_, ...), custom_call_target="tpu_custom_call" | custom-call | flops 3221225472 | bytes 6291456 | tf_op jit(solution)/shard_map/pallas_call | solution.py:156
  114.2 1.5 collective-permute-start.24
  115.7 1.1 collective-permute-start.29
  116.9 2.0 %collective-permute-start.20 = (bf16[128,2048]{1,0:T(8,128)(2,1)S(1)}, bf16[128,2048]{1,0:T(8,128)(2,1)S(1)}, u32[]{:S(2)}, u32[]{:S(2)}) collective-permute-start(bf16[128,2048]{1,0:T(8,128)(2,1)S(1)} %slice.34), channel_id=1, source_target_pairs={{0,8},{8,0},{16,24},{24,16},{1,9},{9,1},{17,25},{25,17},{2,10},{10... | collective-permute-start | bytes 1572872 | tf_op jit(solution)/shard_map/ppermute | solution.py:42
  119.4 8.4 %shard_map.67 = (bf16[64,512]{1,0:T(8,128)(2,1)S(1)}, bf16[64,512]{1,0:T(8,128)(2,1)S(1)}, bf16[64,512]{1,0:T(8,128)(2,1)S(1)}, bf16[64,512]{1,0:T(8,128)(2,1)S(1)}) custom-call(s32[6]{0:T(128)S(1)} %pad_add_fusion.place_ref, f32[4,8,256]{2,1,0:T(8,128)S(1)} %pad_maximum_fusion.1.taps_ref, f32[4,4,128]{2,1,0:T(4,128)S(1)} %maximum_convert_fusion.long_ref, ...), custom_call_target="tpu_custom_call" | custom-call | flops 4294967296 | bytes 8388608 | tf_op jit(solution)/shard_map/pallas_call | solution.py:156
  127.9 1.6 %collective-permute-start.27 = (bf16[64,512]{1,0:T(8,128)(2,1)S(1)}, bf16[64,512]{1,0:T(8,128)(2,1)S(1)}, u32[]{:S(2)}, u32[]{:S(2)}) collective-permute-start(bf16[64,512]{1,0:T(8,128)(2,1)S(1)} %get-tuple-element.85), channel_id=1, source_target_pairs={{0,16},{8,24},{16,0},{24,8},{1,17},{9,25},{17,1},{25,9},{2,18},{10... | collective-permute-start | bytes 196616 | tf_op jit(solution)/shard_map/ppermute | solution.py:42
  129.6 6.2 %collective-permute-done.27.refs_12_ = bf16[64,512]{1,0:T(8,128)(2,1)S(1)} collective-permute-done((bf16[64,512]{1,0:T(8,128)(2,1)S(1)}, bf16[64,512]{1,0:T(8,128)(2,1)S(1)}, u32[]{:S(2)}, u32[]{:S(2)}) %collective-permute-start.27) | collective-permute-done | bytes 65568 | tf_op jit(solution)/shard_map/ppermute | solution.py:42
  135.8 1.1 collective-permute-start.28
  137.6 3.1 %collective-permute-done.28.refs_13_ = bf16[64,512]{1,0:T(8,128)(2,1)S(1)} collective-permute-done((bf16[64,512]{1,0:T(8,128)(2,1)S(1)}, bf16[64,512]{1,0:T(8,128)(2,1)S(1)}, u32[]{:S(2)}, u32[]{:S(2)}) %collective-permute-start.28) | collective-permute-done | bytes 65568 | tf_op jit(solution)/shard_map/ppermute | solution.py:42
  140.7 1.3 collective-permute-done.30.refs_15_
  142.0 1.9 %shard_map.69 = bf16[256,2048]{1,0:T(8,128)(2,1)S(1)} custom-call(s32[6]{0:T(128)S(1)} %pad_add_fusion.place_ref, bf16[256,2048]{1,0:T(8,128)(2,1)S(1)} %copy-done, bf16[256,2048]{1,0:T(8,128)(2,1)S(1)} %collective-permute-done.18.refs_1_, bf16[256,2048]{1,0:T(8,128)(2,1)S(1)} %collective-permute-done.19.refs_2_, ...), custom_call_target="tpu_custom_call" | custom-call | flops 2147483648 | bytes 5242880 | tf_op jit(solution)/shard_map/pallas_call | solution.py:217
  144.0 1.9 %shard_map.68 = f32[256,2048]{1,0:T(8,128)S(1)} custom-call(s32[6]{0:T(128)S(1)} %pad_add_fusion.place_ref, bf16[256,2048]{1,0:T(8,128)(2,1)S(1)} %copy-done, bf16[256,2048]{1,0:T(8,128)(2,1)S(1)} %collective-permute-done.18.refs_1_, bf16[256,2048]{1,0:T(8,128)(2,1)S(1)} %collective-permute-done.19.refs_2_, ...), custom_call_target="tpu_custom_call" | custom-call | flops 2147483648 | bytes 5242880 | tf_op jit(solution)/shard_map/pallas_call | solution.py:217
  146.7 1.3 add_convert_fusion
  (92 shorter events, 7.7 us)
Async XLA Ops:
  6.5 63.4 %all-gather.3.cloned.1.call-start = ((), (), s32[]{:S(2)}) async-start(), calls=%async_computation | async-start | bytes 1310720 | tf_op jit(solution)/shard_map/all_gather | solution.py:288
  7.7 19.5 %copy-start.22 = (f32[7,3,2048]{2,0,1:T(8,128)S(1)}, f32[7,3,2048]{2,0,1:T(8,128)}, u32[]{:S(2)}) copy-start(f32[7,3,2048]{2,0,1:T(8,128)} %param.8) | copy-start | bytes 516100
  7.7 21.1 %slice-start = ((bf16[256,2048]{1,0:T(8,128)(2,1)}), bf16[96,2048]{1,0:T(8,128)(2,1)S(1)}, s32[]{:S(2)}) async-start(bf16[256,2048]{1,0:T(8,128)(2,1)} %param.6), calls=%async_computation.1 | async-start | bytes 786432 | tf_op jit(solution)/shard_map/slice | solution.py:289
  7.7 17.8 %collective-permute-start.3 = (bf16[160,2048]{1,0:T(8,128)(2,1)S(1)}, bf16[160,2048]{1,0:T(8,128)(2,1)S(1)}, u32[]{:S(2)}, u32[]{:S(2)}) collective-permute-start(bf16[160,2048]{1,0:T(8,128)(2,1)S(1)} %slice.30.rest_2_.rest_1_), channel_id=1, source_target_pairs={{0,16},{8,24},{16,0},{24,8},{1,17},{9,25},{17,1},{25,9},{2,18},{10... | collective-permute-start | bytes 1966088 | tf_op jit(solution)/shard_map/ppermute | solution.py:42
  10.7 16.3 %collective-permute-start.2 = (bf16[160,2048]{1,0:T(8,128)(2,1)S(1)}, bf16[160,2048]{1,0:T(8,128)(2,1)}, u32[]{:S(2)}, u32[]{:S(2)}) collective-permute-start(bf16[160,2048]{1,0:T(8,128)(2,1)S(1)} %slice.30.rest_2_.rest_1_), channel_id=1, source_target_pairs={{0,8},{8,0},{16,24},{24,16},{1,9},{9,1},{17,25},{25,17},{2,10},{10... | collective-permute-start | bytes 1966088 | tf_op jit(solution)/shard_map/ppermute | solution.py:42
  13.4 1.5 collective-permute-start.1
  14.1 18.4 %copy-start.1 = (bf16[3,64,2048]{2,1,0:T(8,128)(2,1)S(1)}, bf16[3,64,2048]{2,1,0:T(8,128)(2,1)}, u32[]{:S(2)}) copy-start(bf16[3,64,2048]{2,1,0:T(8,128)(2,1)} %param.7) | copy-start | bytes 2359300
  14.1 0.8 collective-permute-start
  25.5 1.6 %copy-start.11 = (bf16[160,2048]{1,0:T(8,128)(2,1)}, bf16[160,2048]{1,0:T(8,128)(2,1)S(1)}, u32[]{:S(2)}) copy-start(bf16[160,2048]{1,0:T(8,128)(2,1)S(1)} %collective-permute-done.3.rest_10_.rest_9_) | copy-start | bytes 1966084
  27.1 4.5 %collective-permute-start.7 = (bf16[160,2048]{1,0:T(8,128)(2,1)S(1)}, bf16[160,2048]{1,0:T(8,128)(2,1)S(1)}, u32[]{:S(2)}, u32[]{:S(2)}) collective-permute-start(bf16[160,2048]{1,0:T(8,128)(2,1)S(1)} %slice.30.rest_2_.rest_1_), channel_id=1, source_target_pairs={{0,1},{1,0},{2,3},{3,2},{4,5},{5,4},{6,7},{7,6},{8,9},{9,8},{10,11... | collective-permute-start | bytes 1966088 | tf_op jit(solution)/shard_map/ppermute | solution.py:37
  27.5 7.3 %collective-permute-start.8 = (bf16[160,2048]{1,0:T(8,128)(2,1)}, bf16[160,2048]{1,0:T(8,128)(2,1)S(1)}, u32[]{:S(2)}, u32[]{:S(2)}) collective-permute-start(bf16[160,2048]{1,0:T(8,128)(2,1)} %collective-permute-done.2.rest_6_.rest_5_), channel_id=1, source_target_pairs={{0,1},{1,0},{2,3},{3,2},{4,5},{5,4},{6,7},{7,6},{8,9},{9,8},{10,11... | collective-permute-start | bytes 1966088 | tf_op jit(solution)/shard_map/ppermute | solution.py:37
  28.9 9.9 %collective-permute-start.6 = (bf16[176,2048]{1,0:T(8,128)(2,1)S(1)}, bf16[176,2048]{1,0:T(8,128)(2,1)S(1)}, u32[]{:S(2)}, u32[]{:S(2)}) collective-permute-start(bf16[176,2048]{1,0:T(8,128)(2,1)S(1)} %pad_maximum_fusion.rest_3_.rest_2_), channel_id=1, source_target_pairs={{0,1},{1,0},{2,3},{3,2},{4,5},{5,4},{6,7},{7,6},{8,9},{9,8},{10,11... | collective-permute-start | bytes 2162696 | tf_op jit(solution)/shard_map/ppermute | solution.py:37
  29.1 18.5 %collective-permute-start.5 = (bf16[176,2048]{1,0:T(8,128)(2,1)S(1)}, bf16[176,2048]{1,0:T(8,128)(2,1)S(1)}, u32[]{:S(2)}, u32[]{:S(2)}) collective-permute-start(bf16[176,2048]{1,0:T(8,128)(2,1)S(1)} %pad_maximum_fusion.rest_3_.rest_2_), channel_id=1, source_target_pairs={{0,16},{8,24},{16,0},{24,8},{1,17},{9,25},{17,1},{25,9},{2,18},{10... | collective-permute-start | bytes 2162696 | tf_op jit(solution)/shard_map/ppermute | solution.py:42
  30.1 18.2 %collective-permute-start.4 = (bf16[176,2048]{1,0:T(8,128)(2,1)S(1)}, bf16[176,2048]{1,0:T(8,128)(2,1)S(1)}, u32[]{:S(2)}, u32[]{:S(2)}) collective-permute-start(bf16[176,2048]{1,0:T(8,128)(2,1)S(1)} %pad_maximum_fusion.rest_3_.rest_2_), channel_id=1, source_target_pairs={{0,8},{8,0},{16,24},{24,16},{1,9},{9,1},{17,25},{25,17},{2,10},{10... | collective-permute-start | bytes 2162696 | tf_op jit(solution)/shard_map/ppermute | solution.py:42
  32.5 36.5 %collective-permute-start.10 = (bf16[192,2048]{1,0:T(8,128)(2,1)S(1)}, bf16[192,2048]{1,0:T(8,128)(2,1)S(1)}, u32[]{:S(2)}, u32[]{:S(2)}) collective-permute-start(bf16[192,2048]{1,0:T(8,128)(2,1)S(1)} %bitcast.28), channel_id=1, source_target_pairs={{0,2},{2,6},{6,4},{4,0},{1,3},{3,7},{7,5},{5,1},{8,10},{10,14},{14... | collective-permute-start | bytes 2359304 | tf_op jit(solution)/shard_map/ppermute | solution.py:265
  35.6 2.3 %collective-permute-start.9 = (bf16[160,2048]{1,0:T(8,128)(2,1)}, bf16[160,2048]{1,0:T(8,128)(2,1)S(1)}, u32[]{:S(2)}, u32[]{:S(2)}) collective-permute-start(bf16[160,2048]{1,0:T(8,128)(2,1)} %copy-done.11), channel_id=1, source_target_pairs={{0,1},{1,0},{2,3},{3,2},{4,5},{5,4},{6,7},{7,6},{8,9},{9,8},{10,11... | collective-permute-start | bytes 1966088 | tf_op jit(solution)/shard_map/ppermute | solution.py:37
  69.9 3.0 %collective-permute-start.12 = (bf16[176,2048]{1,0:T(8,128)(2,1)}, bf16[176,2048]{1,0:T(8,128)(2,1)S(1)}, u32[]{:S(2)}, u32[]{:S(2)}) collective-permute-start(bf16[176,2048]{1,0:T(8,128)(2,1)} %copy-done.5), channel_id=1, source_target_pairs={{0,1},{1,0},{2,3},{3,2},{4,5},{5,4},{6,7},{7,6},{8,9},{9,8},{10,11... | collective-permute-start | bytes 2162696 | tf_op jit(solution)/shard_map/ppermute | solution.py:37
  70.0 4.1 %collective-permute-start.11 = (bf16[176,2048]{1,0:T(8,128)(2,1)}, bf16[176,2048]{1,0:T(8,128)(2,1)S(1)}, u32[]{:S(2)}, u32[]{:S(2)}) collective-permute-start(bf16[176,2048]{1,0:T(8,128)(2,1)} %copy-done.8), channel_id=1, source_target_pairs={{0,1},{1,0},{2,3},{3,2},{4,5},{5,4},{6,7},{7,6},{8,9},{9,8},{10,11... | collective-permute-start | bytes 2162696 | tf_op jit(solution)/shard_map/ppermute | solution.py:37
  70.5 25.4 %collective-permute-start.15 = (bf16[192,2048]{1,0:T(8,128)(2,1)S(1)}, bf16[192,2048]{1,0:T(8,128)(2,1)S(1)}, u32[]{:S(2)}, u32[]{:S(2)}) collective-permute-start(bf16[192,2048]{1,0:T(8,128)(2,1)S(1)} %collective-permute-done.10.rest_1_), channel_id=1, source_target_pairs={{0,2},{2,6},{6,4},{4,0},{1,3},{3,7},{7,5},{5,1},{8,10},{10,14},{14... | collective-permute-start | bytes 2359304 | tf_op jit(solution)/shard_map/ppermute | solution.py:265
  71.4 24.4 %collective-permute-start.14 = (bf16[176,2048]{1,0:T(8,128)(2,1)}, bf16[176,2048]{1,0:T(8,128)(2,1)S(1)}, u32[]{:S(2)}, u32[]{:S(2)}) collective-permute-start(bf16[176,2048]{1,0:T(8,128)(2,1)} %copy-done.8), channel_id=1, source_target_pairs={{0,16},{8,24},{16,0},{24,8},{1,17},{9,25},{17,1},{25,9},{2,18},{10... | collective-permute-start | bytes 2162696 | tf_op jit(solution)/shard_map/ppermute | solution.py:42
  72.4 23.4 %collective-permute-start.13 = (bf16[160,2048]{1,0:T(8,128)(2,1)}, bf16[160,2048]{1,0:T(8,128)(2,1)S(1)}, u32[]{:S(2)}, u32[]{:S(2)}) collective-permute-start(bf16[160,2048]{1,0:T(8,128)(2,1)} %copy-done.11), channel_id=1, source_target_pairs={{0,8},{8,0},{16,24},{24,16},{1,9},{9,1},{17,25},{25,17},{2,10},{10... | collective-permute-start | bytes 1966088 | tf_op jit(solution)/shard_map/ppermute | solution.py:42
  73.0 41.2 %collective-permute-start.19 = (bf16[256,2048]{1,0:T(8,128)(2,1)}, bf16[256,2048]{1,0:T(8,128)(2,1)S(1)}, u32[]{:S(2)}, u32[]{:S(2)}) collective-permute-start(bf16[256,2048]{1,0:T(8,128)(2,1)} %all-gather.3.cloned.1.call-done), channel_id=1, source_target_pairs={{0,16},{8,24},{16,0},{24,8},{1,17},{9,25},{17,1},{25,9},{2,18},{10... | collective-permute-start | bytes 3145736 | tf_op jit(solution)/shard_map/ppermute | solution.py:42
  74.0 40.2 %collective-permute-start.18 = (bf16[256,2048]{1,0:T(8,128)(2,1)}, bf16[256,2048]{1,0:T(8,128)(2,1)S(1)}, u32[]{:S(2)}, u32[]{:S(2)}) collective-permute-start(bf16[256,2048]{1,0:T(8,128)(2,1)} %all-gather.3.cloned.1.call-done), channel_id=1, source_target_pairs={{0,8},{8,0},{16,24},{24,16},{1,9},{9,1},{17,25},{25,17},{2,10},{10... | collective-permute-start | bytes 3145736 | tf_op jit(solution)/shard_map/ppermute | solution.py:42
  75.5 1.1 copy-start.3
  76.6 1.1 copy-start.6
  77.7 1.1 copy-start.9
  81.0 1.1 copy-start.17
  83.2 16.5 %copy-start.4 = (bf16[176,2048]{1,0:T(8,128)(2,1)S(1)}, bf16[176,2048]{1,0:T(8,128)(2,1)}, u32[]{:S(2)}) copy-start(bf16[176,2048]{1,0:T(8,128)(2,1)} %copy-done.2) | copy-start | bytes 2162692
  83.2 16.5 %copy-start.7 = (bf16[176,2048]{1,0:T(8,128)(2,1)S(1)}, bf16[176,2048]{1,0:T(8,128)(2,1)}, u32[]{:S(2)}) copy-start(bf16[176,2048]{1,0:T(8,128)(2,1)} %copy-done.5) | copy-start | bytes 2162692
  83.2 16.5 %copy-start.10 = (bf16[176,2048]{1,0:T(8,128)(2,1)S(1)}, bf16[176,2048]{1,0:T(8,128)(2,1)}, u32[]{:S(2)}) copy-start(bf16[176,2048]{1,0:T(8,128)(2,1)} %copy-done.8) | copy-start | bytes 2162692
  83.2 16.5 %copy-start.15 = (bf16[160,2048]{1,0:T(8,128)(2,1)S(1)}, bf16[160,2048]{1,0:T(8,128)(2,1)}, u32[]{:S(2)}) copy-start(bf16[160,2048]{1,0:T(8,128)(2,1)} %copy-done.13) | copy-start | bytes 1966084
  83.2 16.5 %copy-start.18 = (bf16[160,2048]{1,0:T(8,128)(2,1)S(1)}, bf16[160,2048]{1,0:T(8,128)(2,1)}, u32[]{:S(2)}) copy-start(bf16[160,2048]{1,0:T(8,128)(2,1)} %copy-done.16) | copy-start | bytes 1966084
  95.8 11.0 %collective-permute-start.17 = (bf16[176,2048]{1,0:T(8,128)(2,1)S(1)}, bf16[176,2048]{1,0:T(8,128)(2,1)S(1)}, u32[]{:S(2)}, u32[]{:S(2)}) collective-permute-start(bf16[176,2048]{1,0:T(8,128)(2,1)S(1)} %collective-permute-done.14.rest_4_.rest_14_), channel_id=1, source_target_pairs={{0,1},{1,0},{2,3},{3,2},{4,5},{5,4},{6,7},{7,6},{8,9},{9,8},{10,11... | collective-permute-start | bytes 2162696 | tf_op jit(solution)/shard_map/ppermute | solution.py:37
  95.9 10.8 %collective-permute-start.16 = (bf16[160,2048]{1,0:T(8,128)(2,1)S(1)}, bf16[160,2048]{1,0:T(8,128)(2,1)S(1)}, u32[]{:S(2)}, u32[]{:S(2)}) collective-permute-start(bf16[160,2048]{1,0:T(8,128)(2,1)S(1)} %collective-permute-done.13.rest_3_.rest_13_), channel_id=1, source_target_pairs={{0,1},{1,0},{2,3},{3,2},{4,5},{5,4},{6,7},{7,6},{8,9},{9,8},{10,11... | collective-permute-start | bytes 1966088 | tf_op jit(solution)/shard_map/ppermute | solution.py:37
  96.4 22.6 %collective-permute-start.22 = (bf16[192,2048]{1,0:T(8,128)(2,1)S(1)}, bf16[192,2048]{1,0:T(8,128)(2,1)S(1)}, u32[]{:S(2)}, u32[]{:S(2)}) collective-permute-start(bf16[192,2048]{1,0:T(8,128)(2,1)S(1)} %collective-permute-done.15.rest_0_.rest_2_), channel_id=1, source_target_pairs={{0,2},{2,6},{6,4},{4,0},{1,3},{3,7},{7,5},{5,1},{8,10},{10,14},{14... | collective-permute-start | bytes 2359304 | tf_op jit(solution)/shard_map/ppermute | solution.py:265
  106.8 10.2 %collective-permute-start.23 = (bf16[128,512]{1,0:T(8,128)(2,1)S(1)}, bf16[128,512]{1,0:T(8,128)(2,1)S(1)}, u32[]{:S(2)}, u32[]{:S(2)}) collective-permute-start(bf16[128,512]{1,0:T(8,128)(2,1)S(1)} %get-tuple-element.81), channel_id=1, source_target_pairs={{0,8},{8,0},{16,24},{24,16},{1,9},{9,1},{17,25},{25,17},{2,10},{10... | collective-permute-start | bytes 393224 | tf_op jit(solution)/shard_map/ppermute | solution.py:42
  106.9 21.0 %collective-permute-start.26 = (bf16[128,512]{1,0:T(8,128)(2,1)S(1)}, bf16[128,512]{1,0:T(8,128)(2,1)S(1)}, u32[]{:S(2)}, u32[]{:S(2)}) collective-permute-start(bf16[128,512]{1,0:T(8,128)(2,1)S(1)} %get-tuple-element.84), channel_id=1, source_target_pairs={{0,16},{8,24},{16,0},{24,8},{1,17},{9,25},{17,1},{25,9},{2,18},{10... | collective-permute-start | bytes 393224 | tf_op jit(solution)/shard_map/ppermute | solution.py:42
  114.2 5.3 %copy-start.21 = (bf16[160,2048]{1,0:T(8,128)(2,1)S(1)}, bf16[160,2048]{1,0:T(8,128)(2,1)}, u32[]{:S(2)}) copy-start(bf16[160,2048]{1,0:T(8,128)(2,1)} %copy-done.19) | copy-start | bytes 1966084
  114.2 15.3 %collective-permute-start.24 = (bf16[64,512]{1,0:T(8,128)(2,1)S(1)}, bf16[64,512]{1,0:T(8,128)(2,1)S(1)}, u32[]{:S(2)}, u32[]{:S(2)}) collective-permute-start(bf16[64,512]{1,0:T(8,128)(2,1)S(1)} %get-tuple-element.82), channel_id=1, source_target_pairs={{0,8},{8,0},{16,24},{24,16},{1,9},{9,1},{17,25},{25,17},{2,10},{10... | collective-permute-start | bytes 196616 | tf_op jit(solution)/shard_map/ppermute | solution.py:42
  115.7 26.3 %collective-permute-start.29 = (bf16[192,512]{1,0:T(8,128)(2,1)S(1)}, bf16[192,512]{1,0:T(8,128)(2,1)S(1)}, u32[]{:S(2)}, u32[]{:S(2)}) collective-permute-start(bf16[192,512]{1,0:T(8,128)(2,1)S(1)} %shard_map.66), channel_id=1, source_target_pairs={{0,24},{8,16},{16,8},{24,0},{1,25},{9,17},{17,9},{25,1},{2,26},{10... | collective-permute-start | bytes 589832 | tf_op jit(solution)/shard_map/ppermute | solution.py:42
  116.9 25.1 %copy-start = (bf16[256,2048]{1,0:T(8,128)(2,1)S(1)}, bf16[256,2048]{1,0:T(8,128)(2,1)}, u32[]{:S(2)}) copy-start(bf16[256,2048]{1,0:T(8,128)(2,1)} %all-gather.3.cloned.1.call-done) | copy-start | bytes 3145732
  116.9 25.1 %collective-permute-start.20 = (bf16[128,2048]{1,0:T(8,128)(2,1)S(1)}, bf16[128,2048]{1,0:T(8,128)(2,1)S(1)}, u32[]{:S(2)}, u32[]{:S(2)}) collective-permute-start(bf16[128,2048]{1,0:T(8,128)(2,1)S(1)} %slice.34), channel_id=1, source_target_pairs={{0,8},{8,0},{16,24},{24,16},{1,9},{9,1},{17,25},{25,17},{2,10},{10... | collective-permute-start | bytes 1572872 | tf_op jit(solution)/shard_map/ppermute | solution.py:42
  119.0 23.1 %collective-permute-start.21 = (bf16[128,2048]{1,0:T(8,128)(2,1)S(1)}, bf16[128,2048]{1,0:T(8,128)(2,1)S(1)}, u32[]{:S(2)}, u32[]{:S(2)}) collective-permute-start(bf16[128,2048]{1,0:T(8,128)(2,1)S(1)} %slice.35), channel_id=1, source_target_pairs={{0,16},{8,24},{16,0},{24,8},{1,17},{9,25},{17,1},{25,9},{2,18},{10... | collective-permute-start | bytes 1572872 | tf_op jit(solution)/shard_map/ppermute | solution.py:42
  127.9 7.9 %collective-permute-start.27 = (bf16[64,512]{1,0:T(8,128)(2,1)S(1)}, bf16[64,512]{1,0:T(8,128)(2,1)S(1)}, u32[]{:S(2)}, u32[]{:S(2)}) collective-permute-start(bf16[64,512]{1,0:T(8,128)(2,1)S(1)} %get-tuple-element.85), channel_id=1, source_target_pairs={{0,16},{8,24},{16,0},{24,8},{1,17},{9,25},{17,1},{25,9},{2,18},{10... | collective-permute-start | bytes 196616 | tf_op jit(solution)/shard_map/ppermute | solution.py:42
  129.5 7.3 %collective-permute-start.25 = (bf16[64,512]{1,0:T(8,128)(2,1)S(1)}, bf16[64,512]{1,0:T(8,128)(2,1)S(1)}, u32[]{:S(2)}, u32[]{:S(2)}) collective-permute-start(bf16[64,512]{1,0:T(8,128)(2,1)S(1)} %get-tuple-element.83), channel_id=1, source_target_pairs={{0,8},{8,0},{16,24},{24,16},{1,9},{9,1},{17,25},{25,17},{2,10},{10... | collective-permute-start | bytes 196616 | tf_op jit(solution)/shard_map/ppermute | solution.py:42
  135.8 5.0 %collective-permute-start.28 = (bf16[64,512]{1,0:T(8,128)(2,1)S(1)}, bf16[64,512]{1,0:T(8,128)(2,1)S(1)}, u32[]{:S(2)}, u32[]{:S(2)}) collective-permute-start(bf16[64,512]{1,0:T(8,128)(2,1)S(1)} %get-tuple-element.86), channel_id=1, source_target_pairs={{0,16},{8,24},{16,0},{24,8},{1,17},{9,25},{17,1},{25,9},{2,18},{10... | collective-permute-start | bytes 196616 | tf_op jit(solution)/shard_map/ppermute | solution.py:42
  136.8 5.2 %collective-permute-start.30 = (bf16[64,512]{1,0:T(8,128)(2,1)S(1)}, bf16[64,512]{1,0:T(8,128)(2,1)S(1)}, u32[]{:S(2)}, u32[]{:S(2)}) collective-permute-start(bf16[64,512]{1,0:T(8,128)(2,1)S(1)} %get-tuple-element.88), channel_id=1, source_target_pairs={{0,24},{8,16},{16,8},{24,0},{1,25},{9,17},{17,9},{25,1},{2,26},{10... | collective-permute-start | bytes 196616 | tf_op jit(solution)/shard_map/ppermute | solution.py:42
  144.0 2.7 %collective-permute-start.31 = (bf16[256,2048]{1,0:T(8,128)(2,1)S(1)}, bf16[256,2048]{1,0:T(8,128)(2,1)S(1)}, u32[]{:S(2)}, u32[]{:S(2)}) collective-permute-start(bf16[256,2048]{1,0:T(8,128)(2,1)S(1)} %shard_map.69), channel_id=1, source_target_pairs={{0,1},{1,0},{2,3},{3,2},{4,5},{5,4},{6,7},{7,6},{8,9},{9,8},{10,11... | collective-permute-start | bytes 3145736 | tf_op jit(solution)/shard_map/ppermute | solution.py:37
  (9 other events, 8.4 us)
Sparse Core Ops, SparseCore 0:
  27.2 42.7 all-gather.2

commit v5 on v4

--- a/solution.py
+++ b/solution.py
@@ -54,14 +54,55 @@
     return lax.dot_general(a, b, (((1,), (1,)), ((), ())), preferred_element_type=jnp.float32)
 
 
-def mix_kernel(steps, slots, parts, place_ref, taps_ref, long_ref, *rest):
+def lay_kernel(parts, place_ref, *refs):
+    pieces, (out_ref, sems) = refs[: len(parts)], refs[len(parts) :]
+    rows = (out_ref.shape[0] - HALO) // 2
+    core = place_ref[0]
+    copies = []
+    for ref, (side, start) in zip(pieces, parts):
+        owner = core if side == 0 else 1 - core
+        end = start + ref.shape[0]
+        bounds = []
+        if start < rows:
+            bounds.append((start, min(end, rows), HALO + owner * rows + start))
+        if end > rows:
+            low = max(start, rows)
+            bounds.append((low, end, owner * (HALO // 2) + low - rows))
+        for low, high, at in bounds:
+            copies.append(
+                pltpu.make_async_copy(
+                    ref.at[pl.ds(low - start, high - low)],
+                    out_ref.at[pl.ds(pl.multiple_of(at, 16), high - low)],
+                    sems.at[len(copies)],
+                )
+            )
+    for copy in copies:
+        copy.start()
+    for copy in copies:
+        copy.wait()
+
+
+def lay(place, rows, parts, pieces):
+    features = pieces[0].shape[1]
+    return pl.pallas_call(
+        functools.partial(lay_kernel, parts),
+        out_shape=jax.ShapeDtypeStruct((HALO + 2 * rows, features), jnp.bfloat16),
+        in_specs=[SMEM] + [pl.BlockSpec(memory_space=pl.ANY)] * len(pieces),
+        out_specs=VMEM,
+        scratch_shapes=[pltpu.SemaphoreType.DMA((2 * len(pieces),))],
+        compiler_params=LIMIT,
+        cost_estimate=pl.CostEstimate(
+            flops=0, bytes_accessed=4 * (HALO + 2 * rows) * features, transcendentals=0
+        ),
+    )(place, *pieces)
+
+
+def mix_kernel(steps, slots, place_ref, taps_ref, long_ref, *rest):
     weights, rest = rest[: len(steps)], rest[len(steps) :]
-    pieces, rest = rest[: len(parts)], rest[len(parts) :]
-    outs, rest = rest[: len(slots)], rest[len(slots) :]
+    tokens, rest = rest[:slots], rest[slots:]
+    outs, rest = rest[:slots], rest[slots:]
     w, first, second, packed, turned, tiles = rest
     span = first.shape[1] - HALO
-    rows = span // 2
-    core = place_ref[0]
     count = WIDE // GSIZE
     band = 64
     blocks = span // TAPS
@@ -82,23 +123,10 @@
             )
             tiles[c * count + g] = square[:, :TAPS].astype(jnp.bfloat16)
 
-    def put(half, value, at):
-        here = pl.ds(pl.multiple_of(at, 16), value.shape[0])
-        first[half, here] = value[:, :LANES]
-        second[half, here] = value[:, LANES:]
-
     def project_unit(n, c, i):
-        for ref, (slot, side, start) in zip(pieces, parts):
-            if slot != slots[i]:
-                continue
-            owner = core if side == 0 else 1 - core
-            value = nt(ref[...], w[c]).astype(jnp.bfloat16).astype(jnp.float32)
-            end = start + ref.shape[0]
-            if start < rows:
-                put(n % 2, value[: min(end, rows) - start], HALO + owner * rows + start)
-            if end > rows:
-                low = max(start, rows)
-                put(n % 2, value[low - start :], owner * (HALO // 2) + low - rows)
+        value = nt(tokens[i][...], w[c]).astype(jnp.bfloat16).astype(jnp.float32)
+        first[n % 2] = value[:, :LANES]
+        second[n % 2] = value[:, LANES:]
 
     def feat(ref, n, at, c, lanes):
         total = None
@@ -107,7 +135,7 @@
             total = term if total is None else total + term
         return total
 
-    units = [(c, i) for c in range(len(steps)) for i in range(len(slots))]
+    units = [(c, i) for c in range(len(steps)) for i in range(slots)]
     project_unit(0, *units[0])
     for n, (c, i) in enumerate(units):
         if n + 1 < len(units):
@@ -147,17 +175,16 @@
                 outs[units[n][1]][at : at + GSIZE, :] = (query * row).astype(jnp.bfloat16)
 
 
-def mix_chunks(steps, slots, rows, place, taps, filters, ws, parts, pieces):
+def mix_chunks(steps, place, taps, filters, ws, tokens):
     features = ws[0].shape[1]
-    chosen = [n for n, part in enumerate(parts) if part[0] in slots]
-    parts, pieces = [parts[n] for n in chosen], [pieces[n] for n in chosen]
+    slots, rows = len(tokens), (tokens[0].shape[0] - HALO) // 2
     weights = [ws[s] for s in steps]
-    units = len(steps) * len(slots)
+    units = len(steps) * slots
     return pl.pallas_call(
-        functools.partial(mix_kernel, steps, slots, parts),
-        out_shape=[jax.ShapeDtypeStruct((len(steps) * WIDE, 2 * rows), jnp.bfloat16)] * len(slots),
-        in_specs=[SMEM] + [VMEM] * (2 + len(weights) + len(pieces)),
-        out_specs=[VMEM] * len(slots),
+        functools.partial(mix_kernel, steps, slots),
+        out_shape=[jax.ShapeDtypeStruct((len(steps) * WIDE, 2 * rows), jnp.bfloat16)] * slots,
+        in_specs=[SMEM] + [VMEM] * (2 + len(weights) + slots),
+        out_specs=[VMEM] * slots,
         scratch_shapes=[
             pltpu.VMEM((len(steps), 4 * WIDE, features), jnp.bfloat16),
             pltpu.VMEM((2, HALO + 2 * rows, LANES), jnp.float32),
@@ -172,7 +199,7 @@
             bytes_accessed=2 * units * 2 * rows * features,
             transcendentals=0,
         ),
-    )(place, taps, filters, *weights, *pieces)
+    )(place, taps, filters, *weights, *tokens)
 
 
 def out_kernel(mirror, order, chips, width, counts, place_ref, *refs):
@@ -274,12 +301,11 @@
     edge = lax.ppermute(tokens[rows - HALO : rows - half], ("z", "core"), pairs(0)) + lax.ppermute(
         tokens[rows - half :], ("z", "core"), pairs(1)
     )
-    run_mix = lambda steps, which: mix_chunks(
-        steps, which, rows, place, taps, filters, ws, parts, pieces
-    )
+    run_mix = lambda steps, which: mix_chunks(steps, place, taps, filters, ws, which)
 
     if slots == 4 and chips == 4 and width == WIDE:
         mid = HALO
+        parts = [(0, 0), (0, mid), (1, 0), (1, mid)]
         ws = [in_weight.reshape(3 * width, features)]
         low = tokens[:mid]
         low_x, low_y = across(low, 1), across(low, 2)
@@ -287,43 +313,43 @@
 
         v = lax.all_gather(v, "z")
         high = jnp.concatenate([tokens[mid:], edge])
-        high_x, high_y, high_twin = across(high, 1), across(high, 2), swap(high)
-        low_twin, low_x_twin, low_y_twin = swap(low), swap(low_x), swap(low_y)
-        ws.append(forward(ws[0]))
-        (high_x, high_y, high_twin, low_twin, low_x_twin, low_y_twin, ws, taps, filters, place, v) = tie(
-            high_x, high_y, high_twin, low_twin, low_x_twin, low_y_twin, ws, taps, filters, place, v
+        high_x, high_y = across(high, 1), across(high, 2)
+        x0 = lay(place, rows, parts, [low, high, swap(low), swap(high)])
+        low_x_twin, low_y_twin = swap(low_x), swap(low_y)
+        (x0, high_x, high_y, low_x_twin, low_y_twin, ws, taps, filters, place, v) = tie(
+            x0, high_x, high_y, low_x_twin, low_y_twin, ws, taps, filters, place, v
         )
 
-        ws = list(ws) + [forward(ws[1])]
+        ws = list(ws) + [forward(ws[0])]
         far_x, far_y = across(low_y, 1), across(high_x, 2)
-        parts = [(r, side, at) for r in range(3) for side in range(2) for at in (0, mid)]
-        pieces = [low, high, low_twin, high_twin]
-        pieces += [low_x, high_x, low_x_twin, swap(high_x)]
-        pieces += [low_y, high_y, low_y_twin, swap(high_y)]
-        early = run_mix((0, 1), (0, 1, 2))
+        x1 = lay(place, rows, parts, [low_x, high_x, low_x_twin, swap(high_x)])
+        x2 = lay(place, rows, parts, [low_y, high_y, low_y_twin, swap(high_y)])
+        mix0 = run_mix((0,), (x0, x1, x2))
         v = v.reshape(chips * width, -1)
         v_x, v_y = across(v, 1), across(v, 2)
-        early, far_x, far_y, ws = tie(early, far_x, far_y, ws)
+        mix0, far_x, far_y, ws = tie(mix0, far_x, far_y, ws)
+
+        ws = list(ws) + [forward(ws[1])]
+        x3 = lay(place, rows, parts, [far_x, far_y, swap(far_x), swap(far_y)])
+        mix1 = run_mix((1,), (x0, x1, x2))
+        far01 = run_mix((0, 1), (x3,))
+        mix1, far01, ws, v_x, v_y = tie(mix1, far01, ws, v_x, v_y)
 
         ws = list(ws) + [forward(ws[2])]
-        parts += [(3, 0, 0), (3, 0, mid), (3, 1, 0), (3, 1, mid)]
-        pieces += [far_x, far_y, swap(far_x), swap(far_y)]
-        (far,) = run_mix((0, 1, 2), (3,))
-        late = run_mix((2,), (0, 1, 2))
-        late, far, v_x, v_y = tie(late, far, v_x, v_y)
         cut = v.shape[0] // 2
-        v = [v, v_x, v_y, across(v_y[:cut], 1), across(v_x[cut:], 2)]
-        last = run_mix((3,), (0, 1, 2, 3))
-        together = [early[0], late[0], last[0]]
-        for r in (1, 2):
-            together += [across(early[r], r), across(late[r], r), across(last[r], r)]
-        together += [across(far, 3), across(last[3], 3)]
-        order = [
-            (3 * r + max(0, s - 1), s * width if s < 2 else 0)
-            for r in range(3)
-            for s in range(chips)
-        ]
-        order += [(9 + s // 3, s % 3 * width) for s in range(chips)]
+        v_far = (across(v_y[:cut], 1), across(v_x[cut:], 2))
+        moved = [[across(mix0[r], r), across(mix1[r], r)] for r in (1, 2)]
+        moved.append([across(far01[0], 3)])
+        mix2 = run_mix((2,), (x0, x1, x2, x3))
+        mix2, moved, ws = tie(mix2, moved, ws)
+
+        mix3 = run_mix((3,), (x0, x1, x2, x3))
+        v = [v, v_x, v_y, *v_far]
+        together = [mix0[0], mix1[0], mix2[0], mix3[0]]
+        for r in (1, 2, 3):
+            together += list(moved[r - 1]) + [across(mix2[r], r), across(mix3[r], r)]
+        order = [(4 * r + s, 0) for r in range(3) for s in range(chips)]
+        order += [(12, 0), (12, width), (13, 0), (14, 0)]
     else:
         v = lax.all_gather(out_weight, ("dp", "z"))
         block = jnp.concatenate([tokens, edge])
@@ -333,14 +359,13 @@
             ws.append(padded.reshape(3 * WIDE, features))
             if s + 1 < chips:
                 w = forward(w)
-        pieces = [block] + [across(block, r) for r in range(1, slots)]
-        pieces += [swap(piece) for piece in pieces]
-        parts = [(r, side, 0) for side in range(2) for r in range(slots)]
+        blocks = [block] + [across(block, r) for r in range(1, slots)]
+        xs = [lay(place, rows, [(0, 0), (1, 0)], [one, swap(one)]) for one in blocks]
         moved = []
         for s in range(chips):
             mixed = []
             for r in range(0, slots, 4):
-                mixed += run_mix((s,), tuple(range(r, min(r + 4, slots))))
+                mixed += run_mix((s,), xs[r : r + 4])
             mixed = [m[:width] for m in mixed]
             moved.append([mixed[0]] + [across(mixed[r], r) for r in range(1, slots)])
         turn = lax.bitwise_xor(dp, jnp.arange(slots))

time: 155 us -> 147 us (0.948)
  local copies, waits for them, and re-layouts: 16.2 us -> 7.81 us
  Pallas kernels: 38.2 us -> 33.2 us
  starting transfers between devices: 30.1 us -> 33.1 us
  waiting for transfers between devices: 54.9 us -> 57.3 us
    ppermute x3, waiting for transfers between devices: 19.6 us -> 3.42 us  [shards(): forward = lambda block: lax.ppermute(block, 'z', ring)]
    ppermute x18 -> x21, waiting for transfers between devices: 31.3 us -> 45.5 us  [across(): return lax.ppermute(block, 'dp', [(i, i ^ r) for i in range(count)])]
    unnamed x47 -> x19, local copies, waits for them, and re-layouts: 12.1 us -> 3.65 us
    all_gather x1, waiting for transfers between devices: 1.02 us -> 7.52 us  [shards(): v = lax.all_gather(v, 'z')]
    ppermute x18 -> x21, starting transfers between devices: 20.9 us -> 26 us  [across(): return lax.ppermute(block, 'dp', [(i, i ^ r) for i in range(count)])]
    pallas_call x4 -> x9, Pallas kernels: 34.4 us -> 29.4 us  [the longest x5 22.5 us: mix_chunks(): pl.pallas_call(functools.partial(mix_kernel, steps, slots), out_shape=[ja...]
    ppermute x3, starting transfers between devices: 5.86 us -> 3.48 us  [shards(): forward = lambda block: lax.ppermute(block, 'z', ring)]
    ppermute x9, waiting for transfers between devices: 2.89 us -> 0.81 us  [swap(): return lax.ppermute(block, 'core', [(0, 1), (1, 0)])]
  transfers between devices with their start and end apart: 33 -> 36, of which waited for: 11 -> 14; matrix products, arithmetic and copies ran while one was open for 2% -> 2% of each run, Pallas kernels for 23% -> 21%
where the time goes in v5:
time: 147 us
  waiting for transfers between devices  57.3 us (39%)
  Pallas kernels  33.2 us (23%)
  starting transfers between devices  33.1 us (23%)
  between operations  13.9 us (9%)
  local copies, waits for them, and re-layouts  7.81 us (5%)
  other arithmetic  1.57 us (1%)
    ppermute x21, waiting for transfers between devices, across(): return lax.ppermute(block, 'dp', [(i, i ^ r) for i in range(count)])  45.5 us
    ppermute x21, starting transfers between devices, across(): return lax.ppermute(block, 'dp', [(i, i ^ r) for i in range(count)])  26 us
    pallas_call x5, Pallas kernels, mix_chunks(): pl.pallas_call(functools.partial(mix_kernel, steps, slots), out_shape=[ja...  22.5 us
    all_gather x1, waiting for transfers between devices, shards(): v = lax.all_gather(v, 'z')  7.52 us
    pallas_call x4, Pallas kernels, lay(): pl.pallas_call(functools.partial(lay_kernel, parts), out_shape=jax.ShapeD...  6.86 us
    pallas_call x2, Pallas kernels, project(): pl.pallas_call(functools.partial(out_kernel, mirror, order, chips, width,...  3.79 us
    unnamed x19, local copies, waits for them, and re-layouts  3.65 us
    ppermute x3, starting transfers between devices, shards(): forward = lambda block: lax.ppermute(block, 'z', ring)  3.48 us
  transfers between devices with their start and end apart: 36, of which 14 were waited for; matrix products, arithmetic and copies ran while one was open for 2% of the time, Pallas kernels for 21%

profile of v5, /device:TPU:0, one launch (start us, length us, event | category | flops | bytes accessed | tf_op | source)
XLA Modules:
  0.0 146.8 jit_solution(15575487669299159487)
XLA Ops:
  6.5 1.1 slice.29.refs_0_
  7.7 3.0 %collective-permute-start.2 = (bf16[160,2048]{1,0:T(8,128)(2,1)S(1)}, bf16[160,2048]{1,0:T(8,128)(2,1)}, u32[]{:S(2)}, u32[]{:S(2)}) collective-permute-start(bf16[160,2048]{1,0:T(8,128)(2,1)S(1)} %slice.29.refs_0_), channel_id=1, source_target_pairs={{0,8},{8,0},{16,24},{24,16},{1,9},{9,1},{17,25},{25,17},{2,10},{10... | collective-permute-start | bytes 1966088 | tf_op jit(solution)/shard_map/ppermute | solution.py:42
  10.7 1.5 %collective-permute-start.3 = (bf16[160,2048]{1,0:T(8,128)(2,1)S(1)}, bf16[160,2048]{1,0:T(8,128)(2,1)}, u32[]{:S(2)}, u32[]{:S(2)}) collective-permute-start(bf16[160,2048]{1,0:T(8,128)(2,1)S(1)} %slice.29.refs_0_), channel_id=1, source_target_pairs={{0,16},{8,24},{16,0},{24,8},{1,17},{9,25},{17,1},{25,9},{2,18},{10... | collective-permute-start | bytes 1966088 | tf_op jit(solution)/shard_map/ppermute | solution.py:42
  12.2 1.1 fusion.5
  14.9 10.7 %collective-permute-done.2.refs_0_ = bf16[160,2048]{1,0:T(8,128)(2,1)} collective-permute-done((bf16[160,2048]{1,0:T(8,128)(2,1)S(1)}, bf16[160,2048]{1,0:T(8,128)(2,1)}, u32[]{:S(2)}, u32[]{:S(2)}) %collective-permute-start.2) | collective-permute-done | bytes 655392 | tf_op jit(solution)/shard_map/ppermute | solution.py:42
  25.6 1.5 collective-permute-done.3.refs_0_
  27.5 0.8 fusion
  29.3 1.7 %collective-permute-start.7 = (bf16[176,2048]{1,0:T(8,128)(2,1)S(1)}, bf16[176,2048]{1,0:T(8,128)(2,1)}, u32[]{:S(2)}, u32[]{:S(2)}) collective-permute-start(bf16[176,2048]{1,0:T(8,128)(2,1)S(1)} %pad_maximum_fusion.refs_1_), channel_id=1, source_target_pairs={{0,16},{8,24},{16,0},{24,8},{1,17},{9,25},{17,1},{25,9},{2,18},{10... | collective-permute-start | bytes 2162696 | tf_op jit(solution)/shard_map/ppermute | solution.py:42
  32.5 1.6 %shard_map.64.rest_1_ = bf16[672,2048]{1,0:T(8,128)(2,1)S(1)} custom-call(s32[6]{0:T(128)S(1)} %pad_add_fusion.place_ref, bf16[160,2048]{1,0:T(8,128)(2,1)S(1)} %slice.29.refs_0_, bf16[176,2048]{1,0:T(8,128)(2,1)S(1)} %pad_maximum_fusion.refs_1_, bf16[160,2048]{1,0:T(8,128)(2,1)S(1)} %collective-permute-done.4.refs_2_, ...), custom_call_target="tpu_custom_call" | custom-call | bytes 5505024 | tf_op jit(solution)/shard_map/pallas_call | solution.py:87
  34.1 0.8 copy-done.4
  35.0 0.8 copy-done.2
  35.9 11.2 %collective-permute-done.6.refs_1_ = bf16[176,2048]{1,0:T(8,128)(2,1)S(1)} collective-permute-done((bf16[176,2048]{1,0:T(8,128)(2,1)S(1)}, bf16[176,2048]{1,0:T(8,128)(2,1)S(1)}, u32[]{:S(2)}, u32[]{:S(2)}) %collective-permute-start.6) | collective-permute-done | bytes 720928 | tf_op jit(solution)/shard_map/ppermute | solution.py:42
  47.1 0.9 copy-done
  47.9 7.5 %all-gather.3.cloned.1.call-done = bf16[256,2048]{1,0:T(8,128)(2,1)} async-done(((bf16[64,2048]{1,0:T(8,128)(2,1)}), bf16[256,2048]{1,0:T(8,128)(2,1)}) %all-gather.3.cloned.1.call-update) | async-done | bytes 1048592 | tf_op jit(solution)/shard_map/all_gather | solution.py:314
  56.0 1.4 collective-permute-start.14
  57.4 1.5 %collective-permute-start.13 = (bf16[176,2048]{1,0:T(8,128)(2,1)}, bf16[176,2048]{1,0:T(8,128)(2,1)S(1)}, u32[]{:S(2)}, u32[]{:S(2)}) collective-permute-start(bf16[176,2048]{1,0:T(8,128)(2,1)} %copy-done), channel_id=1, source_target_pairs={{0,16},{8,24},{16,0},{24,8},{1,17},{9,25},{17,1},{25,9},{2,18},{10... | collective-permute-start | bytes 2162696 | tf_op jit(solution)/shard_map/ppermute | solution.py:42
  58.9 1.5 collective-permute-start.12
  60.9 1.1 copy-done.5
  62.0 1.9 %shard_map.66.rest_3_ = bf16[672,2048]{1,0:T(8,128)(2,1)S(1)} custom-call(s32[6]{0:T(128)S(1)} %pad_add_fusion.place_ref, bf16[160,2048]{1,0:T(8,128)(2,1)} %collective-permute-done.3.refs_0_, bf16[176,2048]{1,0:T(8,128)(2,1)} %collective-permute-done.7.refs_1_, bf16[160,2048]{1,0:T(8,128)(2,1)S(1)} %copy-done.5, ...), custom_call_target="tpu_custom_call" | custom-call | bytes 5505024 | tf_op jit(solution)/shard_map/pallas_call | solution.py:87
  64.6 1.7 %shard_map.65.rest_2_ = bf16[672,2048]{1,0:T(8,128)(2,1)S(1)} custom-call(s32[6]{0:T(128)S(1)} %pad_add_fusion.place_ref, bf16[160,2048]{1,0:T(8,128)(2,1)} %collective-permute-done.2.refs_0_, bf16[176,2048]{1,0:T(8,128)(2,1)S(1)} %copy-done.1, bf16[160,2048]{1,0:T(8,128)(2,1)S(1)} %copy-done.3, bf16[176,2048]{1,0:T(8,128)(2,1)S(1)} %collective-permute-done.10.refs_3_), custom_call_target="tpu_custom_call" | custom-call | bytes 5505024 | tf_op jit(solution)/shard_map/pallas_call | solution.py:87
  66.3 4.3 %shard_map.67 = (bf16[64,512]{1,0:T(8,128)(2,1)S(1)}, bf16[64,512]{1,0:T(8,128)(2,1)S(1)}, bf16[64,512]{1,0:T(8,128)(2,1)S(1)}) custom-call(s32[6]{0:T(128)S(1)} %pad_add_fusion.place_ref, f32[4,8,256]{2,1,0:T(8,128)S(1)} %pad_maximum_fusion.1.taps_ref, f32[4,4,128]{2,1,0:T(4,128)S(1)} %maximum_convert_fusion.long_ref, bf16[192,2048]{1,0:T(8,128)(2,1)S(1)} %bitcast.29, ...), custom_call_target="tpu_custom_call" | custom-call | flops 3221225472 | bytes 6291456 | tf_op jit(solution)/shard_map/pallas_call | solution.py:183
  70.6 6.2 %collective-permute-done.12.refs_0_ = bf16[160,2048]{1,0:T(8,128)(2,1)S(1)} collective-permute-done((bf16[160,2048]{1,0:T(8,128)(2,1)}, bf16[160,2048]{1,0:T(8,128)(2,1)S(1)}, u32[]{:S(2)}, u32[]{:S(2)}) %collective-permute-start.12) | collective-permute-done | bytes 655392 | tf_op jit(solution)/shard_map/ppermute | solution.py:42
  77.3 1.0 collective-permute-start.17
  78.3 4.3 %shard_map.68 = (bf16[64,512]{1,0:T(8,128)(2,1)S(1)}, bf16[64,512]{1,0:T(8,128)(2,1)S(1)}, bf16[64,512]{1,0:T(8,128)(2,1)S(1)}) custom-call(s32[6]{0:T(128)S(1)} %pad_add_fusion.place_ref, f32[4,8,256]{2,1,0:T(8,128)S(1)} %pad_maximum_fusion.1.taps_ref, f32[4,4,128]{2,1,0:T(4,128)S(1)} %maximum_convert_fusion.long_ref, ...), custom_call_target="tpu_custom_call" | custom-call | flops 3221225472 | bytes 6291456 | tf_op jit(solution)/shard_map/pallas_call | solution.py:183
  82.6 1.6 %shard_map.69.rest_2_.rest_4_ = bf16[672,2048]{1,0:T(8,128)(2,1)S(1)} custom-call(s32[6]{0:T(128)S(1)} %pad_add_fusion.place_ref, bf16[160,2048]{1,0:T(8,128)(2,1)S(1)} %collective-permute-done.12.refs_0_, bf16[176,2048]{1,0:T(8,128)(2,1)S(1)} %collective-permute-done.13.refs_1_, bf16[160,2048]{1,0:T(8,128)(2,1)S(1)} %collective-permute-done.15.refs_2_, ...), custom_call_target="tpu_custom_call" | custom-call | bytes 5505024 | tf_op jit(solution)/shard_map/pallas_call | solution.py:87
  84.2 3.2 %shard_map.70 = bf16[128,512]{1,0:T(8,128)(2,1)S(1)} custom-call(s32[6]{0:T(128)S(1)} %pad_add_fusion.place_ref, f32[4,8,256]{2,1,0:T(8,128)S(1)} %pad_maximum_fusion.1.taps_ref, f32[4,4,128]{2,1,0:T(4,128)S(1)} %maximum_convert_fusion.long_ref, bf16[192,2048]{1,0:T(8,128)(2,1)S(1)} %bitcast.30, ...), custom_call_target="tpu_custom_call" | custom-call | flops 2147483648 | bytes 4194304 | tf_op jit(solution)/shard_map/pallas_call | solution.py:183
  87.5 10.2 %collective-permute-done.18.refs_1_ = bf16[256,2048]{1,0:T(8,128)(2,1)S(1)} collective-permute-done((bf16[256,2048]{1,0:T(8,128)(2,1)}, bf16[256,2048]{1,0:T(8,128)(2,1)S(1)}, u32[]{:S(2)}, u32[]{:S(2)}) %collective-permute-start.18) | collective-permute-done | bytes 1048608 | tf_op jit(solution)/shard_map/ppermute | solution.py:42
  97.9 1.0 collective-permute-start.27
  98.9 1.5 collective-permute-start.22
  100.3 1.5 %collective-permute-start.24 = (bf16[64,512]{1,0:T(8,128)(2,1)S(1)}, bf16[64,512]{1,0:T(8,128)(2,1)S(1)}, u32[]{:S(2)}, u32[]{:S(2)}) collective-permute-start(bf16[64,512]{1,0:T(8,128)(2,1)S(1)} %get-tuple-element.96), channel_id=1, source_target_pairs={{0,16},{8,24},{16,0},{24,8},{1,17},{9,25},{17,1},{25,9},{2,18},{10... | collective-permute-start | bytes 196616 | tf_op jit(solution)/shard_map/ppermute | solution.py:42
  102.4 1.5 collective-permute-start.26
  103.9 1.5 %collective-permute-start.25 = (bf16[64,512]{1,0:T(8,128)(2,1)S(1)}, bf16[64,512]{1,0:T(8,128)(2,1)S(1)}, u32[]{:S(2)}, u32[]{:S(2)}) collective-permute-start(bf16[64,512]{1,0:T(8,128)(2,1)S(1)} %get-tuple-element.97), channel_id=1, source_target_pairs={{0,16},{8,24},{16,0},{24,8},{1,17},{9,25},{17,1},{25,9},{2,18},{10... | collective-permute-start | bytes 196616 | tf_op jit(solution)/shard_map/ppermute | solution.py:42
  105.5 1.0 collective-permute-done.24.refs_13_
  106.8 1.7 %collective-permute-start.21 = (bf16[128,2048]{1,0:T(8,128)(2,1)S(1)}, bf16[128,2048]{1,0:T(8,128)(2,1)S(1)}, u32[]{:S(2)}, u32[]{:S(2)}) collective-permute-start(bf16[128,2048]{1,0:T(8,128)(2,1)S(1)} %slice.35), channel_id=1, source_target_pairs={{0,16},{8,24},{16,0},{24,8},{1,17},{9,25},{17,1},{25,9},{2,18},{10... | collective-permute-start | bytes 1572872 | tf_op jit(solution)/shard_map/ppermute | solution.py:42
  108.5 5.3 %shard_map.71 = (bf16[64,512]{1,0:T(8,128)(2,1)S(1)}, bf16[64,512]{1,0:T(8,128)(2,1)S(1)}, bf16[64,512]{1,0:T(8,128)(2,1)S(1)}, bf16[64,512]{1,0:T(8,128)(2,1)S(1)}) custom-call(s32[6]{0:T(128)S(1)} %pad_add_fusion.place_ref, f32[4,8,256]{2,1,0:T(8,128)S(1)} %pad_maximum_fusion.1.taps_ref, f32[4,4,128]{2,1,0:T(4,128)S(1)} %maximum_convert_fusion.long_ref, ...), custom_call_target="tpu_custom_call" | custom-call | flops 4294967296 | bytes 8388608 | tf_op jit(solution)/shard_map/pallas_call | solution.py:183
  113.9 3.4 %collective-permute-done.27.rest_0_ = bf16[192,2048]{1,0:T(8,128)(2,1)S(1)} collective-permute-done((bf16[192,2048]{1,0:T(8,128)(2,1)S(1)}, bf16[192,2048]{1,0:T(8,128)(2,1)S(1)}, u32[]{:S(2)}, u32[]{:S(2)}) %collective-permute-start.27) | collective-permute-done | bytes 786464 | tf_op jit(solution)/shard_map/ppermute | solution.py:292
  117.3 5.3 %shard_map.72 = (bf16[64,512]{1,0:T(8,128)(2,1)S(1)}, bf16[64,512]{1,0:T(8,128)(2,1)S(1)}, bf16[64,512]{1,0:T(8,128)(2,1)S(1)}, bf16[64,512]{1,0:T(8,128)(2,1)S(1)}) custom-call(s32[6]{0:T(128)S(1)} %pad_add_fusion.place_ref, f32[4,8,256]{2,1,0:T(8,128)S(1)} %pad_maximum_fusion.1.taps_ref, f32[4,4,128]{2,1,0:T(4,128)S(1)} %maximum_convert_fusion.long_ref, ...), custom_call_target="tpu_custom_call" | custom-call | flops 4294967296 | bytes 8388608 | tf_op jit(solution)/shard_map/pallas_call | solution.py:183
  122.6 1.5 %collective-permute-start.29 = (bf16[64,512]{1,0:T(8,128)(2,1)S(1)}, bf16[64,512]{1,0:T(8,128)(2,1)S(1)}, u32[]{:S(2)}, u32[]{:S(2)}) collective-permute-start(bf16[64,512]{1,0:T(8,128)(2,1)S(1)} %get-tuple-element.105), channel_id=1, source_target_pairs={{0,8},{8,0},{16,24},{24,16},{1,9},{9,1},{17,25},{25,17},{2,10},{10... | collective-permute-start | bytes 196616 | tf_op jit(solution)/shard_map/ppermute | solution.py:42
  124.2 1.2 collective-permute-start.31
  125.4 0.8 collective-permute-start.33
  126.2 1.5 collective-permute-start.28
  127.7 1.2 collective-permute-start.30
  129.7 0.9 collective-permute-done.33.refs_19_
  130.6 1.3 collective-permute-done.30.refs_15_
  131.9 2.1 %collective-permute-done.32.refs_18_ = bf16[64,512]{1,0:T(8,128)(2,1)S(1)} collective-permute-done((bf16[64,512]{1,0:T(8,128)(2,1)S(1)}, bf16[64,512]{1,0:T(8,128)(2,1)S(1)}, u32[]{:S(2)}, u32[]{:S(2)}) %collective-permute-start.32) | collective-permute-done | bytes 65568 | tf_op jit(solution)/shard_map/ppermute | solution.py:42
  134.1 1.9 %shard_map.74 = bf16[256,2048]{1,0:T(8,128)(2,1)S(1)} custom-call(s32[6]{0:T(128)S(1)} %pad_add_fusion.place_ref, bf16[256,2048]{1,0:T(8,128)(2,1)S(1)} %copy-done.6, bf16[256,2048]{1,0:T(8,128)(2,1)S(1)} %collective-permute-done.18.refs_1_, bf16[256,2048]{1,0:T(8,128)(2,1)S(1)} %collective-permute-done.19.refs_2_, ...), custom_call_target="tpu_custom_call" | custom-call | flops 2147483648 | bytes 5242880 | tf_op jit(solution)/shard_map/pallas_call | solution.py:244
  136.0 1.9 %shard_map.73 = f32[256,2048]{1,0:T(8,128)S(1)} custom-call(s32[6]{0:T(128)S(1)} %pad_add_fusion.place_ref, bf16[256,2048]{1,0:T(8,128)(2,1)S(1)} %copy-done.6, bf16[256,2048]{1,0:T(8,128)(2,1)S(1)} %collective-permute-done.18.refs_1_, bf16[256,2048]{1,0:T(8,128)(2,1)S(1)} %collective-permute-done.19.refs_2_, ...), custom_call_target="tpu_custom_call" | custom-call | flops 2147483648 | bytes 5242880 | tf_op jit(solution)/shard_map/pallas_call | solution.py:244
  138.7 1.3 add_convert_fusion
  (75 shorter events, 9.4 us)
Async XLA Ops:
  6.5 48.9 %all-gather.3.cloned.1.call-start = ((), (), s32[]{:S(2)}) async-start(), calls=%async_computation | async-start | bytes 1310720 | tf_op jit(solution)/shard_map/all_gather | solution.py:314
  7.7 19.4 %copy-start.8 = (f32[7,3,2048]{2,0,1:T(8,128)S(1)}, f32[7,3,2048]{2,0,1:T(8,128)}, u32[]{:S(2)}) copy-start(f32[7,3,2048]{2,0,1:T(8,128)} %param.8) | copy-start | bytes 516100
  7.7 20.6 %slice-start = ((bf16[256,2048]{1,0:T(8,128)(2,1)}), bf16[96,2048]{1,0:T(8,128)(2,1)S(1)}, s32[]{:S(2)}) async-start(bf16[256,2048]{1,0:T(8,128)(2,1)} %param.6), calls=%async_computation.1 | async-start | bytes 786432 | tf_op jit(solution)/shard_map/slice | solution.py:315
  7.7 17.8 %collective-permute-start.2 = (bf16[160,2048]{1,0:T(8,128)(2,1)S(1)}, bf16[160,2048]{1,0:T(8,128)(2,1)}, u32[]{:S(2)}, u32[]{:S(2)}) collective-permute-start(bf16[160,2048]{1,0:T(8,128)(2,1)S(1)} %slice.29.refs_0_), channel_id=1, source_target_pairs={{0,8},{8,0},{16,24},{24,16},{1,9},{9,1},{17,25},{25,17},{2,10},{10... | collective-permute-start | bytes 1966088 | tf_op jit(solution)/shard_map/ppermute | solution.py:42
  10.7 16.3 %collective-permute-start.3 = (bf16[160,2048]{1,0:T(8,128)(2,1)S(1)}, bf16[160,2048]{1,0:T(8,128)(2,1)}, u32[]{:S(2)}, u32[]{:S(2)}) collective-permute-start(bf16[160,2048]{1,0:T(8,128)(2,1)S(1)} %slice.29.refs_0_), channel_id=1, source_target_pairs={{0,16},{8,24},{16,0},{24,8},{1,17},{9,25},{17,1},{25,9},{2,18},{10... | collective-permute-start | bytes 1966088 | tf_op jit(solution)/shard_map/ppermute | solution.py:42
  13.4 1.4 collective-permute-start
  14.1 0.7 collective-permute-start.1
  27.4 4.4 %collective-permute-start.4 = (bf16[160,2048]{1,0:T(8,128)(2,1)S(1)}, bf16[160,2048]{1,0:T(8,128)(2,1)S(1)}, u32[]{:S(2)}, u32[]{:S(2)}) collective-permute-start(bf16[160,2048]{1,0:T(8,128)(2,1)S(1)} %slice.29.refs_0_), channel_id=1, source_target_pairs={{0,1},{1,0},{2,3},{3,2},{4,5},{5,4},{6,7},{7,6},{8,9},{9,8},{10,11... | collective-permute-start | bytes 1966088 | tf_op jit(solution)/shard_map/ppermute | solution.py:37
  28.4 4.1 %collective-permute-start.5 = (bf16[176,2048]{1,0:T(8,128)(2,1)S(1)}, bf16[176,2048]{1,0:T(8,128)(2,1)S(1)}, u32[]{:S(2)}, u32[]{:S(2)}) collective-permute-start(bf16[176,2048]{1,0:T(8,128)(2,1)S(1)} %pad_maximum_fusion.refs_1_), channel_id=1, source_target_pairs={{0,1},{1,0},{2,3},{3,2},{4,5},{5,4},{6,7},{7,6},{8,9},{9,8},{10,11... | collective-permute-start | bytes 2162696 | tf_op jit(solution)/shard_map/ppermute | solution.py:37
  28.9 18.1 %collective-permute-start.6 = (bf16[176,2048]{1,0:T(8,128)(2,1)S(1)}, bf16[176,2048]{1,0:T(8,128)(2,1)S(1)}, u32[]{:S(2)}, u32[]{:S(2)}) collective-permute-start(bf16[176,2048]{1,0:T(8,128)(2,1)S(1)} %pad_maximum_fusion.refs_1_), channel_id=1, source_target_pairs={{0,8},{8,0},{16,24},{24,16},{1,9},{9,1},{17,25},{25,17},{2,10},{10... | collective-permute-start | bytes 2162696 | tf_op jit(solution)/shard_map/ppermute | solution.py:42
  29.3 18.6 %collective-permute-start.7 = (bf16[176,2048]{1,0:T(8,128)(2,1)S(1)}, bf16[176,2048]{1,0:T(8,128)(2,1)}, u32[]{:S(2)}, u32[]{:S(2)}) collective-permute-start(bf16[176,2048]{1,0:T(8,128)(2,1)S(1)} %pad_maximum_fusion.refs_1_), channel_id=1, source_target_pairs={{0,16},{8,24},{16,0},{24,8},{1,17},{9,25},{17,1},{25,9},{2,18},{10... | collective-permute-start | bytes 2162696 | tf_op jit(solution)/shard_map/ppermute | solution.py:42
  31.7 2.4 %collective-permute-start.9 = (bf16[160,2048]{1,0:T(8,128)(2,1)}, bf16[160,2048]{1,0:T(8,128)(2,1)S(1)}, u32[]{:S(2)}, u32[]{:S(2)}) collective-permute-start(bf16[160,2048]{1,0:T(8,128)(2,1)} %collective-permute-done.3.refs_0_), channel_id=1, source_target_pairs={{0,1},{1,0},{2,3},{3,2},{4,5},{5,4},{6,7},{7,6},{8,9},{9,8},{10,11... | collective-permute-start | bytes 1966088 | tf_op jit(solution)/shard_map/ppermute | solution.py:37
  31.8 3.2 %collective-permute-start.8 = (bf16[160,2048]{1,0:T(8,128)(2,1)}, bf16[160,2048]{1,0:T(8,128)(2,1)S(1)}, u32[]{:S(2)}, u32[]{:S(2)}) collective-permute-start(bf16[160,2048]{1,0:T(8,128)(2,1)} %collective-permute-done.2.refs_0_), channel_id=1, source_target_pairs={{0,1},{1,0},{2,3},{3,2},{4,5},{5,4},{6,7},{7,6},{8,9},{9,8},{10,11... | collective-permute-start | bytes 1966088 | tf_op jit(solution)/shard_map/ppermute | solution.py:37
  34.1 0.9 copy-start.4
  35.0 0.8 copy-start.2
  47.1 0.9 copy-start
  55.4 4.9 %collective-permute-start.11 = (bf16[176,2048]{1,0:T(8,128)(2,1)}, bf16[176,2048]{1,0:T(8,128)(2,1)S(1)}, u32[]{:S(2)}, u32[]{:S(2)}) collective-permute-start(bf16[176,2048]{1,0:T(8,128)(2,1)} %collective-permute-done.7.refs_1_), channel_id=1, source_target_pairs={{0,1},{1,0},{2,3},{3,2},{4,5},{5,4},{6,7},{7,6},{8,9},{9,8},{10,11... | collective-permute-start | bytes 2162696 | tf_op jit(solution)/shard_map/ppermute | solution.py:37
  55.5 8.5 %collective-permute-start.10 = (bf16[176,2048]{1,0:T(8,128)(2,1)}, bf16[176,2048]{1,0:T(8,128)(2,1)S(1)}, u32[]{:S(2)}, u32[]{:S(2)}) collective-permute-start(bf16[176,2048]{1,0:T(8,128)(2,1)} %copy-done), channel_id=1, source_target_pairs={{0,1},{1,0},{2,3},{3,2},{4,5},{5,4},{6,7},{7,6},{8,9},{9,8},{10,11... | collective-permute-start | bytes 2162696 | tf_op jit(solution)/shard_map/ppermute | solution.py:37
  56.0 20.8 %collective-permute-start.14 = (bf16[192,2048]{1,0:T(8,128)(2,1)}, bf16[192,2048]{1,0:T(8,128)(2,1)S(1)}, u32[]{:S(2)}, u32[]{:S(2)}) collective-permute-start(bf16[192,2048]{1,0:T(8,128)(2,1)} %bitcast.28), channel_id=1, source_target_pairs={{0,2},{2,6},{6,4},{4,0},{1,3},{3,7},{7,5},{5,1},{8,10},{10,14},{14... | collective-permute-start | bytes 2359304 | tf_op jit(solution)/shard_map/ppermute | solution.py:292
  57.4 19.4 %collective-permute-start.13 = (bf16[176,2048]{1,0:T(8,128)(2,1)}, bf16[176,2048]{1,0:T(8,128)(2,1)S(1)}, u32[]{:S(2)}, u32[]{:S(2)}) collective-permute-start(bf16[176,2048]{1,0:T(8,128)(2,1)} %copy-done), channel_id=1, source_target_pairs={{0,16},{8,24},{16,0},{24,8},{1,17},{9,25},{17,1},{25,9},{2,18},{10... | collective-permute-start | bytes 2162696 | tf_op jit(solution)/shard_map/ppermute | solution.py:42
  58.9 17.9 %collective-permute-start.12 = (bf16[160,2048]{1,0:T(8,128)(2,1)}, bf16[160,2048]{1,0:T(8,128)(2,1)S(1)}, u32[]{:S(2)}, u32[]{:S(2)}) collective-permute-start(bf16[160,2048]{1,0:T(8,128)(2,1)} %collective-permute-done.3.refs_0_), channel_id=1, source_target_pairs={{0,8},{8,0},{16,24},{24,16},{1,9},{9,1},{17,25},{25,17},{2,10},{10... | collective-permute-start | bytes 1966088 | tf_op jit(solution)/shard_map/ppermute | solution.py:42
  60.4 4.2 %copy-start.1 = (bf16[176,2048]{1,0:T(8,128)(2,1)S(1)}, bf16[176,2048]{1,0:T(8,128)(2,1)}, u32[]{:S(2)}) copy-start(bf16[176,2048]{1,0:T(8,128)(2,1)} %copy-done) | copy-start | bytes 2162692
  60.4 4.2 %copy-start.3 = (bf16[160,2048]{1,0:T(8,128)(2,1)S(1)}, bf16[160,2048]{1,0:T(8,128)(2,1)}, u32[]{:S(2)}) copy-start(bf16[160,2048]{1,0:T(8,128)(2,1)} %copy-done.2) | copy-start | bytes 1966084
  60.4 37.3 %collective-permute-start.18 = (bf16[256,2048]{1,0:T(8,128)(2,1)}, bf16[256,2048]{1,0:T(8,128)(2,1)S(1)}, u32[]{:S(2)}, u32[]{:S(2)}) collective-permute-start(bf16[256,2048]{1,0:T(8,128)(2,1)} %all-gather.3.cloned.1.call-done), channel_id=1, source_target_pairs={{0,8},{8,0},{16,24},{24,16},{1,9},{9,1},{17,25},{25,17},{2,10},{10... | collective-permute-start | bytes 3145736 | tf_op jit(solution)/shard_map/ppermute | solution.py:42
  60.9 1.1 copy-start.5
  62.0 1.9 %copy-start.6 = (bf16[256,2048]{1,0:T(8,128)(2,1)S(1)}, bf16[256,2048]{1,0:T(8,128)(2,1)}, u32[]{:S(2)}) copy-start(bf16[256,2048]{1,0:T(8,128)(2,1)} %all-gather.3.cloned.1.call-done) | copy-start | bytes 3145732
  63.9 2.4 %copy-start.7 = (bf16[3,64,2048]{2,1,0:T(8,128)(2,1)S(1)}, bf16[3,64,2048]{2,1,0:T(8,128)(2,1)}, u32[]{:S(2)}) copy-start(bf16[3,64,2048]{2,1,0:T(8,128)(2,1)} %param.7) | copy-start | bytes 2359300
  64.0 33.9 %collective-permute-start.19 = (bf16[256,2048]{1,0:T(8,128)(2,1)S(1)}, bf16[256,2048]{1,0:T(8,128)(2,1)S(1)}, u32[]{:S(2)}, u32[]{:S(2)}) collective-permute-start(bf16[256,2048]{1,0:T(8,128)(2,1)S(1)} %copy-done.6), channel_id=1, source_target_pairs={{0,16},{8,24},{16,0},{24,8},{1,17},{9,25},{17,1},{25,9},{2,18},{10... | collective-permute-start | bytes 3145736 | tf_op jit(solution)/shard_map/ppermute | solution.py:42
  76.8 5.8 %collective-permute-start.16 = (bf16[176,2048]{1,0:T(8,128)(2,1)S(1)}, bf16[176,2048]{1,0:T(8,128)(2,1)S(1)}, u32[]{:S(2)}, u32[]{:S(2)}) collective-permute-start(bf16[176,2048]{1,0:T(8,128)(2,1)S(1)} %collective-permute-done.13.refs_1_), channel_id=1, source_target_pairs={{0,1},{1,0},{2,3},{3,2},{4,5},{5,4},{6,7},{7,6},{8,9},{9,8},{10,11... | collective-permute-start | bytes 2162696 | tf_op jit(solution)/shard_map/ppermute | solution.py:37
  76.8 5.8 %collective-permute-start.15 = (bf16[160,2048]{1,0:T(8,128)(2,1)S(1)}, bf16[160,2048]{1,0:T(8,128)(2,1)S(1)}, u32[]{:S(2)}, u32[]{:S(2)}) collective-permute-start(bf16[160,2048]{1,0:T(8,128)(2,1)S(1)} %collective-permute-done.12.refs_0_), channel_id=1, source_target_pairs={{0,1},{1,0},{2,3},{3,2},{4,5},{5,4},{6,7},{7,6},{8,9},{9,8},{10,11... | collective-permute-start | bytes 1966088 | tf_op jit(solution)/shard_map/ppermute | solution.py:37
  77.3 20.6 %collective-permute-start.17 = (bf16[192,2048]{1,0:T(8,128)(2,1)S(1)}, bf16[192,2048]{1,0:T(8,128)(2,1)S(1)}, u32[]{:S(2)}, u32[]{:S(2)}) collective-permute-start(bf16[192,2048]{1,0:T(8,128)(2,1)S(1)} %collective-permute-done.14.rest_0_.rest_1_), channel_id=1, source_target_pairs={{0,2},{2,6},{6,4},{4,0},{1,3},{3,7},{7,5},{5,1},{8,10},{10,14},{14... | collective-permute-start | bytes 2359304 | tf_op jit(solution)/shard_map/ppermute | solution.py:292
  97.9 19.4 %collective-permute-start.27 = (bf16[192,2048]{1,0:T(8,128)(2,1)S(1)}, bf16[192,2048]{1,0:T(8,128)(2,1)S(1)}, u32[]{:S(2)}, u32[]{:S(2)}) collective-permute-start(bf16[192,2048]{1,0:T(8,128)(2,1)S(1)} %collective-permute-done.17.rest_0_), channel_id=1, source_target_pairs={{0,2},{2,6},{6,4},{4,0},{1,3},{3,7},{7,5},{5,1},{8,10},{10,14},{14... | collective-permute-start | bytes 2359304 | tf_op jit(solution)/shard_map/ppermute | solution.py:292
  98.9 5.0 %collective-permute-start.22 = (bf16[64,512]{1,0:T(8,128)(2,1)S(1)}, bf16[64,512]{1,0:T(8,128)(2,1)S(1)}, u32[]{:S(2)}, u32[]{:S(2)}) collective-permute-start(bf16[64,512]{1,0:T(8,128)(2,1)S(1)} %get-tuple-element.94), channel_id=1, source_target_pairs={{0,8},{8,0},{16,24},{24,16},{1,9},{9,1},{17,25},{25,17},{2,10},{10... | collective-permute-start | bytes 196616 | tf_op jit(solution)/shard_map/ppermute | solution.py:42
  100.3 6.1 %collective-permute-start.24 = (bf16[64,512]{1,0:T(8,128)(2,1)S(1)}, bf16[64,512]{1,0:T(8,128)(2,1)S(1)}, u32[]{:S(2)}, u32[]{:S(2)}) collective-permute-start(bf16[64,512]{1,0:T(8,128)(2,1)S(1)} %get-tuple-element.96), channel_id=1, source_target_pairs={{0,16},{8,24},{16,0},{24,8},{1,17},{9,25},{17,1},{25,9},{2,18},{10... | collective-permute-start | bytes 196616 | tf_op jit(solution)/shard_map/ppermute | solution.py:42
  101.8 5.0 %collective-permute-start.23 = (bf16[64,512]{1,0:T(8,128)(2,1)S(1)}, bf16[64,512]{1,0:T(8,128)(2,1)S(1)}, u32[]{:S(2)}, u32[]{:S(2)}) collective-permute-start(bf16[64,512]{1,0:T(8,128)(2,1)S(1)} %get-tuple-element.95), channel_id=1, source_target_pairs={{0,8},{8,0},{16,24},{24,16},{1,9},{9,1},{17,25},{25,17},{2,10},{10... | collective-permute-start | bytes 196616 | tf_op jit(solution)/shard_map/ppermute | solution.py:42
  102.4 11.5 %collective-permute-start.26 = (bf16[128,512]{1,0:T(8,128)(2,1)S(1)}, bf16[128,512]{1,0:T(8,128)(2,1)S(1)}, u32[]{:S(2)}, u32[]{:S(2)}) collective-permute-start(bf16[128,512]{1,0:T(8,128)(2,1)S(1)} %shard_map.70), channel_id=1, source_target_pairs={{0,24},{8,16},{16,8},{24,0},{1,25},{9,17},{17,9},{25,1},{2,26},{10... | collective-permute-start | bytes 393224 | tf_op jit(solution)/shard_map/ppermute | solution.py:42
  103.9 9.9 %collective-permute-start.25 = (bf16[64,512]{1,0:T(8,128)(2,1)S(1)}, bf16[64,512]{1,0:T(8,128)(2,1)S(1)}, u32[]{:S(2)}, u32[]{:S(2)}) collective-permute-start(bf16[64,512]{1,0:T(8,128)(2,1)S(1)} %get-tuple-element.97), channel_id=1, source_target_pairs={{0,16},{8,24},{16,0},{24,8},{1,17},{9,25},{17,1},{25,9},{2,18},{10... | collective-permute-start | bytes 196616 | tf_op jit(solution)/shard_map/ppermute | solution.py:42
  106.5 19.7 %collective-permute-start.20 = (bf16[128,2048]{1,0:T(8,128)(2,1)S(1)}, bf16[128,2048]{1,0:T(8,128)(2,1)S(1)}, u32[]{:S(2)}, u32[]{:S(2)}) collective-permute-start(bf16[128,2048]{1,0:T(8,128)(2,1)S(1)} %slice.34), channel_id=1, source_target_pairs={{0,8},{8,0},{16,24},{24,16},{1,9},{9,1},{17,25},{25,17},{2,10},{10... | collective-permute-start | bytes 1572872 | tf_op jit(solution)/shard_map/ppermute | solution.py:42
  106.8 20.9 %collective-permute-start.21 = (bf16[128,2048]{1,0:T(8,128)(2,1)S(1)}, bf16[128,2048]{1,0:T(8,128)(2,1)S(1)}, u32[]{:S(2)}, u32[]{:S(2)}) collective-permute-start(bf16[128,2048]{1,0:T(8,128)(2,1)S(1)} %slice.35), channel_id=1, source_target_pairs={{0,16},{8,24},{16,0},{24,8},{1,17},{9,25},{17,1},{25,9},{2,18},{10... | collective-permute-start | bytes 1572872 | tf_op jit(solution)/shard_map/ppermute | solution.py:42
  122.6 6.3 %collective-permute-start.29 = (bf16[64,512]{1,0:T(8,128)(2,1)S(1)}, bf16[64,512]{1,0:T(8,128)(2,1)S(1)}, u32[]{:S(2)}, u32[]{:S(2)}) collective-permute-start(bf16[64,512]{1,0:T(8,128)(2,1)S(1)} %get-tuple-element.105), channel_id=1, source_target_pairs={{0,8},{8,0},{16,24},{24,16},{1,9},{9,1},{17,25},{25,17},{2,10},{10... | collective-permute-start | bytes 196616 | tf_op jit(solution)/shard_map/ppermute | solution.py:42
  124.2 5.5 %collective-permute-start.31 = (bf16[64,512]{1,0:T(8,128)(2,1)S(1)}, bf16[64,512]{1,0:T(8,128)(2,1)S(1)}, u32[]{:S(2)}, u32[]{:S(2)}) collective-permute-start(bf16[64,512]{1,0:T(8,128)(2,1)S(1)} %get-tuple-element.109), channel_id=1, source_target_pairs={{0,16},{8,24},{16,0},{24,8},{1,17},{9,25},{17,1},{25,9},{2,18},{10... | collective-permute-start | bytes 196616 | tf_op jit(solution)/shard_map/ppermute | solution.py:42
  125.4 5.2 %collective-permute-start.33 = (bf16[64,512]{1,0:T(8,128)(2,1)S(1)}, bf16[64,512]{1,0:T(8,128)(2,1)S(1)}, u32[]{:S(2)}, u32[]{:S(2)}) collective-permute-start(bf16[64,512]{1,0:T(8,128)(2,1)S(1)} %get-tuple-element.112), channel_id=1, source_target_pairs={{0,24},{8,16},{16,8},{24,0},{1,25},{9,17},{17,9},{25,1},{2,26},{10... | collective-permute-start | bytes 196616 | tf_op jit(solution)/shard_map/ppermute | solution.py:42
  126.2 4.4 %collective-permute-start.28 = (bf16[64,512]{1,0:T(8,128)(2,1)S(1)}, bf16[64,512]{1,0:T(8,128)(2,1)S(1)}, u32[]{:S(2)}, u32[]{:S(2)}) collective-permute-start(bf16[64,512]{1,0:T(8,128)(2,1)S(1)} %get-tuple-element.104), channel_id=1, source_target_pairs={{0,8},{8,0},{16,24},{24,16},{1,9},{9,1},{17,25},{25,17},{2,10},{10... | collective-permute-start | bytes 196616 | tf_op jit(solution)/shard_map/ppermute | solution.py:42
  127.7 4.3 %collective-permute-start.30 = (bf16[64,512]{1,0:T(8,128)(2,1)S(1)}, bf16[64,512]{1,0:T(8,128)(2,1)S(1)}, u32[]{:S(2)}, u32[]{:S(2)}) collective-permute-start(bf16[64,512]{1,0:T(8,128)(2,1)S(1)} %get-tuple-element.108), channel_id=1, source_target_pairs={{0,16},{8,24},{16,0},{24,8},{1,17},{9,25},{17,1},{25,9},{2,18},{10... | collective-permute-start | bytes 196616 | tf_op jit(solution)/shard_map/ppermute | solution.py:42
  128.9 5.2 %collective-permute-start.32 = (bf16[64,512]{1,0:T(8,128)(2,1)S(1)}, bf16[64,512]{1,0:T(8,128)(2,1)S(1)}, u32[]{:S(2)}, u32[]{:S(2)}) collective-permute-start(bf16[64,512]{1,0:T(8,128)(2,1)S(1)} %get-tuple-element.111), channel_id=1, source_target_pairs={{0,24},{8,16},{16,8},{24,0},{1,25},{9,17},{17,9},{25,1},{2,26},{10... | collective-permute-start | bytes 196616 | tf_op jit(solution)/shard_map/ppermute | solution.py:42
  136.0 2.7 %collective-permute-start.34 = (bf16[256,2048]{1,0:T(8,128)(2,1)S(1)}, bf16[256,2048]{1,0:T(8,128)(2,1)S(1)}, u32[]{:S(2)}, u32[]{:S(2)}) collective-permute-start(bf16[256,2048]{1,0:T(8,128)(2,1)S(1)} %shard_map.74), channel_id=1, source_target_pairs={{0,1},{1,0},{2,3},{3,2},{4,5},{5,4},{6,7},{7,6},{8,9},{9,8},{10,11... | collective-permute-start | bytes 3145736 | tf_op jit(solution)/shard_map/ppermute | solution.py:37
Sparse Core Ops, SparseCore 0:
  27.2 28.2 all-gather.2

commit v6 on v5

--- a/solution.py
+++ b/solution.py
@@ -112,7 +112,7 @@
     for c, step in enumerate(steps):
         w[c, : 2 * WIDE] = weights[c][: 2 * WIDE]
         w[c, 2 * WIDE : 3 * WIDE] = jnp.zeros((WIDE, w.shape[2]), w.dtype)
-        w[c, 3 * WIDE :] = weights[c][2 * WIDE :]
+        w[c, 3 * WIDE :] = weights[c][2 * WIDE : 3 * WIDE]
         filters = long_ref[place_ref[2 + step]]
         for g in range(count):
             line = jnp.concatenate(
@@ -202,7 +202,7 @@
     )(place, taps, filters, *weights, *tokens)
 
 
-def out_kernel(mirror, order, chips, width, counts, place_ref, *refs):
+def out_kernel(mirror, order, width, counts, place_ref, *refs):
     weights, refs = refs[: counts[0]], refs[counts[0] :]
     parts, refs = refs[: counts[1]], refs[counts[1] :]
     out_ref, left, right, total = refs
@@ -215,8 +215,7 @@
         left[...] = parts[0][...]
     else:
         for n, (k, row) in enumerate(order):
-            at = pl.multiple_of((n // chips * chips + place_ref[2 + n % chips]) * width, width)
-            left[pl.ds(at, width)] = parts[k][row : row + width]
+            left[n * width : (n + 1) * width] = parts[k][row : row + width]
     at = 0
     for ref in weights:
         right[at : at + ref.shape[0]] = ref[...]
@@ -237,12 +236,12 @@
                 out_ref[:, here] = value.astype(out_ref.dtype)
 
 
-def project(mirror, order, chips, width, depth, place, v, parts, dtype):
+def project(mirror, order, width, depth, place, v, parts, dtype):
     span, features = parts[0].shape[1], v[0].shape[-1]
     rows = span // 2
     counts = (len(v), len(parts))
     return pl.pallas_call(
-        functools.partial(out_kernel, mirror, order, chips, width, counts),
+        functools.partial(out_kernel, mirror, order, width, counts),
         out_shape=jax.ShapeDtypeStruct((rows, features), dtype),
         in_specs=[SMEM] + [VMEM] * sum(counts),
         out_specs=VMEM,
@@ -306,50 +305,48 @@
     if slots == 4 and chips == 4 and width == WIDE:
         mid = HALO
         parts = [(0, 0), (0, mid), (1, 0), (1, mid)]
-        ws = [in_weight.reshape(3 * width, features)]
-        low = tokens[:mid]
+        spread = lambda one: [one] + [across(one, r) for r in range(1, slots)]
+        ws = [jnp.concatenate([in_weight.reshape(3 * width, features), out_weight])]
+        out_rows = lambda s: ws[s][3 * width :]
+        low, high = tokens[:mid], tokens[mid:]
         low_x, low_y = across(low, 1), across(low, 2)
-        edge, low, low_x, low_y, v, ws[0] = tie(edge, low, low_x, low_y, out_weight, ws[0])
-
-        v = lax.all_gather(v, "z")
-        high = jnp.concatenate([tokens[mid:], edge])
+        edge, low, high, low_x, low_y, ws = tie(edge, low, high, low_x, low_y, ws)
+
+        high = jnp.concatenate([high, edge])
         high_x, high_y = across(high, 1), across(high, 2)
+        ws = [ws[0], forward(ws[0])]
         x0 = lay(place, rows, parts, [low, high, swap(low), swap(high)])
         low_x_twin, low_y_twin = swap(low_x), swap(low_y)
-        (x0, high_x, high_y, low_x_twin, low_y_twin, ws, taps, filters, place, v) = tie(
-            x0, high_x, high_y, low_x_twin, low_y_twin, ws, taps, filters, place, v
+        (x0, high_x, high_y, low_x, low_y, low_x_twin, low_y_twin, ws, taps, filters, place) = tie(
+            x0, high_x, high_y, low_x, low_y, low_x_twin, low_y_twin, ws, taps, filters, place
         )
 
-        ws = list(ws) + [forward(ws[0])]
+        ws = [*ws, forward(ws[1])]
         far_x, far_y = across(low_y, 1), across(high_x, 2)
         x1 = lay(place, rows, parts, [low_x, high_x, low_x_twin, swap(high_x)])
         x2 = lay(place, rows, parts, [low_y, high_y, low_y_twin, swap(high_y)])
         mix0 = run_mix((0,), (x0, x1, x2))
-        v = v.reshape(chips * width, -1)
-        v_x, v_y = across(v, 1), across(v, 2)
-        mix0, far_x, far_y, ws = tie(mix0, far_x, far_y, ws)
-
-        ws = list(ws) + [forward(ws[1])]
+        wide0 = spread(out_rows(0))
+        mix0, far_x, far_y, ws, wide0 = tie(mix0, far_x, far_y, ws, wide0)
+
+        ws = [*ws, forward(ws[2])]
+        wide12 = spread(jnp.concatenate([out_rows(1), out_rows(2)]))
         x3 = lay(place, rows, parts, [far_x, far_y, swap(far_x), swap(far_y)])
-        mix1 = run_mix((1,), (x0, x1, x2))
-        far01 = run_mix((0, 1), (x3,))
-        mix1, far01, ws, v_x, v_y = tie(mix1, far01, ws, v_x, v_y)
-
-        ws = list(ws) + [forward(ws[2])]
-        cut = v.shape[0] // 2
-        v_far = (across(v_y[:cut], 1), across(v_x[cut:], 2))
-        moved = [[across(mix0[r], r), across(mix1[r], r)] for r in (1, 2)]
-        moved.append([across(far01[0], 3)])
-        mix2 = run_mix((2,), (x0, x1, x2, x3))
-        mix2, moved, ws = tie(mix2, moved, ws)
-
+        far = run_mix((0, 1, 2), (x3,))
+        mix12 = run_mix((1, 2), (x0, x1, x2))
+        moved = [[across(mix0[r], r), across(mix12[r], r)] for r in (1, 2)] + [[across(far[0], 3)]]
+        moved, ws, wide12 = tie(moved, ws, wide12)
+
+        wide3 = spread(out_rows(3))
         mix3 = run_mix((3,), (x0, x1, x2, x3))
-        v = [v, v_x, v_y, *v_far]
-        together = [mix0[0], mix1[0], mix2[0], mix3[0]]
+        v = [one for r in range(slots) for one in (wide0[r], wide12[r], wide3[r])]
+        together = [mix0[0], mix12[0], mix3[0]]
         for r in (1, 2, 3):
-            together += list(moved[r - 1]) + [across(mix2[r], r), across(mix3[r], r)]
-        order = [(4 * r + s, 0) for r in range(3) for s in range(chips)]
-        order += [(12, 0), (12, width), (13, 0), (14, 0)]
+            together += [*moved[r - 1], across(mix3[r], r)]
+        order = []
+        for r in range(3):
+            order += [(3 * r, 0), (3 * r + 1, 0), (3 * r + 1, width), (3 * r + 2, 0)]
+        order += [(9, 0), (9, width), (9, 2 * width), (10, 0)]
     else:
         v = lax.all_gather(out_weight, ("dp", "z"))
         block = jnp.concatenate([tokens, edge])
@@ -374,7 +371,7 @@
         order = None
     depth = slots * chips * width
     run = lambda mirror, dtype: project(
-        mirror, order, chips, width, depth, place, v, together, dtype
+        mirror, order, width, depth, place, v, together, dtype
     )
     theirs = swap(run(True, jnp.bfloat16))
     mine = run(False, jnp.float32)

time: 147 us -> 161 us (1.095)
  waiting for transfers between devices: 57.3 us -> 83 us
  between operations: 13.9 us -> 0.39 us
    ppermute x21 -> x23, waiting for transfers between devices: 45.5 us -> 78 us  [across(): return lax.ppermute(block, 'dp', [(i, i ^ r) for i in range(count)])]
    all_gather x1 -> x0, waiting for transfers between devices: 7.52 us -> none  [shards(): v = lax.all_gather(v, 'z')]
    unnamed x19 -> x10, local copies, waits for them, and re-layouts: 3.65 us -> 0.88 us
    ppermute x3, starting transfers between devices: 3.48 us -> 5.74 us  [shards(): forward = lambda block: lax.ppermute(block, 'z', ring)]
    ppermute x21 -> x23, starting transfers between devices: 26 us -> 25 us  [across(): return lax.ppermute(block, 'dp', [(i, i ^ r) for i in range(count)])]
    pallas_call x5 -> x4, Pallas kernels: 22.5 us -> 22.8 us  [mix_chunks(): pl.pallas_call(functools.partial(mix_kernel, steps, slots), out_shape=[ja...]
  transfers between devices with their start and end apart: 36 -> 37, of which waited for: 14 -> 15; matrix products, arithmetic and copies ran while one was open for 2% -> 3% of each run, Pallas kernels for 21% -> 20%
where the time goes in v6:
time: 161 us; the launch traced here: 160 us
  waiting for transfers between devices  83 us (52%)
  starting transfers between devices  34.2 us (21%)
  Pallas kernels  33.9 us (21%)
  local copies, waits for them, and re-layouts  7 us (4%)
  other arithmetic  1.68 us (1%)
    ppermute x23, waiting for transfers between devices, across(): return lax.ppermute(block, 'dp', [(i, i ^ r) for i in range(count)])  78 us
    ppermute x23, starting transfers between devices, across(): return lax.ppermute(block, 'dp', [(i, i ^ r) for i in range(count)])  25 us
    pallas_call x4, Pallas kernels, mix_chunks(): pl.pallas_call(functools.partial(mix_kernel, steps, slots), out_shape=[ja...  22.8 us
    pallas_call x4, Pallas kernels, lay(): pl.pallas_call(functools.partial(lay_kernel, parts), out_shape=jax.ShapeD...  7.34 us
    ppermute x3, starting transfers between devices, shards(): forward = lambda block: lax.ppermute(block, 'z', ring)  5.74 us
    ppermute x3, waiting for transfers between devices, shards(): forward = lambda block: lax.ppermute(block, 'z', ring)  3.9 us
    pallas_call x2, Pallas kernels, project(): pl.pallas_call(functools.partial(out_kernel, mirror, order, width, counts...  3.81 us
  transfers between devices with their start and end apart: 37, of which 15 were waited for; matrix products, arithmetic and copies ran while one was open for 3% of the time, Pallas kernels for 20%

profile of v6, /device:TPU:0, one launch (start us, length us, event | category | flops | bytes accessed | tf_op | source)
XLA Modules:
  0.0 160.2 jit_solution(676807438740693644)
XLA Ops:
  0.0 1.2 slice.35.refs_0_
  1.2 3.0 %collective-permute-start.2 = (bf16[160,2048]{1,0:T(8,128)(2,1)S(1)}, bf16[160,2048]{1,0:T(8,128)(2,1)S(1)}, u32[]{:S(2)}, u32[]{:S(2)}) collective-permute-start(bf16[160,2048]{1,0:T(8,128)(2,1)S(1)} %slice.35.refs_0_), channel_id=1, source_target_pairs={{0,8},{8,0},{16,24},{24,16},{1,9},{9,1},{17,25},{25,17},{2,10},{10... | collective-permute-start | bytes 1966088 | tf_op jit(solution)/shard_map/ppermute | solution.py:42
  4.2 1.5 collective-permute-start.3
  5.8 1.1 fusion.5
  6.9 0.8 collective-permute-start
  8.7 10.3 %collective-permute-done.2.refs_0_ = bf16[160,2048]{1,0:T(8,128)(2,1)S(1)} collective-permute-done((bf16[160,2048]{1,0:T(8,128)(2,1)S(1)}, bf16[160,2048]{1,0:T(8,128)(2,1)S(1)}, u32[]{:S(2)}, u32[]{:S(2)}) %collective-permute-start.2) | collective-permute-done | bytes 655392 | tf_op jit(solution)/shard_map/ppermute | solution.py:42
  19.0 0.8 copy-done
  21.2 1.6 collective-permute-start.10
  22.8 0.8 fusion
  23.5 1.2 reshape.10
  24.8 1.1 collective-permute-start.6
  25.9 1.5 collective-permute-start.7
  28.9 2.2 %shard_map.64.rest_1_.rest_2_ = bf16[672,2048]{1,0:T(8,128)(2,1)S(1)} custom-call(s32[6]{0:T(128)S(1)} %pad_add_fusion.place_ref, bf16[160,2048]{1,0:T(8,128)(2,1)S(1)} %slice.35.refs_0_, bf16[176,2048]{1,0:T(8,128)(2,1)S(1)} %constant_dynamic-update-slice_fusion.refs_1_, bf16[160,2048]{1,0:T(8,128)(2,1)} %collective-permute-done.4.refs_2_, ...), custom_call_target="tpu_custom_call" | custom-call | bytes 5505024 | tf_op jit(solution)/shard_map/pallas_call | solution.py:87
  31.4 11.3 %collective-permute-done.6.refs_1_ = bf16[176,2048]{1,0:T(8,128)(2,1)S(1)} collective-permute-done((bf16[176,2048]{1,0:T(8,128)(2,1)S(1)}, bf16[176,2048]{1,0:T(8,128)(2,1)S(1)}, u32[]{:S(2)}, u32[]{:S(2)}) %collective-permute-start.6) | collective-permute-done | bytes 720928 | tf_op jit(solution)/shard_map/ppermute | solution.py:42
  42.7 0.7 collective-permute-done.7.refs_1_
  43.4 3.9 %collective-permute-done.10.rest_0_.rest_1_ = bf16[256,2048]{1,0:T(8,128)(2,1)} collective-permute-done((bf16[256,2048]{1,0:T(8,128)(2,1)S(1)}, bf16[256,2048]{1,0:T(8,128)(2,1)}, u32[]{:S(2)}, u32[]{:S(2)}) %collective-permute-start.10) | collective-permute-done | bytes 1048608 | tf_op jit(solution)/shard_map/ppermute | solution.py:291
  48.2 1.5 collective-permute-start.14
  49.8 1.0 collective-permute-start.13
  50.8 1.1 collective-permute-start.16
  51.9 1.7 %shard_map.66.rest_3_.rest_4_ = bf16[672,2048]{1,0:T(8,128)(2,1)S(1)} custom-call(s32[6]{0:T(128)S(1)} %pad_add_fusion.place_ref, bf16[160,2048]{1,0:T(8,128)(2,1)} %collective-permute-done.3.refs_0_, bf16[176,2048]{1,0:T(8,128)(2,1)S(1)} %collective-permute-done.7.refs_1_, bf16[160,2048]{1,0:T(8,128)(2,1)S(1)} %collective-permute-done.9.refs_2_, ...), custom_call_target="tpu_custom_call" | custom-call | bytes 5505024 | tf_op jit(solution)/shard_map/pallas_call | solution.py:87
  54.2 1.6 %shard_map.65.rest_2_.rest_3_ = bf16[672,2048]{1,0:T(8,128)(2,1)S(1)} custom-call(s32[6]{0:T(128)S(1)} %pad_add_fusion.place_ref, bf16[160,2048]{1,0:T(8,128)(2,1)S(1)} %copy-done.1, bf16[176,2048]{1,0:T(8,128)(2,1)S(1)} %collective-permute-done.6.refs_1_, bf16[160,2048]{1,0:T(8,128)(2,1)S(1)} %collective-permute-done.8.refs_2_, ...), custom_call_target="tpu_custom_call" | custom-call | bytes 5505024 | tf_op jit(solution)/shard_map/pallas_call | solution.py:87
  55.8 16.4 %collective-permute-done.16.refs_3_ = bf16[64,2048]{1,0:T(8,128)(2,1)S(1)} collective-permute-done((bf16[64,2048]{1,0:T(8,128)(2,1)S(1)}, bf16[64,2048]{1,0:T(8,128)(2,1)S(1)}, u32[]{:S(2)}, u32[]{:S(2)}) %collective-permute-start.16) | collective-permute-done | bytes 262176 | tf_op jit(solution)/shard_map/ppermute | solution.py:42
  72.2 1.0 collective-permute-start.18
  73.2 4.3 %shard_map.67 = (bf16[64,512]{1,0:T(8,128)(2,1)S(1)}, bf16[64,512]{1,0:T(8,128)(2,1)S(1)}, bf16[64,512]{1,0:T(8,128)(2,1)S(1)}) custom-call(s32[6]{0:T(128)S(1)} %pad_add_fusion.place_ref, f32[4,8,256]{2,1,0:T(8,128)S(1)} %pad_maximum_fusion.2.taps_ref, f32[4,4,128]{2,1,0:T(4,128)S(1)} %maximum_convert_fusion.long_ref, ...), custom_call_target="tpu_custom_call" | custom-call | flops 3221225472 | bytes 6291456 | tf_op jit(solution)/shard_map/pallas_call | solution.py:183
  77.5 3.0 %collective-permute-done.18.refs_9_ = bf16[64,2048]{1,0:T(8,128)(2,1)S(1)} collective-permute-done((bf16[64,2048]{1,0:T(8,128)(2,1)S(1)}, bf16[64,2048]{1,0:T(8,128)(2,1)S(1)}, u32[]{:S(2)}, u32[]{:S(2)}) %collective-permute-start.18) | collective-permute-done | bytes 262176 | tf_op jit(solution)/shard_map/ppermute | solution.py:42
  80.5 1.1 collective-permute-start.19
  82.1 3.5 %collective-permute-start.26 = (bf16[256,2048]{1,0:T(8,128)(2,1)S(1)}, bf16[256,2048]{1,0:T(8,128)(2,1)S(1)}, u32[]{:S(2)}, u32[]{:S(2)}) collective-permute-start(bf16[256,2048]{1,0:T(8,128)(2,1)S(1)} %collective-permute-done.15.rest_1_.rest_2_), channel_id=1, source_target_pairs={{0,2},{2,6},{6,4},{4,0},{1,3},{3,7},{7,5},{5,1},{8,10},{10,14},{14... | collective-permute-start | bytes 3145736 | tf_op jit(solution)/shard_map/ppermute | solution.py:291
  85.6 8.3 %shard_map.68 = (bf16[128,512]{1,0:T(8,128)(2,1)S(1)}, bf16[128,512]{1,0:T(8,128)(2,1)S(1)}, bf16[128,512]{1,0:T(8,128)(2,1)S(1)}) custom-call(s32[6]{0:T(128)S(1)} %pad_add_fusion.place_ref, f32[4,8,256]{2,1,0:T(8,128)S(1)} %pad_maximum_fusion.2.taps_ref, f32[4,4,128]{2,1,0:T(4,128)S(1)} %maximum_convert_fusion.long_ref, ...), custom_call_target="tpu_custom_call" | custom-call | flops 6442450944 | bytes 12582912 | tf_op jit(solution)/shard_map/pallas_call | solution.py:183
  93.9 1.0 slice.41
  94.9 1.1 collective-permute-start.20
  96.5 3.7 %collective-permute-done.21.refs_18_ = bf16[64,512]{1,0:T(8,128)(2,1)S(1)} collective-permute-done((bf16[64,512]{1,0:T(8,128)(2,1)S(1)}, bf16[64,512]{1,0:T(8,128)(2,1)S(1)}, u32[]{:S(2)}, u32[]{:S(2)}) %collective-permute-start.21) | collective-permute-done | bytes 65568 | tf_op jit(solution)/shard_map/ppermute | solution.py:42
  100.2 1.0 collective-permute-start.27
  101.7 2.0 %collective-permute-start.29 = (bf16[128,2048]{1,0:T(8,128)(2,1)S(1)}, bf16[128,2048]{1,0:T(8,128)(2,1)S(1)}, u32[]{:S(2)}, u32[]{:S(2)}) collective-permute-start(bf16[128,2048]{1,0:T(8,128)(2,1)S(1)} %pad_maximum_fusion.1.refs_1_), channel_id=1, source_target_pairs={{0,24},{8,16},{16,8},{24,0},{1,25},{9,17},{17,9},{25,1},{2,26},{10... | collective-permute-start | bytes 1572872 | tf_op jit(solution)/shard_map/ppermute | solution.py:42
  103.7 1.8 %shard_map.69.rest_3_.rest_4_ = bf16[672,2048]{1,0:T(8,128)(2,1)S(1)} custom-call(s32[6]{0:T(128)S(1)} %pad_add_fusion.place_ref, bf16[160,2048]{1,0:T(8,128)(2,1)S(1)} %collective-permute-done.13.refs_0_, bf16[176,2048]{1,0:T(8,128)(2,1)S(1)} %collective-permute-done.14.refs_1_, bf16[160,2048]{1,0:T(8,128)(2,1)S(1)} %collective-permute-done.23.refs_2_, ...), custom_call_target="tpu_custom_call" | custom-call | bytes 5505024 | tf_op jit(solution)/shard_map/pallas_call | solution.py:87
  106.1 4.9 %shard_map.70 = bf16[192,512]{1,0:T(8,128)(2,1)S(1)} custom-call(s32[6]{0:T(128)S(1)} %pad_add_fusion.place_ref, f32[4,8,256]{2,1,0:T(8,128)S(1)} %pad_maximum_fusion.2.taps_ref, f32[4,4,128]{2,1,0:T(4,128)S(1)} %maximum_convert_fusion.long_ref, bf16[256,2048]{1,0:T(8,128)(2,1)S(1)} %pad_maximum_fusion.rest_0_, ...), custom_call_target="tpu_custom_call" | custom-call | flops 3221225472 | bytes 6291456 | tf_op jit(solution)/shard_map/pallas_call | solution.py:183
  111.0 16.4 %collective-permute-done.22.refs_19_ = bf16[128,512]{1,0:T(8,128)(2,1)S(1)} collective-permute-done((bf16[128,512]{1,0:T(8,128)(2,1)S(1)}, bf16[128,512]{1,0:T(8,128)(2,1)S(1)}, u32[]{:S(2)}, u32[]{:S(2)}) %collective-permute-start.22) | collective-permute-done | bytes 131104 | tf_op jit(solution)/shard_map/ppermute | solution.py:42
  127.4 1.0 collective-permute-start.25
  128.4 7.4 %collective-permute-done.25.refs_21_ = bf16[192,512]{1,0:T(8,128)(2,1)S(1)} collective-permute-done((bf16[192,512]{1,0:T(8,128)(2,1)S(1)}, bf16[192,512]{1,0:T(8,128)(2,1)S(1)}, u32[]{:S(2)}, u32[]{:S(2)}) %collective-permute-start.25) | collective-permute-done | bytes 196640 | tf_op jit(solution)/shard_map/ppermute | solution.py:42
  135.8 1.1 collective-permute-start.30
  136.9 2.5 %collective-permute-start.32 = (bf16[64,2048]{1,0:T(8,128)(2,1)S(1)}, bf16[64,2048]{1,0:T(8,128)(2,1)S(1)}, u32[]{:S(2)}, u32[]{:S(2)}) collective-permute-start(bf16[64,2048]{1,0:T(8,128)(2,1)S(1)} %slice.43.refs_2_), channel_id=1, source_target_pairs={{0,24},{8,16},{16,8},{24,0},{1,25},{9,17},{17,9},{25,1},{2,26},{10... | collective-permute-start | bytes 786440 | tf_op jit(solution)/shard_map/ppermute | solution.py:42
  139.4 5.3 %shard_map.71 = (bf16[64,512]{1,0:T(8,128)(2,1)S(1)}, bf16[64,512]{1,0:T(8,128)(2,1)S(1)}, bf16[64,512]{1,0:T(8,128)(2,1)S(1)}, bf16[64,512]{1,0:T(8,128)(2,1)S(1)}) custom-call(s32[6]{0:T(128)S(1)} %pad_add_fusion.place_ref, f32[4,8,256]{2,1,0:T(8,128)S(1)} %pad_maximum_fusion.2.taps_ref, f32[4,4,128]{2,1,0:T(4,128)S(1)} %maximum_convert_fusion.long_ref, ...), custom_call_target="tpu_custom_call" | custom-call | flops 4294967296 | bytes 8388608 | tf_op jit(solution)/shard_map/pallas_call | solution.py:183
  144.7 1.1 collective-permute-start.33
  145.8 3.3 %collective-permute-done.33.refs_17_ = bf16[64,512]{1,0:T(8,128)(2,1)S(1)} collective-permute-done((bf16[64,512]{1,0:T(8,128)(2,1)S(1)}, bf16[64,512]{1,0:T(8,128)(2,1)S(1)}, u32[]{:S(2)}, u32[]{:S(2)}) %collective-permute-start.33) | collective-permute-done | bytes 65568 | tf_op jit(solution)/shard_map/ppermute | solution.py:42
  150.0 4.2 %collective-permute-done.35.refs_22_ = bf16[64,512]{1,0:T(8,128)(2,1)S(1)} collective-permute-done((bf16[64,512]{1,0:T(8,128)(2,1)S(1)}, bf16[64,512]{1,0:T(8,128)(2,1)S(1)}, u32[]{:S(2)}, u32[]{:S(2)}) %collective-permute-start.35) | collective-permute-done | bytes 65568 | tf_op jit(solution)/shard_map/ppermute | solution.py:42
  154.2 1.9 %shard_map.73 = bf16[256,2048]{1,0:T(8,128)(2,1)S(1)} custom-call(s32[6]{0:T(128)S(1)} %pad_add_fusion.place_ref, bf16[64,2048]{1,0:T(8,128)(2,1)S(1)} %slice.40.refs_0_, bf16[128,2048]{1,0:T(8,128)(2,1)S(1)} %pad_maximum_fusion.1.refs_1_, bf16[64,2048]{1,0:T(8,128)(2,1)S(1)} %slice.43.refs_2_, bf16[64,2048]{1,0:T(8,128)(2,1)S(1)} %collective-permute-done.16.refs_3_, ...), custom_call_target="tpu_custom_call" | custom-call | flops 2147483648 | bytes 5242880 | tf_op jit(solution)/shard_map/pallas_call | solution.py:243
  156.2 1.9 %shard_map.72 = f32[256,2048]{1,0:T(8,128)S(1)} custom-call(s32[6]{0:T(128)S(1)} %pad_add_fusion.place_ref, bf16[64,2048]{1,0:T(8,128)(2,1)S(1)} %slice.40.refs_0_, bf16[128,2048]{1,0:T(8,128)(2,1)S(1)} %pad_maximum_fusion.1.refs_1_, bf16[64,2048]{1,0:T(8,128)(2,1)S(1)} %slice.43.refs_2_, bf16[64,2048]{1,0:T(8,128)(2,1)S(1)} %collective-permute-done.16.refs_3_, ...), custom_call_target="tpu_custom_call" | custom-call | flops 2147483648 | bytes 5242880 | tf_op jit(solution)/shard_map/pallas_call | solution.py:243
  158.1 0.7 collective-permute-done.36
  158.9 1.3 add_convert_fusion
  (70 shorter events, 8.9 us)
Async XLA Ops:
  0.0 8.4 %copy-start.3 = (bf16[64,2048]{1,0:T(8,128)(2,1)S(1)}, bf16[64,2048]{1,0:T(8,128)(2,1)}, u32[]{:S(2)}) copy-start(bf16[64,2048]{1,0:T(8,128)(2,1)} %param.10) | copy-start | bytes 786436
  0.0 8.4 %copy-start.2 = (bf16[3,64,2048]{2,1,0:T(8,128)(2,1)S(1)}, bf16[3,64,2048]{2,1,0:T(8,128)(2,1)}, u32[]{:S(2)}) copy-start(bf16[3,64,2048]{2,1,0:T(8,128)(2,1)} %param.7) | copy-start | bytes 2359300
  1.2 17.7 %collective-permute-start.2 = (bf16[160,2048]{1,0:T(8,128)(2,1)S(1)}, bf16[160,2048]{1,0:T(8,128)(2,1)S(1)}, u32[]{:S(2)}, u32[]{:S(2)}) collective-permute-start(bf16[160,2048]{1,0:T(8,128)(2,1)S(1)} %slice.35.refs_0_), channel_id=1, source_target_pairs={{0,8},{8,0},{16,24},{24,16},{1,9},{9,1},{17,25},{25,17},{2,10},{10... | collective-permute-start | bytes 1966088 | tf_op jit(solution)/shard_map/ppermute | solution.py:42
  4.2 16.3 %collective-permute-start.3 = (bf16[160,2048]{1,0:T(8,128)(2,1)S(1)}, bf16[160,2048]{1,0:T(8,128)(2,1)}, u32[]{:S(2)}, u32[]{:S(2)}) collective-permute-start(bf16[160,2048]{1,0:T(8,128)(2,1)S(1)} %slice.35.refs_0_), channel_id=1, source_target_pairs={{0,16},{8,24},{16,0},{24,8},{1,17},{9,25},{17,1},{25,9},{2,18},{10... | collective-permute-start | bytes 1966088 | tf_op jit(solution)/shard_map/ppermute | solution.py:42
  6.9 13.7 %slice-start = ((bf16[256,2048]{1,0:T(8,128)(2,1)}), bf16[96,2048]{1,0:T(8,128)(2,1)S(1)}, s32[]{:S(2)}) async-start(bf16[256,2048]{1,0:T(8,128)(2,1)} %param.6), calls=%async_computation | async-start | bytes 786432 | tf_op jit(solution)/shard_map/slice | solution.py:311
  6.9 1.6 %collective-permute-start = (bf16[80,2048]{1,0:T(8,128)(2,1)S(1)}, bf16[80,2048]{1,0:T(8,128)(2,1)S(1)}, u32[]{:S(2)}, u32[]{:S(2)}) collective-permute-start(bf16[80,2048]{1,0:T(8,128)(2,1)S(1)} %get-tuple-element.106), channel_id=1, source_target_pairs={{1,2},{3,4},{5,6},{9,10},{11,12},{13,14},{17,18},{19,20},{21,22},{... | collective-permute-start | bytes 983048 | tf_op jit(solution)/shard_map/ppermute | solution.py:300
  7.7 0.8 collective-permute-start.1
  19.0 0.8 copy-start
  20.6 7.6 %collective-permute-start.5 = (bf16[176,2048]{1,0:T(8,128)(2,1)S(1)}, bf16[176,2048]{1,0:T(8,128)(2,1)S(1)}, u32[]{:S(2)}, u32[]{:S(2)}) collective-permute-start(bf16[176,2048]{1,0:T(8,128)(2,1)S(1)} %constant_dynamic-update-slice_fusion.refs_1_), channel_id=1, source_target_pairs={{0,1},{1,0},{2,3},{3,2},{4,5},{5,4},{6,7},{7,6},{8,9},{9,8},{10,11... | collective-permute-start | bytes 2162696 | tf_op jit(solution)/shard_map/ppermute | solution.py:37
  20.7 7.4 %collective-permute-start.4 = (bf16[160,2048]{1,0:T(8,128)(2,1)S(1)}, bf16[160,2048]{1,0:T(8,128)(2,1)}, u32[]{:S(2)}, u32[]{:S(2)}) collective-permute-start(bf16[160,2048]{1,0:T(8,128)(2,1)S(1)} %slice.35.refs_0_), channel_id=1, source_target_pairs={{0,1},{1,0},{2,3},{3,2},{4,5},{5,4},{6,7},{7,6},{8,9},{9,8},{10,11... | collective-permute-start | bytes 1966088 | tf_op jit(solution)/shard_map/ppermute | solution.py:37
  21.2 26.1 %collective-permute-start.10 = (bf16[256,2048]{1,0:T(8,128)(2,1)S(1)}, bf16[256,2048]{1,0:T(8,128)(2,1)}, u32[]{:S(2)}, u32[]{:S(2)}) collective-permute-start(bf16[256,2048]{1,0:T(8,128)(2,1)S(1)} %pad_maximum_fusion.rest_0_), channel_id=1, source_target_pairs={{0,2},{2,6},{6,4},{4,0},{1,3},{3,7},{7,5},{5,1},{8,10},{10,14},{14... | collective-permute-start | bytes 3145736 | tf_op jit(solution)/shard_map/ppermute | solution.py:291
  24.8 17.9 %collective-permute-start.6 = (bf16[176,2048]{1,0:T(8,128)(2,1)S(1)}, bf16[176,2048]{1,0:T(8,128)(2,1)S(1)}, u32[]{:S(2)}, u32[]{:S(2)}) collective-permute-start(bf16[176,2048]{1,0:T(8,128)(2,1)S(1)} %constant_dynamic-update-slice_fusion.refs_1_), channel_id=1, source_target_pairs={{0,8},{8,0},{16,24},{24,16},{1,9},{9,1},{17,25},{25,17},{2,10},{10... | collective-permute-start | bytes 2162696 | tf_op jit(solution)/shard_map/ppermute | solution.py:42
  25.9 17.6 %collective-permute-start.7 = (bf16[176,2048]{1,0:T(8,128)(2,1)S(1)}, bf16[176,2048]{1,0:T(8,128)(2,1)S(1)}, u32[]{:S(2)}, u32[]{:S(2)}) collective-permute-start(bf16[176,2048]{1,0:T(8,128)(2,1)S(1)} %constant_dynamic-update-slice_fusion.refs_1_), channel_id=1, source_target_pairs={{0,16},{8,24},{16,0},{24,8},{1,17},{9,25},{17,1},{25,9},{2,18},{10... | collective-permute-start | bytes 2162696 | tf_op jit(solution)/shard_map/ppermute | solution.py:42
  28.1 3.0 %collective-permute-start.8 = (bf16[160,2048]{1,0:T(8,128)(2,1)}, bf16[160,2048]{1,0:T(8,128)(2,1)S(1)}, u32[]{:S(2)}, u32[]{:S(2)}) collective-permute-start(bf16[160,2048]{1,0:T(8,128)(2,1)} %copy-done), channel_id=1, source_target_pairs={{0,1},{1,0},{2,3},{3,2},{4,5},{5,4},{6,7},{7,6},{8,9},{9,8},{10,11... | collective-permute-start | bytes 1966088 | tf_op jit(solution)/shard_map/ppermute | solution.py:37
  28.2 3.2 %collective-permute-start.9 = (bf16[160,2048]{1,0:T(8,128)(2,1)}, bf16[160,2048]{1,0:T(8,128)(2,1)S(1)}, u32[]{:S(2)}, u32[]{:S(2)}) collective-permute-start(bf16[160,2048]{1,0:T(8,128)(2,1)} %collective-permute-done.3.refs_0_), channel_id=1, source_target_pairs={{0,1},{1,0},{2,3},{3,2},{4,5},{5,4},{6,7},{7,6},{8,9},{9,8},{10,11... | collective-permute-start | bytes 1966088 | tf_op jit(solution)/shard_map/ppermute | solution.py:37
  47.3 3.5 %collective-permute-start.12 = (bf16[176,2048]{1,0:T(8,128)(2,1)S(1)}, bf16[176,2048]{1,0:T(8,128)(2,1)S(1)}, u32[]{:S(2)}, u32[]{:S(2)}) collective-permute-start(bf16[176,2048]{1,0:T(8,128)(2,1)S(1)} %collective-permute-done.7.refs_1_), channel_id=1, source_target_pairs={{0,1},{1,0},{2,3},{3,2},{4,5},{5,4},{6,7},{7,6},{8,9},{9,8},{10,11... | collective-permute-start | bytes 2162696 | tf_op jit(solution)/shard_map/ppermute | solution.py:37
  47.3 33.2 %collective-permute-start.15 = (bf16[256,2048]{1,0:T(8,128)(2,1)}, bf16[256,2048]{1,0:T(8,128)(2,1)S(1)}, u32[]{:S(2)}, u32[]{:S(2)}) collective-permute-start(bf16[256,2048]{1,0:T(8,128)(2,1)} %collective-permute-done.10.rest_0_.rest_1_), channel_id=1, source_target_pairs={{0,2},{2,6},{6,4},{4,0},{1,3},{3,7},{7,5},{5,1},{8,10},{10,14},{14... | collective-permute-start | bytes 3145736 | tf_op jit(solution)/shard_map/ppermute | solution.py:291
  48.0 5.6 %collective-permute-start.11 = (bf16[176,2048]{1,0:T(8,128)(2,1)S(1)}, bf16[176,2048]{1,0:T(8,128)(2,1)S(1)}, u32[]{:S(2)}, u32[]{:S(2)}) collective-permute-start(bf16[176,2048]{1,0:T(8,128)(2,1)S(1)} %collective-permute-done.6.refs_1_), channel_id=1, source_target_pairs={{0,1},{1,0},{2,3},{3,2},{4,5},{5,4},{6,7},{7,6},{8,9},{9,8},{10,11... | collective-permute-start | bytes 2162696 | tf_op jit(solution)/shard_map/ppermute | solution.py:37
  48.2 32.3 %collective-permute-start.14 = (bf16[176,2048]{1,0:T(8,128)(2,1)S(1)}, bf16[176,2048]{1,0:T(8,128)(2,1)S(1)}, u32[]{:S(2)}, u32[]{:S(2)}) collective-permute-start(bf16[176,2048]{1,0:T(8,128)(2,1)S(1)} %collective-permute-done.6.refs_1_), channel_id=1, source_target_pairs={{0,16},{8,24},{16,0},{24,8},{1,17},{9,25},{17,1},{25,9},{2,18},{10... | collective-permute-start | bytes 2162696 | tf_op jit(solution)/shard_map/ppermute | solution.py:42
  49.8 30.7 %collective-permute-start.13 = (bf16[160,2048]{1,0:T(8,128)(2,1)}, bf16[160,2048]{1,0:T(8,128)(2,1)S(1)}, u32[]{:S(2)}, u32[]{:S(2)}) collective-permute-start(bf16[160,2048]{1,0:T(8,128)(2,1)} %collective-permute-done.3.refs_0_), channel_id=1, source_target_pairs={{0,8},{8,0},{16,24},{24,16},{1,9},{9,1},{17,25},{25,17},{2,10},{10... | collective-permute-start | bytes 1966088 | tf_op jit(solution)/shard_map/ppermute | solution.py:42
  50.8 3.4 %copy-start.1 = (bf16[160,2048]{1,0:T(8,128)(2,1)S(1)}, bf16[160,2048]{1,0:T(8,128)(2,1)}, u32[]{:S(2)}) copy-start(bf16[160,2048]{1,0:T(8,128)(2,1)} %copy-done) | copy-start | bytes 1966084
  50.8 21.4 %collective-permute-start.16 = (bf16[64,2048]{1,0:T(8,128)(2,1)S(1)}, bf16[64,2048]{1,0:T(8,128)(2,1)S(1)}, u32[]{:S(2)}, u32[]{:S(2)}) collective-permute-start(bf16[64,2048]{1,0:T(8,128)(2,1)S(1)} %slice.40.refs_0_), channel_id=1, source_target_pairs={{0,8},{8,0},{16,24},{24,16},{1,9},{9,1},{17,25},{25,17},{2,10},{10... | collective-permute-start | bytes 786440 | tf_op jit(solution)/shard_map/ppermute | solution.py:42
  53.6 23.8 %collective-permute-start.17 = (bf16[64,2048]{1,0:T(8,128)(2,1)S(1)}, bf16[64,2048]{1,0:T(8,128)(2,1)S(1)}, u32[]{:S(2)}, u32[]{:S(2)}) collective-permute-start(bf16[64,2048]{1,0:T(8,128)(2,1)S(1)} %slice.40.refs_0_), channel_id=1, source_target_pairs={{0,16},{8,24},{16,0},{24,8},{1,17},{9,25},{17,1},{25,9},{2,18},{10... | collective-permute-start | bytes 786440 | tf_op jit(solution)/shard_map/ppermute | solution.py:42
  72.2 8.3 %collective-permute-start.18 = (bf16[64,2048]{1,0:T(8,128)(2,1)S(1)}, bf16[64,2048]{1,0:T(8,128)(2,1)S(1)}, u32[]{:S(2)}, u32[]{:S(2)}) collective-permute-start(bf16[64,2048]{1,0:T(8,128)(2,1)S(1)} %slice.40.refs_0_), channel_id=1, source_target_pairs={{0,24},{8,16},{16,8},{24,0},{1,25},{9,17},{17,9},{25,1},{2,26},{10... | collective-permute-start | bytes 786440 | tf_op jit(solution)/shard_map/ppermute | solution.py:42
  80.5 15.4 %collective-permute-start.19 = (bf16[64,512]{1,0:T(8,128)(2,1)S(1)}, bf16[64,512]{1,0:T(8,128)(2,1)S(1)}, u32[]{:S(2)}, u32[]{:S(2)}) collective-permute-start(bf16[64,512]{1,0:T(8,128)(2,1)S(1)} %get-tuple-element.77), channel_id=1, source_target_pairs={{0,8},{8,0},{16,24},{24,16},{1,9},{9,1},{17,25},{25,17},{2,10},{10... | collective-permute-start | bytes 196616 | tf_op jit(solution)/shard_map/ppermute | solution.py:42
  81.6 19.6 %collective-permute-start.23 = (bf16[160,2048]{1,0:T(8,128)(2,1)S(1)}, bf16[160,2048]{1,0:T(8,128)(2,1)S(1)}, u32[]{:S(2)}, u32[]{:S(2)}) collective-permute-start(bf16[160,2048]{1,0:T(8,128)(2,1)S(1)} %collective-permute-done.13.refs_0_), channel_id=1, source_target_pairs={{0,1},{1,0},{2,3},{3,2},{4,5},{5,4},{6,7},{7,6},{8,9},{9,8},{10,11... | collective-permute-start | bytes 1966088 | tf_op jit(solution)/shard_map/ppermute | solution.py:37
  81.6 20.1 %collective-permute-start.24 = (bf16[176,2048]{1,0:T(8,128)(2,1)S(1)}, bf16[176,2048]{1,0:T(8,128)(2,1)S(1)}, u32[]{:S(2)}, u32[]{:S(2)}) collective-permute-start(bf16[176,2048]{1,0:T(8,128)(2,1)S(1)} %collective-permute-done.14.refs_1_), channel_id=1, source_target_pairs={{0,1},{1,0},{2,3},{3,2},{4,5},{5,4},{6,7},{7,6},{8,9},{9,8},{10,11... | collective-permute-start | bytes 2162696 | tf_op jit(solution)/shard_map/ppermute | solution.py:37
  82.1 53.7 %collective-permute-start.26 = (bf16[256,2048]{1,0:T(8,128)(2,1)S(1)}, bf16[256,2048]{1,0:T(8,128)(2,1)S(1)}, u32[]{:S(2)}, u32[]{:S(2)}) collective-permute-start(bf16[256,2048]{1,0:T(8,128)(2,1)S(1)} %collective-permute-done.15.rest_1_.rest_2_), channel_id=1, source_target_pairs={{0,2},{2,6},{6,4},{4,0},{1,3},{3,7},{7,5},{5,1},{8,10},{10,14},{14... | collective-permute-start | bytes 3145736 | tf_op jit(solution)/shard_map/ppermute | solution.py:291
  94.9 10.6 %collective-permute-start.20 = (bf16[128,512]{1,0:T(8,128)(2,1)S(1)}, bf16[128,512]{1,0:T(8,128)(2,1)S(1)}, u32[]{:S(2)}, u32[]{:S(2)}) collective-permute-start(bf16[128,512]{1,0:T(8,128)(2,1)S(1)} %get-tuple-element.80), channel_id=1, source_target_pairs={{0,8},{8,0},{16,24},{24,16},{1,9},{9,1},{17,25},{25,17},{2,10},{10... | collective-permute-start | bytes 393224 | tf_op jit(solution)/shard_map/ppermute | solution.py:42
  95.9 4.3 %collective-permute-start.21 = (bf16[64,512]{1,0:T(8,128)(2,1)S(1)}, bf16[64,512]{1,0:T(8,128)(2,1)S(1)}, u32[]{:S(2)}, u32[]{:S(2)}) collective-permute-start(bf16[64,512]{1,0:T(8,128)(2,1)S(1)} %get-tuple-element.81), channel_id=1, source_target_pairs={{0,16},{8,24},{16,0},{24,8},{1,17},{9,25},{17,1},{25,9},{2,18},{10... | collective-permute-start | bytes 196616 | tf_op jit(solution)/shard_map/ppermute | solution.py:42
  100.2 28.2 %collective-permute-start.27 = (bf16[128,2048]{1,0:T(8,128)(2,1)S(1)}, bf16[128,2048]{1,0:T(8,128)(2,1)S(1)}, u32[]{:S(2)}, u32[]{:S(2)}) collective-permute-start(bf16[128,2048]{1,0:T(8,128)(2,1)S(1)} %pad_maximum_fusion.1.refs_1_), channel_id=1, source_target_pairs={{0,8},{8,0},{16,24},{24,16},{1,9},{9,1},{17,25},{25,17},{2,10},{10... | collective-permute-start | bytes 1572872 | tf_op jit(solution)/shard_map/ppermute | solution.py:42
  101.2 27.1 %collective-permute-start.28 = (bf16[128,2048]{1,0:T(8,128)(2,1)S(1)}, bf16[128,2048]{1,0:T(8,128)(2,1)S(1)}, u32[]{:S(2)}, u32[]{:S(2)}) collective-permute-start(bf16[128,2048]{1,0:T(8,128)(2,1)S(1)} %pad_maximum_fusion.1.refs_1_), channel_id=1, source_target_pairs={{0,16},{8,24},{16,0},{24,8},{1,17},{9,25},{17,1},{25,9},{2,18},{10... | collective-permute-start | bytes 1572872 | tf_op jit(solution)/shard_map/ppermute | solution.py:42
  101.7 26.6 %collective-permute-start.29 = (bf16[128,2048]{1,0:T(8,128)(2,1)S(1)}, bf16[128,2048]{1,0:T(8,128)(2,1)S(1)}, u32[]{:S(2)}, u32[]{:S(2)}) collective-permute-start(bf16[128,2048]{1,0:T(8,128)(2,1)S(1)} %pad_maximum_fusion.1.refs_1_), channel_id=1, source_target_pairs={{0,24},{8,16},{16,8},{24,0},{1,25},{9,17},{17,9},{25,1},{2,26},{10... | collective-permute-start | bytes 1572872 | tf_op jit(solution)/shard_map/ppermute | solution.py:42
  105.5 21.9 %collective-permute-start.22 = (bf16[128,512]{1,0:T(8,128)(2,1)S(1)}, bf16[128,512]{1,0:T(8,128)(2,1)S(1)}, u32[]{:S(2)}, u32[]{:S(2)}) collective-permute-start(bf16[128,512]{1,0:T(8,128)(2,1)S(1)} %get-tuple-element.82), channel_id=1, source_target_pairs={{0,16},{8,24},{16,0},{24,8},{1,17},{9,25},{17,1},{25,9},{2,18},{10... | collective-permute-start | bytes 393224 | tf_op jit(solution)/shard_map/ppermute | solution.py:42
  127.4 8.4 %collective-permute-start.25 = (bf16[192,512]{1,0:T(8,128)(2,1)S(1)}, bf16[192,512]{1,0:T(8,128)(2,1)S(1)}, u32[]{:S(2)}, u32[]{:S(2)}) collective-permute-start(bf16[192,512]{1,0:T(8,128)(2,1)S(1)} %shard_map.70), channel_id=1, source_target_pairs={{0,24},{8,16},{16,8},{24,0},{1,25},{9,17},{17,9},{25,1},{2,26},{10... | collective-permute-start | bytes 589832 | tf_op jit(solution)/shard_map/ppermute | solution.py:42
  135.8 18.4 %collective-permute-start.30 = (bf16[64,2048]{1,0:T(8,128)(2,1)S(1)}, bf16[64,2048]{1,0:T(8,128)(2,1)S(1)}, u32[]{:S(2)}, u32[]{:S(2)}) collective-permute-start(bf16[64,2048]{1,0:T(8,128)(2,1)S(1)} %slice.43.refs_2_), channel_id=1, source_target_pairs={{0,8},{8,0},{16,24},{24,16},{1,9},{9,1},{17,25},{25,17},{2,10},{10... | collective-permute-start | bytes 786440 | tf_op jit(solution)/shard_map/ppermute | solution.py:42
  136.9 17.4 %collective-permute-start.31 = (bf16[64,2048]{1,0:T(8,128)(2,1)S(1)}, bf16[64,2048]{1,0:T(8,128)(2,1)S(1)}, u32[]{:S(2)}, u32[]{:S(2)}) collective-permute-start(bf16[64,2048]{1,0:T(8,128)(2,1)S(1)} %slice.43.refs_2_), channel_id=1, source_target_pairs={{0,16},{8,24},{16,0},{24,8},{1,17},{9,25},{17,1},{25,9},{2,18},{10... | collective-permute-start | bytes 786440 | tf_op jit(solution)/shard_map/ppermute | solution.py:42
  136.9 17.4 %collective-permute-start.32 = (bf16[64,2048]{1,0:T(8,128)(2,1)S(1)}, bf16[64,2048]{1,0:T(8,128)(2,1)S(1)}, u32[]{:S(2)}, u32[]{:S(2)}) collective-permute-start(bf16[64,2048]{1,0:T(8,128)(2,1)S(1)} %slice.43.refs_2_), channel_id=1, source_target_pairs={{0,24},{8,16},{16,8},{24,0},{1,25},{9,17},{17,9},{25,1},{2,26},{10... | collective-permute-start | bytes 786440 | tf_op jit(solution)/shard_map/ppermute | solution.py:42
  144.7 4.3 %collective-permute-start.33 = (bf16[64,512]{1,0:T(8,128)(2,1)S(1)}, bf16[64,512]{1,0:T(8,128)(2,1)S(1)}, u32[]{:S(2)}, u32[]{:S(2)}) collective-permute-start(bf16[64,512]{1,0:T(8,128)(2,1)S(1)} %get-tuple-element.99), channel_id=1, source_target_pairs={{0,8},{8,0},{16,24},{24,16},{1,9},{9,1},{17,25},{25,17},{2,10},{10... | collective-permute-start | bytes 196616 | tf_op jit(solution)/shard_map/ppermute | solution.py:42
  145.8 4.3 %collective-permute-start.34 = (bf16[64,512]{1,0:T(8,128)(2,1)S(1)}, bf16[64,512]{1,0:T(8,128)(2,1)S(1)}, u32[]{:S(2)}, u32[]{:S(2)}) collective-permute-start(bf16[64,512]{1,0:T(8,128)(2,1)S(1)} %get-tuple-element.102), channel_id=1, source_target_pairs={{0,16},{8,24},{16,0},{24,8},{1,17},{9,25},{17,1},{25,9},{2,18},{10... | collective-permute-start | bytes 196616 | tf_op jit(solution)/shard_map/ppermute | solution.py:42
  149.0 5.2 %collective-permute-start.35 = (bf16[64,512]{1,0:T(8,128)(2,1)S(1)}, bf16[64,512]{1,0:T(8,128)(2,1)S(1)}, u32[]{:S(2)}, u32[]{:S(2)}) collective-permute-start(bf16[64,512]{1,0:T(8,128)(2,1)S(1)} %get-tuple-element.104), channel_id=1, source_target_pairs={{0,24},{8,16},{16,8},{24,0},{1,25},{9,17},{17,9},{25,1},{2,26},{10... | collective-permute-start | bytes 196616 | tf_op jit(solution)/shard_map/ppermute | solution.py:42
  156.1 2.7 %collective-permute-start.36 = (bf16[256,2048]{1,0:T(8,128)(2,1)S(1)}, bf16[256,2048]{1,0:T(8,128)(2,1)S(1)}, u32[]{:S(2)}, u32[]{:S(2)}) collective-permute-start(bf16[256,2048]{1,0:T(8,128)(2,1)S(1)} %shard_map.73), channel_id=1, source_target_pairs={{0,1},{1,0},{2,3},{3,2},{4,5},{5,4},{6,7},{7,6},{8,9},{9,8},{10,11... | collective-permute-start | bytes 3145736 | tf_op jit(solution)/shard_map/ppermute | solution.py:37

commit v7 on v6

--- a/solution.py
+++ b/solution.py
@@ -305,47 +305,49 @@
     if slots == 4 and chips == 4 and width == WIDE:
         mid = HALO
         parts = [(0, 0), (0, mid), (1, 0), (1, mid)]
-        spread = lambda one: [one] + [across(one, r) for r in range(1, slots)]
-        ws = [jnp.concatenate([in_weight.reshape(3 * width, features), out_weight])]
-        out_rows = lambda s: ws[s][3 * width :]
+        ws, vs = [in_weight.reshape(3 * width, features)], [out_weight, forward(out_weight)]
         low, high = tokens[:mid], tokens[mid:]
         low_x, low_y = across(low, 1), across(low, 2)
-        edge, low, high, low_x, low_y, ws = tie(edge, low, high, low_x, low_y, ws)
+        edge, low, high, low_x, low_y, ws, vs = tie(edge, low, high, low_x, low_y, ws, vs)
 
         high = jnp.concatenate([high, edge])
         high_x, high_y = across(high, 1), across(high, 2)
-        ws = [ws[0], forward(ws[0])]
+        ws, vs = [ws[0], forward(ws[0])], [*vs, forward(vs[1])]
         x0 = lay(place, rows, parts, [low, high, swap(low), swap(high)])
         low_x_twin, low_y_twin = swap(low_x), swap(low_y)
-        (x0, high_x, high_y, low_x, low_y, low_x_twin, low_y_twin, ws, taps, filters, place) = tie(
-            x0, high_x, high_y, low_x, low_y, low_x_twin, low_y_twin, ws, taps, filters, place
+        both = lambda one: [one, across(one, 1), across(one, 2)]
+        (x0, high_x, high_y, low_x, low_y, low_x_twin, low_y_twin, ws, vs, taps, filters, place) = tie(
+            x0, high_x, high_y, low_x, low_y, low_x_twin, low_y_twin, ws, vs, taps, filters, place
         )
 
-        ws = [*ws, forward(ws[1])]
+        ws, vs = [*ws, forward(ws[1])], [*vs, forward(vs[2])]
         far_x, far_y = across(low_y, 1), across(high_x, 2)
+        v1 = both(jnp.concatenate([vs[0], vs[1]]))
         x1 = lay(place, rows, parts, [low_x, high_x, low_x_twin, swap(high_x)])
         x2 = lay(place, rows, parts, [low_y, high_y, low_y_twin, swap(high_y)])
-        mix0 = run_mix((0,), (x0, x1, x2))
-        wide0 = spread(out_rows(0))
-        mix0, far_x, far_y, ws, wide0 = tie(mix0, far_x, far_y, ws, wide0)
+        mix01 = run_mix((0, 1), (x0, x1, x2))
+        mix01, far_x, far_y, ws, vs, v1 = tie(mix01, far_x, far_y, ws, vs, v1)
 
         ws = [*ws, forward(ws[2])]
-        wide12 = spread(jnp.concatenate([out_rows(1), out_rows(2)]))
+        v0, v1 = across(v1[2][:width], 1), [*v1, across(v1[1][width:], 2)]
+        v2, v3 = both(vs[2]), both(vs[3])
+        moved = [[across(mix01[r], r)] for r in (1, 2)]
         x3 = lay(place, rows, parts, [far_x, far_y, swap(far_x), swap(far_y)])
+        mix2 = run_mix((2,), (x0, x1, x2))
         far = run_mix((0, 1, 2), (x3,))
-        mix12 = run_mix((1, 2), (x0, x1, x2))
-        moved = [[across(mix0[r], r), across(mix12[r], r)] for r in (1, 2)] + [[across(far[0], 3)]]
-        moved, ws, wide12 = tie(moved, ws, wide12)
-
-        wide3 = spread(out_rows(3))
+        mix2, far, moved, ws, v0, v1, v2, v3 = tie(mix2, far, moved, ws, v0, v1, v2, v3)
+
+        v2, v3 = [*v2, across(v2[2], 1)], [*v3, across(v3[1], 2)]
         mix3 = run_mix((3,), (x0, x1, x2, x3))
-        v = [one for r in range(slots) for one in (wide0[r], wide12[r], wide3[r])]
-        together = [mix0[0], mix12[0], mix3[0]]
-        for r in (1, 2, 3):
-            together += [*moved[r - 1], across(mix3[r], r)]
+        v = [one[r] for r in range(slots) for one in (v1, v2, v3)]
+        v.insert(9, v0)
+        together = [mix01[0], mix2[0], mix3[0]]
+        for r in (1, 2):
+            together += [*moved[r - 1], across(mix2[r], r), across(mix3[r], r)]
+        together += [across(far[0], 3), across(mix3[3], 3)]
         order = []
         for r in range(3):
-            order += [(3 * r, 0), (3 * r + 1, 0), (3 * r + 1, width), (3 * r + 2, 0)]
+            order += [(3 * r, 0), (3 * r, width), (3 * r + 1, 0), (3 * r + 2, 0)]
         order += [(9, 0), (9, width), (9, 2 * width), (10, 0)]
     else:
         v = lax.all_gather(out_weight, ("dp", "z"))

time: 161 us -> 142 us (0.88)
  waiting for transfers between devices: 83 us -> 55.2 us
  starting transfers between devices: 34.2 us -> 44.7 us
    ppermute x23 -> x24, waiting for transfers between devices: 78 us -> 38.8 us  [across(): return lax.ppermute(block, 'dp', [(i, i ^ r) for i in range(count)])]
    ppermute x3 -> x6, waiting for transfers between devices: 3.9 us -> 16 us  [shards(): forward = lambda block: lax.ppermute(block, 'z', ring)]
    ppermute x3 -> x6, starting transfers between devices: 5.74 us -> 10.9 us  [shards(): forward = lambda block: lax.ppermute(block, 'z', ring)]
    ppermute x9, starting transfers between devices: 1.94 us -> 5.64 us  [swap(): return lax.ppermute(block, 'core', [(0, 1), (1, 0)])]
    ppermute x23 -> x24, starting transfers between devices: 25 us -> 26.8 us  [across(): return lax.ppermute(block, 'dp', [(i, i ^ r) for i in range(count)])]
  transfers between devices with their start and end apart: 37 -> 41, of which waited for: 15 -> 21; matrix products, arithmetic and copies ran while one was open for 3% -> 4% of each run, Pallas kernels for 20% -> 22%
where the time goes in v7:
time: 142 us
  waiting for transfers between devices  55.2 us (39%)
  starting transfers between devices  44.7 us (31%)
  Pallas kernels  33.3 us (23%)
  local copies, waits for them, and re-layouts  6.79 us (5%)
  other arithmetic  1.51 us (1%)
    ppermute x24, waiting for transfers between devices, across(): return lax.ppermute(block, 'dp', [(i, i ^ r) for i in range(count)])  38.8 us
    ppermute x24, starting transfers between devices, across(): return lax.ppermute(block, 'dp', [(i, i ^ r) for i in range(count)])  26.8 us
    pallas_call x4, Pallas kernels, mix_chunks(): pl.pallas_call(functools.partial(mix_kernel, steps, slots), out_shape=[ja...  21.6 us
    ppermute x6, waiting for transfers between devices, shards(): forward = lambda block: lax.ppermute(block, 'z', ring)  16 us
    ppermute x6, starting transfers between devices, shards(): forward = lambda block: lax.ppermute(block, 'z', ring)  10.9 us
    pallas_call x4, Pallas kernels, lay(): pl.pallas_call(functools.partial(lay_kernel, parts), out_shape=jax.ShapeD...  7.07 us
    ppermute x9, starting transfers between devices, swap(): return lax.ppermute(block, 'core', [(0, 1), (1, 0)])  5.64 us
    pallas_call x2, Pallas kernels, project(): pl.pallas_call(functools.partial(out_kernel, mirror, order, width, counts...  4.66 us
  transfers between devices with their start and end apart: 41, of which 21 were waited for; matrix products, arithmetic and copies ran while one was open for 4% of the time, Pallas kernels for 22%

profile of v7, /device:TPU:0, one launch (start us, length us, event | category | flops | bytes accessed | tf_op | source)
XLA Modules:
  0.0 141.9 jit_solution(14757741763530141309)
XLA Ops:
  0.0 1.2 slice.29.refs_0_
  1.2 3.0 %collective-permute-start.2 = (bf16[160,2048]{1,0:T(8,128)(2,1)S(1)}, bf16[160,2048]{1,0:T(8,128)(2,1)S(1)}, u32[]{:S(2)}, u32[]{:S(2)}) collective-permute-start(bf16[160,2048]{1,0:T(8,128)(2,1)S(1)} %slice.29.refs_0_), channel_id=1, source_target_pairs={{0,8},{8,0},{16,24},{24,16},{1,9},{9,1},{17,25},{25,17},{2,10},{10... | collective-permute-start | bytes 1966088 | tf_op jit(solution)/shard_map/ppermute | solution.py:42
  4.2 1.5 %collective-permute-start.3 = (bf16[160,2048]{1,0:T(8,128)(2,1)S(1)}, bf16[160,2048]{1,0:T(8,128)(2,1)S(1)}, u32[]{:S(2)}, u32[]{:S(2)}) collective-permute-start(bf16[160,2048]{1,0:T(8,128)(2,1)S(1)} %slice.29.refs_0_), channel_id=1, source_target_pairs={{0,16},{8,24},{16,0},{24,8},{1,17},{9,25},{17,1},{25,9},{2,18},{10... | collective-permute-start | bytes 1966088 | tf_op jit(solution)/shard_map/ppermute | solution.py:42
  5.7 1.1 fusion.5
  8.2 2.2 %collective-permute-start.4 = (bf16[64,2048]{1,0:T(8,128)(2,1)}, bf16[64,2048]{1,0:T(8,128)(2,1)S(1)}, u32[]{:S(2)}, u32[]{:S(2)}) collective-permute-start(bf16[64,2048]{1,0:T(8,128)(2,1)} %param.10), channel_id=1, source_target_pairs={{0,2},{2,6},{6,4},{4,0},{1,3},{3,7},{7,5},{5,1},{8,10},{10,14},{14... | collective-permute-start | bytes 786440 | tf_op jit(solution)/shard_map/ppermute | solution.py:291
  10.6 6.9 %collective-permute-done.4 = bf16[64,2048]{1,0:T(8,128)(2,1)S(1)} collective-permute-done((bf16[64,2048]{1,0:T(8,128)(2,1)}, bf16[64,2048]{1,0:T(8,128)(2,1)S(1)}, u32[]{:S(2)}, u32[]{:S(2)}) %collective-permute-start.4) | collective-permute-done | bytes 262176 | tf_op jit(solution)/shard_map/ppermute | solution.py:291
  17.5 1.5 %collective-permute-done.2.refs_0_ = bf16[160,2048]{1,0:T(8,128)(2,1)S(1)} collective-permute-done((bf16[160,2048]{1,0:T(8,128)(2,1)S(1)}, bf16[160,2048]{1,0:T(8,128)(2,1)S(1)}, u32[]{:S(2)}, u32[]{:S(2)}) %collective-permute-start.2) | collective-permute-done | bytes 655392 | tf_op jit(solution)/shard_map/ppermute | solution.py:42
  18.9 1.5 %collective-permute-done.3.refs_0_ = bf16[160,2048]{1,0:T(8,128)(2,1)S(1)} collective-permute-done((bf16[160,2048]{1,0:T(8,128)(2,1)S(1)}, bf16[160,2048]{1,0:T(8,128)(2,1)S(1)}, u32[]{:S(2)}, u32[]{:S(2)}) %collective-permute-start.3) | collective-permute-done | bytes 655392 | tf_op jit(solution)/shard_map/ppermute | solution.py:42
  20.5 3.9 %collective-permute-start.6 = (bf16[176,2048]{1,0:T(8,128)(2,1)S(1)}, bf16[176,2048]{1,0:T(8,128)(2,1)S(1)}, u32[]{:S(2)}, u32[]{:S(2)}) collective-permute-start(bf16[176,2048]{1,0:T(8,128)(2,1)S(1)} %constant_dynamic-update-slice_fusion.refs_1_), channel_id=1, source_target_pairs={{0,1},{1,0},{2,3},{3,2},{4,5},{5,4},{6,7},{7,6},{8,9},{9,8},{10,11... | collective-permute-start | bytes 2162696 | tf_op jit(solution)/shard_map/ppermute | solution.py:37
  24.4 2.1 %collective-permute-start.12 = (bf16[64,2048]{1,0:T(8,128)(2,1)}, bf16[64,2048]{1,0:T(8,128)(2,1)}, u32[]{:S(2)}, u32[]{:S(2)}) collective-permute-start(bf16[64,2048]{1,0:T(8,128)(2,1)} %copy-done.2), channel_id=1, source_target_pairs={{0,2},{2,6},{6,4},{4,0},{1,3},{3,7},{7,5},{5,1},{8,10},{10,14},{14... | collective-permute-start | bytes 786440 | tf_op jit(solution)/shard_map/ppermute | solution.py:291
  27.3 1.9 %reshape.10 = f32[7,3,16,2,64]{4,3,2,0,1:T(2,128)} reshape(f32[7,3,2048]{2,0,1:T(8,128)} %param.8) | data formatting | bytes 344064 | tf_op jit(solution)/shard_map/reshape | solution.py:263
  29.2 0.9 constant_dynamic-slice_fusion.4
  31.2 3.1 %collective-permute-done.12.refs_1_ = bf16[64,2048]{1,0:T(8,128)(2,1)} collective-permute-done((bf16[64,2048]{1,0:T(8,128)(2,1)}, bf16[64,2048]{1,0:T(8,128)(2,1)}, u32[]{:S(2)}, u32[]{:S(2)}) %collective-permute-start.12) | collective-permute-done | bytes 262176 | tf_op jit(solution)/shard_map/ppermute | solution.py:291
  34.3 1.4 collective-permute-start.11
  37.2 2.2 %shard_map.64.rest_2_.rest_1_ = bf16[672,2048]{1,0:T(8,128)(2,1)S(1)} custom-call(s32[6]{0:T(128)S(1)} %pad_add_fusion.place_ref, bf16[160,2048]{1,0:T(8,128)(2,1)S(1)} %slice.29.refs_0_, bf16[176,2048]{1,0:T(8,128)(2,1)S(1)} %constant_dynamic-update-slice_fusion.refs_1_, bf16[160,2048]{1,0:T(8,128)(2,1)} %collective-permute-done.5.refs_2_, ...), custom_call_target="tpu_custom_call" | custom-call | bytes 5505024 | tf_op jit(solution)/shard_map/pallas_call | solution.py:87
  39.6 8.9 %collective-permute-done.7.refs_1_ = bf16[176,2048]{1,0:T(8,128)(2,1)S(1)} collective-permute-done((bf16[176,2048]{1,0:T(8,128)(2,1)S(1)}, bf16[176,2048]{1,0:T(8,128)(2,1)S(1)}, u32[]{:S(2)}, u32[]{:S(2)}) %collective-permute-start.7) | collective-permute-done | bytes 720928 | tf_op jit(solution)/shard_map/ppermute | solution.py:42
  48.7 5.9 %collective-permute-done.11.rest_1_ = bf16[192,2048]{1,0:T(8,128)(2,1)S(1)} collective-permute-done((bf16[192,2048]{1,0:T(8,128)(2,1)}, bf16[192,2048]{1,0:T(8,128)(2,1)S(1)}, u32[]{:S(2)}, u32[]{:S(2)}) %collective-permute-start.11) | collective-permute-done | bytes 786464 | tf_op jit(solution)/shard_map/ppermute | solution.py:291
  55.6 1.5 %collective-permute-start.18 = (bf16[64,2048]{1,0:T(8,128)(2,1)}, bf16[64,2048]{1,0:T(8,128)(2,1)S(1)}, u32[]{:S(2)}, u32[]{:S(2)}) collective-permute-start(bf16[64,2048]{1,0:T(8,128)(2,1)} %collective-permute-done.12.refs_1_), channel_id=1, source_target_pairs={{0,2},{2,6},{6,4},{4,0},{1,3},{3,7},{7,5},{5,1},{8,10},{10,14},{14... | collective-permute-start | bytes 786440 | tf_op jit(solution)/shard_map/ppermute | solution.py:291
  57.2 3.3 %collective-permute-start.17 = (bf16[192,2048]{1,0:T(8,128)(2,1)S(1)}, bf16[192,2048]{1,0:T(8,128)(2,1)S(1)}, u32[]{:S(2)}, u32[]{:S(2)}) collective-permute-start(bf16[192,2048]{1,0:T(8,128)(2,1)S(1)} %collective-permute-done.11.rest_1_), channel_id=1, source_target_pairs={{0,2},{2,6},{6,4},{4,0},{1,3},{3,7},{7,5},{5,1},{8,10},{10,14},{14... | collective-permute-start | bytes 2359304 | tf_op jit(solution)/shard_map/ppermute | solution.py:291
  61.0 1.6 %shard_map.66.rest_4_.rest_3_ = bf16[672,2048]{1,0:T(8,128)(2,1)S(1)} custom-call(s32[6]{0:T(128)S(1)} %pad_add_fusion.place_ref, bf16[160,2048]{1,0:T(8,128)(2,1)S(1)} %collective-permute-done.3.refs_0_, bf16[176,2048]{1,0:T(8,128)(2,1)S(1)} %collective-permute-done.8.refs_1_, bf16[160,2048]{1,0:T(8,128)(2,1)S(1)} %collective-permute-done.10.refs_2_, ...), custom_call_target="tpu_custom_call" | custom-call | bytes 5505024 | tf_op jit(solution)/shard_map/pallas_call | solution.py:87
  62.7 1.6 %collective-permute-start.19 = (bf16[128,2048]{1,0:T(8,128)(2,1)S(1)}, bf16[128,2048]{1,0:T(8,128)(2,1)S(1)}, u32[]{:S(2)}, u32[]{:S(2)}) collective-permute-start(bf16[128,2048]{1,0:T(8,128)(2,1)S(1)} %constant_dynamic-update-slice_fusion.2.refs_0_), channel_id=1, source_target_pairs={{0,8},{8,0},{16,24},{24,16},{1,9},{9,1},{17,25},{25,17},{2,10},{10... | collective-permute-start | bytes 1572872 | tf_op jit(solution)/shard_map/ppermute | solution.py:42
  64.3 1.6 %shard_map.65.rest_3_.rest_2_ = bf16[672,2048]{1,0:T(8,128)(2,1)S(1)} custom-call(s32[6]{0:T(128)S(1)} %pad_add_fusion.place_ref, bf16[160,2048]{1,0:T(8,128)(2,1)S(1)} %collective-permute-done.2.refs_0_, bf16[176,2048]{1,0:T(8,128)(2,1)S(1)} %collective-permute-done.7.refs_1_, bf16[160,2048]{1,0:T(8,128)(2,1)S(1)} %collective-permute-done.9.refs_2_, ...), custom_call_target="tpu_custom_call" | custom-call | bytes 5505024 | tf_op jit(solution)/shard_map/pallas_call | solution.py:87
  66.0 1.5 %collective-permute-start.20 = (bf16[128,2048]{1,0:T(8,128)(2,1)S(1)}, bf16[128,2048]{1,0:T(8,128)(2,1)S(1)}, u32[]{:S(2)}, u32[]{:S(2)}) collective-permute-start(bf16[128,2048]{1,0:T(8,128)(2,1)S(1)} %constant_dynamic-update-slice_fusion.2.refs_0_), channel_id=1, source_target_pairs={{0,16},{8,24},{16,0},{24,8},{1,17},{9,25},{17,1},{25,9},{2,18},{10... | collective-permute-start | bytes 1572872 | tf_op jit(solution)/shard_map/ppermute | solution.py:42
  67.5 7.6 %shard_map.67 = (bf16[128,512]{1,0:T(8,128)(2,1)S(1)}, bf16[128,512]{1,0:T(8,128)(2,1)S(1)}, bf16[128,512]{1,0:T(8,128)(2,1)S(1)}) custom-call(s32[6]{0:T(128)S(1)} %pad_add_fusion.place_ref, f32[4,8,256]{2,1,0:T(8,128)S(1)} %pad_maximum_fusion.taps_ref, f32[4,4,128]{2,1,0:T(4,128)S(1)} %maximum_convert_fusion.long_ref, bf16[192,2048]{1,0:T(8,128)(2,1)S(1)} %bitcast.27, ...), custom_call_target="tpu_custom_call" | custom-call | flops 6442450944 | bytes 12582912 | tf_op jit(solution)/shard_map/pallas_call | solution.py:183
  75.1 12.4 %collective-permute-done.19.refs_3_ = bf16[128,2048]{1,0:T(8,128)(2,1)S(1)} collective-permute-done((bf16[128,2048]{1,0:T(8,128)(2,1)S(1)}, bf16[128,2048]{1,0:T(8,128)(2,1)S(1)}, u32[]{:S(2)}, u32[]{:S(2)}) %collective-permute-start.19) | collective-permute-done | bytes 524320 | tf_op jit(solution)/shard_map/ppermute | solution.py:42
  89.1 1.6 %collective-permute-start.27 = (bf16[64,2048]{1,0:T(8,128)(2,1)S(1)}, bf16[64,2048]{1,0:T(8,128)(2,1)S(1)}, u32[]{:S(2)}, u32[]{:S(2)}) collective-permute-start(bf16[64,2048]{1,0:T(8,128)(2,1)S(1)} %slice.35), channel_id=1, source_target_pairs={{0,16},{8,24},{16,0},{24,8},{1,17},{9,25},{17,1},{25,9},{2,18},{10... | collective-permute-start | bytes 786440 | tf_op jit(solution)/shard_map/ppermute | solution.py:42
  90.7 1.5 %collective-permute-start.23 = (bf16[128,512]{1,0:T(8,128)(2,1)S(1)}, bf16[128,512]{1,0:T(8,128)(2,1)S(1)}, u32[]{:S(2)}, u32[]{:S(2)}) collective-permute-start(bf16[128,512]{1,0:T(8,128)(2,1)S(1)} %get-tuple-element.103), channel_id=1, source_target_pairs={{0,8},{8,0},{16,24},{24,16},{1,9},{9,1},{17,25},{25,17},{2,10},{10... | collective-permute-start | bytes 393224 | tf_op jit(solution)/shard_map/ppermute | solution.py:42
  92.8 4.3 %shard_map.68 = (bf16[64,512]{1,0:T(8,128)(2,1)S(1)}, bf16[64,512]{1,0:T(8,128)(2,1)S(1)}, bf16[64,512]{1,0:T(8,128)(2,1)S(1)}) custom-call(s32[6]{0:T(128)S(1)} %pad_add_fusion.place_ref, f32[4,8,256]{2,1,0:T(8,128)S(1)} %pad_maximum_fusion.taps_ref, f32[4,4,128]{2,1,0:T(4,128)S(1)} %maximum_convert_fusion.long_ref, ...), custom_call_target="tpu_custom_call" | custom-call | flops 3221225472 | bytes 6291456 | tf_op jit(solution)/shard_map/pallas_call | solution.py:183
  97.1 1.6 %shard_map.69.rest_3_.rest_4_ = bf16[672,2048]{1,0:T(8,128)(2,1)S(1)} custom-call(s32[6]{0:T(128)S(1)} %pad_add_fusion.place_ref, bf16[160,2048]{1,0:T(8,128)(2,1)S(1)} %collective-permute-done.15.refs_0_, bf16[176,2048]{1,0:T(8,128)(2,1)S(1)} %collective-permute-done.16.refs_1_, bf16[160,2048]{1,0:T(8,128)(2,1)S(1)} %collective-permute-done.21.refs_2_, ...), custom_call_target="tpu_custom_call" | custom-call | bytes 5505024 | tf_op jit(solution)/shard_map/pallas_call | solution.py:87
  100.3 1.1 collective-permute-start.29
  101.5 1.5 %collective-permute-start.30 = (bf16[64,2048]{1,0:T(8,128)(2,1)S(1)}, bf16[64,2048]{1,0:T(8,128)(2,1)S(1)}, u32[]{:S(2)}, u32[]{:S(2)}) collective-permute-start(bf16[64,2048]{1,0:T(8,128)(2,1)S(1)} %collective-permute-done.18.refs_2_), channel_id=1, source_target_pairs={{0,8},{8,0},{16,24},{24,16},{1,9},{9,1},{17,25},{25,17},{2,10},{10... | collective-permute-start | bytes 786440 | tf_op jit(solution)/shard_map/ppermute | solution.py:42
  103.5 4.3 %shard_map.70 = bf16[192,512]{1,0:T(8,128)(2,1)S(1)} custom-call(s32[6]{0:T(128)S(1)} %pad_add_fusion.place_ref, f32[4,8,256]{2,1,0:T(8,128)S(1)} %pad_maximum_fusion.taps_ref, f32[4,4,128]{2,1,0:T(4,128)S(1)} %maximum_convert_fusion.long_ref, bf16[192,2048]{1,0:T(8,128)(2,1)S(1)} %bitcast.28, bf16[192,2048]{1,0:T(8,128)(2,1)S(1)} %collective-permute-done.11.rest_1_, ...), custom_call_target="tpu_custom_call" | custom-call | flops 3221225472 | bytes 6291456 | tf_op jit(solution)/shard_map/pallas_call | solution.py:183
  107.7 1.1 collective-permute-done.28.refs_4_
  109.8 2.7 %collective-permute-done.30.refs_5_ = bf16[64,2048]{1,0:T(8,128)(2,1)S(1)} collective-permute-done((bf16[64,2048]{1,0:T(8,128)(2,1)S(1)}, bf16[64,2048]{1,0:T(8,128)(2,1)S(1)}, u32[]{:S(2)}, u32[]{:S(2)}) %collective-permute-start.30) | collective-permute-done | bytes 262176 | tf_op jit(solution)/shard_map/ppermute | solution.py:42
  112.5 1.2 collective-permute-done.31.refs_8_
  114.2 1.4 %collective-permute-start.33 = (bf16[64,2048]{1,0:T(8,128)(2,1)S(1)}, bf16[64,2048]{1,0:T(8,128)(2,1)S(1)}, u32[]{:S(2)}, u32[]{:S(2)}) collective-permute-start(bf16[64,2048]{1,0:T(8,128)(2,1)S(1)} %collective-permute-done.30.refs_5_), channel_id=1, source_target_pairs={{0,16},{8,24},{16,0},{24,8},{1,17},{9,25},{17,1},{25,9},{2,18},{10... | collective-permute-start | bytes 786440 | tf_op jit(solution)/shard_map/ppermute | solution.py:42
  115.6 5.4 %shard_map.71 = (bf16[64,512]{1,0:T(8,128)(2,1)S(1)}, bf16[64,512]{1,0:T(8,128)(2,1)S(1)}, bf16[64,512]{1,0:T(8,128)(2,1)S(1)}, bf16[64,512]{1,0:T(8,128)(2,1)S(1)}) custom-call(s32[6]{0:T(128)S(1)} %pad_add_fusion.place_ref, f32[4,8,256]{2,1,0:T(8,128)S(1)} %pad_maximum_fusion.taps_ref, f32[4,4,128]{2,1,0:T(4,128)S(1)} %maximum_convert_fusion.long_ref, ...), custom_call_target="tpu_custom_call" | custom-call | flops 4294967296 | bytes 8388608 | tf_op jit(solution)/shard_map/pallas_call | solution.py:183
  121.6 1.5 %collective-permute-start.38 = (bf16[192,512]{1,0:T(8,128)(2,1)S(1)}, bf16[192,512]{1,0:T(8,128)(2,1)S(1)}, u32[]{:S(2)}, u32[]{:S(2)}) collective-permute-start(bf16[192,512]{1,0:T(8,128)(2,1)S(1)} %shard_map.70), channel_id=1, source_target_pairs={{0,24},{8,16},{16,8},{24,0},{1,25},{9,17},{17,9},{25,1},{2,26},{10... | collective-permute-start | bytes 589832 | tf_op jit(solution)/shard_map/ppermute | solution.py:42
  123.1 1.4 collective-permute-start.37
  124.6 1.5 %collective-permute-done.35.refs_18_ = bf16[64,512]{1,0:T(8,128)(2,1)S(1)} collective-permute-done((bf16[64,512]{1,0:T(8,128)(2,1)S(1)}, bf16[64,512]{1,0:T(8,128)(2,1)S(1)}, u32[]{:S(2)}, u32[]{:S(2)}) %collective-permute-start.35) | collective-permute-done | bytes 65568 | tf_op jit(solution)/shard_map/ppermute | solution.py:42
  126.1 1.1 collective-permute-start.39
  127.2 1.7 %collective-permute-done.37.refs_21_ = bf16[64,512]{1,0:T(8,128)(2,1)S(1)} collective-permute-done((bf16[64,512]{1,0:T(8,128)(2,1)S(1)}, bf16[64,512]{1,0:T(8,128)(2,1)S(1)}, u32[]{:S(2)}, u32[]{:S(2)}) %collective-permute-start.37) | collective-permute-done | bytes 65568 | tf_op jit(solution)/shard_map/ppermute | solution.py:42
  128.9 1.7 %collective-permute-start.34 = (bf16[64,512]{1,0:T(8,128)(2,1)S(1)}, bf16[64,512]{1,0:T(8,128)(2,1)S(1)}, u32[]{:S(2)}, u32[]{:S(2)}) collective-permute-start(bf16[64,512]{1,0:T(8,128)(2,1)S(1)} %get-tuple-element.126), channel_id=1, source_target_pairs={{0,8},{8,0},{16,24},{24,16},{1,9},{9,1},{17,25},{25,17},{2,10},{10... | collective-permute-start | bytes 196616 | tf_op jit(solution)/shard_map/ppermute | solution.py:42
  131.7 1.4 %collective-permute-done.34.refs_17_ = bf16[64,512]{1,0:T(8,128)(2,1)S(1)} collective-permute-done((bf16[64,512]{1,0:T(8,128)(2,1)S(1)}, bf16[64,512]{1,0:T(8,128)(2,1)S(1)}, u32[]{:S(2)}, u32[]{:S(2)}) %collective-permute-start.34) | collective-permute-done | bytes 65568 | tf_op jit(solution)/shard_map/ppermute | solution.py:42
  133.2 2.4 %collective-permute-done.36.refs_20_ = bf16[64,512]{1,0:T(8,128)(2,1)S(1)} collective-permute-done((bf16[64,512]{1,0:T(8,128)(2,1)S(1)}, bf16[64,512]{1,0:T(8,128)(2,1)S(1)}, u32[]{:S(2)}, u32[]{:S(2)}) %collective-permute-start.36) | collective-permute-done | bytes 65568 | tf_op jit(solution)/shard_map/ppermute | solution.py:42
  135.5 2.3 %shard_map.73 = bf16[256,2048]{1,0:T(8,128)(2,1)S(1)} custom-call(s32[6]{0:T(128)S(1)} %pad_add_fusion.place_ref, bf16[128,2048]{1,0:T(8,128)(2,1)S(1)} %constant_dynamic-update-slice_fusion.2.refs_0_, bf16[64,2048]{1,0:T(8,128)(2,1)} %collective-permute-done.12.refs_1_, bf16[64,2048]{1,0:T(8,128)(2,1)S(1)} %collective-permute-done.18.refs_2_, ...), custom_call_target="tpu_custom_call" | custom-call | flops 2147483648 | bytes 5242880 | tf_op jit(solution)/shard_map/pallas_call | solution.py:243
  138.0 2.3 %shard_map.72 = f32[256,2048]{1,0:T(8,128)S(1)} custom-call(s32[6]{0:T(128)S(1)} %pad_add_fusion.place_ref, bf16[128,2048]{1,0:T(8,128)(2,1)S(1)} %constant_dynamic-update-slice_fusion.2.refs_0_, bf16[64,2048]{1,0:T(8,128)(2,1)} %collective-permute-done.12.refs_1_, bf16[64,2048]{1,0:T(8,128)(2,1)S(1)} %collective-permute-done.18.refs_2_, ...), custom_call_target="tpu_custom_call" | custom-call | flops 2147483648 | bytes 5242880 | tf_op jit(solution)/shard_map/pallas_call | solution.py:243
  140.6 1.3 add_convert_fusion
  (76 shorter events, 14.8 us)
Async XLA Ops:
  0.0 20.4 %slice-start = ((bf16[256,2048]{1,0:T(8,128)(2,1)}), bf16[96,2048]{1,0:T(8,128)(2,1)S(1)}, s32[]{:S(2)}) async-start(bf16[256,2048]{1,0:T(8,128)(2,1)} %param.6), calls=%async_computation | async-start | bytes 786432 | tf_op jit(solution)/shard_map/slice | solution.py:309
  1.2 17.7 %collective-permute-start.2 = (bf16[160,2048]{1,0:T(8,128)(2,1)S(1)}, bf16[160,2048]{1,0:T(8,128)(2,1)S(1)}, u32[]{:S(2)}, u32[]{:S(2)}) collective-permute-start(bf16[160,2048]{1,0:T(8,128)(2,1)S(1)} %slice.29.refs_0_), channel_id=1, source_target_pairs={{0,8},{8,0},{16,24},{24,16},{1,9},{9,1},{17,25},{25,17},{2,10},{10... | collective-permute-start | bytes 1966088 | tf_op jit(solution)/shard_map/ppermute | solution.py:42
  4.2 16.2 %collective-permute-start.3 = (bf16[160,2048]{1,0:T(8,128)(2,1)S(1)}, bf16[160,2048]{1,0:T(8,128)(2,1)S(1)}, u32[]{:S(2)}, u32[]{:S(2)}) collective-permute-start(bf16[160,2048]{1,0:T(8,128)(2,1)S(1)} %slice.29.refs_0_), channel_id=1, source_target_pairs={{0,16},{8,24},{16,0},{24,8},{1,17},{9,25},{17,1},{25,9},{2,18},{10... | collective-permute-start | bytes 1966088 | tf_op jit(solution)/shard_map/ppermute | solution.py:42
  6.9 3.6 %collective-permute-start = (bf16[80,2048]{1,0:T(8,128)(2,1)S(1)}, bf16[80,2048]{1,0:T(8,128)(2,1)S(1)}, u32[]{:S(2)}, u32[]{:S(2)}) collective-permute-start(bf16[80,2048]{1,0:T(8,128)(2,1)S(1)} %get-tuple-element.134), channel_id=1, source_target_pairs={{1,2},{3,4},{5,6},{9,10},{11,12},{13,14},{17,18},{19,20},{21,22},{... | collective-permute-start | bytes 983048 | tf_op jit(solution)/shard_map/ppermute | solution.py:300
  7.5 2.9 %collective-permute-start.1 = (bf16[80,2048]{1,0:T(8,128)(2,1)S(1)}, bf16[80,2048]{1,0:T(8,128)(2,1)S(1)}, u32[]{:S(2)}, u32[]{:S(2)}) collective-permute-start(bf16[80,2048]{1,0:T(8,128)(2,1)S(1)} %get-tuple-element.133), channel_id=1, source_target_pairs={{1,3},{3,5},{5,7},{9,11},{11,13},{13,15},{17,19},{19,21},{21,23},{... | collective-permute-start | bytes 983048 | tf_op jit(solution)/shard_map/ppermute | solution.py:300
  8.2 9.2 %collective-permute-start.4 = (bf16[64,2048]{1,0:T(8,128)(2,1)}, bf16[64,2048]{1,0:T(8,128)(2,1)S(1)}, u32[]{:S(2)}, u32[]{:S(2)}) collective-permute-start(bf16[64,2048]{1,0:T(8,128)(2,1)} %param.10), channel_id=1, source_target_pairs={{0,2},{2,6},{6,4},{4,0},{1,3},{3,7},{7,5},{5,1},{8,10},{10,14},{14... | collective-permute-start | bytes 786440 | tf_op jit(solution)/shard_map/ppermute | solution.py:291
  17.5 3.0 %copy-start.2 = (bf16[64,2048]{1,0:T(8,128)(2,1)}, bf16[64,2048]{1,0:T(8,128)(2,1)S(1)}, u32[]{:S(2)}) copy-start(bf16[64,2048]{1,0:T(8,128)(2,1)S(1)} %collective-permute-done.4) | copy-start | bytes 786436
  20.5 16.1 %collective-permute-start.6 = (bf16[176,2048]{1,0:T(8,128)(2,1)S(1)}, bf16[176,2048]{1,0:T(8,128)(2,1)S(1)}, u32[]{:S(2)}, u32[]{:S(2)}) collective-permute-start(bf16[176,2048]{1,0:T(8,128)(2,1)S(1)} %constant_dynamic-update-slice_fusion.refs_1_), channel_id=1, source_target_pairs={{0,1},{1,0},{2,3},{3,2},{4,5},{5,4},{6,7},{7,6},{8,9},{9,8},{10,11... | collective-permute-start | bytes 2162696 | tf_op jit(solution)/shard_map/ppermute | solution.py:37
  24.4 12.1 %collective-permute-start.5 = (bf16[160,2048]{1,0:T(8,128)(2,1)S(1)}, bf16[160,2048]{1,0:T(8,128)(2,1)}, u32[]{:S(2)}, u32[]{:S(2)}) collective-permute-start(bf16[160,2048]{1,0:T(8,128)(2,1)S(1)} %slice.29.refs_0_), channel_id=1, source_target_pairs={{0,1},{1,0},{2,3},{3,2},{4,5},{5,4},{6,7},{7,6},{8,9},{9,8},{10,11... | collective-permute-start | bytes 1966088 | tf_op jit(solution)/shard_map/ppermute | solution.py:37
  24.4 9.9 %collective-permute-start.12 = (bf16[64,2048]{1,0:T(8,128)(2,1)}, bf16[64,2048]{1,0:T(8,128)(2,1)}, u32[]{:S(2)}, u32[]{:S(2)}) collective-permute-start(bf16[64,2048]{1,0:T(8,128)(2,1)} %copy-done.2), channel_id=1, source_target_pairs={{0,2},{2,6},{6,4},{4,0},{1,3},{3,7},{7,5},{5,1},{8,10},{10,14},{14... | collective-permute-start | bytes 786440 | tf_op jit(solution)/shard_map/ppermute | solution.py:291
  30.1 18.3 %collective-permute-start.7 = (bf16[176,2048]{1,0:T(8,128)(2,1)S(1)}, bf16[176,2048]{1,0:T(8,128)(2,1)S(1)}, u32[]{:S(2)}, u32[]{:S(2)}) collective-permute-start(bf16[176,2048]{1,0:T(8,128)(2,1)S(1)} %constant_dynamic-update-slice_fusion.refs_1_), channel_id=1, source_target_pairs={{0,8},{8,0},{16,24},{24,16},{1,9},{9,1},{17,25},{25,17},{2,10},{10... | collective-permute-start | bytes 2162696 | tf_op jit(solution)/shard_map/ppermute | solution.py:42
  30.7 18.0 %collective-permute-start.8 = (bf16[176,2048]{1,0:T(8,128)(2,1)S(1)}, bf16[176,2048]{1,0:T(8,128)(2,1)S(1)}, u32[]{:S(2)}, u32[]{:S(2)}) collective-permute-start(bf16[176,2048]{1,0:T(8,128)(2,1)S(1)} %constant_dynamic-update-slice_fusion.refs_1_), channel_id=1, source_target_pairs={{0,16},{8,24},{16,0},{24,8},{1,17},{9,25},{17,1},{25,9},{2,18},{10... | collective-permute-start | bytes 2162696 | tf_op jit(solution)/shard_map/ppermute | solution.py:42
  34.3 20.3 %collective-permute-start.11 = (bf16[192,2048]{1,0:T(8,128)(2,1)}, bf16[192,2048]{1,0:T(8,128)(2,1)S(1)}, u32[]{:S(2)}, u32[]{:S(2)}) collective-permute-start(bf16[192,2048]{1,0:T(8,128)(2,1)} %bitcast.26), channel_id=1, source_target_pairs={{0,2},{2,6},{6,4},{4,0},{1,3},{3,7},{7,5},{5,1},{8,10},{10,14},{14... | collective-permute-start | bytes 2359304 | tf_op jit(solution)/shard_map/ppermute | solution.py:291
  36.5 3.0 %collective-permute-start.10 = (bf16[160,2048]{1,0:T(8,128)(2,1)S(1)}, bf16[160,2048]{1,0:T(8,128)(2,1)S(1)}, u32[]{:S(2)}, u32[]{:S(2)}) collective-permute-start(bf16[160,2048]{1,0:T(8,128)(2,1)S(1)} %collective-permute-done.3.refs_0_), channel_id=1, source_target_pairs={{0,1},{1,0},{2,3},{3,2},{4,5},{5,4},{6,7},{7,6},{8,9},{9,8},{10,11... | collective-permute-start | bytes 1966088 | tf_op jit(solution)/shard_map/ppermute | solution.py:37
  36.5 3.0 %collective-permute-start.9 = (bf16[160,2048]{1,0:T(8,128)(2,1)S(1)}, bf16[160,2048]{1,0:T(8,128)(2,1)S(1)}, u32[]{:S(2)}, u32[]{:S(2)}) collective-permute-start(bf16[160,2048]{1,0:T(8,128)(2,1)S(1)} %collective-permute-done.2.refs_0_), channel_id=1, source_target_pairs={{0,1},{1,0},{2,3},{3,2},{4,5},{5,4},{6,7},{7,6},{8,9},{9,8},{10,11... | collective-permute-start | bytes 1966088 | tf_op jit(solution)/shard_map/ppermute | solution.py:37
  37.2 19.9 %copy-start.1 = (bf16[64,2048]{1,0:T(8,128)(2,1)S(1)}, bf16[64,2048]{1,0:T(8,128)(2,1)}, u32[]{:S(2)}) copy-start(bf16[64,2048]{1,0:T(8,128)(2,1)} %param.10) | copy-start | bytes 786436
  37.2 23.8 %copy-start.3 = (bf16[64,2048]{1,0:T(8,128)(2,1)S(1)}, bf16[64,2048]{1,0:T(8,128)(2,1)}, u32[]{:S(2)}) copy-start(bf16[64,2048]{1,0:T(8,128)(2,1)} %copy-done.2) | copy-start | bytes 786436
  54.6 5.9 %collective-permute-start.14 = (bf16[176,2048]{1,0:T(8,128)(2,1)S(1)}, bf16[176,2048]{1,0:T(8,128)(2,1)S(1)}, u32[]{:S(2)}, u32[]{:S(2)}) collective-permute-start(bf16[176,2048]{1,0:T(8,128)(2,1)S(1)} %collective-permute-done.8.refs_1_), channel_id=1, source_target_pairs={{0,1},{1,0},{2,3},{3,2},{4,5},{5,4},{6,7},{7,6},{8,9},{9,8},{10,11... | collective-permute-start | bytes 2162696 | tf_op jit(solution)/shard_map/ppermute | solution.py:37
  54.6 8.1 %collective-permute-start.13 = (bf16[176,2048]{1,0:T(8,128)(2,1)S(1)}, bf16[176,2048]{1,0:T(8,128)(2,1)S(1)}, u32[]{:S(2)}, u32[]{:S(2)}) collective-permute-start(bf16[176,2048]{1,0:T(8,128)(2,1)S(1)} %collective-permute-done.7.refs_1_), channel_id=1, source_target_pairs={{0,1},{1,0},{2,3},{3,2},{4,5},{5,4},{6,7},{7,6},{8,9},{9,8},{10,11... | collective-permute-start | bytes 2162696 | tf_op jit(solution)/shard_map/ppermute | solution.py:37
  55.1 32.4 %collective-permute-start.16 = (bf16[176,2048]{1,0:T(8,128)(2,1)S(1)}, bf16[176,2048]{1,0:T(8,128)(2,1)S(1)}, u32[]{:S(2)}, u32[]{:S(2)}) collective-permute-start(bf16[176,2048]{1,0:T(8,128)(2,1)S(1)} %collective-permute-done.7.refs_1_), channel_id=1, source_target_pairs={{0,16},{8,24},{16,0},{24,8},{1,17},{9,25},{17,1},{25,9},{2,18},{10... | collective-permute-start | bytes 2162696 | tf_op jit(solution)/shard_map/ppermute | solution.py:42
  55.6 10.3 %collective-permute-start.18 = (bf16[64,2048]{1,0:T(8,128)(2,1)}, bf16[64,2048]{1,0:T(8,128)(2,1)S(1)}, u32[]{:S(2)}, u32[]{:S(2)}) collective-permute-start(bf16[64,2048]{1,0:T(8,128)(2,1)} %collective-permute-done.12.refs_1_), channel_id=1, source_target_pairs={{0,2},{2,6},{6,4},{4,0},{1,3},{3,7},{7,5},{5,1},{8,10},{10,14},{14... | collective-permute-start | bytes 786440 | tf_op jit(solution)/shard_map/ppermute | solution.py:291
  57.2 30.4 %collective-permute-start.17 = (bf16[192,2048]{1,0:T(8,128)(2,1)S(1)}, bf16[192,2048]{1,0:T(8,128)(2,1)S(1)}, u32[]{:S(2)}, u32[]{:S(2)}) collective-permute-start(bf16[192,2048]{1,0:T(8,128)(2,1)S(1)} %collective-permute-done.11.rest_1_), channel_id=1, source_target_pairs={{0,2},{2,6},{6,4},{4,0},{1,3},{3,7},{7,5},{5,1},{8,10},{10,14},{14... | collective-permute-start | bytes 2359304 | tf_op jit(solution)/shard_map/ppermute | solution.py:291
  60.5 27.0 %collective-permute-start.15 = (bf16[160,2048]{1,0:T(8,128)(2,1)S(1)}, bf16[160,2048]{1,0:T(8,128)(2,1)S(1)}, u32[]{:S(2)}, u32[]{:S(2)}) collective-permute-start(bf16[160,2048]{1,0:T(8,128)(2,1)S(1)} %collective-permute-done.3.refs_0_), channel_id=1, source_target_pairs={{0,8},{8,0},{16,24},{24,16},{1,9},{9,1},{17,25},{25,17},{2,10},{10... | collective-permute-start | bytes 1966088 | tf_op jit(solution)/shard_map/ppermute | solution.py:42
  62.7 4.8 %copy-start = (bf16[3,64,2048]{2,1,0:T(8,128)(2,1)S(1)}, bf16[3,64,2048]{2,1,0:T(8,128)(2,1)}, u32[]{:S(2)}) copy-start(bf16[3,64,2048]{2,1,0:T(8,128)(2,1)} %param.7) | copy-start | bytes 2359300
  62.7 24.8 %collective-permute-start.19 = (bf16[128,2048]{1,0:T(8,128)(2,1)S(1)}, bf16[128,2048]{1,0:T(8,128)(2,1)S(1)}, u32[]{:S(2)}, u32[]{:S(2)}) collective-permute-start(bf16[128,2048]{1,0:T(8,128)(2,1)S(1)} %constant_dynamic-update-slice_fusion.2.refs_0_), channel_id=1, source_target_pairs={{0,8},{8,0},{16,24},{24,16},{1,9},{9,1},{17,25},{25,17},{2,10},{10... | collective-permute-start | bytes 1572872 | tf_op jit(solution)/shard_map/ppermute | solution.py:42
  66.0 21.6 %collective-permute-start.20 = (bf16[128,2048]{1,0:T(8,128)(2,1)S(1)}, bf16[128,2048]{1,0:T(8,128)(2,1)S(1)}, u32[]{:S(2)}, u32[]{:S(2)}) collective-permute-start(bf16[128,2048]{1,0:T(8,128)(2,1)S(1)} %constant_dynamic-update-slice_fusion.2.refs_0_), channel_id=1, source_target_pairs={{0,16},{8,24},{16,0},{24,8},{1,17},{9,25},{17,1},{25,9},{2,18},{10... | collective-permute-start | bytes 1572872 | tf_op jit(solution)/shard_map/ppermute | solution.py:42
  87.5 4.7 %collective-permute-start.22 = (bf16[176,2048]{1,0:T(8,128)(2,1)S(1)}, bf16[176,2048]{1,0:T(8,128)(2,1)S(1)}, u32[]{:S(2)}, u32[]{:S(2)}) collective-permute-start(bf16[176,2048]{1,0:T(8,128)(2,1)S(1)} %collective-permute-done.16.refs_1_), channel_id=1, source_target_pairs={{0,1},{1,0},{2,3},{3,2},{4,5},{5,4},{6,7},{7,6},{8,9},{9,8},{10,11... | collective-permute-start | bytes 2162696 | tf_op jit(solution)/shard_map/ppermute | solution.py:37
  87.6 3.1 %collective-permute-start.21 = (bf16[160,2048]{1,0:T(8,128)(2,1)S(1)}, bf16[160,2048]{1,0:T(8,128)(2,1)S(1)}, u32[]{:S(2)}, u32[]{:S(2)}) collective-permute-start(bf16[160,2048]{1,0:T(8,128)(2,1)S(1)} %collective-permute-done.15.refs_0_), channel_id=1, source_target_pairs={{0,1},{1,0},{2,3},{3,2},{4,5},{5,4},{6,7},{7,6},{8,9},{9,8},{10,11... | collective-permute-start | bytes 1966088 | tf_op jit(solution)/shard_map/ppermute | solution.py:37
  88.1 25.5 %collective-permute-start.25 = (bf16[192,2048]{1,0:T(8,128)(2,1)S(1)}, bf16[192,2048]{1,0:T(8,128)(2,1)S(1)}, u32[]{:S(2)}, u32[]{:S(2)}) collective-permute-start(bf16[192,2048]{1,0:T(8,128)(2,1)S(1)} %collective-permute-done.17.rest_0_.rest_2_), channel_id=1, source_target_pairs={{0,2},{2,6},{6,4},{4,0},{1,3},{3,7},{7,5},{5,1},{8,10},{10,14},{14... | collective-permute-start | bytes 2359304 | tf_op jit(solution)/shard_map/ppermute | solution.py:291
  88.5 12.9 %collective-permute-start.26 = (bf16[64,2048]{1,0:T(8,128)(2,1)S(1)}, bf16[64,2048]{1,0:T(8,128)(2,1)S(1)}, u32[]{:S(2)}, u32[]{:S(2)}) collective-permute-start(bf16[64,2048]{1,0:T(8,128)(2,1)S(1)} %slice.34), channel_id=1, source_target_pairs={{0,8},{8,0},{16,24},{24,16},{1,9},{9,1},{17,25},{25,17},{2,10},{10... | collective-permute-start | bytes 786440 | tf_op jit(solution)/shard_map/ppermute | solution.py:42
  89.1 13.8 %collective-permute-start.27 = (bf16[64,2048]{1,0:T(8,128)(2,1)S(1)}, bf16[64,2048]{1,0:T(8,128)(2,1)S(1)}, u32[]{:S(2)}, u32[]{:S(2)}) collective-permute-start(bf16[64,2048]{1,0:T(8,128)(2,1)S(1)} %slice.35), channel_id=1, source_target_pairs={{0,16},{8,24},{16,0},{24,8},{1,17},{9,25},{17,1},{25,9},{2,18},{10... | collective-permute-start | bytes 786440 | tf_op jit(solution)/shard_map/ppermute | solution.py:42
  90.7 8.7 %collective-permute-start.23 = (bf16[128,512]{1,0:T(8,128)(2,1)S(1)}, bf16[128,512]{1,0:T(8,128)(2,1)S(1)}, u32[]{:S(2)}, u32[]{:S(2)}) collective-permute-start(bf16[128,512]{1,0:T(8,128)(2,1)S(1)} %get-tuple-element.103), channel_id=1, source_target_pairs={{0,8},{8,0},{16,24},{24,16},{1,9},{9,1},{17,25},{25,17},{2,10},{10... | collective-permute-start | bytes 393224 | tf_op jit(solution)/shard_map/ppermute | solution.py:42
  92.2 8.1 %collective-permute-start.24 = (bf16[128,512]{1,0:T(8,128)(2,1)S(1)}, bf16[128,512]{1,0:T(8,128)(2,1)S(1)}, u32[]{:S(2)}, u32[]{:S(2)}) collective-permute-start(bf16[128,512]{1,0:T(8,128)(2,1)S(1)} %get-tuple-element.104), channel_id=1, source_target_pairs={{0,16},{8,24},{16,0},{24,8},{1,17},{9,25},{17,1},{25,9},{2,18},{10... | collective-permute-start | bytes 393224 | tf_op jit(solution)/shard_map/ppermute | solution.py:42
  99.4 9.5 %collective-permute-start.28 = (bf16[64,2048]{1,0:T(8,128)(2,1)}, bf16[64,2048]{1,0:T(8,128)(2,1)S(1)}, u32[]{:S(2)}, u32[]{:S(2)}) collective-permute-start(bf16[64,2048]{1,0:T(8,128)(2,1)} %collective-permute-done.12.refs_1_), channel_id=1, source_target_pairs={{0,8},{8,0},{16,24},{24,16},{1,9},{9,1},{17,25},{25,17},{2,10},{10... | collective-permute-start | bytes 786440 | tf_op jit(solution)/shard_map/ppermute | solution.py:42
  100.3 9.5 %collective-permute-start.29 = (bf16[64,2048]{1,0:T(8,128)(2,1)}, bf16[64,2048]{1,0:T(8,128)(2,1)S(1)}, u32[]{:S(2)}, u32[]{:S(2)}) collective-permute-start(bf16[64,2048]{1,0:T(8,128)(2,1)} %collective-permute-done.12.refs_1_), channel_id=1, source_target_pairs={{0,16},{8,24},{16,0},{24,8},{1,17},{9,25},{17,1},{25,9},{2,18},{10... | collective-permute-start | bytes 786440 | tf_op jit(solution)/shard_map/ppermute | solution.py:42
  101.5 11.0 %collective-permute-start.30 = (bf16[64,2048]{1,0:T(8,128)(2,1)S(1)}, bf16[64,2048]{1,0:T(8,128)(2,1)S(1)}, u32[]{:S(2)}, u32[]{:S(2)}) collective-permute-start(bf16[64,2048]{1,0:T(8,128)(2,1)S(1)} %collective-permute-done.18.refs_2_), channel_id=1, source_target_pairs={{0,8},{8,0},{16,24},{24,16},{1,9},{9,1},{17,25},{25,17},{2,10},{10... | collective-permute-start | bytes 786440 | tf_op jit(solution)/shard_map/ppermute | solution.py:42
  103.0 10.7 %collective-permute-start.31 = (bf16[64,2048]{1,0:T(8,128)(2,1)S(1)}, bf16[64,2048]{1,0:T(8,128)(2,1)S(1)}, u32[]{:S(2)}, u32[]{:S(2)}) collective-permute-start(bf16[64,2048]{1,0:T(8,128)(2,1)S(1)} %collective-permute-done.18.refs_2_), channel_id=1, source_target_pairs={{0,16},{8,24},{16,0},{24,8},{1,17},{9,25},{17,1},{25,9},{2,18},{10... | collective-permute-start | bytes 786440 | tf_op jit(solution)/shard_map/ppermute | solution.py:42
  113.7 21.9 %collective-permute-start.32 = (bf16[64,2048]{1,0:T(8,128)(2,1)S(1)}, bf16[64,2048]{1,0:T(8,128)(2,1)S(1)}, u32[]{:S(2)}, u32[]{:S(2)}) collective-permute-start(bf16[64,2048]{1,0:T(8,128)(2,1)S(1)} %collective-permute-done.29.refs_7_), channel_id=1, source_target_pairs={{0,8},{8,0},{16,24},{24,16},{1,9},{9,1},{17,25},{25,17},{2,10},{10... | collective-permute-start | bytes 786440 | tf_op jit(solution)/shard_map/ppermute | solution.py:42
  114.2 21.3 %collective-permute-start.33 = (bf16[64,2048]{1,0:T(8,128)(2,1)S(1)}, bf16[64,2048]{1,0:T(8,128)(2,1)S(1)}, u32[]{:S(2)}, u32[]{:S(2)}) collective-permute-start(bf16[64,2048]{1,0:T(8,128)(2,1)S(1)} %collective-permute-done.30.refs_5_), channel_id=1, source_target_pairs={{0,16},{8,24},{16,0},{24,8},{1,17},{9,25},{17,1},{25,9},{2,18},{10... | collective-permute-start | bytes 786440 | tf_op jit(solution)/shard_map/ppermute | solution.py:42
  121.0 5.1 %collective-permute-start.35 = (bf16[64,512]{1,0:T(8,128)(2,1)S(1)}, bf16[64,512]{1,0:T(8,128)(2,1)S(1)}, u32[]{:S(2)}, u32[]{:S(2)}) collective-permute-start(bf16[64,512]{1,0:T(8,128)(2,1)S(1)} %get-tuple-element.127), channel_id=1, source_target_pairs={{0,8},{8,0},{16,24},{24,16},{1,9},{9,1},{17,25},{25,17},{2,10},{10... | collective-permute-start | bytes 196616 | tf_op jit(solution)/shard_map/ppermute | solution.py:42
  121.6 13.9 %collective-permute-start.38 = (bf16[192,512]{1,0:T(8,128)(2,1)S(1)}, bf16[192,512]{1,0:T(8,128)(2,1)S(1)}, u32[]{:S(2)}, u32[]{:S(2)}) collective-permute-start(bf16[192,512]{1,0:T(8,128)(2,1)S(1)} %shard_map.70), channel_id=1, source_target_pairs={{0,24},{8,16},{16,8},{24,0},{1,25},{9,17},{17,9},{25,1},{2,26},{10... | collective-permute-start | bytes 589832 | tf_op jit(solution)/shard_map/ppermute | solution.py:42
  123.1 5.8 %collective-permute-start.37 = (bf16[64,512]{1,0:T(8,128)(2,1)S(1)}, bf16[64,512]{1,0:T(8,128)(2,1)S(1)}, u32[]{:S(2)}, u32[]{:S(2)}) collective-permute-start(bf16[64,512]{1,0:T(8,128)(2,1)S(1)} %get-tuple-element.130), channel_id=1, source_target_pairs={{0,16},{8,24},{16,0},{24,8},{1,17},{9,25},{17,1},{25,9},{2,18},{10... | collective-permute-start | bytes 196616 | tf_op jit(solution)/shard_map/ppermute | solution.py:42
  126.1 5.2 %collective-permute-start.39 = (bf16[64,512]{1,0:T(8,128)(2,1)S(1)}, bf16[64,512]{1,0:T(8,128)(2,1)S(1)}, u32[]{:S(2)}, u32[]{:S(2)}) collective-permute-start(bf16[64,512]{1,0:T(8,128)(2,1)S(1)} %get-tuple-element.132), channel_id=1, source_target_pairs={{0,24},{8,16},{16,8},{24,0},{1,25},{9,17},{17,9},{25,1},{2,26},{10... | collective-permute-start | bytes 196616 | tf_op jit(solution)/shard_map/ppermute | solution.py:42
  128.9 4.3 %collective-permute-start.34 = (bf16[64,512]{1,0:T(8,128)(2,1)S(1)}, bf16[64,512]{1,0:T(8,128)(2,1)S(1)}, u32[]{:S(2)}, u32[]{:S(2)}) collective-permute-start(bf16[64,512]{1,0:T(8,128)(2,1)S(1)} %get-tuple-element.126), channel_id=1, source_target_pairs={{0,8},{8,0},{16,24},{24,16},{1,9},{9,1},{17,25},{25,17},{2,10},{10... | collective-permute-start | bytes 196616 | tf_op jit(solution)/shard_map/ppermute | solution.py:42
  131.3 4.3 %collective-permute-start.36 = (bf16[64,512]{1,0:T(8,128)(2,1)S(1)}, bf16[64,512]{1,0:T(8,128)(2,1)S(1)}, u32[]{:S(2)}, u32[]{:S(2)}) collective-permute-start(bf16[64,512]{1,0:T(8,128)(2,1)S(1)} %get-tuple-element.129), channel_id=1, source_target_pairs={{0,16},{8,24},{16,0},{24,8},{1,17},{9,25},{17,1},{25,9},{2,18},{10... | collective-permute-start | bytes 196616 | tf_op jit(solution)/shard_map/ppermute | solution.py:42
  137.9 2.7 %collective-permute-start.40 = (bf16[256,2048]{1,0:T(8,128)(2,1)S(1)}, bf16[256,2048]{1,0:T(8,128)(2,1)S(1)}, u32[]{:S(2)}, u32[]{:S(2)}) collective-permute-start(bf16[256,2048]{1,0:T(8,128)(2,1)S(1)} %shard_map.73), channel_id=1, source_target_pairs={{0,1},{1,0},{2,3},{3,2},{4,5},{5,4},{6,7},{7,6},{8,9},{9,8},{10,11... | collective-permute-start | bytes 3145736 | tf_op jit(solution)/shard_map/ppermute | solution.py:37

commit v8 on v7

--- a/solution.py
+++ b/solution.py
@@ -308,43 +308,47 @@
         ws, vs = [in_weight.reshape(3 * width, features)], [out_weight, forward(out_weight)]
         low, high = tokens[:mid], tokens[mid:]
         low_x, low_y = across(low, 1), across(low, 2)
-        edge, low, high, low_x, low_y, ws, vs = tie(edge, low, high, low_x, low_y, ws, vs)
+        edge, low, high, low_x, low_y, ws, vs, taps, filters, place = tie(
+            edge, low, high, low_x, low_y, ws, vs, taps, filters, place
+        )
 
         high = jnp.concatenate([high, edge])
         high_x, high_y = across(high, 1), across(high, 2)
-        ws, vs = [ws[0], forward(ws[0])], [*vs, forward(vs[1])]
+        ws = [ws[0], forward(ws[0])]
         x0 = lay(place, rows, parts, [low, high, swap(low), swap(high)])
         low_x_twin, low_y_twin = swap(low_x), swap(low_y)
         both = lambda one: [one, across(one, 1), across(one, 2)]
-        (x0, high_x, high_y, low_x, low_y, low_x_twin, low_y_twin, ws, vs, taps, filters, place) = tie(
-            x0, high_x, high_y, low_x, low_y, low_x_twin, low_y_twin, ws, vs, taps, filters, place
+        x0, vs = tie(x0, vs)
+        vs = [*vs, forward(vs[1])]
+        v0 = both(vs[0])
+        (x0, high_x, high_y, low_x, low_y, low_x_twin, low_y_twin, ws, vs, v0) = tie(
+            x0, high_x, high_y, low_x, low_y, low_x_twin, low_y_twin, ws, vs, v0
         )
 
         ws, vs = [*ws, forward(ws[1])], [*vs, forward(vs[2])]
         far_x, far_y = across(low_y, 1), across(high_x, 2)
-        v1 = both(jnp.concatenate([vs[0], vs[1]]))
+        v1 = both(vs[1])
         x1 = lay(place, rows, parts, [low_x, high_x, low_x_twin, swap(high_x)])
         x2 = lay(place, rows, parts, [low_y, high_y, low_y_twin, swap(high_y)])
         mix01 = run_mix((0, 1), (x0, x1, x2))
         mix01, far_x, far_y, ws, vs, v1 = tie(mix01, far_x, far_y, ws, vs, v1)
 
         ws = [*ws, forward(ws[2])]
-        v0, v1 = across(v1[2][:width], 1), [*v1, across(v1[1][width:], 2)]
+        v0, v1 = [*v0, across(v0[2], 1)], [*v1, across(v1[1], 2)]
         v2, v3 = both(vs[2]), both(vs[3])
-        moved = [[across(mix01[r], r)] for r in (1, 2)]
         x3 = lay(place, rows, parts, [far_x, far_y, swap(far_x), swap(far_y)])
         mix2 = run_mix((2,), (x0, x1, x2))
         far = run_mix((0, 1, 2), (x3,))
+        moved = [[across(mix01[r], r), across(mix2[r], r)] for r in (1, 2)] + [across(far[0], 3)]
         mix2, far, moved, ws, v0, v1, v2, v3 = tie(mix2, far, moved, ws, v0, v1, v2, v3)
 
         v2, v3 = [*v2, across(v2[2], 1)], [*v3, across(v3[1], 2)]
         mix3 = run_mix((3,), (x0, x1, x2, x3))
-        v = [one[r] for r in range(slots) for one in (v1, v2, v3)]
-        v.insert(9, v0)
+        v = [one[r] for r in range(slots) for one in (v0, v1, v2, v3)]
         together = [mix01[0], mix2[0], mix3[0]]
         for r in (1, 2):
-            together += [*moved[r - 1], across(mix2[r], r), across(mix3[r], r)]
-        together += [across(far[0], 3), across(mix3[3], 3)]
+            together += [*moved[r - 1], across(mix3[r], r)]
+        together += [moved[2], across(mix3[3], 3)]
         order = []
         for r in range(3):
             order += [(3 * r, 0), (3 * r, width), (3 * r + 1, 0), (3 * r + 2, 0)]

time: 142 us -> 140 us (0.986)
  waiting for transfers between devices: 55.2 us -> 48.8 us
  starting transfers between devices: 44.7 us -> 48.6 us
  Pallas kernels: 33.3 us -> 31.8 us
    ppermute x6, waiting for transfers between devices: 16 us -> 6.56 us  [shards(): forward = lambda block: lax.ppermute(block, 'z', ring)]
    ppermute x6, starting transfers between devices: 10.9 us -> 13.8 us  [shards(): forward = lambda block: lax.ppermute(block, 'z', ring)]
    ppermute x24 -> x26, waiting for transfers between devices: 38.8 us -> 41 us  [across(): return lax.ppermute(block, 'dp', [(i, i ^ r) for i in range(count)])]
    ppermute x24 -> x26, starting transfers between devices: 26.8 us -> 25.9 us  [across(): return lax.ppermute(block, 'dp', [(i, i ^ r) for i in range(count)])]
  transfers between devices with their start and end apart: 41 -> 43, of which waited for: 21 -> 21; matrix products, arithmetic and copies ran while one was open for 4% -> 6% of each run, Pallas kernels for 22% -> 21%
where the time goes in v8:
time: 140 us
  waiting for transfers between devices  48.8 us (35%)
  starting transfers between devices  48.6 us (35%)
  Pallas kernels  31.8 us (23%)
  local copies, waits for them, and re-layouts  7.59 us (5%)
  other arithmetic  2.61 us (2%)
    ppermute x26, waiting for transfers between devices, across(): return lax.ppermute(block, 'dp', [(i, i ^ r) for i in range(count)])  41 us
    ppermute x26, starting transfers between devices, across(): return lax.ppermute(block, 'dp', [(i, i ^ r) for i in range(count)])  25.9 us
    pallas_call x4, Pallas kernels, mix_chunks(): pl.pallas_call(functools.partial(mix_kernel, steps, slots), out_shape=[ja...  21.6 us
    ppermute x6, starting transfers between devices, shards(): forward = lambda block: lax.ppermute(block, 'z', ring)  13.8 us
    ppermute x6, waiting for transfers between devices, shards(): forward = lambda block: lax.ppermute(block, 'z', ring)  6.56 us
    pallas_call x4, Pallas kernels, lay(): pl.pallas_call(functools.partial(lay_kernel, parts), out_shape=jax.ShapeD...  6.47 us
    ppermute x9, starting transfers between devices, swap(): return lax.ppermute(block, 'core', [(0, 1), (1, 0)])  6.18 us
    pallas_call x2, Pallas kernels, project(): pl.pallas_call(functools.partial(out_kernel, mirror, order, width, counts...  3.81 us
  transfers between devices with their start and end apart: 43, of which 21 were waited for; matrix products, arithmetic and copies ran while one was open for 6% of the time, Pallas kernels for 21%

profile of v8, /device:TPU:0, one launch (start us, length us, event | category | flops | bytes accessed | tf_op | source)
XLA Modules:
  0.0 139.7 jit_solution(18066690504815872997)
XLA Ops:
  0.0 1.2 slice.23.refs_0_
  1.2 3.0 %collective-permute-start.2 = (bf16[160,2048]{1,0:T(8,128)(2,1)S(1)}, bf16[160,2048]{1,0:T(8,128)(2,1)S(1)}, u32[]{:S(2)}, u32[]{:S(2)}) collective-permute-start(bf16[160,2048]{1,0:T(8,128)(2,1)S(1)} %slice.23.refs_0_), channel_id=1, source_target_pairs={{0,8},{8,0},{16,24},{24,16},{1,9},{9,1},{17,25},{25,17},{2,10},{10... | collective-permute-start | bytes 1966088 | tf_op jit(solution)/shard_map/ppermute | solution.py:42
  4.2 1.5 %collective-permute-start.3 = (bf16[160,2048]{1,0:T(8,128)(2,1)S(1)}, bf16[160,2048]{1,0:T(8,128)(2,1)S(1)}, u32[]{:S(2)}, u32[]{:S(2)}) collective-permute-start(bf16[160,2048]{1,0:T(8,128)(2,1)S(1)} %slice.23.refs_0_), channel_id=1, source_target_pairs={{0,16},{8,24},{16,0},{24,8},{1,17},{9,25},{17,1},{25,9},{2,18},{10... | collective-permute-start | bytes 1966088 | tf_op jit(solution)/shard_map/ppermute | solution.py:42
  5.7 2.0 %fusion.5 = (bf16[80,2048]{1,0:T(8,128)(2,1)}, bf16[80,2048]{1,0:T(8,128)(2,1)}) fusion(bf16[256,2048]{1,0:T(8,128)(2,1)} %param.6), kind=kLoop, calls=%fused_computation.22 | loop fusion | bytes 1310720 | tf_op jit(solution)/shard_map/slice | solution.py:301
  7.7 1.4 collective-permute-start
  9.1 1.4 collective-permute-start.1
  10.5 1.5 %collective-permute-start.4 = (bf16[64,2048]{1,0:T(8,128)(2,1)}, bf16[64,2048]{1,0:T(8,128)(2,1)S(1)}, u32[]{:S(2)}, u32[]{:S(2)}) collective-permute-start(bf16[64,2048]{1,0:T(8,128)(2,1)} %refs_0_.1), channel_id=1, source_target_pairs={{0,2},{2,6},{6,4},{4,0},{1,3},{3,7},{7,5},{5,1},{8,10},{10,14},{14... | collective-permute-start | bytes 786440 | tf_op jit(solution)/shard_map/ppermute | solution.py:291
  12.0 1.9 %reshape.10 = f32[7,3,16,2,64]{4,3,2,0,1:T(2,128)} reshape(f32[7,3,2048]{2,0,1:T(8,128)} %param.8) | data formatting | bytes 344064 | tf_op jit(solution)/shard_map/reshape | solution.py:263
  16.6 1.2 add.55
  17.7 1.3 collective-permute-done.4.refs_1_
  19.0 1.4 collective-permute-done.3.refs_0_
  20.4 4.4 %collective-permute-start.5 = (bf16[160,2048]{1,0:T(8,128)(2,1)S(1)}, bf16[160,2048]{1,0:T(8,128)(2,1)S(1)}, u32[]{:S(2)}, u32[]{:S(2)}) collective-permute-start(bf16[160,2048]{1,0:T(8,128)(2,1)S(1)} %slice.23.refs_0_), channel_id=1, source_target_pairs={{0,1},{1,0},{2,3},{3,2},{4,5},{5,4},{6,7},{7,6},{8,9},{9,8},{10,11... | collective-permute-start | bytes 1966088 | tf_op jit(solution)/shard_map/ppermute | solution.py:37
  26.6 2.1 %collective-permute-start.11 = (bf16[192,2048]{1,0:T(8,128)(2,1)S(1)}, bf16[192,2048]{1,0:T(8,128)(2,1)S(1)}, u32[]{:S(2)}, u32[]{:S(2)}) collective-permute-start(bf16[192,2048]{1,0:T(8,128)(2,1)S(1)} %bitcast.26), channel_id=1, source_target_pairs={{0,2},{2,6},{6,4},{4,0},{1,3},{3,7},{7,5},{5,1},{8,10},{10,14},{14... | collective-permute-start | bytes 2359304 | tf_op jit(solution)/shard_map/ppermute | solution.py:291
  29.2 1.6 %shard_map.64.rest_2_.rest_1_ = bf16[672,2048]{1,0:T(8,128)(2,1)S(1)} custom-call(s32[6]{0:T(128)S(1)} %pad_add_fusion.place_ref, bf16[160,2048]{1,0:T(8,128)(2,1)S(1)} %slice.23.refs_0_, bf16[176,2048]{1,0:T(8,128)(2,1)S(1)} %constant_dynamic-update-slice_fusion.refs_1_, bf16[160,2048]{1,0:T(8,128)(2,1)S(1)} %collective-permute-done.5.refs_2_, ...), custom_call_target="tpu_custom_call" | custom-call | bytes 5505024 | tf_op jit(solution)/shard_map/pallas_call | solution.py:87
  30.8 3.9 %collective-permute-start.12 = (bf16[64,2048]{1,0:T(8,128)(2,1)S(1)}, bf16[64,2048]{1,0:T(8,128)(2,1)S(1)}, u32[]{:S(2)}, u32[]{:S(2)}) collective-permute-start(bf16[64,2048]{1,0:T(8,128)(2,1)S(1)} %collective-permute-done.4.refs_1_), channel_id=1, source_target_pairs={{0,2},{2,6},{6,4},{4,0},{1,3},{3,7},{7,5},{5,1},{8,10},{10,14},{14... | collective-permute-start | bytes 786440 | tf_op jit(solution)/shard_map/ppermute | solution.py:291
  34.8 1.0 collective-permute-start.13
  35.8 8.2 %collective-permute-done.7.refs_1_ = bf16[176,2048]{1,0:T(8,128)(2,1)S(1)} collective-permute-done((bf16[176,2048]{1,0:T(8,128)(2,1)S(1)}, bf16[176,2048]{1,0:T(8,128)(2,1)S(1)}, u32[]{:S(2)}, u32[]{:S(2)}) %collective-permute-start.7) | collective-permute-done | bytes 720928 | tf_op jit(solution)/shard_map/ppermute | solution.py:42
  44.5 3.2 %collective-permute-done.8.refs_1_ = bf16[176,2048]{1,0:T(8,128)(2,1)S(1)} collective-permute-done((bf16[176,2048]{1,0:T(8,128)(2,1)S(1)}, bf16[176,2048]{1,0:T(8,128)(2,1)S(1)}, u32[]{:S(2)}, u32[]{:S(2)}) %collective-permute-start.8) | collective-permute-done | bytes 720928 | tf_op jit(solution)/shard_map/ppermute | solution.py:42
  47.9 5.1 %collective-permute-done.12.refs_2_ = bf16[64,2048]{1,0:T(8,128)(2,1)S(1)} collective-permute-done((bf16[64,2048]{1,0:T(8,128)(2,1)S(1)}, bf16[64,2048]{1,0:T(8,128)(2,1)S(1)}, u32[]{:S(2)}, u32[]{:S(2)}) %collective-permute-start.12) | collective-permute-done | bytes 262176 | tf_op jit(solution)/shard_map/ppermute | solution.py:291
  53.5 3.4 %collective-permute-start.20 = (bf16[64,2048]{1,0:T(8,128)(2,1)S(1)}, bf16[64,2048]{1,0:T(8,128)(2,1)S(1)}, u32[]{:S(2)}, u32[]{:S(2)}) collective-permute-start(bf16[64,2048]{1,0:T(8,128)(2,1)S(1)} %collective-permute-done.12.refs_2_), channel_id=1, source_target_pairs={{0,2},{2,6},{6,4},{4,0},{1,3},{3,7},{7,5},{5,1},{8,10},{10,14},{14... | collective-permute-start | bytes 786440 | tf_op jit(solution)/shard_map/ppermute | solution.py:291
  56.8 2.6 %collective-permute-start.19 = (bf16[192,2048]{1,0:T(8,128)(2,1)S(1)}, bf16[192,2048]{1,0:T(8,128)(2,1)S(1)}, u32[]{:S(2)}, u32[]{:S(2)}) collective-permute-start(bf16[192,2048]{1,0:T(8,128)(2,1)S(1)} %collective-permute-done.11.rest_1_), channel_id=1, source_target_pairs={{0,2},{2,6},{6,4},{4,0},{1,3},{3,7},{7,5},{5,1},{8,10},{10,14},{14... | collective-permute-start | bytes 2359304 | tf_op jit(solution)/shard_map/ppermute | solution.py:291
  60.7 1.6 %shard_map.66.rest_4_.rest_3_ = bf16[672,2048]{1,0:T(8,128)(2,1)S(1)} custom-call(s32[6]{0:T(128)S(1)} %pad_add_fusion.place_ref, bf16[160,2048]{1,0:T(8,128)(2,1)S(1)} %collective-permute-done.3.refs_0_, bf16[176,2048]{1,0:T(8,128)(2,1)S(1)} %collective-permute-done.8.refs_1_, bf16[160,2048]{1,0:T(8,128)(2,1)S(1)} %collective-permute-done.10.refs_2_, ...), custom_call_target="tpu_custom_call" | custom-call | bytes 5505024 | tf_op jit(solution)/shard_map/pallas_call | solution.py:87
  62.4 1.3 collective-permute-start.21
  63.7 1.6 %shard_map.65.rest_3_.rest_2_ = bf16[672,2048]{1,0:T(8,128)(2,1)S(1)} custom-call(s32[6]{0:T(128)S(1)} %pad_add_fusion.place_ref, bf16[160,2048]{1,0:T(8,128)(2,1)S(1)} %collective-permute-done.2.refs_0_, bf16[176,2048]{1,0:T(8,128)(2,1)S(1)} %collective-permute-done.7.refs_1_, bf16[160,2048]{1,0:T(8,128)(2,1)S(1)} %collective-permute-done.9.refs_2_, ...), custom_call_target="tpu_custom_call" | custom-call | bytes 5505024 | tf_op jit(solution)/shard_map/pallas_call | solution.py:87
  65.3 1.6 %collective-permute-start.22 = (bf16[64,2048]{1,0:T(8,128)(2,1)S(1)}, bf16[64,2048]{1,0:T(8,128)(2,1)S(1)}, u32[]{:S(2)}, u32[]{:S(2)}) collective-permute-start(bf16[64,2048]{1,0:T(8,128)(2,1)S(1)} %collective-permute-done.4.refs_1_), channel_id=1, source_target_pairs={{0,16},{8,24},{16,0},{24,8},{1,17},{9,25},{17,1},{25,9},{2,18},{10... | collective-permute-start | bytes 786440 | tf_op jit(solution)/shard_map/ppermute | solution.py:42
  66.9 7.6 %shard_map.67 = (bf16[128,512]{1,0:T(8,128)(2,1)S(1)}, bf16[128,512]{1,0:T(8,128)(2,1)S(1)}, bf16[128,512]{1,0:T(8,128)(2,1)S(1)}) custom-call(s32[6]{0:T(128)S(1)} %pad_add_fusion.place_ref, f32[4,8,256]{2,1,0:T(8,128)S(1)} %pad_maximum_fusion.taps_ref, f32[4,4,128]{2,1,0:T(4,128)S(1)} %maximum_convert_fusion.long_ref, bf16[192,2048]{1,0:T(8,128)(2,1)S(1)} %bitcast.27, ...), custom_call_target="tpu_custom_call" | custom-call | flops 6442450944 | bytes 12582912 | tf_op jit(solution)/shard_map/pallas_call | solution.py:183
  74.5 6.9 %collective-permute-done.21.refs_5_ = bf16[64,2048]{1,0:T(8,128)(2,1)S(1)} collective-permute-done((bf16[64,2048]{1,0:T(8,128)(2,1)S(1)}, bf16[64,2048]{1,0:T(8,128)(2,1)S(1)}, u32[]{:S(2)}, u32[]{:S(2)}) %collective-permute-start.21) | collective-permute-done | bytes 262176 | tf_op jit(solution)/shard_map/ppermute | solution.py:42
  81.4 1.2 collective-permute-done.22.refs_9_
  84.8 4.3 %shard_map.68 = (bf16[64,512]{1,0:T(8,128)(2,1)S(1)}, bf16[64,512]{1,0:T(8,128)(2,1)S(1)}, bf16[64,512]{1,0:T(8,128)(2,1)S(1)}) custom-call(s32[6]{0:T(128)S(1)} %pad_add_fusion.place_ref, f32[4,8,256]{2,1,0:T(8,128)S(1)} %pad_maximum_fusion.taps_ref, f32[4,4,128]{2,1,0:T(4,128)S(1)} %maximum_convert_fusion.long_ref, ...), custom_call_target="tpu_custom_call" | custom-call | flops 3221225472 | bytes 6291456 | tf_op jit(solution)/shard_map/pallas_call | solution.py:183
  89.1 2.3 %collective-permute-done.31.refs_12_ = bf16[64,2048]{1,0:T(8,128)(2,1)S(1)} collective-permute-done((bf16[64,2048]{1,0:T(8,128)(2,1)S(1)}, bf16[64,2048]{1,0:T(8,128)(2,1)S(1)}, u32[]{:S(2)}, u32[]{:S(2)}) %collective-permute-start.31) | collective-permute-done | bytes 262176 | tf_op jit(solution)/shard_map/ppermute | solution.py:42
  92.3 3.5 %collective-permute-done.26.refs_20_ = bf16[64,512]{1,0:T(8,128)(2,1)S(1)} collective-permute-done((bf16[64,512]{1,0:T(8,128)(2,1)S(1)}, bf16[64,512]{1,0:T(8,128)(2,1)S(1)}, u32[]{:S(2)}, u32[]{:S(2)}) %collective-permute-start.26) | collective-permute-done | bytes 65568 | tf_op jit(solution)/shard_map/ppermute | solution.py:42
  97.0 1.5 %collective-permute-start.28 = (bf16[64,512]{1,0:T(8,128)(2,1)S(1)}, bf16[64,512]{1,0:T(8,128)(2,1)S(1)}, u32[]{:S(2)}, u32[]{:S(2)}) collective-permute-start(bf16[64,512]{1,0:T(8,128)(2,1)S(1)} %get-tuple-element.108), channel_id=1, source_target_pairs={{0,16},{8,24},{16,0},{24,8},{1,17},{9,25},{17,1},{25,9},{2,18},{10... | collective-permute-start | bytes 196616 | tf_op jit(solution)/shard_map/ppermute | solution.py:42
  98.6 1.6 %shard_map.69.rest_3_.rest_4_ = bf16[672,2048]{1,0:T(8,128)(2,1)S(1)} custom-call(s32[6]{0:T(128)S(1)} %pad_add_fusion.place_ref, bf16[160,2048]{1,0:T(8,128)(2,1)S(1)} %collective-permute-done.17.refs_0_, bf16[176,2048]{1,0:T(8,128)(2,1)S(1)} %collective-permute-done.18.refs_1_, bf16[160,2048]{1,0:T(8,128)(2,1)S(1)} %collective-permute-done.23.refs_2_, ...), custom_call_target="tpu_custom_call" | custom-call | bytes 5505024 | tf_op jit(solution)/shard_map/pallas_call | solution.py:87
  100.2 2.0 %collective-permute-done.28.refs_23_ = bf16[64,512]{1,0:T(8,128)(2,1)S(1)} collective-permute-done((bf16[64,512]{1,0:T(8,128)(2,1)S(1)}, bf16[64,512]{1,0:T(8,128)(2,1)S(1)}, u32[]{:S(2)}, u32[]{:S(2)}) %collective-permute-start.28) | collective-permute-done | bytes 65568 | tf_op jit(solution)/shard_map/ppermute | solution.py:42
  102.2 1.2 collective-permute-start.33
  104.9 1.4 %collective-permute-start.36 = (bf16[64,2048]{1,0:T(8,128)(2,1)S(1)}, bf16[64,2048]{1,0:T(8,128)(2,1)S(1)}, u32[]{:S(2)}, u32[]{:S(2)}) collective-permute-start(bf16[64,2048]{1,0:T(8,128)(2,1)S(1)} %collective-permute-done.20.refs_3_), channel_id=1, source_target_pairs={{0,16},{8,24},{16,0},{24,8},{1,17},{9,25},{17,1},{25,9},{2,18},{10... | collective-permute-start | bytes 786440 | tf_op jit(solution)/shard_map/ppermute | solution.py:42
  106.3 4.3 %shard_map.70 = bf16[192,512]{1,0:T(8,128)(2,1)S(1)} custom-call(s32[6]{0:T(128)S(1)} %pad_add_fusion.place_ref, f32[4,8,256]{2,1,0:T(8,128)S(1)} %pad_maximum_fusion.taps_ref, f32[4,4,128]{2,1,0:T(4,128)S(1)} %maximum_convert_fusion.long_ref, bf16[192,2048]{1,0:T(8,128)(2,1)S(1)} %bitcast.28, bf16[192,2048]{1,0:T(8,128)(2,1)S(1)} %collective-permute-done.11.rest_1_, ...), custom_call_target="tpu_custom_call" | custom-call | flops 3221225472 | bytes 6291456 | tf_op jit(solution)/shard_map/pallas_call | solution.py:183
  112.5 2.8 %collective-permute-done.35.refs_7_ = bf16[64,2048]{1,0:T(8,128)(2,1)S(1)} collective-permute-done((bf16[64,2048]{1,0:T(8,128)(2,1)S(1)}, bf16[64,2048]{1,0:T(8,128)(2,1)S(1)}, u32[]{:S(2)}, u32[]{:S(2)}) %collective-permute-start.35) | collective-permute-done | bytes 262176 | tf_op jit(solution)/shard_map/ppermute | solution.py:42
  115.4 2.4 %collective-permute-done.36.refs_11_ = bf16[64,2048]{1,0:T(8,128)(2,1)S(1)} collective-permute-done((bf16[64,2048]{1,0:T(8,128)(2,1)S(1)}, bf16[64,2048]{1,0:T(8,128)(2,1)S(1)}, u32[]{:S(2)}, u32[]{:S(2)}) %collective-permute-start.36) | collective-permute-done | bytes 262176 | tf_op jit(solution)/shard_map/ppermute | solution.py:42
  117.8 1.3 collective-permute-done.29.refs_25_
  119.1 1.1 collective-permute-start.37
  120.7 5.4 %shard_map.71 = (bf16[64,512]{1,0:T(8,128)(2,1)S(1)}, bf16[64,512]{1,0:T(8,128)(2,1)S(1)}, bf16[64,512]{1,0:T(8,128)(2,1)S(1)}, bf16[64,512]{1,0:T(8,128)(2,1)S(1)}) custom-call(s32[6]{0:T(128)S(1)} %pad_add_fusion.place_ref, f32[4,8,256]{2,1,0:T(8,128)S(1)} %pad_maximum_fusion.taps_ref, f32[4,4,128]{2,1,0:T(4,128)S(1)} %maximum_convert_fusion.long_ref, ...), custom_call_target="tpu_custom_call" | custom-call | flops 4294967296 | bytes 8388608 | tf_op jit(solution)/shard_map/pallas_call | solution.py:183
  126.9 1.7 %collective-permute-start.40 = (bf16[64,512]{1,0:T(8,128)(2,1)S(1)}, bf16[64,512]{1,0:T(8,128)(2,1)S(1)}, u32[]{:S(2)}, u32[]{:S(2)}) collective-permute-start(bf16[64,512]{1,0:T(8,128)(2,1)S(1)} %get-tuple-element.146), channel_id=1, source_target_pairs={{0,16},{8,24},{16,0},{24,8},{1,17},{9,25},{17,1},{25,9},{2,18},{10... | collective-permute-start | bytes 196616 | tf_op jit(solution)/shard_map/ppermute | solution.py:42
  128.6 1.0 collective-permute-start.41
  131.2 2.6 %collective-permute-done.41.refs_26_ = bf16[64,512]{1,0:T(8,128)(2,1)S(1)} collective-permute-done((bf16[64,512]{1,0:T(8,128)(2,1)S(1)}, bf16[64,512]{1,0:T(8,128)(2,1)S(1)}, u32[]{:S(2)}, u32[]{:S(2)}) %collective-permute-start.41) | collective-permute-done | bytes 65568 | tf_op jit(solution)/shard_map/ppermute | solution.py:42
  133.8 1.9 %shard_map.73 = bf16[256,2048]{1,0:T(8,128)(2,1)S(1)} custom-call(s32[6]{0:T(128)S(1)} %pad_add_fusion.place_ref, bf16[64,2048]{1,0:T(8,128)(2,1)S(1)} %copy-done.1, bf16[64,2048]{1,0:T(8,128)(2,1)S(1)} %collective-permute-done.4.refs_1_, bf16[64,2048]{1,0:T(8,128)(2,1)S(1)} %collective-permute-done.12.refs_2_, ...), custom_call_target="tpu_custom_call" | custom-call | flops 2147483648 | bytes 5242880 | tf_op jit(solution)/shard_map/pallas_call | solution.py:243
  135.7 1.9 %shard_map.72 = f32[256,2048]{1,0:T(8,128)S(1)} custom-call(s32[6]{0:T(128)S(1)} %pad_add_fusion.place_ref, bf16[64,2048]{1,0:T(8,128)(2,1)S(1)} %copy-done.1, bf16[64,2048]{1,0:T(8,128)(2,1)S(1)} %collective-permute-done.4.refs_1_, bf16[64,2048]{1,0:T(8,128)(2,1)S(1)} %collective-permute-done.12.refs_2_, ...), custom_call_target="tpu_custom_call" | custom-call | flops 2147483648 | bytes 5242880 | tf_op jit(solution)/shard_map/pallas_call | solution.py:243
  138.4 1.3 add_convert_fusion
  (72 shorter events, 18.8 us)
Async XLA Ops:
  0.0 20.4 %slice-start = ((bf16[256,2048]{1,0:T(8,128)(2,1)}), bf16[96,2048]{1,0:T(8,128)(2,1)S(1)}, s32[]{:S(2)}) async-start(bf16[256,2048]{1,0:T(8,128)(2,1)} %param.6), calls=%async_computation | async-start | bytes 786432 | tf_op jit(solution)/shard_map/slice | solution.py:309
  1.2 25.4 %copy-start = (bf16[3,64,2048]{2,1,0:T(8,128)(2,1)S(1)}, bf16[3,64,2048]{2,1,0:T(8,128)(2,1)}, u32[]{:S(2)}) copy-start(bf16[3,64,2048]{2,1,0:T(8,128)(2,1)} %param.7) | copy-start | bytes 2359300
  1.2 17.8 %collective-permute-start.2 = (bf16[160,2048]{1,0:T(8,128)(2,1)S(1)}, bf16[160,2048]{1,0:T(8,128)(2,1)S(1)}, u32[]{:S(2)}, u32[]{:S(2)}) collective-permute-start(bf16[160,2048]{1,0:T(8,128)(2,1)S(1)} %slice.23.refs_0_), channel_id=1, source_target_pairs={{0,8},{8,0},{16,24},{24,16},{1,9},{9,1},{17,25},{25,17},{2,10},{10... | collective-permute-start | bytes 1966088 | tf_op jit(solution)/shard_map/ppermute | solution.py:42
  4.2 16.2 %collective-permute-start.3 = (bf16[160,2048]{1,0:T(8,128)(2,1)S(1)}, bf16[160,2048]{1,0:T(8,128)(2,1)S(1)}, u32[]{:S(2)}, u32[]{:S(2)}) collective-permute-start(bf16[160,2048]{1,0:T(8,128)(2,1)S(1)} %slice.23.refs_0_), channel_id=1, source_target_pairs={{0,16},{8,24},{16,0},{24,8},{1,17},{9,25},{17,1},{25,9},{2,18},{10... | collective-permute-start | bytes 1966088 | tf_op jit(solution)/shard_map/ppermute | solution.py:42
  7.7 8.8 %collective-permute-start = (bf16[80,2048]{1,0:T(8,128)(2,1)}, bf16[80,2048]{1,0:T(8,128)(2,1)}, u32[]{:S(2)}, u32[]{:S(2)}) collective-permute-start(bf16[80,2048]{1,0:T(8,128)(2,1)} %get-tuple-element.150), channel_id=1, source_target_pairs={{1,2},{3,4},{5,6},{9,10},{11,12},{13,14},{17,18},{19,20},{21,22},{... | collective-permute-start | bytes 983048 | tf_op jit(solution)/shard_map/ppermute | solution.py:300
  9.1 7.5 %collective-permute-start.1 = (bf16[80,2048]{1,0:T(8,128)(2,1)}, bf16[80,2048]{1,0:T(8,128)(2,1)}, u32[]{:S(2)}, u32[]{:S(2)}) collective-permute-start(bf16[80,2048]{1,0:T(8,128)(2,1)} %get-tuple-element.149), channel_id=1, source_target_pairs={{1,3},{3,5},{5,7},{9,11},{11,13},{13,15},{17,19},{19,21},{21,23},{... | collective-permute-start | bytes 983048 | tf_op jit(solution)/shard_map/ppermute | solution.py:300
  10.5 8.6 %collective-permute-start.4 = (bf16[64,2048]{1,0:T(8,128)(2,1)}, bf16[64,2048]{1,0:T(8,128)(2,1)S(1)}, u32[]{:S(2)}, u32[]{:S(2)}) collective-permute-start(bf16[64,2048]{1,0:T(8,128)(2,1)} %refs_0_.1), channel_id=1, source_target_pairs={{0,2},{2,6},{6,4},{4,0},{1,3},{3,7},{7,5},{5,1},{8,10},{10,14},{14... | collective-permute-start | bytes 786440 | tf_op jit(solution)/shard_map/ppermute | solution.py:291
  20.4 6.2 %collective-permute-start.5 = (bf16[160,2048]{1,0:T(8,128)(2,1)S(1)}, bf16[160,2048]{1,0:T(8,128)(2,1)S(1)}, u32[]{:S(2)}, u32[]{:S(2)}) collective-permute-start(bf16[160,2048]{1,0:T(8,128)(2,1)S(1)} %slice.23.refs_0_), channel_id=1, source_target_pairs={{0,1},{1,0},{2,3},{3,2},{4,5},{5,4},{6,7},{7,6},{8,9},{9,8},{10,11... | collective-permute-start | bytes 1966088 | tf_op jit(solution)/shard_map/ppermute | solution.py:37
  24.9 9.9 %copy-start.1 = (bf16[64,2048]{1,0:T(8,128)(2,1)S(1)}, bf16[64,2048]{1,0:T(8,128)(2,1)}, u32[]{:S(2)}) copy-start(bf16[64,2048]{1,0:T(8,128)(2,1)} %refs_0_.1) | copy-start | bytes 786436
  24.9 3.8 %collective-permute-start.6 = (bf16[176,2048]{1,0:T(8,128)(2,1)S(1)}, bf16[176,2048]{1,0:T(8,128)(2,1)S(1)}, u32[]{:S(2)}, u32[]{:S(2)}) collective-permute-start(bf16[176,2048]{1,0:T(8,128)(2,1)S(1)} %constant_dynamic-update-slice_fusion.refs_1_), channel_id=1, source_target_pairs={{0,1},{1,0},{2,3},{3,2},{4,5},{5,4},{6,7},{7,6},{8,9},{9,8},{10,11... | collective-permute-start | bytes 2162696 | tf_op jit(solution)/shard_map/ppermute | solution.py:37
  25.0 19.0 %collective-permute-start.7 = (bf16[176,2048]{1,0:T(8,128)(2,1)S(1)}, bf16[176,2048]{1,0:T(8,128)(2,1)S(1)}, u32[]{:S(2)}, u32[]{:S(2)}) collective-permute-start(bf16[176,2048]{1,0:T(8,128)(2,1)S(1)} %constant_dynamic-update-slice_fusion.refs_1_), channel_id=1, source_target_pairs={{0,8},{8,0},{16,24},{24,16},{1,9},{9,1},{17,25},{25,17},{2,10},{10... | collective-permute-start | bytes 2162696 | tf_op jit(solution)/shard_map/ppermute | solution.py:42
  25.6 5.2 %collective-permute-start.9 = (bf16[160,2048]{1,0:T(8,128)(2,1)S(1)}, bf16[160,2048]{1,0:T(8,128)(2,1)S(1)}, u32[]{:S(2)}, u32[]{:S(2)}) collective-permute-start(bf16[160,2048]{1,0:T(8,128)(2,1)S(1)} %collective-permute-done.2.refs_0_), channel_id=1, source_target_pairs={{0,1},{1,0},{2,3},{3,2},{4,5},{5,4},{6,7},{7,6},{8,9},{9,8},{10,11... | collective-permute-start | bytes 1966088 | tf_op jit(solution)/shard_map/ppermute | solution.py:37
  25.8 9.0 %collective-permute-start.10 = (bf16[160,2048]{1,0:T(8,128)(2,1)S(1)}, bf16[160,2048]{1,0:T(8,128)(2,1)S(1)}, u32[]{:S(2)}, u32[]{:S(2)}) collective-permute-start(bf16[160,2048]{1,0:T(8,128)(2,1)S(1)} %collective-permute-done.3.refs_0_), channel_id=1, source_target_pairs={{0,1},{1,0},{2,3},{3,2},{4,5},{5,4},{6,7},{7,6},{8,9},{9,8},{10,11... | collective-permute-start | bytes 1966088 | tf_op jit(solution)/shard_map/ppermute | solution.py:37
  26.6 21.3 %collective-permute-start.11 = (bf16[192,2048]{1,0:T(8,128)(2,1)S(1)}, bf16[192,2048]{1,0:T(8,128)(2,1)S(1)}, u32[]{:S(2)}, u32[]{:S(2)}) collective-permute-start(bf16[192,2048]{1,0:T(8,128)(2,1)S(1)} %bitcast.26), channel_id=1, source_target_pairs={{0,2},{2,6},{6,4},{4,0},{1,3},{3,7},{7,5},{5,1},{8,10},{10,14},{14... | collective-permute-start | bytes 2359304 | tf_op jit(solution)/shard_map/ppermute | solution.py:291
  28.7 19.0 %collective-permute-start.8 = (bf16[176,2048]{1,0:T(8,128)(2,1)S(1)}, bf16[176,2048]{1,0:T(8,128)(2,1)S(1)}, u32[]{:S(2)}, u32[]{:S(2)}) collective-permute-start(bf16[176,2048]{1,0:T(8,128)(2,1)S(1)} %constant_dynamic-update-slice_fusion.refs_1_), channel_id=1, source_target_pairs={{0,16},{8,24},{16,0},{24,8},{1,17},{9,25},{17,1},{25,9},{2,18},{10... | collective-permute-start | bytes 2162696 | tf_op jit(solution)/shard_map/ppermute | solution.py:42
  30.8 22.1 %collective-permute-start.12 = (bf16[64,2048]{1,0:T(8,128)(2,1)S(1)}, bf16[64,2048]{1,0:T(8,128)(2,1)S(1)}, u32[]{:S(2)}, u32[]{:S(2)}) collective-permute-start(bf16[64,2048]{1,0:T(8,128)(2,1)S(1)} %collective-permute-done.4.refs_1_), channel_id=1, source_target_pairs={{0,2},{2,6},{6,4},{4,0},{1,3},{3,7},{7,5},{5,1},{8,10},{10,14},{14... | collective-permute-start | bytes 786440 | tf_op jit(solution)/shard_map/ppermute | solution.py:291
  34.8 18.2 %collective-permute-start.13 = (bf16[64,2048]{1,0:T(8,128)(2,1)S(1)}, bf16[64,2048]{1,0:T(8,128)(2,1)S(1)}, u32[]{:S(2)}, u32[]{:S(2)}) collective-permute-start(bf16[64,2048]{1,0:T(8,128)(2,1)S(1)} %copy-done.1), channel_id=1, source_target_pairs={{0,8},{8,0},{16,24},{24,16},{1,9},{9,1},{17,25},{25,17},{2,10},{10... | collective-permute-start | bytes 786440 | tf_op jit(solution)/shard_map/ppermute | solution.py:42
  44.0 8.9 %collective-permute-start.14 = (bf16[64,2048]{1,0:T(8,128)(2,1)S(1)}, bf16[64,2048]{1,0:T(8,128)(2,1)S(1)}, u32[]{:S(2)}, u32[]{:S(2)}) collective-permute-start(bf16[64,2048]{1,0:T(8,128)(2,1)S(1)} %copy-done.1), channel_id=1, source_target_pairs={{0,16},{8,24},{16,0},{24,8},{1,17},{9,25},{17,1},{25,9},{2,18},{10... | collective-permute-start | bytes 786440 | tf_op jit(solution)/shard_map/ppermute | solution.py:42
  52.9 7.0 %collective-permute-start.16 = (bf16[176,2048]{1,0:T(8,128)(2,1)S(1)}, bf16[176,2048]{1,0:T(8,128)(2,1)S(1)}, u32[]{:S(2)}, u32[]{:S(2)}) collective-permute-start(bf16[176,2048]{1,0:T(8,128)(2,1)S(1)} %collective-permute-done.8.refs_1_), channel_id=1, source_target_pairs={{0,1},{1,0},{2,3},{3,2},{4,5},{5,4},{6,7},{7,6},{8,9},{9,8},{10,11... | collective-permute-start | bytes 2162696 | tf_op jit(solution)/shard_map/ppermute | solution.py:37
  52.9 9.4 %collective-permute-start.15 = (bf16[176,2048]{1,0:T(8,128)(2,1)S(1)}, bf16[176,2048]{1,0:T(8,128)(2,1)S(1)}, u32[]{:S(2)}, u32[]{:S(2)}) collective-permute-start(bf16[176,2048]{1,0:T(8,128)(2,1)S(1)} %collective-permute-done.7.refs_1_), channel_id=1, source_target_pairs={{0,1},{1,0},{2,3},{3,2},{4,5},{5,4},{6,7},{7,6},{8,9},{9,8},{10,11... | collective-permute-start | bytes 2162696 | tf_op jit(solution)/shard_map/ppermute | solution.py:37
  53.5 11.8 %collective-permute-start.20 = (bf16[64,2048]{1,0:T(8,128)(2,1)S(1)}, bf16[64,2048]{1,0:T(8,128)(2,1)S(1)}, u32[]{:S(2)}, u32[]{:S(2)}) collective-permute-start(bf16[64,2048]{1,0:T(8,128)(2,1)S(1)} %collective-permute-done.12.refs_2_), channel_id=1, source_target_pairs={{0,2},{2,6},{6,4},{4,0},{1,3},{3,7},{7,5},{5,1},{8,10},{10,14},{14... | collective-permute-start | bytes 786440 | tf_op jit(solution)/shard_map/ppermute | solution.py:291
  56.8 25.8 %collective-permute-start.19 = (bf16[192,2048]{1,0:T(8,128)(2,1)S(1)}, bf16[192,2048]{1,0:T(8,128)(2,1)S(1)}, u32[]{:S(2)}, u32[]{:S(2)}) collective-permute-start(bf16[192,2048]{1,0:T(8,128)(2,1)S(1)} %collective-permute-done.11.rest_1_), channel_id=1, source_target_pairs={{0,2},{2,6},{6,4},{4,0},{1,3},{3,7},{7,5},{5,1},{8,10},{10,14},{14... | collective-permute-start | bytes 2359304 | tf_op jit(solution)/shard_map/ppermute | solution.py:291
  59.4 23.2 %collective-permute-start.18 = (bf16[176,2048]{1,0:T(8,128)(2,1)S(1)}, bf16[176,2048]{1,0:T(8,128)(2,1)S(1)}, u32[]{:S(2)}, u32[]{:S(2)}) collective-permute-start(bf16[176,2048]{1,0:T(8,128)(2,1)S(1)} %collective-permute-done.7.refs_1_), channel_id=1, source_target_pairs={{0,16},{8,24},{16,0},{24,8},{1,17},{9,25},{17,1},{25,9},{2,18},{10... | collective-permute-start | bytes 2162696 | tf_op jit(solution)/shard_map/ppermute | solution.py:42
  59.9 22.7 %collective-permute-start.17 = (bf16[160,2048]{1,0:T(8,128)(2,1)S(1)}, bf16[160,2048]{1,0:T(8,128)(2,1)S(1)}, u32[]{:S(2)}, u32[]{:S(2)}) collective-permute-start(bf16[160,2048]{1,0:T(8,128)(2,1)S(1)} %collective-permute-done.3.refs_0_), channel_id=1, source_target_pairs={{0,8},{8,0},{16,24},{24,16},{1,9},{9,1},{17,25},{25,17},{2,10},{10... | collective-permute-start | bytes 1966088 | tf_op jit(solution)/shard_map/ppermute | solution.py:42
  62.4 19.1 %collective-permute-start.21 = (bf16[64,2048]{1,0:T(8,128)(2,1)S(1)}, bf16[64,2048]{1,0:T(8,128)(2,1)S(1)}, u32[]{:S(2)}, u32[]{:S(2)}) collective-permute-start(bf16[64,2048]{1,0:T(8,128)(2,1)S(1)} %collective-permute-done.4.refs_1_), channel_id=1, source_target_pairs={{0,8},{8,0},{16,24},{24,16},{1,9},{9,1},{17,25},{25,17},{2,10},{10... | collective-permute-start | bytes 786440 | tf_op jit(solution)/shard_map/ppermute | solution.py:42
  65.3 17.3 %collective-permute-start.22 = (bf16[64,2048]{1,0:T(8,128)(2,1)S(1)}, bf16[64,2048]{1,0:T(8,128)(2,1)S(1)}, u32[]{:S(2)}, u32[]{:S(2)}) collective-permute-start(bf16[64,2048]{1,0:T(8,128)(2,1)S(1)} %collective-permute-done.4.refs_1_), channel_id=1, source_target_pairs={{0,16},{8,24},{16,0},{24,8},{1,17},{9,25},{17,1},{25,9},{2,18},{10... | collective-permute-start | bytes 786440 | tf_op jit(solution)/shard_map/ppermute | solution.py:42
  82.6 14.4 %collective-permute-start.24 = (bf16[176,2048]{1,0:T(8,128)(2,1)S(1)}, bf16[176,2048]{1,0:T(8,128)(2,1)S(1)}, u32[]{:S(2)}, u32[]{:S(2)}) collective-permute-start(bf16[176,2048]{1,0:T(8,128)(2,1)S(1)} %collective-permute-done.18.refs_1_), channel_id=1, source_target_pairs={{0,1},{1,0},{2,3},{3,2},{4,5},{5,4},{6,7},{7,6},{8,9},{9,8},{10,11... | collective-permute-start | bytes 2162696 | tf_op jit(solution)/shard_map/ppermute | solution.py:37
  82.7 13.8 %collective-permute-start.23 = (bf16[160,2048]{1,0:T(8,128)(2,1)S(1)}, bf16[160,2048]{1,0:T(8,128)(2,1)S(1)}, u32[]{:S(2)}, u32[]{:S(2)}) collective-permute-start(bf16[160,2048]{1,0:T(8,128)(2,1)S(1)} %collective-permute-done.17.refs_0_), channel_id=1, source_target_pairs={{0,1},{1,0},{2,3},{3,2},{4,5},{5,4},{6,7},{7,6},{8,9},{9,8},{10,11... | collective-permute-start | bytes 1966088 | tf_op jit(solution)/shard_map/ppermute | solution.py:37
  83.2 8.3 %collective-permute-start.31 = (bf16[64,2048]{1,0:T(8,128)(2,1)S(1)}, bf16[64,2048]{1,0:T(8,128)(2,1)S(1)}, u32[]{:S(2)}, u32[]{:S(2)}) collective-permute-start(bf16[64,2048]{1,0:T(8,128)(2,1)S(1)} %collective-permute-done.14.refs_8_), channel_id=1, source_target_pairs={{0,8},{8,0},{16,24},{24,16},{1,9},{9,1},{17,25},{25,17},{2,10},{10... | collective-permute-start | bytes 786440 | tf_op jit(solution)/shard_map/ppermute | solution.py:42
  84.0 33.8 %collective-permute-start.30 = (bf16[192,2048]{1,0:T(8,128)(2,1)S(1)}, bf16[192,2048]{1,0:T(8,128)(2,1)S(1)}, u32[]{:S(2)}, u32[]{:S(2)}) collective-permute-start(bf16[192,2048]{1,0:T(8,128)(2,1)S(1)} %collective-permute-done.19.rest_0_.rest_2_), channel_id=1, source_target_pairs={{0,2},{2,6},{6,4},{4,0},{1,3},{3,7},{7,5},{5,1},{8,10},{10,14},{14... | collective-permute-start | bytes 2359304 | tf_op jit(solution)/shard_map/ppermute | solution.py:291
  84.3 20.6 %collective-permute-start.32 = (bf16[64,2048]{1,0:T(8,128)(2,1)S(1)}, bf16[64,2048]{1,0:T(8,128)(2,1)S(1)}, u32[]{:S(2)}, u32[]{:S(2)}) collective-permute-start(bf16[64,2048]{1,0:T(8,128)(2,1)S(1)} %collective-permute-done.21.refs_5_), channel_id=1, source_target_pairs={{0,16},{8,24},{16,0},{24,8},{1,17},{9,25},{17,1},{25,9},{2,18},{10... | collective-permute-start | bytes 786440 | tf_op jit(solution)/shard_map/ppermute | solution.py:42
  91.5 4.3 %collective-permute-start.26 = (bf16[64,512]{1,0:T(8,128)(2,1)S(1)}, bf16[64,512]{1,0:T(8,128)(2,1)S(1)}, u32[]{:S(2)}, u32[]{:S(2)}) collective-permute-start(bf16[64,512]{1,0:T(8,128)(2,1)S(1)} %get-tuple-element.107), channel_id=1, source_target_pairs={{0,8},{8,0},{16,24},{24,16},{1,9},{9,1},{17,25},{25,17},{2,10},{10... | collective-permute-start | bytes 196616 | tf_op jit(solution)/shard_map/ppermute | solution.py:42
  95.7 7.7 %collective-permute-start.25 = (bf16[128,512]{1,0:T(8,128)(2,1)S(1)}, bf16[128,512]{1,0:T(8,128)(2,1)S(1)}, u32[]{:S(2)}, u32[]{:S(2)}) collective-permute-start(bf16[128,512]{1,0:T(8,128)(2,1)S(1)} %get-tuple-element.113), channel_id=1, source_target_pairs={{0,8},{8,0},{16,24},{24,16},{1,9},{9,1},{17,25},{25,17},{2,10},{10... | collective-permute-start | bytes 393224 | tf_op jit(solution)/shard_map/ppermute | solution.py:42
  96.5 7.5 %collective-permute-start.27 = (bf16[128,512]{1,0:T(8,128)(2,1)S(1)}, bf16[128,512]{1,0:T(8,128)(2,1)S(1)}, u32[]{:S(2)}, u32[]{:S(2)}) collective-permute-start(bf16[128,512]{1,0:T(8,128)(2,1)S(1)} %get-tuple-element.114), channel_id=1, source_target_pairs={{0,16},{8,24},{16,0},{24,8},{1,17},{9,25},{17,1},{25,9},{2,18},{10... | collective-permute-start | bytes 393224 | tf_op jit(solution)/shard_map/ppermute | solution.py:42
  97.0 5.2 %collective-permute-start.28 = (bf16[64,512]{1,0:T(8,128)(2,1)S(1)}, bf16[64,512]{1,0:T(8,128)(2,1)S(1)}, u32[]{:S(2)}, u32[]{:S(2)}) collective-permute-start(bf16[64,512]{1,0:T(8,128)(2,1)S(1)} %get-tuple-element.108), channel_id=1, source_target_pairs={{0,16},{8,24},{16,0},{24,8},{1,17},{9,25},{17,1},{25,9},{2,18},{10... | collective-permute-start | bytes 196616 | tf_op jit(solution)/shard_map/ppermute | solution.py:42
  102.2 9.2 %collective-permute-start.33 = (bf16[64,2048]{1,0:T(8,128)(2,1)S(1)}, bf16[64,2048]{1,0:T(8,128)(2,1)S(1)}, u32[]{:S(2)}, u32[]{:S(2)}) collective-permute-start(bf16[64,2048]{1,0:T(8,128)(2,1)S(1)} %collective-permute-done.12.refs_2_), channel_id=1, source_target_pairs={{0,8},{8,0},{16,24},{24,16},{1,9},{9,1},{17,25},{25,17},{2,10},{10... | collective-permute-start | bytes 786440 | tf_op jit(solution)/shard_map/ppermute | solution.py:42
  103.4 9.1 %collective-permute-start.34 = (bf16[64,2048]{1,0:T(8,128)(2,1)S(1)}, bf16[64,2048]{1,0:T(8,128)(2,1)S(1)}, u32[]{:S(2)}, u32[]{:S(2)}) collective-permute-start(bf16[64,2048]{1,0:T(8,128)(2,1)S(1)} %collective-permute-done.12.refs_2_), channel_id=1, source_target_pairs={{0,16},{8,24},{16,0},{24,8},{1,17},{9,25},{17,1},{25,9},{2,18},{10... | collective-permute-start | bytes 786440 | tf_op jit(solution)/shard_map/ppermute | solution.py:42
  104.1 11.3 %collective-permute-start.35 = (bf16[64,2048]{1,0:T(8,128)(2,1)S(1)}, bf16[64,2048]{1,0:T(8,128)(2,1)S(1)}, u32[]{:S(2)}, u32[]{:S(2)}) collective-permute-start(bf16[64,2048]{1,0:T(8,128)(2,1)S(1)} %collective-permute-done.20.refs_3_), channel_id=1, source_target_pairs={{0,8},{8,0},{16,24},{24,16},{1,9},{9,1},{17,25},{25,17},{2,10},{10... | collective-permute-start | bytes 786440 | tf_op jit(solution)/shard_map/ppermute | solution.py:42
  104.9 12.9 %collective-permute-start.36 = (bf16[64,2048]{1,0:T(8,128)(2,1)S(1)}, bf16[64,2048]{1,0:T(8,128)(2,1)S(1)}, u32[]{:S(2)}, u32[]{:S(2)}) collective-permute-start(bf16[64,2048]{1,0:T(8,128)(2,1)S(1)} %collective-permute-done.20.refs_3_), channel_id=1, source_target_pairs={{0,16},{8,24},{16,0},{24,8},{1,17},{9,25},{17,1},{25,9},{2,18},{10... | collective-permute-start | bytes 786440 | tf_op jit(solution)/shard_map/ppermute | solution.py:42
  111.4 7.6 %collective-permute-start.29 = (bf16[192,512]{1,0:T(8,128)(2,1)S(1)}, bf16[192,512]{1,0:T(8,128)(2,1)S(1)}, u32[]{:S(2)}, u32[]{:S(2)}) collective-permute-start(bf16[192,512]{1,0:T(8,128)(2,1)S(1)} %shard_map.70), channel_id=1, source_target_pairs={{0,24},{8,16},{16,8},{24,0},{1,25},{9,17},{17,9},{25,1},{2,26},{10... | collective-permute-start | bytes 589832 | tf_op jit(solution)/shard_map/ppermute | solution.py:42
  119.1 14.7 %collective-permute-start.37 = (bf16[64,2048]{1,0:T(8,128)(2,1)S(1)}, bf16[64,2048]{1,0:T(8,128)(2,1)S(1)}, u32[]{:S(2)}, u32[]{:S(2)}) collective-permute-start(bf16[64,2048]{1,0:T(8,128)(2,1)S(1)} %collective-permute-done.34.refs_10_), channel_id=1, source_target_pairs={{0,8},{8,0},{16,24},{24,16},{1,9},{9,1},{17,25},{25,17},{2,10},{10... | collective-permute-start | bytes 786440 | tf_op jit(solution)/shard_map/ppermute | solution.py:42
  120.2 13.5 %collective-permute-start.38 = (bf16[64,2048]{1,0:T(8,128)(2,1)S(1)}, bf16[64,2048]{1,0:T(8,128)(2,1)S(1)}, u32[]{:S(2)}, u32[]{:S(2)}) collective-permute-start(bf16[64,2048]{1,0:T(8,128)(2,1)S(1)} %collective-permute-done.35.refs_7_), channel_id=1, source_target_pairs={{0,16},{8,24},{16,0},{24,8},{1,17},{9,25},{17,1},{25,9},{2,18},{10... | collective-permute-start | bytes 786440 | tf_op jit(solution)/shard_map/ppermute | solution.py:42
  126.1 4.3 %collective-permute-start.39 = (bf16[64,512]{1,0:T(8,128)(2,1)S(1)}, bf16[64,512]{1,0:T(8,128)(2,1)S(1)}, u32[]{:S(2)}, u32[]{:S(2)}) collective-permute-start(bf16[64,512]{1,0:T(8,128)(2,1)S(1)} %get-tuple-element.143), channel_id=1, source_target_pairs={{0,8},{8,0},{16,24},{24,16},{1,9},{9,1},{17,25},{25,17},{2,10},{10... | collective-permute-start | bytes 196616 | tf_op jit(solution)/shard_map/ppermute | solution.py:42
  126.9 4.3 %collective-permute-start.40 = (bf16[64,512]{1,0:T(8,128)(2,1)S(1)}, bf16[64,512]{1,0:T(8,128)(2,1)S(1)}, u32[]{:S(2)}, u32[]{:S(2)}) collective-permute-start(bf16[64,512]{1,0:T(8,128)(2,1)S(1)} %get-tuple-element.146), channel_id=1, source_target_pairs={{0,16},{8,24},{16,0},{24,8},{1,17},{9,25},{17,1},{25,9},{2,18},{10... | collective-permute-start | bytes 196616 | tf_op jit(solution)/shard_map/ppermute | solution.py:42
  128.6 5.2 %collective-permute-start.41 = (bf16[64,512]{1,0:T(8,128)(2,1)S(1)}, bf16[64,512]{1,0:T(8,128)(2,1)S(1)}, u32[]{:S(2)}, u32[]{:S(2)}) collective-permute-start(bf16[64,512]{1,0:T(8,128)(2,1)S(1)} %get-tuple-element.148), channel_id=1, source_target_pairs={{0,24},{8,16},{16,8},{24,0},{1,25},{9,17},{17,9},{25,1},{2,26},{10... | collective-permute-start | bytes 196616 | tf_op jit(solution)/shard_map/ppermute | solution.py:42
  135.7 2.7 %collective-permute-start.42 = (bf16[256,2048]{1,0:T(8,128)(2,1)S(1)}, bf16[256,2048]{1,0:T(8,128)(2,1)S(1)}, u32[]{:S(2)}, u32[]{:S(2)}) collective-permute-start(bf16[256,2048]{1,0:T(8,128)(2,1)S(1)} %shard_map.73), channel_id=1, source_target_pairs={{0,1},{1,0},{2,3},{3,2},{4,5},{5,4},{6,7},{7,6},{8,9},{9,8},{10,11... | collective-permute-start | bytes 3145736 | tf_op jit(solution)/shard_map/ppermute | solution.py:37

commit v9 on v8

--- a/solution.py
+++ b/solution.py
@@ -331,7 +331,8 @@
         x1 = lay(place, rows, parts, [low_x, high_x, low_x_twin, swap(high_x)])
         x2 = lay(place, rows, parts, [low_y, high_y, low_y_twin, swap(high_y)])
         mix01 = run_mix((0, 1), (x0, x1, x2))
-        mix01, far_x, far_y, ws, vs, v1 = tie(mix01, far_x, far_y, ws, vs, v1)
+        moved = [[across(mix01[r], r)] for r in (1, 2)]
+        mix01, moved, far_x, far_y, ws, vs, v1 = tie(mix01, moved, far_x, far_y, ws, vs, v1)
 
         ws = [*ws, forward(ws[2])]
         v0, v1 = [*v0, across(v0[2], 1)], [*v1, across(v1[1], 2)]
@@ -339,8 +340,8 @@
         x3 = lay(place, rows, parts, [far_x, far_y, swap(far_x), swap(far_y)])
         mix2 = run_mix((2,), (x0, x1, x2))
         far = run_mix((0, 1, 2), (x3,))
-        moved = [[across(mix01[r], r), across(mix2[r], r)] for r in (1, 2)] + [across(far[0], 3)]
-        mix2, far, moved, ws, v0, v1, v2, v3 = tie(mix2, far, moved, ws, v0, v1, v2, v3)
+        moved = [[*moved[r - 1], across(mix2[r], r)] for r in (1, 2)] + [across(far[0], 3)]
+        mix2, far, moved, ws, v0, v1 = tie(mix2, far, moved, ws, v0, v1)
 
         v2, v3 = [*v2, across(v2[2], 1)], [*v3, across(v3[1], 2)]
         mix3 = run_mix((3,), (x0, x1, x2, x3))

time: 140 us -> 137 us (0.979)
  waiting for transfers between devices: 48.8 us -> 43.5 us
  starting transfers between devices: 48.6 us -> 50.5 us
    ppermute x26, waiting for transfers between devices: 41 us -> 34.6 us  [across(): return lax.ppermute(block, 'dp', [(i, i ^ r) for i in range(count)])]
    ppermute x26, starting transfers between devices: 25.9 us -> 27.8 us  [across(): return lax.ppermute(block, 'dp', [(i, i ^ r) for i in range(count)])]
  transfers between devices with their start and end apart: 43 -> 43, of which waited for: 21 -> 17; matrix products, arithmetic and copies ran while one was open for 6% -> 6% of each run, Pallas kernels for 21% -> 22%
where the time goes in v9:
time: 137 us; the launch traced here: 136 us
  starting transfers between devices  50.5 us (37%)
  waiting for transfers between devices  43.5 us (32%)
  Pallas kernels  31.9 us (23%)
  local copies, waits for them, and re-layouts  7.6 us (6%)
  other arithmetic  2.61 us (2%)
    ppermute x26, waiting for transfers between devices, across(): return lax.ppermute(block, 'dp', [(i, i ^ r) for i in range(count)])  34.6 us
    ppermute x26, starting transfers between devices, across(): return lax.ppermute(block, 'dp', [(i, i ^ r) for i in range(count)])  27.8 us
    pallas_call x4, Pallas kernels, mix_chunks(): pl.pallas_call(functools.partial(mix_kernel, steps, slots), out_shape=[ja...  21.6 us
    ppermute x6, starting transfers between devices, shards(): forward = lambda block: lax.ppermute(block, 'z', ring)  13.8 us
    ppermute x6, waiting for transfers between devices, shards(): forward = lambda block: lax.ppermute(block, 'z', ring)  6.56 us
    pallas_call x4, Pallas kernels, lay(): pl.pallas_call(functools.partial(lay_kernel, parts), out_shape=jax.ShapeD...  6.47 us
    ppermute x9, starting transfers between devices, swap(): return lax.ppermute(block, 'core', [(0, 1), (1, 0)])  6.11 us
    pallas_call x2, Pallas kernels, project(): pl.pallas_call(functools.partial(out_kernel, mirror, order, width, counts...  3.81 us
  transfers between devices with their start and end apart: 43, of which 17 were waited for; matrix products, arithmetic and copies ran while one was open for 6% of the time, Pallas kernels for 22%

profile of v9, /device:TPU:0, one launch (start us, length us, event | category | flops | bytes accessed | tf_op | source)
XLA Modules:
  0.0 136.4 jit_solution(15209175094998586019)
XLA Ops:
  0.0 1.2 slice.23.refs_0_
  1.2 3.0 %collective-permute-start.2 = (bf16[160,2048]{1,0:T(8,128)(2,1)S(1)}, bf16[160,2048]{1,0:T(8,128)(2,1)S(1)}, u32[]{:S(2)}, u32[]{:S(2)}) collective-permute-start(bf16[160,2048]{1,0:T(8,128)(2,1)S(1)} %slice.23.refs_0_), channel_id=1, source_target_pairs={{0,8},{8,0},{16,24},{24,16},{1,9},{9,1},{17,25},{25,17},{2,10},{10... | collective-permute-start | bytes 1966088 | tf_op jit(solution)/shard_map/ppermute | solution.py:42
  4.2 1.5 %collective-permute-start.3 = (bf16[160,2048]{1,0:T(8,128)(2,1)S(1)}, bf16[160,2048]{1,0:T(8,128)(2,1)S(1)}, u32[]{:S(2)}, u32[]{:S(2)}) collective-permute-start(bf16[160,2048]{1,0:T(8,128)(2,1)S(1)} %slice.23.refs_0_), channel_id=1, source_target_pairs={{0,16},{8,24},{16,0},{24,8},{1,17},{9,25},{17,1},{25,9},{2,18},{10... | collective-permute-start | bytes 1966088 | tf_op jit(solution)/shard_map/ppermute | solution.py:42
  5.7 2.0 %fusion.5 = (bf16[80,2048]{1,0:T(8,128)(2,1)}, bf16[80,2048]{1,0:T(8,128)(2,1)}) fusion(bf16[256,2048]{1,0:T(8,128)(2,1)} %param.6), kind=kLoop, calls=%fused_computation.22 | loop fusion | bytes 1310720 | tf_op jit(solution)/shard_map/slice | solution.py:301
  7.7 1.4 %collective-permute-start = (bf16[80,2048]{1,0:T(8,128)(2,1)}, bf16[80,2048]{1,0:T(8,128)(2,1)}, u32[]{:S(2)}, u32[]{:S(2)}) collective-permute-start(bf16[80,2048]{1,0:T(8,128)(2,1)} %get-tuple-element.138), channel_id=1, source_target_pairs={{1,2},{3,4},{5,6},{9,10},{11,12},{13,14},{17,18},{19,20},{21,22},{... | collective-permute-start | bytes 983048 | tf_op jit(solution)/shard_map/ppermute | solution.py:300
  9.1 1.4 %collective-permute-start.1 = (bf16[80,2048]{1,0:T(8,128)(2,1)}, bf16[80,2048]{1,0:T(8,128)(2,1)}, u32[]{:S(2)}, u32[]{:S(2)}) collective-permute-start(bf16[80,2048]{1,0:T(8,128)(2,1)} %get-tuple-element.137), channel_id=1, source_target_pairs={{1,3},{3,5},{5,7},{9,11},{11,13},{13,15},{17,19},{19,21},{21,23},{... | collective-permute-start | bytes 983048 | tf_op jit(solution)/shard_map/ppermute | solution.py:300
  10.5 1.5 %collective-permute-start.4 = (bf16[64,2048]{1,0:T(8,128)(2,1)}, bf16[64,2048]{1,0:T(8,128)(2,1)S(1)}, u32[]{:S(2)}, u32[]{:S(2)}) collective-permute-start(bf16[64,2048]{1,0:T(8,128)(2,1)} %refs_0_.1), channel_id=1, source_target_pairs={{0,2},{2,6},{6,4},{4,0},{1,3},{3,7},{7,5},{5,1},{8,10},{10,14},{14... | collective-permute-start | bytes 786440 | tf_op jit(solution)/shard_map/ppermute | solution.py:291
  12.0 1.9 %reshape.10 = f32[7,3,16,2,64]{4,3,2,0,1:T(2,128)} reshape(f32[7,3,2048]{2,0,1:T(8,128)} %param.8) | data formatting | bytes 344064 | tf_op jit(solution)/shard_map/reshape | solution.py:263
  13.9 0.9 constant_dynamic-slice_fusion.5
  16.6 1.2 add.55
  17.7 1.3 collective-permute-done.4.refs_1_
  19.0 1.4 collective-permute-done.3.refs_0_
  20.5 4.4 %collective-permute-start.6 = (bf16[176,2048]{1,0:T(8,128)(2,1)S(1)}, bf16[176,2048]{1,0:T(8,128)(2,1)S(1)}, u32[]{:S(2)}, u32[]{:S(2)}) collective-permute-start(bf16[176,2048]{1,0:T(8,128)(2,1)S(1)} %constant_dynamic-update-slice_fusion.refs_1_), channel_id=1, source_target_pairs={{0,1},{1,0},{2,3},{3,2},{4,5},{5,4},{6,7},{7,6},{8,9},{9,8},{10,11... | collective-permute-start | bytes 2162696 | tf_op jit(solution)/shard_map/ppermute | solution.py:37
  26.0 1.6 %collective-permute-done.5.refs_2_ = bf16[160,2048]{1,0:T(8,128)(2,1)S(1)} collective-permute-done((bf16[160,2048]{1,0:T(8,128)(2,1)S(1)}, bf16[160,2048]{1,0:T(8,128)(2,1)S(1)}, u32[]{:S(2)}, u32[]{:S(2)}) %collective-permute-start.5) | collective-permute-done | bytes 655392 | tf_op jit(solution)/shard_map/ppermute | solution.py:37
  27.7 2.1 %collective-permute-start.11 = (bf16[192,2048]{1,0:T(8,128)(2,1)S(1)}, bf16[192,2048]{1,0:T(8,128)(2,1)S(1)}, u32[]{:S(2)}, u32[]{:S(2)}) collective-permute-start(bf16[192,2048]{1,0:T(8,128)(2,1)S(1)} %bitcast.26), channel_id=1, source_target_pairs={{0,2},{2,6},{6,4},{4,0},{1,3},{3,7},{7,5},{5,1},{8,10},{10,14},{14... | collective-permute-start | bytes 2359304 | tf_op jit(solution)/shard_map/ppermute | solution.py:291
  30.3 1.6 %shard_map.64.rest_2_.rest_1_ = bf16[672,2048]{1,0:T(8,128)(2,1)S(1)} custom-call(s32[6]{0:T(128)S(1)} %pad_add_fusion.place_ref, bf16[160,2048]{1,0:T(8,128)(2,1)S(1)} %slice.23.refs_0_, bf16[176,2048]{1,0:T(8,128)(2,1)S(1)} %constant_dynamic-update-slice_fusion.refs_1_, bf16[160,2048]{1,0:T(8,128)(2,1)S(1)} %collective-permute-done.5.refs_2_, ...), custom_call_target="tpu_custom_call" | custom-call | bytes 5505024 | tf_op jit(solution)/shard_map/pallas_call | solution.py:87
  31.9 3.9 %collective-permute-start.12 = (bf16[64,2048]{1,0:T(8,128)(2,1)S(1)}, bf16[64,2048]{1,0:T(8,128)(2,1)S(1)}, u32[]{:S(2)}, u32[]{:S(2)}) collective-permute-start(bf16[64,2048]{1,0:T(8,128)(2,1)S(1)} %collective-permute-done.4.refs_1_), channel_id=1, source_target_pairs={{0,2},{2,6},{6,4},{4,0},{1,3},{3,7},{7,5},{5,1},{8,10},{10,14},{14... | collective-permute-start | bytes 786440 | tf_op jit(solution)/shard_map/ppermute | solution.py:291
  36.4 7.5 %collective-permute-done.7.refs_1_ = bf16[176,2048]{1,0:T(8,128)(2,1)S(1)} collective-permute-done((bf16[176,2048]{1,0:T(8,128)(2,1)S(1)}, bf16[176,2048]{1,0:T(8,128)(2,1)S(1)}, u32[]{:S(2)}, u32[]{:S(2)}) %collective-permute-start.7) | collective-permute-done | bytes 720928 | tf_op jit(solution)/shard_map/ppermute | solution.py:42
  44.4 4.3 %collective-permute-done.8.refs_1_ = bf16[176,2048]{1,0:T(8,128)(2,1)S(1)} collective-permute-done((bf16[176,2048]{1,0:T(8,128)(2,1)S(1)}, bf16[176,2048]{1,0:T(8,128)(2,1)S(1)}, u32[]{:S(2)}, u32[]{:S(2)}) %collective-permute-start.8) | collective-permute-done | bytes 720928 | tf_op jit(solution)/shard_map/ppermute | solution.py:42
  48.9 5.1 %collective-permute-done.12.refs_2_ = bf16[64,2048]{1,0:T(8,128)(2,1)S(1)} collective-permute-done((bf16[64,2048]{1,0:T(8,128)(2,1)S(1)}, bf16[64,2048]{1,0:T(8,128)(2,1)S(1)}, u32[]{:S(2)}, u32[]{:S(2)}) %collective-permute-start.12) | collective-permute-done | bytes 262176 | tf_op jit(solution)/shard_map/ppermute | solution.py:291
  54.5 3.4 %collective-permute-start.22 = (bf16[64,2048]{1,0:T(8,128)(2,1)S(1)}, bf16[64,2048]{1,0:T(8,128)(2,1)S(1)}, u32[]{:S(2)}, u32[]{:S(2)}) collective-permute-start(bf16[64,2048]{1,0:T(8,128)(2,1)S(1)} %collective-permute-done.12.refs_2_), channel_id=1, source_target_pairs={{0,2},{2,6},{6,4},{4,0},{1,3},{3,7},{7,5},{5,1},{8,10},{10,14},{14... | collective-permute-start | bytes 786440 | tf_op jit(solution)/shard_map/ppermute | solution.py:291
  57.9 2.6 %collective-permute-start.21 = (bf16[192,2048]{1,0:T(8,128)(2,1)S(1)}, bf16[192,2048]{1,0:T(8,128)(2,1)S(1)}, u32[]{:S(2)}, u32[]{:S(2)}) collective-permute-start(bf16[192,2048]{1,0:T(8,128)(2,1)S(1)} %collective-permute-done.11.rest_1_), channel_id=1, source_target_pairs={{0,2},{2,6},{6,4},{4,0},{1,3},{3,7},{7,5},{5,1},{8,10},{10,14},{14... | collective-permute-start | bytes 2359304 | tf_op jit(solution)/shard_map/ppermute | solution.py:291
  61.5 1.6 %shard_map.66.rest_4_.rest_3_ = bf16[672,2048]{1,0:T(8,128)(2,1)S(1)} custom-call(s32[6]{0:T(128)S(1)} %pad_add_fusion.place_ref, bf16[160,2048]{1,0:T(8,128)(2,1)S(1)} %collective-permute-done.3.refs_0_, bf16[176,2048]{1,0:T(8,128)(2,1)S(1)} %collective-permute-done.8.refs_1_, bf16[160,2048]{1,0:T(8,128)(2,1)S(1)} %collective-permute-done.10.refs_2_, ...), custom_call_target="tpu_custom_call" | custom-call | bytes 5505024 | tf_op jit(solution)/shard_map/pallas_call | solution.py:87
  63.2 1.6 %collective-permute-start.23 = (bf16[64,2048]{1,0:T(8,128)(2,1)S(1)}, bf16[64,2048]{1,0:T(8,128)(2,1)S(1)}, u32[]{:S(2)}, u32[]{:S(2)}) collective-permute-start(bf16[64,2048]{1,0:T(8,128)(2,1)S(1)} %collective-permute-done.4.refs_1_), channel_id=1, source_target_pairs={{0,8},{8,0},{16,24},{24,16},{1,9},{9,1},{17,25},{25,17},{2,10},{10... | collective-permute-start | bytes 786440 | tf_op jit(solution)/shard_map/ppermute | solution.py:42
  64.7 1.6 %shard_map.65.rest_3_.rest_2_ = bf16[672,2048]{1,0:T(8,128)(2,1)S(1)} custom-call(s32[6]{0:T(128)S(1)} %pad_add_fusion.place_ref, bf16[160,2048]{1,0:T(8,128)(2,1)S(1)} %collective-permute-done.2.refs_0_, bf16[176,2048]{1,0:T(8,128)(2,1)S(1)} %collective-permute-done.7.refs_1_, bf16[160,2048]{1,0:T(8,128)(2,1)S(1)} %collective-permute-done.9.refs_2_, ...), custom_call_target="tpu_custom_call" | custom-call | bytes 5505024 | tf_op jit(solution)/shard_map/pallas_call | solution.py:87
  66.4 1.6 %collective-permute-start.24 = (bf16[64,2048]{1,0:T(8,128)(2,1)S(1)}, bf16[64,2048]{1,0:T(8,128)(2,1)S(1)}, u32[]{:S(2)}, u32[]{:S(2)}) collective-permute-start(bf16[64,2048]{1,0:T(8,128)(2,1)S(1)} %collective-permute-done.4.refs_1_), channel_id=1, source_target_pairs={{0,16},{8,24},{16,0},{24,8},{1,17},{9,25},{17,1},{25,9},{2,18},{10... | collective-permute-start | bytes 786440 | tf_op jit(solution)/shard_map/ppermute | solution.py:42
  67.9 7.6 %shard_map.67 = (bf16[128,512]{1,0:T(8,128)(2,1)S(1)}, bf16[128,512]{1,0:T(8,128)(2,1)S(1)}, bf16[128,512]{1,0:T(8,128)(2,1)S(1)}) custom-call(s32[6]{0:T(128)S(1)} %pad_add_fusion.place_ref, f32[4,8,256]{2,1,0:T(8,128)S(1)} %pad_maximum_fusion.taps_ref, f32[4,4,128]{2,1,0:T(4,128)S(1)} %maximum_convert_fusion.long_ref, bf16[192,2048]{1,0:T(8,128)(2,1)S(1)} %bitcast.27, ...), custom_call_target="tpu_custom_call" | custom-call | flops 6442450944 | bytes 12582912 | tf_op jit(solution)/shard_map/pallas_call | solution.py:183
  75.6 6.9 %collective-permute-done.23.refs_5_ = bf16[64,2048]{1,0:T(8,128)(2,1)S(1)} collective-permute-done((bf16[64,2048]{1,0:T(8,128)(2,1)S(1)}, bf16[64,2048]{1,0:T(8,128)(2,1)S(1)}, u32[]{:S(2)}, u32[]{:S(2)}) %collective-permute-start.23) | collective-permute-done | bytes 262176 | tf_op jit(solution)/shard_map/ppermute | solution.py:42
  84.6 2.9 %collective-permute-done.17.refs_19_ = bf16[128,512]{1,0:T(8,128)(2,1)S(1)} collective-permute-done((bf16[128,512]{1,0:T(8,128)(2,1)S(1)}, bf16[128,512]{1,0:T(8,128)(2,1)S(1)}, u32[]{:S(2)}, u32[]{:S(2)}) %collective-permute-start.17) | collective-permute-done | bytes 131104 | tf_op jit(solution)/shard_map/ppermute | solution.py:42
  87.5 1.2 collective-permute-done.18.refs_22_
  90.3 4.3 %shard_map.68 = (bf16[64,512]{1,0:T(8,128)(2,1)S(1)}, bf16[64,512]{1,0:T(8,128)(2,1)S(1)}, bf16[64,512]{1,0:T(8,128)(2,1)S(1)}) custom-call(s32[6]{0:T(128)S(1)} %pad_add_fusion.place_ref, f32[4,8,256]{2,1,0:T(8,128)S(1)} %pad_maximum_fusion.taps_ref, f32[4,4,128]{2,1,0:T(4,128)S(1)} %maximum_convert_fusion.long_ref, ...), custom_call_target="tpu_custom_call" | custom-call | flops 3221225472 | bytes 6291456 | tf_op jit(solution)/shard_map/pallas_call | solution.py:183
  94.7 1.2 collective-permute-start.27
  96.8 1.1 collective-permute-start.32
  97.9 1.6 %shard_map.69.rest_3_.rest_4_ = bf16[672,2048]{1,0:T(8,128)(2,1)S(1)} custom-call(s32[6]{0:T(128)S(1)} %pad_add_fusion.place_ref, bf16[160,2048]{1,0:T(8,128)(2,1)S(1)} %collective-permute-done.19.refs_0_, bf16[176,2048]{1,0:T(8,128)(2,1)S(1)} %collective-permute-done.20.refs_1_, bf16[160,2048]{1,0:T(8,128)(2,1)S(1)} %collective-permute-done.25.refs_2_, ...), custom_call_target="tpu_custom_call" | custom-call | bytes 5505024 | tf_op jit(solution)/shard_map/pallas_call | solution.py:87
  99.6 1.0 collective-permute-start.35
  100.5 1.5 %collective-permute-start.34 = (bf16[64,2048]{1,0:T(8,128)(2,1)S(1)}, bf16[64,2048]{1,0:T(8,128)(2,1)S(1)}, u32[]{:S(2)}, u32[]{:S(2)}) collective-permute-start(bf16[64,2048]{1,0:T(8,128)(2,1)S(1)} %collective-permute-done.22.refs_3_), channel_id=1, source_target_pairs={{0,8},{8,0},{16,24},{24,16},{1,9},{9,1},{17,25},{25,17},{2,10},{10... | collective-permute-start | bytes 786440 | tf_op jit(solution)/shard_map/ppermute | solution.py:42
  102.0 4.3 %shard_map.70 = bf16[192,512]{1,0:T(8,128)(2,1)S(1)} custom-call(s32[6]{0:T(128)S(1)} %pad_add_fusion.place_ref, f32[4,8,256]{2,1,0:T(8,128)S(1)} %pad_maximum_fusion.taps_ref, f32[4,4,128]{2,1,0:T(4,128)S(1)} %maximum_convert_fusion.long_ref, bf16[192,2048]{1,0:T(8,128)(2,1)S(1)} %bitcast.28, bf16[192,2048]{1,0:T(8,128)(2,1)S(1)} %collective-permute-done.11.rest_1_, ...), custom_call_target="tpu_custom_call" | custom-call | flops 3221225472 | bytes 6291456 | tf_op jit(solution)/shard_map/pallas_call | solution.py:183
  106.3 1.2 collective-permute-start.29
  108.3 6.2 %collective-permute-done.35.refs_10_ = bf16[64,2048]{1,0:T(8,128)(2,1)S(1)} collective-permute-done((bf16[64,2048]{1,0:T(8,128)(2,1)S(1)}, bf16[64,2048]{1,0:T(8,128)(2,1)S(1)}, u32[]{:S(2)}, u32[]{:S(2)}) %collective-permute-start.35) | collective-permute-done | bytes 262176 | tf_op jit(solution)/shard_map/ppermute | solution.py:42
  114.5 1.3 collective-permute-start.36
  115.8 1.4 %collective-permute-start.37 = (bf16[64,2048]{1,0:T(8,128)(2,1)S(1)}, bf16[64,2048]{1,0:T(8,128)(2,1)S(1)}, u32[]{:S(2)}, u32[]{:S(2)}) collective-permute-start(bf16[64,2048]{1,0:T(8,128)(2,1)S(1)} %collective-permute-done.35.refs_10_), channel_id=1, source_target_pairs={{0,8},{8,0},{16,24},{24,16},{1,9},{9,1},{17,25},{25,17},{2,10},{10... | collective-permute-start | bytes 786440 | tf_op jit(solution)/shard_map/ppermute | solution.py:42
  118.0 5.4 %shard_map.71 = (bf16[64,512]{1,0:T(8,128)(2,1)S(1)}, bf16[64,512]{1,0:T(8,128)(2,1)S(1)}, bf16[64,512]{1,0:T(8,128)(2,1)S(1)}, bf16[64,512]{1,0:T(8,128)(2,1)S(1)}) custom-call(s32[6]{0:T(128)S(1)} %pad_add_fusion.place_ref, f32[4,8,256]{2,1,0:T(8,128)S(1)} %pad_maximum_fusion.taps_ref, f32[4,4,128]{2,1,0:T(4,128)S(1)} %maximum_convert_fusion.long_ref, ...), custom_call_target="tpu_custom_call" | custom-call | flops 4294967296 | bytes 8388608 | tf_op jit(solution)/shard_map/pallas_call | solution.py:183
  124.0 1.3 collective-permute-start.40
  125.3 1.6 %collective-permute-start.41 = (bf16[64,512]{1,0:T(8,128)(2,1)S(1)}, bf16[64,512]{1,0:T(8,128)(2,1)S(1)}, u32[]{:S(2)}, u32[]{:S(2)}) collective-permute-start(bf16[64,512]{1,0:T(8,128)(2,1)S(1)} %get-tuple-element.136), channel_id=1, source_target_pairs={{0,24},{8,16},{16,8},{24,0},{1,25},{9,17},{17,9},{25,1},{2,26},{10... | collective-permute-start | bytes 196616 | tf_op jit(solution)/shard_map/ppermute | solution.py:42
  128.3 2.2 %collective-permute-done.41.refs_26_ = bf16[64,512]{1,0:T(8,128)(2,1)S(1)} collective-permute-done((bf16[64,512]{1,0:T(8,128)(2,1)S(1)}, bf16[64,512]{1,0:T(8,128)(2,1)S(1)}, u32[]{:S(2)}, u32[]{:S(2)}) %collective-permute-start.41) | collective-permute-done | bytes 65568 | tf_op jit(solution)/shard_map/ppermute | solution.py:42
  130.5 1.9 %shard_map.73 = bf16[256,2048]{1,0:T(8,128)(2,1)S(1)} custom-call(s32[6]{0:T(128)S(1)} %pad_add_fusion.place_ref, bf16[64,2048]{1,0:T(8,128)(2,1)S(1)} %copy-done.1, bf16[64,2048]{1,0:T(8,128)(2,1)S(1)} %collective-permute-done.4.refs_1_, bf16[64,2048]{1,0:T(8,128)(2,1)S(1)} %collective-permute-done.12.refs_2_, ...), custom_call_target="tpu_custom_call" | custom-call | flops 2147483648 | bytes 5242880 | tf_op jit(solution)/shard_map/pallas_call | solution.py:243
  132.4 1.9 %shard_map.72 = f32[256,2048]{1,0:T(8,128)S(1)} custom-call(s32[6]{0:T(128)S(1)} %pad_add_fusion.place_ref, bf16[64,2048]{1,0:T(8,128)(2,1)S(1)} %copy-done.1, bf16[64,2048]{1,0:T(8,128)(2,1)S(1)} %collective-permute-done.4.refs_1_, bf16[64,2048]{1,0:T(8,128)(2,1)S(1)} %collective-permute-done.12.refs_2_, ...), custom_call_target="tpu_custom_call" | custom-call | flops 2147483648 | bytes 5242880 | tf_op jit(solution)/shard_map/pallas_call | solution.py:243
  135.1 1.3 add_convert_fusion
  (72 shorter events, 15.3 us)
Async XLA Ops:
  0.0 20.4 %slice-start = ((bf16[256,2048]{1,0:T(8,128)(2,1)}), bf16[96,2048]{1,0:T(8,128)(2,1)S(1)}, s32[]{:S(2)}) async-start(bf16[256,2048]{1,0:T(8,128)(2,1)} %param.6), calls=%async_computation | async-start | bytes 786432 | tf_op jit(solution)/shard_map/slice | solution.py:309
  1.2 26.5 %copy-start = (bf16[3,64,2048]{2,1,0:T(8,128)(2,1)S(1)}, bf16[3,64,2048]{2,1,0:T(8,128)(2,1)}, u32[]{:S(2)}) copy-start(bf16[3,64,2048]{2,1,0:T(8,128)(2,1)} %param.7) | copy-start | bytes 2359300
  1.2 17.8 %collective-permute-start.2 = (bf16[160,2048]{1,0:T(8,128)(2,1)S(1)}, bf16[160,2048]{1,0:T(8,128)(2,1)S(1)}, u32[]{:S(2)}, u32[]{:S(2)}) collective-permute-start(bf16[160,2048]{1,0:T(8,128)(2,1)S(1)} %slice.23.refs_0_), channel_id=1, source_target_pairs={{0,8},{8,0},{16,24},{24,16},{1,9},{9,1},{17,25},{25,17},{2,10},{10... | collective-permute-start | bytes 1966088 | tf_op jit(solution)/shard_map/ppermute | solution.py:42
  4.2 16.2 %collective-permute-start.3 = (bf16[160,2048]{1,0:T(8,128)(2,1)S(1)}, bf16[160,2048]{1,0:T(8,128)(2,1)S(1)}, u32[]{:S(2)}, u32[]{:S(2)}) collective-permute-start(bf16[160,2048]{1,0:T(8,128)(2,1)S(1)} %slice.23.refs_0_), channel_id=1, source_target_pairs={{0,16},{8,24},{16,0},{24,8},{1,17},{9,25},{17,1},{25,9},{2,18},{10... | collective-permute-start | bytes 1966088 | tf_op jit(solution)/shard_map/ppermute | solution.py:42
  7.7 8.8 %collective-permute-start = (bf16[80,2048]{1,0:T(8,128)(2,1)}, bf16[80,2048]{1,0:T(8,128)(2,1)}, u32[]{:S(2)}, u32[]{:S(2)}) collective-permute-start(bf16[80,2048]{1,0:T(8,128)(2,1)} %get-tuple-element.138), channel_id=1, source_target_pairs={{1,2},{3,4},{5,6},{9,10},{11,12},{13,14},{17,18},{19,20},{21,22},{... | collective-permute-start | bytes 983048 | tf_op jit(solution)/shard_map/ppermute | solution.py:300
  9.1 7.5 %collective-permute-start.1 = (bf16[80,2048]{1,0:T(8,128)(2,1)}, bf16[80,2048]{1,0:T(8,128)(2,1)}, u32[]{:S(2)}, u32[]{:S(2)}) collective-permute-start(bf16[80,2048]{1,0:T(8,128)(2,1)} %get-tuple-element.137), channel_id=1, source_target_pairs={{1,3},{3,5},{5,7},{9,11},{11,13},{13,15},{17,19},{19,21},{21,23},{... | collective-permute-start | bytes 983048 | tf_op jit(solution)/shard_map/ppermute | solution.py:300
  10.5 8.6 %collective-permute-start.4 = (bf16[64,2048]{1,0:T(8,128)(2,1)}, bf16[64,2048]{1,0:T(8,128)(2,1)S(1)}, u32[]{:S(2)}, u32[]{:S(2)}) collective-permute-start(bf16[64,2048]{1,0:T(8,128)(2,1)} %refs_0_.1), channel_id=1, source_target_pairs={{0,2},{2,6},{6,4},{4,0},{1,3},{3,7},{7,5},{5,1},{8,10},{10,14},{14... | collective-permute-start | bytes 786440 | tf_op jit(solution)/shard_map/ppermute | solution.py:291
  20.5 15.4 %copy-start.1 = (bf16[64,2048]{1,0:T(8,128)(2,1)S(1)}, bf16[64,2048]{1,0:T(8,128)(2,1)}, u32[]{:S(2)}) copy-start(bf16[64,2048]{1,0:T(8,128)(2,1)} %refs_0_.1) | copy-start | bytes 786436
  20.5 9.3 %collective-permute-start.6 = (bf16[176,2048]{1,0:T(8,128)(2,1)S(1)}, bf16[176,2048]{1,0:T(8,128)(2,1)S(1)}, u32[]{:S(2)}, u32[]{:S(2)}) collective-permute-start(bf16[176,2048]{1,0:T(8,128)(2,1)S(1)} %constant_dynamic-update-slice_fusion.refs_1_), channel_id=1, source_target_pairs={{0,1},{1,0},{2,3},{3,2},{4,5},{5,4},{6,7},{7,6},{8,9},{9,8},{10,11... | collective-permute-start | bytes 2162696 | tf_op jit(solution)/shard_map/ppermute | solution.py:37
  24.9 2.8 %collective-permute-start.5 = (bf16[160,2048]{1,0:T(8,128)(2,1)S(1)}, bf16[160,2048]{1,0:T(8,128)(2,1)S(1)}, u32[]{:S(2)}, u32[]{:S(2)}) collective-permute-start(bf16[160,2048]{1,0:T(8,128)(2,1)S(1)} %slice.23.refs_0_), channel_id=1, source_target_pairs={{0,1},{1,0},{2,3},{3,2},{4,5},{5,4},{6,7},{7,6},{8,9},{9,8},{10,11... | collective-permute-start | bytes 1966088 | tf_op jit(solution)/shard_map/ppermute | solution.py:37
  25.0 18.9 %collective-permute-start.7 = (bf16[176,2048]{1,0:T(8,128)(2,1)S(1)}, bf16[176,2048]{1,0:T(8,128)(2,1)S(1)}, u32[]{:S(2)}, u32[]{:S(2)}) collective-permute-start(bf16[176,2048]{1,0:T(8,128)(2,1)S(1)} %constant_dynamic-update-slice_fusion.refs_1_), channel_id=1, source_target_pairs={{0,8},{8,0},{16,24},{24,16},{1,9},{9,1},{17,25},{25,17},{2,10},{10... | collective-permute-start | bytes 2162696 | tf_op jit(solution)/shard_map/ppermute | solution.py:42
  25.5 6.4 %collective-permute-start.10 = (bf16[160,2048]{1,0:T(8,128)(2,1)S(1)}, bf16[160,2048]{1,0:T(8,128)(2,1)S(1)}, u32[]{:S(2)}, u32[]{:S(2)}) collective-permute-start(bf16[160,2048]{1,0:T(8,128)(2,1)S(1)} %collective-permute-done.3.refs_0_), channel_id=1, source_target_pairs={{0,1},{1,0},{2,3},{3,2},{4,5},{5,4},{6,7},{7,6},{8,9},{9,8},{10,11... | collective-permute-start | bytes 1966088 | tf_op jit(solution)/shard_map/ppermute | solution.py:37
  25.7 10.2 %collective-permute-start.9 = (bf16[160,2048]{1,0:T(8,128)(2,1)S(1)}, bf16[160,2048]{1,0:T(8,128)(2,1)S(1)}, u32[]{:S(2)}, u32[]{:S(2)}) collective-permute-start(bf16[160,2048]{1,0:T(8,128)(2,1)S(1)} %collective-permute-done.2.refs_0_), channel_id=1, source_target_pairs={{0,1},{1,0},{2,3},{3,2},{4,5},{5,4},{6,7},{7,6},{8,9},{9,8},{10,11... | collective-permute-start | bytes 1966088 | tf_op jit(solution)/shard_map/ppermute | solution.py:37
  27.7 21.3 %collective-permute-start.11 = (bf16[192,2048]{1,0:T(8,128)(2,1)S(1)}, bf16[192,2048]{1,0:T(8,128)(2,1)S(1)}, u32[]{:S(2)}, u32[]{:S(2)}) collective-permute-start(bf16[192,2048]{1,0:T(8,128)(2,1)S(1)} %bitcast.26), channel_id=1, source_target_pairs={{0,2},{2,6},{6,4},{4,0},{1,3},{3,7},{7,5},{5,1},{8,10},{10,14},{14... | collective-permute-start | bytes 2359304 | tf_op jit(solution)/shard_map/ppermute | solution.py:291
  29.8 19.0 %collective-permute-start.8 = (bf16[176,2048]{1,0:T(8,128)(2,1)S(1)}, bf16[176,2048]{1,0:T(8,128)(2,1)S(1)}, u32[]{:S(2)}, u32[]{:S(2)}) collective-permute-start(bf16[176,2048]{1,0:T(8,128)(2,1)S(1)} %constant_dynamic-update-slice_fusion.refs_1_), channel_id=1, source_target_pairs={{0,16},{8,24},{16,0},{24,8},{1,17},{9,25},{17,1},{25,9},{2,18},{10... | collective-permute-start | bytes 2162696 | tf_op jit(solution)/shard_map/ppermute | solution.py:42
  31.9 22.1 %collective-permute-start.12 = (bf16[64,2048]{1,0:T(8,128)(2,1)S(1)}, bf16[64,2048]{1,0:T(8,128)(2,1)S(1)}, u32[]{:S(2)}, u32[]{:S(2)}) collective-permute-start(bf16[64,2048]{1,0:T(8,128)(2,1)S(1)} %collective-permute-done.4.refs_1_), channel_id=1, source_target_pairs={{0,2},{2,6},{6,4},{4,0},{1,3},{3,7},{7,5},{5,1},{8,10},{10,14},{14... | collective-permute-start | bytes 786440 | tf_op jit(solution)/shard_map/ppermute | solution.py:291
  35.8 18.2 %collective-permute-start.13 = (bf16[64,2048]{1,0:T(8,128)(2,1)S(1)}, bf16[64,2048]{1,0:T(8,128)(2,1)S(1)}, u32[]{:S(2)}, u32[]{:S(2)}) collective-permute-start(bf16[64,2048]{1,0:T(8,128)(2,1)S(1)} %copy-done.1), channel_id=1, source_target_pairs={{0,8},{8,0},{16,24},{24,16},{1,9},{9,1},{17,25},{25,17},{2,10},{10... | collective-permute-start | bytes 786440 | tf_op jit(solution)/shard_map/ppermute | solution.py:42
  43.9 10.1 %collective-permute-start.14 = (bf16[64,2048]{1,0:T(8,128)(2,1)S(1)}, bf16[64,2048]{1,0:T(8,128)(2,1)S(1)}, u32[]{:S(2)}, u32[]{:S(2)}) collective-permute-start(bf16[64,2048]{1,0:T(8,128)(2,1)S(1)} %copy-done.1), channel_id=1, source_target_pairs={{0,16},{8,24},{16,0},{24,8},{1,17},{9,25},{17,1},{25,9},{2,18},{10... | collective-permute-start | bytes 786440 | tf_op jit(solution)/shard_map/ppermute | solution.py:42
  54.0 7.0 %collective-permute-start.16 = (bf16[176,2048]{1,0:T(8,128)(2,1)S(1)}, bf16[176,2048]{1,0:T(8,128)(2,1)S(1)}, u32[]{:S(2)}, u32[]{:S(2)}) collective-permute-start(bf16[176,2048]{1,0:T(8,128)(2,1)S(1)} %collective-permute-done.8.refs_1_), channel_id=1, source_target_pairs={{0,1},{1,0},{2,3},{3,2},{4,5},{5,4},{6,7},{7,6},{8,9},{9,8},{10,11... | collective-permute-start | bytes 2162696 | tf_op jit(solution)/shard_map/ppermute | solution.py:37
  54.0 9.1 %collective-permute-start.15 = (bf16[176,2048]{1,0:T(8,128)(2,1)S(1)}, bf16[176,2048]{1,0:T(8,128)(2,1)S(1)}, u32[]{:S(2)}, u32[]{:S(2)}) collective-permute-start(bf16[176,2048]{1,0:T(8,128)(2,1)S(1)} %collective-permute-done.7.refs_1_), channel_id=1, source_target_pairs={{0,1},{1,0},{2,3},{3,2},{4,5},{5,4},{6,7},{7,6},{8,9},{9,8},{10,11... | collective-permute-start | bytes 2162696 | tf_op jit(solution)/shard_map/ppermute | solution.py:37
  54.5 11.8 %collective-permute-start.22 = (bf16[64,2048]{1,0:T(8,128)(2,1)S(1)}, bf16[64,2048]{1,0:T(8,128)(2,1)S(1)}, u32[]{:S(2)}, u32[]{:S(2)}) collective-permute-start(bf16[64,2048]{1,0:T(8,128)(2,1)S(1)} %collective-permute-done.12.refs_2_), channel_id=1, source_target_pairs={{0,2},{2,6},{6,4},{4,0},{1,3},{3,7},{7,5},{5,1},{8,10},{10,14},{14... | collective-permute-start | bytes 786440 | tf_op jit(solution)/shard_map/ppermute | solution.py:291
  57.9 26.7 %collective-permute-start.21 = (bf16[192,2048]{1,0:T(8,128)(2,1)S(1)}, bf16[192,2048]{1,0:T(8,128)(2,1)S(1)}, u32[]{:S(2)}, u32[]{:S(2)}) collective-permute-start(bf16[192,2048]{1,0:T(8,128)(2,1)S(1)} %collective-permute-done.11.rest_1_), channel_id=1, source_target_pairs={{0,2},{2,6},{6,4},{4,0},{1,3},{3,7},{7,5},{5,1},{8,10},{10,14},{14... | collective-permute-start | bytes 2359304 | tf_op jit(solution)/shard_map/ppermute | solution.py:291
  60.5 24.1 %collective-permute-start.20 = (bf16[176,2048]{1,0:T(8,128)(2,1)S(1)}, bf16[176,2048]{1,0:T(8,128)(2,1)S(1)}, u32[]{:S(2)}, u32[]{:S(2)}) collective-permute-start(bf16[176,2048]{1,0:T(8,128)(2,1)S(1)} %collective-permute-done.7.refs_1_), channel_id=1, source_target_pairs={{0,16},{8,24},{16,0},{24,8},{1,17},{9,25},{17,1},{25,9},{2,18},{10... | collective-permute-start | bytes 2162696 | tf_op jit(solution)/shard_map/ppermute | solution.py:42
  61.0 23.6 %collective-permute-start.19 = (bf16[160,2048]{1,0:T(8,128)(2,1)S(1)}, bf16[160,2048]{1,0:T(8,128)(2,1)S(1)}, u32[]{:S(2)}, u32[]{:S(2)}) collective-permute-start(bf16[160,2048]{1,0:T(8,128)(2,1)S(1)} %collective-permute-done.3.refs_0_), channel_id=1, source_target_pairs={{0,8},{8,0},{16,24},{24,16},{1,9},{9,1},{17,25},{25,17},{2,10},{10... | collective-permute-start | bytes 1966088 | tf_op jit(solution)/shard_map/ppermute | solution.py:42
  63.2 19.3 %collective-permute-start.23 = (bf16[64,2048]{1,0:T(8,128)(2,1)S(1)}, bf16[64,2048]{1,0:T(8,128)(2,1)S(1)}, u32[]{:S(2)}, u32[]{:S(2)}) collective-permute-start(bf16[64,2048]{1,0:T(8,128)(2,1)S(1)} %collective-permute-done.4.refs_1_), channel_id=1, source_target_pairs={{0,8},{8,0},{16,24},{24,16},{1,9},{9,1},{17,25},{25,17},{2,10},{10... | collective-permute-start | bytes 786440 | tf_op jit(solution)/shard_map/ppermute | solution.py:42
  66.4 17.3 %collective-permute-start.24 = (bf16[64,2048]{1,0:T(8,128)(2,1)S(1)}, bf16[64,2048]{1,0:T(8,128)(2,1)S(1)}, u32[]{:S(2)}, u32[]{:S(2)}) collective-permute-start(bf16[64,2048]{1,0:T(8,128)(2,1)S(1)} %collective-permute-done.4.refs_1_), channel_id=1, source_target_pairs={{0,16},{8,24},{16,0},{24,8},{1,17},{9,25},{17,1},{25,9},{2,18},{10... | collective-permute-start | bytes 786440 | tf_op jit(solution)/shard_map/ppermute | solution.py:42
  82.5 5.0 %collective-permute-start.17 = (bf16[128,512]{1,0:T(8,128)(2,1)S(1)}, bf16[128,512]{1,0:T(8,128)(2,1)S(1)}, u32[]{:S(2)}, u32[]{:S(2)}) collective-permute-start(bf16[128,512]{1,0:T(8,128)(2,1)S(1)} %get-tuple-element.95), channel_id=1, source_target_pairs={{0,8},{8,0},{16,24},{24,16},{1,9},{9,1},{17,25},{25,17},{2,10},{10... | collective-permute-start | bytes 393224 | tf_op jit(solution)/shard_map/ppermute | solution.py:42
  83.7 5.0 %collective-permute-start.18 = (bf16[128,512]{1,0:T(8,128)(2,1)S(1)}, bf16[128,512]{1,0:T(8,128)(2,1)S(1)}, u32[]{:S(2)}, u32[]{:S(2)}) collective-permute-start(bf16[128,512]{1,0:T(8,128)(2,1)S(1)} %get-tuple-element.96), channel_id=1, source_target_pairs={{0,16},{8,24},{16,0},{24,8},{1,17},{9,25},{17,1},{25,9},{2,18},{10... | collective-permute-start | bytes 393224 | tf_op jit(solution)/shard_map/ppermute | solution.py:42
  88.6 8.2 %collective-permute-start.26 = (bf16[176,2048]{1,0:T(8,128)(2,1)S(1)}, bf16[176,2048]{1,0:T(8,128)(2,1)S(1)}, u32[]{:S(2)}, u32[]{:S(2)}) collective-permute-start(bf16[176,2048]{1,0:T(8,128)(2,1)S(1)} %collective-permute-done.20.refs_1_), channel_id=1, source_target_pairs={{0,1},{1,0},{2,3},{3,2},{4,5},{5,4},{6,7},{7,6},{8,9},{9,8},{10,11... | collective-permute-start | bytes 2162696 | tf_op jit(solution)/shard_map/ppermute | solution.py:37
  88.6 7.3 %collective-permute-start.25 = (bf16[160,2048]{1,0:T(8,128)(2,1)S(1)}, bf16[160,2048]{1,0:T(8,128)(2,1)S(1)}, u32[]{:S(2)}, u32[]{:S(2)}) collective-permute-start(bf16[160,2048]{1,0:T(8,128)(2,1)S(1)} %collective-permute-done.19.refs_0_), channel_id=1, source_target_pairs={{0,1},{1,0},{2,3},{3,2},{4,5},{5,4},{6,7},{7,6},{8,9},{9,8},{10,11... | collective-permute-start | bytes 1966088 | tf_op jit(solution)/shard_map/ppermute | solution.py:37
  89.1 10.4 %collective-permute-start.31 = (bf16[64,2048]{1,0:T(8,128)(2,1)S(1)}, bf16[64,2048]{1,0:T(8,128)(2,1)S(1)}, u32[]{:S(2)}, u32[]{:S(2)}) collective-permute-start(bf16[64,2048]{1,0:T(8,128)(2,1)S(1)} %collective-permute-done.14.refs_8_), channel_id=1, source_target_pairs={{0,8},{8,0},{16,24},{24,16},{1,9},{9,1},{17,25},{25,17},{2,10},{10... | collective-permute-start | bytes 786440 | tf_op jit(solution)/shard_map/ppermute | solution.py:42
  90.0 27.2 %collective-permute-start.30 = (bf16[192,2048]{1,0:T(8,128)(2,1)S(1)}, bf16[192,2048]{1,0:T(8,128)(2,1)S(1)}, u32[]{:S(2)}, u32[]{:S(2)}) collective-permute-start(bf16[192,2048]{1,0:T(8,128)(2,1)S(1)} %collective-permute-done.21.rest_0_.rest_2_), channel_id=1, source_target_pairs={{0,2},{2,6},{6,4},{4,0},{1,3},{3,7},{7,5},{5,1},{8,10},{10,14},{14... | collective-permute-start | bytes 2359304 | tf_op jit(solution)/shard_map/ppermute | solution.py:291
  94.7 5.9 %collective-permute-start.27 = (bf16[64,512]{1,0:T(8,128)(2,1)S(1)}, bf16[64,512]{1,0:T(8,128)(2,1)S(1)}, u32[]{:S(2)}, u32[]{:S(2)}) collective-permute-start(bf16[64,512]{1,0:T(8,128)(2,1)S(1)} %get-tuple-element.101), channel_id=1, source_target_pairs={{0,8},{8,0},{16,24},{24,16},{1,9},{9,1},{17,25},{25,17},{2,10},{10... | collective-permute-start | bytes 196616 | tf_op jit(solution)/shard_map/ppermute | solution.py:42
  95.9 10.4 %collective-permute-start.28 = (bf16[64,512]{1,0:T(8,128)(2,1)S(1)}, bf16[64,512]{1,0:T(8,128)(2,1)S(1)}, u32[]{:S(2)}, u32[]{:S(2)}) collective-permute-start(bf16[64,512]{1,0:T(8,128)(2,1)S(1)} %get-tuple-element.102), channel_id=1, source_target_pairs={{0,16},{8,24},{16,0},{24,8},{1,17},{9,25},{17,1},{25,9},{2,18},{10... | collective-permute-start | bytes 196616 | tf_op jit(solution)/shard_map/ppermute | solution.py:42
  96.8 10.7 %collective-permute-start.32 = (bf16[64,2048]{1,0:T(8,128)(2,1)S(1)}, bf16[64,2048]{1,0:T(8,128)(2,1)S(1)}, u32[]{:S(2)}, u32[]{:S(2)}) collective-permute-start(bf16[64,2048]{1,0:T(8,128)(2,1)S(1)} %collective-permute-done.23.refs_5_), channel_id=1, source_target_pairs={{0,16},{8,24},{16,0},{24,8},{1,17},{9,25},{17,1},{25,9},{2,18},{10... | collective-permute-start | bytes 786440 | tf_op jit(solution)/shard_map/ppermute | solution.py:42
  99.6 14.9 %collective-permute-start.35 = (bf16[64,2048]{1,0:T(8,128)(2,1)S(1)}, bf16[64,2048]{1,0:T(8,128)(2,1)S(1)}, u32[]{:S(2)}, u32[]{:S(2)}) collective-permute-start(bf16[64,2048]{1,0:T(8,128)(2,1)S(1)} %collective-permute-done.12.refs_2_), channel_id=1, source_target_pairs={{0,16},{8,24},{16,0},{24,8},{1,17},{9,25},{17,1},{25,9},{2,18},{10... | collective-permute-start | bytes 786440 | tf_op jit(solution)/shard_map/ppermute | solution.py:42
  100.5 15.3 %collective-permute-start.34 = (bf16[64,2048]{1,0:T(8,128)(2,1)S(1)}, bf16[64,2048]{1,0:T(8,128)(2,1)S(1)}, u32[]{:S(2)}, u32[]{:S(2)}) collective-permute-start(bf16[64,2048]{1,0:T(8,128)(2,1)S(1)} %collective-permute-done.22.refs_3_), channel_id=1, source_target_pairs={{0,8},{8,0},{16,24},{24,16},{1,9},{9,1},{17,25},{25,17},{2,10},{10... | collective-permute-start | bytes 786440 | tf_op jit(solution)/shard_map/ppermute | solution.py:42
  106.3 11.7 %collective-permute-start.29 = (bf16[192,512]{1,0:T(8,128)(2,1)S(1)}, bf16[192,512]{1,0:T(8,128)(2,1)S(1)}, u32[]{:S(2)}, u32[]{:S(2)}) collective-permute-start(bf16[192,512]{1,0:T(8,128)(2,1)S(1)} %shard_map.70), channel_id=1, source_target_pairs={{0,24},{8,16},{16,8},{24,0},{1,25},{9,17},{17,9},{25,1},{2,26},{10... | collective-permute-start | bytes 589832 | tf_op jit(solution)/shard_map/ppermute | solution.py:42
  107.5 16.5 %collective-permute-start.33 = (bf16[64,2048]{1,0:T(8,128)(2,1)S(1)}, bf16[64,2048]{1,0:T(8,128)(2,1)S(1)}, u32[]{:S(2)}, u32[]{:S(2)}) collective-permute-start(bf16[64,2048]{1,0:T(8,128)(2,1)S(1)} %collective-permute-done.12.refs_2_), channel_id=1, source_target_pairs={{0,8},{8,0},{16,24},{24,16},{1,9},{9,1},{17,25},{25,17},{2,10},{10... | collective-permute-start | bytes 786440 | tf_op jit(solution)/shard_map/ppermute | solution.py:42
  114.5 10.8 %collective-permute-start.36 = (bf16[64,2048]{1,0:T(8,128)(2,1)S(1)}, bf16[64,2048]{1,0:T(8,128)(2,1)S(1)}, u32[]{:S(2)}, u32[]{:S(2)}) collective-permute-start(bf16[64,2048]{1,0:T(8,128)(2,1)S(1)} %collective-permute-done.22.refs_3_), channel_id=1, source_target_pairs={{0,16},{8,24},{16,0},{24,8},{1,17},{9,25},{17,1},{25,9},{2,18},{10... | collective-permute-start | bytes 786440 | tf_op jit(solution)/shard_map/ppermute | solution.py:42
  115.8 11.1 %collective-permute-start.37 = (bf16[64,2048]{1,0:T(8,128)(2,1)S(1)}, bf16[64,2048]{1,0:T(8,128)(2,1)S(1)}, u32[]{:S(2)}, u32[]{:S(2)}) collective-permute-start(bf16[64,2048]{1,0:T(8,128)(2,1)S(1)} %collective-permute-done.35.refs_10_), channel_id=1, source_target_pairs={{0,8},{8,0},{16,24},{24,16},{1,9},{9,1},{17,25},{25,17},{2,10},{10... | collective-permute-start | bytes 786440 | tf_op jit(solution)/shard_map/ppermute | solution.py:42
  117.2 10.0 %collective-permute-start.38 = (bf16[64,2048]{1,0:T(8,128)(2,1)S(1)}, bf16[64,2048]{1,0:T(8,128)(2,1)S(1)}, u32[]{:S(2)}, u32[]{:S(2)}) collective-permute-start(bf16[64,2048]{1,0:T(8,128)(2,1)S(1)} %collective-permute-done.34.refs_7_), channel_id=1, source_target_pairs={{0,16},{8,24},{16,0},{24,8},{1,17},{9,25},{17,1},{25,9},{2,18},{10... | collective-permute-start | bytes 786440 | tf_op jit(solution)/shard_map/ppermute | solution.py:42
  123.3 4.3 %collective-permute-start.39 = (bf16[64,512]{1,0:T(8,128)(2,1)S(1)}, bf16[64,512]{1,0:T(8,128)(2,1)S(1)}, u32[]{:S(2)}, u32[]{:S(2)}) collective-permute-start(bf16[64,512]{1,0:T(8,128)(2,1)S(1)} %get-tuple-element.131), channel_id=1, source_target_pairs={{0,8},{8,0},{16,24},{24,16},{1,9},{9,1},{17,25},{25,17},{2,10},{10... | collective-permute-start | bytes 196616 | tf_op jit(solution)/shard_map/ppermute | solution.py:42
  124.0 4.3 %collective-permute-start.40 = (bf16[64,512]{1,0:T(8,128)(2,1)S(1)}, bf16[64,512]{1,0:T(8,128)(2,1)S(1)}, u32[]{:S(2)}, u32[]{:S(2)}) collective-permute-start(bf16[64,512]{1,0:T(8,128)(2,1)S(1)} %get-tuple-element.134), channel_id=1, source_target_pairs={{0,16},{8,24},{16,0},{24,8},{1,17},{9,25},{17,1},{25,9},{2,18},{10... | collective-permute-start | bytes 196616 | tf_op jit(solution)/shard_map/ppermute | solution.py:42
  125.3 5.2 %collective-permute-start.41 = (bf16[64,512]{1,0:T(8,128)(2,1)S(1)}, bf16[64,512]{1,0:T(8,128)(2,1)S(1)}, u32[]{:S(2)}, u32[]{:S(2)}) collective-permute-start(bf16[64,512]{1,0:T(8,128)(2,1)S(1)} %get-tuple-element.136), channel_id=1, source_target_pairs={{0,24},{8,16},{16,8},{24,0},{1,25},{9,17},{17,9},{25,1},{2,26},{10... | collective-permute-start | bytes 196616 | tf_op jit(solution)/shard_map/ppermute | solution.py:42
  132.4 2.7 %collective-permute-start.42 = (bf16[256,2048]{1,0:T(8,128)(2,1)S(1)}, bf16[256,2048]{1,0:T(8,128)(2,1)S(1)}, u32[]{:S(2)}, u32[]{:S(2)}) collective-permute-start(bf16[256,2048]{1,0:T(8,128)(2,1)S(1)} %shard_map.73), channel_id=1, source_target_pairs={{0,1},{1,0},{2,3},{3,2},{4,5},{5,4},{6,7},{7,6},{8,9},{9,8},{10,11... | collective-permute-start | bytes 3145736 | tf_op jit(solution)/shard_map/ppermute | solution.py:37

commit v10 on v9

--- a/solution.py
+++ b/solution.py
@@ -319,20 +319,22 @@
         low_x_twin, low_y_twin = swap(low_x), swap(low_y)
         both = lambda one: [one, across(one, 1), across(one, 2)]
         x0, vs = tie(x0, vs)
-        vs = [*vs, forward(vs[1])]
+        third = forward(vs[1])
         v0 = both(vs[0])
         (x0, high_x, high_y, low_x, low_y, low_x_twin, low_y_twin, ws, vs, v0) = tie(
             x0, high_x, high_y, low_x, low_y, low_x_twin, low_y_twin, ws, vs, v0
         )
 
-        ws, vs = [*ws, forward(ws[1])], [*vs, forward(vs[2])]
+        ws = [*ws, forward(ws[1])]
         far_x, far_y = across(low_y, 1), across(high_x, 2)
         v1 = both(vs[1])
         x1 = lay(place, rows, parts, [low_x, high_x, low_x_twin, swap(high_x)])
         x2 = lay(place, rows, parts, [low_y, high_y, low_y_twin, swap(high_y)])
+        x1, third = tie(x1, third)
+        vs = [*vs, third, forward(third)]
         mix01 = run_mix((0, 1), (x0, x1, x2))
         moved = [[across(mix01[r], r)] for r in (1, 2)]
-        mix01, moved, far_x, far_y, ws, vs, v1 = tie(mix01, moved, far_x, far_y, ws, vs, v1)
+        mix01, moved, far_x, far_y, ws, vs[2], v1 = tie(mix01, moved, far_x, far_y, ws, vs[2], v1)
 
         ws = [*ws, forward(ws[2])]
         v0, v1 = [*v0, across(v0[2], 1)], [*v1, across(v1[1], 2)]

time: 137 us -> 136 us (level)
    ppermute x26, waiting for transfers between devices: 34.6 us -> 41.2 us  [across(): return lax.ppermute(block, 'dp', [(i, i ^ r) for i in range(count)])]
    ppermute x6, waiting for transfers between devices: 6.56 us -> 2.05 us  [shards(): forward = lambda block: lax.ppermute(block, 'z', ring)]
    ppermute x6, starting transfers between devices: 13.8 us -> 10.2 us  [shards(): forward = lambda block: lax.ppermute(block, 'z', ring)]
    ppermute x26, starting transfers between devices: 27.8 us -> 30.1 us  [across(): return lax.ppermute(block, 'dp', [(i, i ^ r) for i in range(count)])]
    ppermute x9, waiting for transfers between devices: 2.38 us -> 0.83 us  [swap(): return lax.ppermute(block, 'core', [(0, 1), (1, 0)])]
  transfers between devices with their start and end apart: 43 -> 43, of which waited for: 17 -> 18; matrix products, arithmetic and copies ran while one was open for 6% -> 6% of each run, Pallas kernels for 22% -> 22%
where the time goes in v10:
time: 136 us
  starting transfers between devices  49.2 us (36%)
  waiting for transfers between devices  44 us (32%)
  Pallas kernels  31.8 us (23%)
  local copies, waits for them, and re-layouts  7.6 us (6%)
  other arithmetic  2.61 us (2%)
    ppermute x26, waiting for transfers between devices, across(): return lax.ppermute(block, 'dp', [(i, i ^ r) for i in range(count)])  41.2 us
    ppermute x26, starting transfers between devices, across(): return lax.ppermute(block, 'dp', [(i, i ^ r) for i in range(count)])  30.1 us
    pallas_call x4, Pallas kernels, mix_chunks(): pl.pallas_call(functools.partial(mix_kernel, steps, slots), out_shape=[ja...  21.6 us
    ppermute x6, starting transfers between devices, shards(): forward = lambda block: lax.ppermute(block, 'z', ring)  10.2 us
    pallas_call x4, Pallas kernels, lay(): pl.pallas_call(functools.partial(lay_kernel, parts), out_shape=jax.ShapeD...  6.47 us
    ppermute x9, starting transfers between devices, swap(): return lax.ppermute(block, 'core', [(0, 1), (1, 0)])  6.12 us
    pallas_call x2, Pallas kernels, project(): pl.pallas_call(functools.partial(out_kernel, mirror, order, width, counts...  3.8 us
  transfers between devices with their start and end apart: 43, of which 18 were waited for; matrix products, arithmetic and copies ran while one was open for 6% of the time, Pallas kernels for 22%

profile of v10, /device:TPU:0, one launch (start us, length us, event | category | flops | bytes accessed | tf_op | source)
XLA Modules:
  0.0 135.6 jit_solution(8215351895655681437)
XLA Ops:
  0.0 1.2 slice.23.refs_0_
  1.2 3.0 %collective-permute-start.2 = (bf16[160,2048]{1,0:T(8,128)(2,1)S(1)}, bf16[160,2048]{1,0:T(8,128)(2,1)S(1)}, u32[]{:S(2)}, u32[]{:S(2)}) collective-permute-start(bf16[160,2048]{1,0:T(8,128)(2,1)S(1)} %slice.23.refs_0_), channel_id=1, source_target_pairs={{0,8},{8,0},{16,24},{24,16},{1,9},{9,1},{17,25},{25,17},{2,10},{10... | collective-permute-start | bytes 1966088 | tf_op jit(solution)/shard_map/ppermute | solution.py:42
  4.2 1.5 %collective-permute-start.3 = (bf16[160,2048]{1,0:T(8,128)(2,1)S(1)}, bf16[160,2048]{1,0:T(8,128)(2,1)S(1)}, u32[]{:S(2)}, u32[]{:S(2)}) collective-permute-start(bf16[160,2048]{1,0:T(8,128)(2,1)S(1)} %slice.23.refs_0_), channel_id=1, source_target_pairs={{0,16},{8,24},{16,0},{24,8},{1,17},{9,25},{17,1},{25,9},{2,18},{10... | collective-permute-start | bytes 1966088 | tf_op jit(solution)/shard_map/ppermute | solution.py:42
  5.7 2.0 %fusion.5 = (bf16[80,2048]{1,0:T(8,128)(2,1)}, bf16[80,2048]{1,0:T(8,128)(2,1)}) fusion(bf16[256,2048]{1,0:T(8,128)(2,1)} %param.6), kind=kLoop, calls=%fused_computation.22 | loop fusion | bytes 1310720 | tf_op jit(solution)/shard_map/slice | solution.py:301
  7.7 1.4 %collective-permute-start = (bf16[80,2048]{1,0:T(8,128)(2,1)}, bf16[80,2048]{1,0:T(8,128)(2,1)}, u32[]{:S(2)}, u32[]{:S(2)}) collective-permute-start(bf16[80,2048]{1,0:T(8,128)(2,1)} %get-tuple-element.138), channel_id=1, source_target_pairs={{1,2},{3,4},{5,6},{9,10},{11,12},{13,14},{17,18},{19,20},{21,22},{... | collective-permute-start | bytes 983048 | tf_op jit(solution)/shard_map/ppermute | solution.py:300
  9.1 1.4 %collective-permute-start.1 = (bf16[80,2048]{1,0:T(8,128)(2,1)}, bf16[80,2048]{1,0:T(8,128)(2,1)}, u32[]{:S(2)}, u32[]{:S(2)}) collective-permute-start(bf16[80,2048]{1,0:T(8,128)(2,1)} %get-tuple-element.137), channel_id=1, source_target_pairs={{1,3},{3,5},{5,7},{9,11},{11,13},{13,15},{17,19},{19,21},{21,23},{... | collective-permute-start | bytes 983048 | tf_op jit(solution)/shard_map/ppermute | solution.py:300
  10.5 1.5 %collective-permute-start.4 = (bf16[64,2048]{1,0:T(8,128)(2,1)}, bf16[64,2048]{1,0:T(8,128)(2,1)S(1)}, u32[]{:S(2)}, u32[]{:S(2)}) collective-permute-start(bf16[64,2048]{1,0:T(8,128)(2,1)} %refs_0_.1), channel_id=1, source_target_pairs={{0,2},{2,6},{6,4},{4,0},{1,3},{3,7},{7,5},{5,1},{8,10},{10,14},{14... | collective-permute-start | bytes 786440 | tf_op jit(solution)/shard_map/ppermute | solution.py:291
  12.0 1.9 %reshape.10 = f32[7,3,16,2,64]{4,3,2,0,1:T(2,128)} reshape(f32[7,3,2048]{2,0,1:T(8,128)} %param.8) | data formatting | bytes 344064 | tf_op jit(solution)/shard_map/reshape | solution.py:263
  13.9 0.9 constant_dynamic-slice_fusion.5
  16.6 1.2 add.55
  17.7 1.3 collective-permute-done.4.refs_1_
  19.0 1.4 %collective-permute-done.3.refs_0_ = bf16[160,2048]{1,0:T(8,128)(2,1)S(1)} collective-permute-done((bf16[160,2048]{1,0:T(8,128)(2,1)S(1)}, bf16[160,2048]{1,0:T(8,128)(2,1)S(1)}, u32[]{:S(2)}, u32[]{:S(2)}) %collective-permute-start.3) | collective-permute-done | bytes 655392 | tf_op jit(solution)/shard_map/ppermute | solution.py:42
  20.5 4.4 %collective-permute-start.6 = (bf16[176,2048]{1,0:T(8,128)(2,1)S(1)}, bf16[176,2048]{1,0:T(8,128)(2,1)S(1)}, u32[]{:S(2)}, u32[]{:S(2)}) collective-permute-start(bf16[176,2048]{1,0:T(8,128)(2,1)S(1)} %constant_dynamic-update-slice_fusion.refs_1_), channel_id=1, source_target_pairs={{0,1},{1,0},{2,3},{3,2},{4,5},{5,4},{6,7},{7,6},{8,9},{9,8},{10,11... | collective-permute-start | bytes 2162696 | tf_op jit(solution)/shard_map/ppermute | solution.py:37
  25.5 2.1 %collective-permute-start.11 = (bf16[192,2048]{1,0:T(8,128)(2,1)S(1)}, bf16[192,2048]{1,0:T(8,128)(2,1)S(1)}, u32[]{:S(2)}, u32[]{:S(2)}) collective-permute-start(bf16[192,2048]{1,0:T(8,128)(2,1)S(1)} %bitcast.26), channel_id=1, source_target_pairs={{0,2},{2,6},{6,4},{4,0},{1,3},{3,7},{7,5},{5,1},{8,10},{10,14},{14... | collective-permute-start | bytes 2359304 | tf_op jit(solution)/shard_map/ppermute | solution.py:291
  28.7 1.6 %shard_map.64.rest_2_.rest_1_ = bf16[672,2048]{1,0:T(8,128)(2,1)S(1)} custom-call(s32[6]{0:T(128)S(1)} %pad_add_fusion.place_ref, bf16[160,2048]{1,0:T(8,128)(2,1)S(1)} %slice.23.refs_0_, bf16[176,2048]{1,0:T(8,128)(2,1)S(1)} %constant_dynamic-update-slice_fusion.refs_1_, bf16[160,2048]{1,0:T(8,128)(2,1)S(1)} %collective-permute-done.5.refs_2_, ...), custom_call_target="tpu_custom_call" | custom-call | bytes 5505024 | tf_op jit(solution)/shard_map/pallas_call | solution.py:87
  30.4 1.6 %collective-permute-start.12 = (bf16[64,2048]{1,0:T(8,128)(2,1)S(1)}, bf16[64,2048]{1,0:T(8,128)(2,1)S(1)}, u32[]{:S(2)}, u32[]{:S(2)}) collective-permute-start(bf16[64,2048]{1,0:T(8,128)(2,1)S(1)} %copy-done.1), channel_id=1, source_target_pairs={{0,8},{8,0},{16,24},{24,16},{1,9},{9,1},{17,25},{25,17},{2,10},{10... | collective-permute-start | bytes 786440 | tf_op jit(solution)/shard_map/ppermute | solution.py:42
  31.9 1.5 %collective-permute-start.13 = (bf16[64,2048]{1,0:T(8,128)(2,1)S(1)}, bf16[64,2048]{1,0:T(8,128)(2,1)S(1)}, u32[]{:S(2)}, u32[]{:S(2)}) collective-permute-start(bf16[64,2048]{1,0:T(8,128)(2,1)S(1)} %copy-done.1), channel_id=1, source_target_pairs={{0,16},{8,24},{16,0},{24,8},{1,17},{9,25},{17,1},{25,9},{2,18},{10... | collective-permute-start | bytes 786440 | tf_op jit(solution)/shard_map/ppermute | solution.py:42
  33.5 13.2 %collective-permute-done.7.refs_1_ = bf16[176,2048]{1,0:T(8,128)(2,1)S(1)} collective-permute-done((bf16[176,2048]{1,0:T(8,128)(2,1)S(1)}, bf16[176,2048]{1,0:T(8,128)(2,1)S(1)}, u32[]{:S(2)}, u32[]{:S(2)}) %collective-permute-start.7) | collective-permute-done | bytes 720928 | tf_op jit(solution)/shard_map/ppermute | solution.py:42
  47.2 4.5 %collective-permute-done.12.refs_4_ = bf16[64,2048]{1,0:T(8,128)(2,1)S(1)} collective-permute-done((bf16[64,2048]{1,0:T(8,128)(2,1)S(1)}, bf16[64,2048]{1,0:T(8,128)(2,1)S(1)}, u32[]{:S(2)}, u32[]{:S(2)}) %collective-permute-start.12) | collective-permute-done | bytes 262176 | tf_op jit(solution)/shard_map/ppermute | solution.py:42
  52.5 3.6 %collective-permute-start.15 = (bf16[64,2048]{1,0:T(8,128)(2,1)S(1)}, bf16[64,2048]{1,0:T(8,128)(2,1)S(1)}, u32[]{:S(2)}, u32[]{:S(2)}) collective-permute-start(bf16[64,2048]{1,0:T(8,128)(2,1)S(1)} %collective-permute-done.4.refs_1_), channel_id=1, source_target_pairs={{0,2},{2,6},{6,4},{4,0},{1,3},{3,7},{7,5},{5,1},{8,10},{10,14},{14... | collective-permute-start | bytes 786440 | tf_op jit(solution)/shard_map/ppermute | solution.py:291
  56.1 2.4 %collective-permute-start.21 = (bf16[192,2048]{1,0:T(8,128)(2,1)S(1)}, bf16[192,2048]{1,0:T(8,128)(2,1)S(1)}, u32[]{:S(2)}, u32[]{:S(2)}) collective-permute-start(bf16[192,2048]{1,0:T(8,128)(2,1)S(1)} %collective-permute-done.11.rest_1_), channel_id=1, source_target_pairs={{0,2},{2,6},{6,4},{4,0},{1,3},{3,7},{7,5},{5,1},{8,10},{10,14},{14... | collective-permute-start | bytes 2359304 | tf_op jit(solution)/shard_map/ppermute | solution.py:291
  58.9 1.5 %collective-permute-start.22 = (bf16[64,2048]{1,0:T(8,128)(2,1)S(1)}, bf16[64,2048]{1,0:T(8,128)(2,1)S(1)}, u32[]{:S(2)}, u32[]{:S(2)}) collective-permute-start(bf16[64,2048]{1,0:T(8,128)(2,1)S(1)} %collective-permute-done.4.refs_1_), channel_id=1, source_target_pairs={{0,8},{8,0},{16,24},{24,16},{1,9},{9,1},{17,25},{25,17},{2,10},{10... | collective-permute-start | bytes 786440 | tf_op jit(solution)/shard_map/ppermute | solution.py:42
  60.4 1.6 %shard_map.65.rest_3_.rest_2_ = bf16[672,2048]{1,0:T(8,128)(2,1)S(1)} custom-call(s32[6]{0:T(128)S(1)} %pad_add_fusion.place_ref, bf16[160,2048]{1,0:T(8,128)(2,1)S(1)} %collective-permute-done.2.refs_0_, bf16[176,2048]{1,0:T(8,128)(2,1)S(1)} %collective-permute-done.7.refs_1_, bf16[160,2048]{1,0:T(8,128)(2,1)S(1)} %collective-permute-done.9.refs_2_, ...), custom_call_target="tpu_custom_call" | custom-call | bytes 5505024 | tf_op jit(solution)/shard_map/pallas_call | solution.py:87
  63.7 1.1 collective-permute-start.19
  64.8 1.6 %shard_map.66.rest_4_.rest_3_ = bf16[672,2048]{1,0:T(8,128)(2,1)S(1)} custom-call(s32[6]{0:T(128)S(1)} %pad_add_fusion.place_ref, bf16[160,2048]{1,0:T(8,128)(2,1)S(1)} %collective-permute-done.3.refs_0_, bf16[176,2048]{1,0:T(8,128)(2,1)S(1)} %collective-permute-done.8.refs_1_, bf16[160,2048]{1,0:T(8,128)(2,1)S(1)} %collective-permute-done.10.refs_2_, ...), custom_call_target="tpu_custom_call" | custom-call | bytes 5505024 | tf_op jit(solution)/shard_map/pallas_call | solution.py:87
  66.4 7.6 %shard_map.67 = (bf16[128,512]{1,0:T(8,128)(2,1)S(1)}, bf16[128,512]{1,0:T(8,128)(2,1)S(1)}, bf16[128,512]{1,0:T(8,128)(2,1)S(1)}) custom-call(s32[6]{0:T(128)S(1)} %pad_add_fusion.place_ref, f32[4,8,256]{2,1,0:T(8,128)S(1)} %pad_maximum_fusion.taps_ref, f32[4,4,128]{2,1,0:T(4,128)S(1)} %maximum_convert_fusion.long_ref, bf16[192,2048]{1,0:T(8,128)(2,1)S(1)} %bitcast.27, ...), custom_call_target="tpu_custom_call" | custom-call | flops 6442450944 | bytes 12582912 | tf_op jit(solution)/shard_map/pallas_call | solution.py:183
  74.0 1.0 collective-permute-start.17
  75.0 6.5 %collective-permute-done.23.refs_9_ = bf16[64,2048]{1,0:T(8,128)(2,1)S(1)} collective-permute-done((bf16[64,2048]{1,0:T(8,128)(2,1)S(1)}, bf16[64,2048]{1,0:T(8,128)(2,1)S(1)}, u32[]{:S(2)}, u32[]{:S(2)}) %collective-permute-start.23) | collective-permute-done | bytes 262176 | tf_op jit(solution)/shard_map/ppermute | solution.py:42
  82.1 1.1 collective-permute-done.17.refs_19_
  83.2 3.3 %collective-permute-done.18.refs_22_ = bf16[128,512]{1,0:T(8,128)(2,1)S(1)} collective-permute-done((bf16[128,512]{1,0:T(8,128)(2,1)S(1)}, bf16[128,512]{1,0:T(8,128)(2,1)S(1)}, u32[]{:S(2)}, u32[]{:S(2)}) %collective-permute-start.18) | collective-permute-done | bytes 131104 | tf_op jit(solution)/shard_map/ppermute | solution.py:42
  87.0 1.5 %collective-permute-start.30 = (bf16[64,2048]{1,0:T(8,128)(2,1)S(1)}, bf16[64,2048]{1,0:T(8,128)(2,1)S(1)}, u32[]{:S(2)}, u32[]{:S(2)}) collective-permute-start(bf16[64,2048]{1,0:T(8,128)(2,1)S(1)} %collective-permute-done.13.refs_8_), channel_id=1, source_target_pairs={{0,8},{8,0},{16,24},{24,16},{1,9},{9,1},{17,25},{25,17},{2,10},{10... | collective-permute-start | bytes 786440 | tf_op jit(solution)/shard_map/ppermute | solution.py:42
  89.1 4.3 %shard_map.68 = (bf16[64,512]{1,0:T(8,128)(2,1)S(1)}, bf16[64,512]{1,0:T(8,128)(2,1)S(1)}, bf16[64,512]{1,0:T(8,128)(2,1)S(1)}) custom-call(s32[6]{0:T(128)S(1)} %pad_add_fusion.place_ref, f32[4,8,256]{2,1,0:T(8,128)S(1)} %pad_maximum_fusion.taps_ref, f32[4,4,128]{2,1,0:T(4,128)S(1)} %maximum_convert_fusion.long_ref, ...), custom_call_target="tpu_custom_call" | custom-call | flops 3221225472 | bytes 6291456 | tf_op jit(solution)/shard_map/pallas_call | solution.py:183
  94.8 1.6 %shard_map.69.rest_3_.rest_4_ = bf16[672,2048]{1,0:T(8,128)(2,1)S(1)} custom-call(s32[6]{0:T(128)S(1)} %pad_add_fusion.place_ref, bf16[160,2048]{1,0:T(8,128)(2,1)S(1)} %collective-permute-done.19.refs_0_, bf16[176,2048]{1,0:T(8,128)(2,1)S(1)} %collective-permute-done.20.refs_1_, bf16[160,2048]{1,0:T(8,128)(2,1)S(1)} %collective-permute-done.24.refs_2_, ...), custom_call_target="tpu_custom_call" | custom-call | bytes 5505024 | tf_op jit(solution)/shard_map/pallas_call | solution.py:87
  96.5 1.3 collective-permute-start.31
  98.6 1.5 %collective-permute-start.34 = (bf16[64,2048]{1,0:T(8,128)(2,1)S(1)}, bf16[64,2048]{1,0:T(8,128)(2,1)S(1)}, u32[]{:S(2)}, u32[]{:S(2)}) collective-permute-start(bf16[64,2048]{1,0:T(8,128)(2,1)S(1)} %collective-permute-done.32.refs_3_), channel_id=1, source_target_pairs={{0,8},{8,0},{16,24},{24,16},{1,9},{9,1},{17,25},{25,17},{2,10},{10... | collective-permute-start | bytes 786440 | tf_op jit(solution)/shard_map/ppermute | solution.py:42
  100.1 4.3 %shard_map.70 = bf16[192,512]{1,0:T(8,128)(2,1)S(1)} custom-call(s32[6]{0:T(128)S(1)} %pad_add_fusion.place_ref, f32[4,8,256]{2,1,0:T(8,128)S(1)} %pad_maximum_fusion.taps_ref, f32[4,4,128]{2,1,0:T(4,128)S(1)} %maximum_convert_fusion.long_ref, bf16[192,2048]{1,0:T(8,128)(2,1)S(1)} %bitcast.28, bf16[192,2048]{1,0:T(8,128)(2,1)S(1)} %collective-permute-done.11.rest_1_, ...), custom_call_target="tpu_custom_call" | custom-call | flops 3221225472 | bytes 6291456 | tf_op jit(solution)/shard_map/pallas_call | solution.py:183
  104.4 1.3 collective-permute-start.28
  105.7 2.2 %collective-permute-done.31.refs_13_ = bf16[64,2048]{1,0:T(8,128)(2,1)S(1)} collective-permute-done((bf16[64,2048]{1,0:T(8,128)(2,1)S(1)}, bf16[64,2048]{1,0:T(8,128)(2,1)S(1)}, u32[]{:S(2)}, u32[]{:S(2)}) %collective-permute-start.31) | collective-permute-done | bytes 262176 | tf_op jit(solution)/shard_map/ppermute | solution.py:42
  107.9 1.5 %collective-permute-start.33 = (bf16[64,2048]{1,0:T(8,128)(2,1)S(1)}, bf16[64,2048]{1,0:T(8,128)(2,1)S(1)}, u32[]{:S(2)}, u32[]{:S(2)}) collective-permute-start(bf16[64,2048]{1,0:T(8,128)(2,1)S(1)} %collective-permute-done.15.refs_2_), channel_id=1, source_target_pairs={{0,8},{8,0},{16,24},{24,16},{1,9},{9,1},{17,25},{25,17},{2,10},{10... | collective-permute-start | bytes 786440 | tf_op jit(solution)/shard_map/ppermute | solution.py:42
  109.4 4.7 %collective-permute-done.35.refs_10_ = bf16[64,2048]{1,0:T(8,128)(2,1)S(1)} collective-permute-done((bf16[64,2048]{1,0:T(8,128)(2,1)S(1)}, bf16[64,2048]{1,0:T(8,128)(2,1)S(1)}, u32[]{:S(2)}, u32[]{:S(2)}) %collective-permute-start.35) | collective-permute-done | bytes 262176 | tf_op jit(solution)/shard_map/ppermute | solution.py:42
  115.0 1.1 collective-permute-start.37
  116.1 1.3 collective-permute-start.38
  117.3 5.4 %shard_map.71 = (bf16[64,512]{1,0:T(8,128)(2,1)S(1)}, bf16[64,512]{1,0:T(8,128)(2,1)S(1)}, bf16[64,512]{1,0:T(8,128)(2,1)S(1)}, bf16[64,512]{1,0:T(8,128)(2,1)S(1)}) custom-call(s32[6]{0:T(128)S(1)} %pad_add_fusion.place_ref, f32[4,8,256]{2,1,0:T(8,128)S(1)} %pad_maximum_fusion.taps_ref, f32[4,4,128]{2,1,0:T(4,128)S(1)} %maximum_convert_fusion.long_ref, ...), custom_call_target="tpu_custom_call" | custom-call | flops 4294967296 | bytes 8388608 | tf_op jit(solution)/shard_map/pallas_call | solution.py:183
  124.5 1.8 %collective-permute-start.41 = (bf16[64,512]{1,0:T(8,128)(2,1)S(1)}, bf16[64,512]{1,0:T(8,128)(2,1)S(1)}, u32[]{:S(2)}, u32[]{:S(2)}) collective-permute-start(bf16[64,512]{1,0:T(8,128)(2,1)S(1)} %get-tuple-element.136), channel_id=1, source_target_pairs={{0,24},{8,16},{16,8},{24,0},{1,25},{9,17},{17,9},{25,1},{2,26},{10... | collective-permute-start | bytes 196616 | tf_op jit(solution)/shard_map/ppermute | solution.py:42
  127.8 1.8 %collective-permute-done.41.refs_26_ = bf16[64,512]{1,0:T(8,128)(2,1)S(1)} collective-permute-done((bf16[64,512]{1,0:T(8,128)(2,1)S(1)}, bf16[64,512]{1,0:T(8,128)(2,1)S(1)}, u32[]{:S(2)}, u32[]{:S(2)}) %collective-permute-start.41) | collective-permute-done | bytes 65568 | tf_op jit(solution)/shard_map/ppermute | solution.py:42
  129.6 1.9 %shard_map.73 = bf16[256,2048]{1,0:T(8,128)(2,1)S(1)} custom-call(s32[6]{0:T(128)S(1)} %pad_add_fusion.place_ref, bf16[64,2048]{1,0:T(8,128)(2,1)S(1)} %copy-done.1, bf16[64,2048]{1,0:T(8,128)(2,1)S(1)} %collective-permute-done.4.refs_1_, bf16[64,2048]{1,0:T(8,128)(2,1)S(1)} %collective-permute-done.15.refs_2_, ...), custom_call_target="tpu_custom_call" | custom-call | flops 2147483648 | bytes 5242880 | tf_op jit(solution)/shard_map/pallas_call | solution.py:243
  131.6 1.9 %shard_map.72 = f32[256,2048]{1,0:T(8,128)S(1)} custom-call(s32[6]{0:T(128)S(1)} %pad_add_fusion.place_ref, bf16[64,2048]{1,0:T(8,128)(2,1)S(1)} %copy-done.1, bf16[64,2048]{1,0:T(8,128)(2,1)S(1)} %collective-permute-done.4.refs_1_, bf16[64,2048]{1,0:T(8,128)(2,1)S(1)} %collective-permute-done.15.refs_2_, ...), custom_call_target="tpu_custom_call" | custom-call | flops 2147483648 | bytes 5242880 | tf_op jit(solution)/shard_map/pallas_call | solution.py:243
  134.3 1.3 add_convert_fusion
  (72 shorter events, 15.8 us)
Async XLA Ops:
  0.0 20.4 %slice-start = ((bf16[256,2048]{1,0:T(8,128)(2,1)}), bf16[96,2048]{1,0:T(8,128)(2,1)S(1)}, s32[]{:S(2)}) async-start(bf16[256,2048]{1,0:T(8,128)(2,1)} %param.6), calls=%async_computation | async-start | bytes 786432 | tf_op jit(solution)/shard_map/slice | solution.py:309
  1.2 24.3 %copy-start = (bf16[3,64,2048]{2,1,0:T(8,128)(2,1)S(1)}, bf16[3,64,2048]{2,1,0:T(8,128)(2,1)}, u32[]{:S(2)}) copy-start(bf16[3,64,2048]{2,1,0:T(8,128)(2,1)} %param.7) | copy-start | bytes 2359300
  1.2 17.8 %collective-permute-start.2 = (bf16[160,2048]{1,0:T(8,128)(2,1)S(1)}, bf16[160,2048]{1,0:T(8,128)(2,1)S(1)}, u32[]{:S(2)}, u32[]{:S(2)}) collective-permute-start(bf16[160,2048]{1,0:T(8,128)(2,1)S(1)} %slice.23.refs_0_), channel_id=1, source_target_pairs={{0,8},{8,0},{16,24},{24,16},{1,9},{9,1},{17,25},{25,17},{2,10},{10... | collective-permute-start | bytes 1966088 | tf_op jit(solution)/shard_map/ppermute | solution.py:42
  4.2 16.2 %collective-permute-start.3 = (bf16[160,2048]{1,0:T(8,128)(2,1)S(1)}, bf16[160,2048]{1,0:T(8,128)(2,1)S(1)}, u32[]{:S(2)}, u32[]{:S(2)}) collective-permute-start(bf16[160,2048]{1,0:T(8,128)(2,1)S(1)} %slice.23.refs_0_), channel_id=1, source_target_pairs={{0,16},{8,24},{16,0},{24,8},{1,17},{9,25},{17,1},{25,9},{2,18},{10... | collective-permute-start | bytes 1966088 | tf_op jit(solution)/shard_map/ppermute | solution.py:42
  7.7 8.8 %collective-permute-start = (bf16[80,2048]{1,0:T(8,128)(2,1)}, bf16[80,2048]{1,0:T(8,128)(2,1)}, u32[]{:S(2)}, u32[]{:S(2)}) collective-permute-start(bf16[80,2048]{1,0:T(8,128)(2,1)} %get-tuple-element.138), channel_id=1, source_target_pairs={{1,2},{3,4},{5,6},{9,10},{11,12},{13,14},{17,18},{19,20},{21,22},{... | collective-permute-start | bytes 983048 | tf_op jit(solution)/shard_map/ppermute | solution.py:300
  9.1 7.5 %collective-permute-start.1 = (bf16[80,2048]{1,0:T(8,128)(2,1)}, bf16[80,2048]{1,0:T(8,128)(2,1)}, u32[]{:S(2)}, u32[]{:S(2)}) collective-permute-start(bf16[80,2048]{1,0:T(8,128)(2,1)} %get-tuple-element.137), channel_id=1, source_target_pairs={{1,3},{3,5},{5,7},{9,11},{11,13},{13,15},{17,19},{19,21},{21,23},{... | collective-permute-start | bytes 983048 | tf_op jit(solution)/shard_map/ppermute | solution.py:300
  10.5 8.6 %collective-permute-start.4 = (bf16[64,2048]{1,0:T(8,128)(2,1)}, bf16[64,2048]{1,0:T(8,128)(2,1)S(1)}, u32[]{:S(2)}, u32[]{:S(2)}) collective-permute-start(bf16[64,2048]{1,0:T(8,128)(2,1)} %refs_0_.1), channel_id=1, source_target_pairs={{0,2},{2,6},{6,4},{4,0},{1,3},{3,7},{7,5},{5,1},{8,10},{10,14},{14... | collective-permute-start | bytes 786440 | tf_op jit(solution)/shard_map/ppermute | solution.py:291
  20.5 9.9 %copy-start.1 = (bf16[64,2048]{1,0:T(8,128)(2,1)S(1)}, bf16[64,2048]{1,0:T(8,128)(2,1)}, u32[]{:S(2)}) copy-start(bf16[64,2048]{1,0:T(8,128)(2,1)} %refs_0_.1) | copy-start | bytes 786436
  20.5 7.7 %collective-permute-start.6 = (bf16[176,2048]{1,0:T(8,128)(2,1)S(1)}, bf16[176,2048]{1,0:T(8,128)(2,1)S(1)}, u32[]{:S(2)}, u32[]{:S(2)}) collective-permute-start(bf16[176,2048]{1,0:T(8,128)(2,1)S(1)} %constant_dynamic-update-slice_fusion.refs_1_), channel_id=1, source_target_pairs={{0,1},{1,0},{2,3},{3,2},{4,5},{5,4},{6,7},{7,6},{8,9},{9,8},{10,11... | collective-permute-start | bytes 2162696 | tf_op jit(solution)/shard_map/ppermute | solution.py:37
  24.9 2.8 %collective-permute-start.5 = (bf16[160,2048]{1,0:T(8,128)(2,1)S(1)}, bf16[160,2048]{1,0:T(8,128)(2,1)S(1)}, u32[]{:S(2)}, u32[]{:S(2)}) collective-permute-start(bf16[160,2048]{1,0:T(8,128)(2,1)S(1)} %slice.23.refs_0_), channel_id=1, source_target_pairs={{0,1},{1,0},{2,3},{3,2},{4,5},{5,4},{6,7},{7,6},{8,9},{9,8},{10,11... | collective-permute-start | bytes 1966088 | tf_op jit(solution)/shard_map/ppermute | solution.py:37
  25.0 5.4 %collective-permute-start.10 = (bf16[160,2048]{1,0:T(8,128)(2,1)S(1)}, bf16[160,2048]{1,0:T(8,128)(2,1)S(1)}, u32[]{:S(2)}, u32[]{:S(2)}) collective-permute-start(bf16[160,2048]{1,0:T(8,128)(2,1)S(1)} %collective-permute-done.3.refs_0_), channel_id=1, source_target_pairs={{0,1},{1,0},{2,3},{3,2},{4,5},{5,4},{6,7},{7,6},{8,9},{9,8},{10,11... | collective-permute-start | bytes 1966088 | tf_op jit(solution)/shard_map/ppermute | solution.py:37
  25.4 6.5 %collective-permute-start.9 = (bf16[160,2048]{1,0:T(8,128)(2,1)S(1)}, bf16[160,2048]{1,0:T(8,128)(2,1)S(1)}, u32[]{:S(2)}, u32[]{:S(2)}) collective-permute-start(bf16[160,2048]{1,0:T(8,128)(2,1)S(1)} %collective-permute-done.2.refs_0_), channel_id=1, source_target_pairs={{0,1},{1,0},{2,3},{3,2},{4,5},{5,4},{6,7},{7,6},{8,9},{9,8},{10,11... | collective-permute-start | bytes 1966088 | tf_op jit(solution)/shard_map/ppermute | solution.py:37
  25.5 21.7 %collective-permute-start.11 = (bf16[192,2048]{1,0:T(8,128)(2,1)S(1)}, bf16[192,2048]{1,0:T(8,128)(2,1)S(1)}, u32[]{:S(2)}, u32[]{:S(2)}) collective-permute-start(bf16[192,2048]{1,0:T(8,128)(2,1)S(1)} %bitcast.26), channel_id=1, source_target_pairs={{0,2},{2,6},{6,4},{4,0},{1,3},{3,7},{7,5},{5,1},{8,10},{10,14},{14... | collective-permute-start | bytes 2359304 | tf_op jit(solution)/shard_map/ppermute | solution.py:291
  27.7 19.0 %collective-permute-start.7 = (bf16[176,2048]{1,0:T(8,128)(2,1)S(1)}, bf16[176,2048]{1,0:T(8,128)(2,1)S(1)}, u32[]{:S(2)}, u32[]{:S(2)}) collective-permute-start(bf16[176,2048]{1,0:T(8,128)(2,1)S(1)} %constant_dynamic-update-slice_fusion.refs_1_), channel_id=1, source_target_pairs={{0,8},{8,0},{16,24},{24,16},{1,9},{9,1},{17,25},{25,17},{2,10},{10... | collective-permute-start | bytes 2162696 | tf_op jit(solution)/shard_map/ppermute | solution.py:42
  28.2 19.0 %collective-permute-start.8 = (bf16[176,2048]{1,0:T(8,128)(2,1)S(1)}, bf16[176,2048]{1,0:T(8,128)(2,1)S(1)}, u32[]{:S(2)}, u32[]{:S(2)}) collective-permute-start(bf16[176,2048]{1,0:T(8,128)(2,1)S(1)} %constant_dynamic-update-slice_fusion.refs_1_), channel_id=1, source_target_pairs={{0,16},{8,24},{16,0},{24,8},{1,17},{9,25},{17,1},{25,9},{2,18},{10... | collective-permute-start | bytes 2162696 | tf_op jit(solution)/shard_map/ppermute | solution.py:42
  30.4 21.3 %collective-permute-start.12 = (bf16[64,2048]{1,0:T(8,128)(2,1)S(1)}, bf16[64,2048]{1,0:T(8,128)(2,1)S(1)}, u32[]{:S(2)}, u32[]{:S(2)}) collective-permute-start(bf16[64,2048]{1,0:T(8,128)(2,1)S(1)} %copy-done.1), channel_id=1, source_target_pairs={{0,8},{8,0},{16,24},{24,16},{1,9},{9,1},{17,25},{25,17},{2,10},{10... | collective-permute-start | bytes 786440 | tf_op jit(solution)/shard_map/ppermute | solution.py:42
  31.9 20.0 %collective-permute-start.13 = (bf16[64,2048]{1,0:T(8,128)(2,1)S(1)}, bf16[64,2048]{1,0:T(8,128)(2,1)S(1)}, u32[]{:S(2)}, u32[]{:S(2)}) collective-permute-start(bf16[64,2048]{1,0:T(8,128)(2,1)S(1)} %copy-done.1), channel_id=1, source_target_pairs={{0,16},{8,24},{16,0},{24,8},{1,17},{9,25},{17,1},{25,9},{2,18},{10... | collective-permute-start | bytes 786440 | tf_op jit(solution)/shard_map/ppermute | solution.py:42
  52.0 7.0 %collective-permute-start.14 = (bf16[176,2048]{1,0:T(8,128)(2,1)S(1)}, bf16[176,2048]{1,0:T(8,128)(2,1)S(1)}, u32[]{:S(2)}, u32[]{:S(2)}) collective-permute-start(bf16[176,2048]{1,0:T(8,128)(2,1)S(1)} %collective-permute-done.7.refs_1_), channel_id=1, source_target_pairs={{0,1},{1,0},{2,3},{3,2},{4,5},{5,4},{6,7},{7,6},{8,9},{9,8},{10,11... | collective-permute-start | bytes 2162696 | tf_op jit(solution)/shard_map/ppermute | solution.py:37
  52.0 11.7 %collective-permute-start.16 = (bf16[176,2048]{1,0:T(8,128)(2,1)S(1)}, bf16[176,2048]{1,0:T(8,128)(2,1)S(1)}, u32[]{:S(2)}, u32[]{:S(2)}) collective-permute-start(bf16[176,2048]{1,0:T(8,128)(2,1)S(1)} %collective-permute-done.8.refs_1_), channel_id=1, source_target_pairs={{0,1},{1,0},{2,3},{3,2},{4,5},{5,4},{6,7},{7,6},{8,9},{9,8},{10,11... | collective-permute-start | bytes 2162696 | tf_op jit(solution)/shard_map/ppermute | solution.py:37
  52.5 10.3 %collective-permute-start.15 = (bf16[64,2048]{1,0:T(8,128)(2,1)S(1)}, bf16[64,2048]{1,0:T(8,128)(2,1)S(1)}, u32[]{:S(2)}, u32[]{:S(2)}) collective-permute-start(bf16[64,2048]{1,0:T(8,128)(2,1)S(1)} %collective-permute-done.4.refs_1_), channel_id=1, source_target_pairs={{0,2},{2,6},{6,4},{4,0},{1,3},{3,7},{7,5},{5,1},{8,10},{10,14},{14... | collective-permute-start | bytes 786440 | tf_op jit(solution)/shard_map/ppermute | solution.py:291
  56.1 26.0 %collective-permute-start.21 = (bf16[192,2048]{1,0:T(8,128)(2,1)S(1)}, bf16[192,2048]{1,0:T(8,128)(2,1)S(1)}, u32[]{:S(2)}, u32[]{:S(2)}) collective-permute-start(bf16[192,2048]{1,0:T(8,128)(2,1)S(1)} %collective-permute-done.11.rest_1_), channel_id=1, source_target_pairs={{0,2},{2,6},{6,4},{4,0},{1,3},{3,7},{7,5},{5,1},{8,10},{10,14},{14... | collective-permute-start | bytes 2359304 | tf_op jit(solution)/shard_map/ppermute | solution.py:291
  58.4 23.6 %collective-permute-start.20 = (bf16[176,2048]{1,0:T(8,128)(2,1)S(1)}, bf16[176,2048]{1,0:T(8,128)(2,1)S(1)}, u32[]{:S(2)}, u32[]{:S(2)}) collective-permute-start(bf16[176,2048]{1,0:T(8,128)(2,1)S(1)} %collective-permute-done.7.refs_1_), channel_id=1, source_target_pairs={{0,16},{8,24},{16,0},{24,8},{1,17},{9,25},{17,1},{25,9},{2,18},{10... | collective-permute-start | bytes 2162696 | tf_op jit(solution)/shard_map/ppermute | solution.py:42
  58.9 15.1 %collective-permute-start.22 = (bf16[64,2048]{1,0:T(8,128)(2,1)S(1)}, bf16[64,2048]{1,0:T(8,128)(2,1)S(1)}, u32[]{:S(2)}, u32[]{:S(2)}) collective-permute-start(bf16[64,2048]{1,0:T(8,128)(2,1)S(1)} %collective-permute-done.4.refs_1_), channel_id=1, source_target_pairs={{0,8},{8,0},{16,24},{24,16},{1,9},{9,1},{17,25},{25,17},{2,10},{10... | collective-permute-start | bytes 786440 | tf_op jit(solution)/shard_map/ppermute | solution.py:42
  62.8 18.8 %collective-permute-start.23 = (bf16[64,2048]{1,0:T(8,128)(2,1)S(1)}, bf16[64,2048]{1,0:T(8,128)(2,1)S(1)}, u32[]{:S(2)}, u32[]{:S(2)}) collective-permute-start(bf16[64,2048]{1,0:T(8,128)(2,1)S(1)} %collective-permute-done.4.refs_1_), channel_id=1, source_target_pairs={{0,16},{8,24},{16,0},{24,8},{1,17},{9,25},{17,1},{25,9},{2,18},{10... | collective-permute-start | bytes 786440 | tf_op jit(solution)/shard_map/ppermute | solution.py:42
  63.7 18.4 %collective-permute-start.19 = (bf16[160,2048]{1,0:T(8,128)(2,1)S(1)}, bf16[160,2048]{1,0:T(8,128)(2,1)S(1)}, u32[]{:S(2)}, u32[]{:S(2)}) collective-permute-start(bf16[160,2048]{1,0:T(8,128)(2,1)S(1)} %collective-permute-done.3.refs_0_), channel_id=1, source_target_pairs={{0,8},{8,0},{16,24},{24,16},{1,9},{9,1},{17,25},{25,17},{2,10},{10... | collective-permute-start | bytes 1966088 | tf_op jit(solution)/shard_map/ppermute | solution.py:42
  74.0 9.2 %collective-permute-start.17 = (bf16[128,512]{1,0:T(8,128)(2,1)S(1)}, bf16[128,512]{1,0:T(8,128)(2,1)S(1)}, u32[]{:S(2)}, u32[]{:S(2)}) collective-permute-start(bf16[128,512]{1,0:T(8,128)(2,1)S(1)} %get-tuple-element.96), channel_id=1, source_target_pairs={{0,8},{8,0},{16,24},{24,16},{1,9},{9,1},{17,25},{25,17},{2,10},{10... | collective-permute-start | bytes 393224 | tf_op jit(solution)/shard_map/ppermute | solution.py:42
  81.5 5.0 %collective-permute-start.18 = (bf16[128,512]{1,0:T(8,128)(2,1)S(1)}, bf16[128,512]{1,0:T(8,128)(2,1)S(1)}, u32[]{:S(2)}, u32[]{:S(2)}) collective-permute-start(bf16[128,512]{1,0:T(8,128)(2,1)S(1)} %get-tuple-element.97), channel_id=1, source_target_pairs={{0,16},{8,24},{16,0},{24,8},{1,17},{9,25},{17,1},{25,9},{2,18},{10... | collective-permute-start | bytes 393224 | tf_op jit(solution)/shard_map/ppermute | solution.py:42
  86.5 7.6 %collective-permute-start.25 = (bf16[176,2048]{1,0:T(8,128)(2,1)S(1)}, bf16[176,2048]{1,0:T(8,128)(2,1)S(1)}, u32[]{:S(2)}, u32[]{:S(2)}) collective-permute-start(bf16[176,2048]{1,0:T(8,128)(2,1)S(1)} %collective-permute-done.20.refs_1_), channel_id=1, source_target_pairs={{0,1},{1,0},{2,3},{3,2},{4,5},{5,4},{6,7},{7,6},{8,9},{9,8},{10,11... | collective-permute-start | bytes 2162696 | tf_op jit(solution)/shard_map/ppermute | solution.py:37
  86.5 7.0 %collective-permute-start.24 = (bf16[160,2048]{1,0:T(8,128)(2,1)S(1)}, bf16[160,2048]{1,0:T(8,128)(2,1)S(1)}, u32[]{:S(2)}, u32[]{:S(2)}) collective-permute-start(bf16[160,2048]{1,0:T(8,128)(2,1)S(1)} %collective-permute-done.19.refs_0_), channel_id=1, source_target_pairs={{0,1},{1,0},{2,3},{3,2},{4,5},{5,4},{6,7},{7,6},{8,9},{9,8},{10,11... | collective-permute-start | bytes 1966088 | tf_op jit(solution)/shard_map/ppermute | solution.py:37
  87.0 9.5 %collective-permute-start.30 = (bf16[64,2048]{1,0:T(8,128)(2,1)S(1)}, bf16[64,2048]{1,0:T(8,128)(2,1)S(1)}, u32[]{:S(2)}, u32[]{:S(2)}) collective-permute-start(bf16[64,2048]{1,0:T(8,128)(2,1)S(1)} %collective-permute-done.13.refs_8_), channel_id=1, source_target_pairs={{0,8},{8,0},{16,24},{24,16},{1,9},{9,1},{17,25},{25,17},{2,10},{10... | collective-permute-start | bytes 786440 | tf_op jit(solution)/shard_map/ppermute | solution.py:42
  88.5 10.1 %collective-permute-start.32 = (bf16[64,2048]{1,0:T(8,128)(2,1)S(1)}, bf16[64,2048]{1,0:T(8,128)(2,1)S(1)}, u32[]{:S(2)}, u32[]{:S(2)}) collective-permute-start(bf16[64,2048]{1,0:T(8,128)(2,1)S(1)} %collective-permute-done.15.refs_2_), channel_id=1, source_target_pairs={{0,2},{2,6},{6,4},{4,0},{1,3},{3,7},{7,5},{5,1},{8,10},{10,14},{14... | collective-permute-start | bytes 786440 | tf_op jit(solution)/shard_map/ppermute | solution.py:291
  88.8 27.2 %collective-permute-start.29 = (bf16[192,2048]{1,0:T(8,128)(2,1)S(1)}, bf16[192,2048]{1,0:T(8,128)(2,1)S(1)}, u32[]{:S(2)}, u32[]{:S(2)}) collective-permute-start(bf16[192,2048]{1,0:T(8,128)(2,1)S(1)} %collective-permute-done.21.rest_0_.rest_2_), channel_id=1, source_target_pairs={{0,2},{2,6},{6,4},{4,0},{1,3},{3,7},{7,5},{5,1},{8,10},{10,14},{14... | collective-permute-start | bytes 2359304 | tf_op jit(solution)/shard_map/ppermute | solution.py:291
  93.5 4.3 %collective-permute-start.26 = (bf16[64,512]{1,0:T(8,128)(2,1)S(1)}, bf16[64,512]{1,0:T(8,128)(2,1)S(1)}, u32[]{:S(2)}, u32[]{:S(2)}) collective-permute-start(bf16[64,512]{1,0:T(8,128)(2,1)S(1)} %get-tuple-element.102), channel_id=1, source_target_pairs={{0,8},{8,0},{16,24},{24,16},{1,9},{9,1},{17,25},{25,17},{2,10},{10... | collective-permute-start | bytes 196616 | tf_op jit(solution)/shard_map/ppermute | solution.py:42
  94.1 10.3 %collective-permute-start.27 = (bf16[64,512]{1,0:T(8,128)(2,1)S(1)}, bf16[64,512]{1,0:T(8,128)(2,1)S(1)}, u32[]{:S(2)}, u32[]{:S(2)}) collective-permute-start(bf16[64,512]{1,0:T(8,128)(2,1)S(1)} %get-tuple-element.103), channel_id=1, source_target_pairs={{0,16},{8,24},{16,0},{24,8},{1,17},{9,25},{17,1},{25,9},{2,18},{10... | collective-permute-start | bytes 196616 | tf_op jit(solution)/shard_map/ppermute | solution.py:42
  96.5 11.4 %collective-permute-start.31 = (bf16[64,2048]{1,0:T(8,128)(2,1)S(1)}, bf16[64,2048]{1,0:T(8,128)(2,1)S(1)}, u32[]{:S(2)}, u32[]{:S(2)}) collective-permute-start(bf16[64,2048]{1,0:T(8,128)(2,1)S(1)} %collective-permute-done.22.refs_5_), channel_id=1, source_target_pairs={{0,16},{8,24},{16,0},{24,8},{1,17},{9,25},{17,1},{25,9},{2,18},{10... | collective-permute-start | bytes 786440 | tf_op jit(solution)/shard_map/ppermute | solution.py:42
  97.8 16.2 %collective-permute-start.35 = (bf16[64,2048]{1,0:T(8,128)(2,1)S(1)}, bf16[64,2048]{1,0:T(8,128)(2,1)S(1)}, u32[]{:S(2)}, u32[]{:S(2)}) collective-permute-start(bf16[64,2048]{1,0:T(8,128)(2,1)S(1)} %collective-permute-done.15.refs_2_), channel_id=1, source_target_pairs={{0,16},{8,24},{16,0},{24,8},{1,17},{9,25},{17,1},{25,9},{2,18},{10... | collective-permute-start | bytes 786440 | tf_op jit(solution)/shard_map/ppermute | solution.py:42
  98.6 16.3 %collective-permute-start.34 = (bf16[64,2048]{1,0:T(8,128)(2,1)S(1)}, bf16[64,2048]{1,0:T(8,128)(2,1)S(1)}, u32[]{:S(2)}, u32[]{:S(2)}) collective-permute-start(bf16[64,2048]{1,0:T(8,128)(2,1)S(1)} %collective-permute-done.32.refs_3_), channel_id=1, source_target_pairs={{0,8},{8,0},{16,24},{24,16},{1,9},{9,1},{17,25},{25,17},{2,10},{10... | collective-permute-start | bytes 786440 | tf_op jit(solution)/shard_map/ppermute | solution.py:42
  104.4 13.0 %collective-permute-start.28 = (bf16[192,512]{1,0:T(8,128)(2,1)S(1)}, bf16[192,512]{1,0:T(8,128)(2,1)S(1)}, u32[]{:S(2)}, u32[]{:S(2)}) collective-permute-start(bf16[192,512]{1,0:T(8,128)(2,1)S(1)} %shard_map.70), channel_id=1, source_target_pairs={{0,24},{8,16},{16,8},{24,0},{1,25},{9,17},{17,9},{25,1},{2,26},{10... | collective-permute-start | bytes 589832 | tf_op jit(solution)/shard_map/ppermute | solution.py:42
  107.9 15.7 %collective-permute-start.33 = (bf16[64,2048]{1,0:T(8,128)(2,1)S(1)}, bf16[64,2048]{1,0:T(8,128)(2,1)S(1)}, u32[]{:S(2)}, u32[]{:S(2)}) collective-permute-start(bf16[64,2048]{1,0:T(8,128)(2,1)S(1)} %collective-permute-done.15.refs_2_), channel_id=1, source_target_pairs={{0,8},{8,0},{16,24},{24,16},{1,9},{9,1},{17,25},{25,17},{2,10},{10... | collective-permute-start | bytes 786440 | tf_op jit(solution)/shard_map/ppermute | solution.py:42
  114.1 10.4 %collective-permute-start.36 = (bf16[64,2048]{1,0:T(8,128)(2,1)S(1)}, bf16[64,2048]{1,0:T(8,128)(2,1)S(1)}, u32[]{:S(2)}, u32[]{:S(2)}) collective-permute-start(bf16[64,2048]{1,0:T(8,128)(2,1)S(1)} %collective-permute-done.32.refs_3_), channel_id=1, source_target_pairs={{0,16},{8,24},{16,0},{24,8},{1,17},{9,25},{17,1},{25,9},{2,18},{10... | collective-permute-start | bytes 786440 | tf_op jit(solution)/shard_map/ppermute | solution.py:42
  115.0 11.3 %collective-permute-start.37 = (bf16[64,2048]{1,0:T(8,128)(2,1)S(1)}, bf16[64,2048]{1,0:T(8,128)(2,1)S(1)}, u32[]{:S(2)}, u32[]{:S(2)}) collective-permute-start(bf16[64,2048]{1,0:T(8,128)(2,1)S(1)} %collective-permute-done.35.refs_10_), channel_id=1, source_target_pairs={{0,8},{8,0},{16,24},{24,16},{1,9},{9,1},{17,25},{25,17},{2,10},{10... | collective-permute-start | bytes 786440 | tf_op jit(solution)/shard_map/ppermute | solution.py:42
  116.1 10.4 %collective-permute-start.38 = (bf16[64,2048]{1,0:T(8,128)(2,1)S(1)}, bf16[64,2048]{1,0:T(8,128)(2,1)S(1)}, u32[]{:S(2)}, u32[]{:S(2)}) collective-permute-start(bf16[64,2048]{1,0:T(8,128)(2,1)S(1)} %collective-permute-done.34.refs_7_), channel_id=1, source_target_pairs={{0,16},{8,24},{16,0},{24,8},{1,17},{9,25},{17,1},{25,9},{2,18},{10... | collective-permute-start | bytes 786440 | tf_op jit(solution)/shard_map/ppermute | solution.py:42
  122.7 4.3 %collective-permute-start.39 = (bf16[64,512]{1,0:T(8,128)(2,1)S(1)}, bf16[64,512]{1,0:T(8,128)(2,1)S(1)}, u32[]{:S(2)}, u32[]{:S(2)}) collective-permute-start(bf16[64,512]{1,0:T(8,128)(2,1)S(1)} %get-tuple-element.131), channel_id=1, source_target_pairs={{0,8},{8,0},{16,24},{24,16},{1,9},{9,1},{17,25},{25,17},{2,10},{10... | collective-permute-start | bytes 196616 | tf_op jit(solution)/shard_map/ppermute | solution.py:42
  123.6 4.3 %collective-permute-start.40 = (bf16[64,512]{1,0:T(8,128)(2,1)S(1)}, bf16[64,512]{1,0:T(8,128)(2,1)S(1)}, u32[]{:S(2)}, u32[]{:S(2)}) collective-permute-start(bf16[64,512]{1,0:T(8,128)(2,1)S(1)} %get-tuple-element.134), channel_id=1, source_target_pairs={{0,16},{8,24},{16,0},{24,8},{1,17},{9,25},{17,1},{25,9},{2,18},{10... | collective-permute-start | bytes 196616 | tf_op jit(solution)/shard_map/ppermute | solution.py:42
  124.5 5.2 %collective-permute-start.41 = (bf16[64,512]{1,0:T(8,128)(2,1)S(1)}, bf16[64,512]{1,0:T(8,128)(2,1)S(1)}, u32[]{:S(2)}, u32[]{:S(2)}) collective-permute-start(bf16[64,512]{1,0:T(8,128)(2,1)S(1)} %get-tuple-element.136), channel_id=1, source_target_pairs={{0,24},{8,16},{16,8},{24,0},{1,25},{9,17},{17,9},{25,1},{2,26},{10... | collective-permute-start | bytes 196616 | tf_op jit(solution)/shard_map/ppermute | solution.py:42
  131.5 2.7 %collective-permute-start.42 = (bf16[256,2048]{1,0:T(8,128)(2,1)S(1)}, bf16[256,2048]{1,0:T(8,128)(2,1)S(1)}, u32[]{:S(2)}, u32[]{:S(2)}) collective-permute-start(bf16[256,2048]{1,0:T(8,128)(2,1)S(1)} %shard_map.73), channel_id=1, source_target_pairs={{0,1},{1,0},{2,3},{3,2},{4,5},{5,4},{6,7},{7,6},{8,9},{9,8},{10,11... | collective-permute-start | bytes 3145736 | tf_op jit(solution)/shard_map/ppermute | solution.py:37
